TPU v7x, 32 devices: a whole 2x2x4 slice. The times are simulated.
32 devices in a mesh: section: 2 (over x), ctx: 4 (over y, core), tp: 4 (over z).
Axes of the slice: x: 2, y: 2, z: 4, core: 2. Of those that a mesh axis runs over, the one named last changes fastest.
Arguments:
- tokens_in: bfloat16 [8, 1024, 1, 2048], P(None, ('ctx', 'tp')), may hold values from -6 to 6
- cotangent: bfloat16 [8, 1024, 1, 2048], P(None, ('ctx', 'tp')), may hold values from -6 to 6
- plan: int32 [8], replicated, may hold values from 0 to 7, each once
- positions: int32 [1, 1024], replicated, may hold values from 0 to 2047, as said below
- norm_gain: float32 [2, 2, 2048], P('section'), may hold values from 0.5 to 1.5
- norm_shift: float32 [2, 2, 2048], P('section'), may hold values from -2 to 2
- w_qkv: bfloat16 [2, 3, 2048, 2048], P('section', None, None, 'tp'), may hold values from -0.125 to 0.125
- b_qkv: float32 [2, 3, 2048], P('section', None, 'tp'), may hold values from -2 to 2
- w_out: bfloat16 [2, 2048, 2048], P('section', 'tp'), may hold values from -1.5 to 1.5
- w_gate_up: bfloat16 [2, 2, 2048, 5632], P('section', None, None, 'tp'), may hold values from -0.125 to 0.125
- down_weight: bfloat16 [2, 5632, 2048], P('section', 'tp'), may hold values from -0.078125 to 0.078125
Outputs:
- section_ends: bfloat16 [2, 8, 1024, 1, 2048], P('section', None, ('ctx', 'tp'))
- grad_gain: float32 [2, 2, 2048], P('section', None, ('ctx', 'tp'))
- grad_shift: float32 [2, 2, 2048], P('section', None, ('ctx', 'tp'))
- grad_bias: float32 [2, 3, 2048], P('section', None, ('ctx', 'tp'))
- grad_qkv: float32 [2, 3, 2048, 2048], P('section', None, 'ctx', 'tp')
- grad_out: float32 [2, 2048, 2048], P('section', 'tp', 'ctx')
- grad_gate_up: float32 [2, 2, 2048, 5632], P('section', None, 'ctx', 'tp')
- grad_down: float32 [2, 5632, 2048], P('section', 'tp', 'ctx')
Inputs may be any that keep to these rules, and one draw needn't show every extreme that they name: Each sequence's positions rise strictly from one token to the next, by 1 to 3; every sequence starts at the least and ends at the most.
All inputs are finite; a program needn't handle non-finite values.
Results may differ from a plain program's by a relative error of at most 0.02.
Values may be sent and summed in bfloat16 or wider, within the bound.
No kernel may reach another device: no remote copies, remote signals or barrier semaphores. Data moves between devices by JAX's collectives and lax.ppermute only.
A program may use at most 320 MiB of HBM per device.

v0:
```python
import jax
import jax.numpy as jnp
from jax import lax
from jax.sharding import PartitionSpec as P

HEAD_WIDTH = 64
ROT = 16


def passed_along(block, axis, distance):
    devices = range(lax.axis_size(axis))
    route = [(i - distance, i) for i in devices if i - distance in devices]
    return lax.ppermute(block, axis, route)


def normalize(stream, gain_vec, shift_vec):
    centre = stream - jnp.mean(stream, axis=-1, keepdims=True)
    spread = jnp.mean(centre * centre, axis=-1, keepdims=True)
    return centre * lax.rsqrt(spread + 1e-05) * gain_vec + shift_vec


def norm_back(stream, grad_in, gain_vec):
    centre = stream - jnp.mean(stream, axis=-1, keepdims=True)
    inv_std = lax.rsqrt(jnp.mean(centre * centre, axis=-1, keepdims=True) + 1e-05)
    unit = centre * inv_std
    scaled = grad_in * gain_vec
    result = inv_std * (
        scaled
        - jnp.mean(scaled, axis=-1, keepdims=True)
        - unit * jnp.mean(scaled * unit, axis=-1, keepdims=True)
    )
    return (result, jnp.sum(grad_in * unit, axis=(0, 1)), jnp.sum(grad_in, axis=(0, 1)))


def rotary(tensor, cosine, sine):
    half_rot = ROT // 2
    front = tensor[..., :ROT]
    turned = jnp.concatenate([-front[..., half_rot:], front[..., :half_rot]], axis=-1)
    return jnp.concatenate([front * cosine + turned * sine, tensor[..., ROT:]], axis=-1)


def unrotary(tensor, cosine, sine):
    half_rot = ROT // 2
    front = tensor[..., :ROT]
    turned = jnp.concatenate([-front[..., half_rot:], front[..., :half_rot]], axis=-1)
    return jnp.concatenate([front * cosine - turned * sine, tensor[..., ROT:]], axis=-1)


def tables(position_rows):
    freqs = 10000.0 ** (-jnp.arange(ROT // 2, dtype=jnp.float32) * 2.0 / ROT)
    angles = position_rows.T.astype(jnp.float32)[:, :, None] * freqs
    angles = jnp.concatenate([angles, angles], axis=-1)[:, :, None, :]
    return (jnp.cos(angles), jnp.sin(angles))


def attention_scores(queries, key_heads, allowed):
    scores = jnp.einsum(
        "qshe,kshe->shqk", queries, key_heads, preferred_element_type=jnp.float32
    ) * HEAD_WIDTH ** (-0.5)
    return jnp.where(allowed, scores, -1e30)


def forward_layer(layer_in, weights, context_rows):
    gain_vec, shift_vec, w_qkv, b_qkv, w_out, w_gate_up, down_weight = weights
    cosine, sine, allowed = context_rows
    normed = normalize(layer_in, gain_vec[0], shift_vec[0]).astype(jnp.bfloat16)
    normed_all = lax.all_gather(normed, "tp", axis=0, tiled=True)
    block_len, seq_count, width = normed_all.shape
    columns = w_qkv.shape[2]
    head_count = columns // HEAD_WIDTH
    mixed = (
        jnp.einsum("rsd,cde->crse", normed_all, w_qkv, preferred_element_type=jnp.float32)
        + b_qkv[:, None, None, :]
    )
    queries = rotary(
        mixed[0].reshape(block_len, seq_count, head_count, HEAD_WIDTH), cosine, sine
    ).astype(jnp.bfloat16)
    key_own = rotary(
        mixed[1].reshape(block_len, seq_count, head_count, HEAD_WIDTH), cosine, sine
    ).astype(jnp.bfloat16)
    key_own = key_own.reshape(block_len, seq_count, columns)
    value_own = mixed[2].astype(jnp.bfloat16)
    key_all, value_all = (
        lax.all_gather(key_own, "ctx", axis=0, tiled=True),
        lax.all_gather(value_own, "ctx", axis=0, tiled=True),
    )
    key_heads = key_all.reshape(key_all.shape[0], seq_count, head_count, HEAD_WIDTH)
    value_heads = value_all.reshape(value_all.shape[0], seq_count, head_count, HEAD_WIDTH)
    scores = attention_scores(queries, key_heads, allowed)
    top_score = jnp.max(scores, axis=-1, keepdims=True)
    log_total = top_score + jnp.log(jnp.sum(jnp.exp(scores - top_score), axis=-1, keepdims=True))
    probability = jnp.exp(scores - log_total)
    attended = jnp.einsum(
        "shqk,kshe->qshe",
        probability.astype(jnp.bfloat16),
        value_heads,
        preferred_element_type=jnp.float32,
    )
    attended = attended.astype(jnp.bfloat16).reshape(block_len, seq_count, columns)
    piece = attended
    hidden_state = layer_in + lax.psum_scatter(
        jnp.einsum("rse,ed->rsd", piece, w_out, preferred_element_type=jnp.float32).astype(
            jnp.bfloat16
        ),
        "tp",
        scatter_dimension=0,
        tiled=True,
    ).astype(jnp.float32)
    normed_two = normalize(hidden_state, gain_vec[1], shift_vec[1]).astype(jnp.bfloat16)
    normed_two_all = lax.all_gather(normed_two, "tp", axis=0, tiled=True)
    gate_up = jnp.einsum(
        "rsd,cdf->crsf", normed_two_all, w_gate_up, preferred_element_type=jnp.float32
    )
    gated_activation = (jax.nn.silu(gate_up[0]) * gate_up[1]).astype(jnp.bfloat16)
    piece = gated_activation
    layer_out = hidden_state + lax.psum_scatter(
        jnp.einsum("rsf,fd->rsd", piece, down_weight, preferred_element_type=jnp.float32).astype(
            jnp.bfloat16
        ),
        "tp",
        scatter_dimension=0,
        tiled=True,
    ).astype(jnp.float32)
    stored = (
        layer_in,
        normed_all,
        queries,
        key_all,
        value_all,
        log_total,
        attended,
        hidden_state,
        normed_two_all,
        gate_up,
    )
    return (layer_out, stored)


def backward_layer(grad_out, stored, weights, context_rows):
    gain_vec, shift_vec, w_qkv, b_qkv, w_out, w_gate_up, down_weight = weights
    cosine, sine, allowed = context_rows
    (
        layer_in,
        normed_all,
        queries,
        key_all,
        value_all,
        log_total,
        attended,
        hidden_state,
        normed_two_all,
        gate_up,
    ) = stored
    block_len, seq_count, columns = attended.shape
    head_count = columns // HEAD_WIDTH
    mlp_grad = lax.all_gather(grad_out.astype(jnp.bfloat16), "tp", axis=0, tiled=True)
    gate_part = gate_up[0]
    up_part = gate_up[1]
    sigma = jax.nn.sigmoid(gate_part)
    swish = gate_part * sigma
    gated_activation = (swish * up_part).astype(jnp.bfloat16)
    down_grad = jnp.einsum(
        "rsf,rsd->fd", gated_activation, mlp_grad, preferred_element_type=jnp.float32
    )
    act_grad = jnp.einsum("rsd,fd->rsf", mlp_grad, down_weight, preferred_element_type=jnp.float32)
    gate_up_grad = jnp.stack(
        [act_grad * up_part * sigma * (1.0 + gate_part * (1.0 - sigma)), act_grad * swish]
    ).astype(jnp.bfloat16)
    gu_grad = jnp.einsum(
        "rsd,crsf->cdf", normed_two_all, gate_up_grad, preferred_element_type=jnp.float32
    )
    piece = gate_up_grad
    two_grad = lax.psum_scatter(
        jnp.einsum("crsf,cdf->rsd", piece, w_gate_up, preferred_element_type=jnp.float32).astype(
            jnp.bfloat16
        ),
        "tp",
        scatter_dimension=0,
        tiled=True,
    ).astype(jnp.float32)
    hidden_grad, gain_two, shift_two = norm_back(hidden_state, two_grad, gain_vec[1])
    hidden_grad = grad_out + hidden_grad
    attn_grad = lax.all_gather(hidden_grad.astype(jnp.bfloat16), "tp", axis=0, tiled=True)
    out_grad = jnp.einsum("rse,rsd->ed", attended, attn_grad, preferred_element_type=jnp.float32)
    ctx_grad = jnp.einsum("rsd,ed->rse", attn_grad, w_out, preferred_element_type=jnp.float32)
    ctx_grad = ctx_grad.astype(jnp.bfloat16).reshape(block_len, seq_count, head_count, HEAD_WIDTH)
    key_heads = key_all.reshape(key_all.shape[0], seq_count, head_count, HEAD_WIDTH)
    value_heads = value_all.reshape(value_all.shape[0], seq_count, head_count, HEAD_WIDTH)
    scores = attention_scores(queries, key_heads, allowed)
    probability = jnp.exp(scores - log_total)
    value_grad = jnp.einsum(
        "shqk,qshe->kshe",
        probability.astype(jnp.bfloat16),
        ctx_grad,
        preferred_element_type=jnp.float32,
    )
    prob_grad = jnp.einsum(
        "qshe,kshe->shqk", ctx_grad, value_heads, preferred_element_type=jnp.float32
    )
    score_grad = probability * (
        prob_grad - jnp.sum(probability * prob_grad, axis=-1, keepdims=True)
    )
    score_grad = score_grad.astype(jnp.bfloat16)
    query_grad = jnp.einsum(
        "shqk,kshe->qshe", score_grad, key_heads, preferred_element_type=jnp.float32
    ) * HEAD_WIDTH ** (-0.5)
    key_grad = jnp.einsum(
        "shqk,qshe->kshe", score_grad, queries, preferred_element_type=jnp.float32
    ) * HEAD_WIDTH ** (-0.5)
    key_back, value_back = (
        lax.psum_scatter(
            key_grad.astype(jnp.bfloat16), "ctx", scatter_dimension=0, tiled=True
        ).astype(jnp.float32),
        lax.psum_scatter(
            value_grad.astype(jnp.bfloat16), "ctx", scatter_dimension=0, tiled=True
        ).astype(jnp.float32),
    )
    qkv_grad = jnp.stack(
        [
            unrotary(query_grad, cosine, sine).reshape(block_len, seq_count, columns),
            unrotary(key_back, cosine, sine).reshape(block_len, seq_count, columns),
            value_back.reshape(block_len, seq_count, columns),
        ]
    ).astype(jnp.bfloat16)
    bias_grad = jnp.sum(qkv_grad.astype(jnp.float32), axis=(1, 2))
    qkv_weight_grad = jnp.einsum(
        "rsd,crse->cde", normed_all, qkv_grad, preferred_element_type=jnp.float32
    )
    piece = qkv_grad
    one_grad = lax.psum_scatter(
        jnp.einsum("crse,cde->rsd", piece, w_qkv, preferred_element_type=jnp.float32).astype(
            jnp.bfloat16
        ),
        "tp",
        scatter_dimension=0,
        tiled=True,
    ).astype(jnp.float32)
    input_grad, gain_one, shift_one = norm_back(layer_in, one_grad, gain_vec[0])
    input_grad = hidden_grad + input_grad
    weight_terms = (qkv_weight_grad, out_grad, gu_grad, down_grad)
    return (
        input_grad,
        (
            weight_terms,
            jnp.stack([gain_one, gain_two]),
            jnp.stack([shift_one, shift_two]),
            bias_grad,
        ),
    )


def spread(terms, columns, tp_index):
    weight_terms, gain_terms, shift_terms, bias_terms = terms
    qkv_term, out_term, gu_term, down_term = weight_terms
    scattered = (
        lax.psum_scatter(
            qkv_term.astype(jnp.bfloat16), "ctx", scatter_dimension=1, tiled=True
        ).astype(jnp.float32),
        lax.psum_scatter(
            out_term.astype(jnp.bfloat16), "ctx", scatter_dimension=1, tiled=True
        ).astype(jnp.float32),
        lax.psum_scatter(
            gu_term.astype(jnp.bfloat16), "ctx", scatter_dimension=1, tiled=True
        ).astype(jnp.float32),
        lax.psum_scatter(
            down_term.astype(jnp.bfloat16), "ctx", scatter_dimension=1, tiled=True
        ).astype(jnp.float32),
    )
    bias_full = lax.dynamic_update_slice_in_dim(
        jnp.zeros((3, gain_terms.shape[1]), jnp.float32), bias_terms, tp_index * columns, 1
    )
    gain_part, shift_part, bias_part = (
        lax.psum_scatter(gain_terms, ("ctx", "tp"), scatter_dimension=1, tiled=True),
        lax.psum_scatter(shift_terms, ("ctx", "tp"), scatter_dimension=1, tiled=True),
        lax.psum_scatter(bias_full, ("ctx", "tp"), scatter_dimension=1, tiled=True),
    )
    return (tuple(scattered), gain_part, shift_part, bias_part)


def per_device(
    tokens_in,
    cotangent,
    plan,
    positions,
    norm_gain,
    norm_shift,
    w_qkv,
    b_qkv,
    w_out,
    w_gate_up,
    down_weight,
):
    weights = (
        norm_gain[0],
        norm_shift[0],
        w_qkv[0],
        b_qkv[0],
        w_out[0],
        w_gate_up[0],
        down_weight[0],
    )
    micro_count = tokens_in.shape[0]
    local_row_slice = tokens_in.shape[1]
    width = tokens_in.shape[3]
    columns = w_qkv.shape[3]
    ff_local = w_gate_up.shape[3]
    tp_count = lax.axis_size("tp")
    ctx_count = lax.axis_size("ctx")
    block_len = local_row_slice * tp_count
    section_index = lax.axis_index("section")
    ctx_index = lax.axis_index("ctx")
    tp_index = lax.axis_index("tp")
    block_pos = lax.dynamic_slice_in_dim(positions, ctx_index * block_len, block_len, 1)
    cosine, sine = tables(block_pos)
    allowed = (positions[:, None, :] <= block_pos[:, :, None])[:, None]
    context_rows = (cosine, sine, allowed)
    zero_rows = jnp.zeros(tokens_in.shape[1:], jnp.bfloat16)

    def forward_step(carry, step_index):
        arriving = passed_along(carry, "section", 1)
        micro = jnp.clip(step_index, 0, micro_count - 1)
        fresh = lax.dynamic_index_in_dim(tokens_in, plan[micro], 0, keepdims=False)
        layer_in = jnp.where(section_index == 0, fresh, arriving).astype(jnp.float32)
        layer_out, stored = forward_layer(layer_in, weights, context_rows)
        sent = layer_out.astype(jnp.bfloat16)
        return (sent, (sent, stored))

    steps_all = jnp.arange(micro_count + 1, dtype=jnp.int32)
    unused, (outputs, stored_all) = lax.scan(forward_step, zero_rows, steps_all)
    share = width // ctx_count
    fine_share = width // (ctx_count * tp_count)
    totals = (
        (
            jnp.zeros((3, share, columns), jnp.float32),
            jnp.zeros((columns, share), jnp.float32),
            jnp.zeros((2, share, ff_local), jnp.float32),
            jnp.zeros((ff_local, share), jnp.float32),
        ),
        jnp.zeros((2, fine_share), jnp.float32),
        jnp.zeros((2, fine_share), jnp.float32),
        jnp.zeros((3, fine_share), jnp.float32),
    )

    def backward_step(carry, bundle):
        send_back, running = carry
        step_index, stored = bundle
        arriving = passed_along(send_back, "section", -1)
        micro = step_index - section_index
        valid_step = ((micro >= 0) & (micro < micro_count)).astype(jnp.float32)
        target = lax.dynamic_index_in_dim(
            cotangent, jnp.clip(micro, 0, micro_count - 1), 0, keepdims=False
        )
        grad_out = jnp.where(section_index == 1, target, arriving).astype(jnp.float32)
        input_grad, terms = backward_layer(grad_out, stored, weights, context_rows)
        terms = jax.tree.map(lambda tensor: tensor * valid_step, terms)
        terms = spread(terms, columns, tp_index)
        running = jax.tree.map(jnp.add, running, terms)
        sent = input_grad.astype(jnp.bfloat16)
        return ((sent, running), sent)

    (unused_back, totals), input_grads = lax.scan(
        backward_step, (zero_rows, totals), (steps_all, stored_all), reverse=True
    )
    weight_parts, gain_part, shift_part, bias_part = totals
    section_ends = jnp.where(section_index == 0, input_grads[:micro_count], outputs[1:])[None]
    return (
        section_ends,
        gain_part[None],
        shift_part[None],
        bias_part[None],
        weight_parts[0][None],
        weight_parts[1][None],
        weight_parts[2][None],
        weight_parts[3][None],
    )


def solution(mesh):
    placed = (
        P(None, ("ctx", "tp"), None, None),
        P(None, ("ctx", "tp"), None, None),
        P(),
        P(),
        P("section", None, None),
        P("section", None, None),
        P("section", None, None, "tp"),
        P("section", None, "tp"),
        P("section", "tp", None),
        P("section", None, None, "tp"),
        P("section", "tp", None),
    )
    return jax.shard_map(
        per_device,
        mesh=mesh,
        in_specs=placed,
        out_specs=(
            P("section", None, ("ctx", "tp"), None, None),
            P("section", None, ("ctx", "tp")),
            P("section", None, ("ctx", "tp")),
            P("section", None, ("ctx", "tp")),
            P("section", None, "ctx", "tp"),
            P("section", "tp", "ctx"),
            P("section", None, "ctx", "tp"),
            P("section", "tp", "ctx"),
        ),
        check_vma=False,
    )
```

profile of v0, /device:TPU:0, one launch (start us, length us, event | category | flops | bytes accessed | tf_op | source)
XLA Modules:
  0.0 7629.6 jit_solution(3929320735889003535)
XLA Ops:
  11.0 1768.6 %while.66 = (s32[]{:T(128)}, bf16[64,1,2048]{2,0,1:T(8,128)(2,1)}, bf16[9,64,1,2048]{3,1,2,0:T(8,128)(2,1)}, f32[9,64,1,2048]{3,1,2,0:T(8,128)}, bf16[9,256,1,20...) while((s32[]{:T(128)}, bf16[64,1,2048]{2,0,1:T(8,128)(2,1)}, ...), condition=%wide.region_9.10_spmd.clone, body=%wide.region_0.9_spmd.clone.sunk | while | flops 7148042240 | bytes 175899984 | solution.py:329
  1781.5 5828.1 %while.67 = (s32[]{:T(128)}, bf16[64,1,2048]{2,0,1:T(8,128)(2,1)}, f32[3,512,512]{1,2,0:T(8,128)}, f32[512,512]{1,0:T(8,128)}, f32[2,512,1408]{1,2,0:T(8,128)}, ...) while((s32[]{:T(128)}, bf16[64,1,2048]{2,0,1:T(8,128)(2,1)}, ...), condition=%wide.region_36.37_spmd.clone, body=%wide.region_10.36_spmd.clone.sunk | while | flops 14585109504 | bytes 457771648 | solution.py:361
  2034.9 34.8 reduce-scatter.50.cloned.1.call-done
  2070.6 32.8 reduce-scatter.40.cloned.1.call-done
  2108.1 56.7 reduce-scatter.46.cloned.1.call-done
  2165.7 59.0 reduce-scatter.48.cloned.1.call-done
  2225.6 56.1 reduce-scatter.44.cloned.1.call-done
  2285.1 57.4 reduce-scatter.38.cloned.1.call-done
  2345.0 92.2 %reduce-scatter.42.cloned.1.call-done = bf16[2,512,1408]{1,2,0:T(8,128)(2,1)} async-done(((bf16[2,2048,1408]{1,2,0:T(8,128)(2,1)}), bf16[2,512,1408]{1,2,0:T(8,128)(2,1)}) %reduce-scatter.42.cloned.1.call-update) | async-done | bytes 2883600 | tf_op jit(solution)/shard_map/while/body/eval_jaxpr/reduce_scatter | solution.py:262
  2679.0 34.7 reduce-scatter.50.cloned.1.call-done
  2714.6 32.8 reduce-scatter.40.cloned.1.call-done
  2752.4 56.3 reduce-scatter.46.cloned.1.call-done
  2809.6 59.2 reduce-scatter.48.cloned.1.call-done
  2869.7 56.1 reduce-scatter.44.cloned.1.call-done
  2930.1 56.7 reduce-scatter.38.cloned.1.call-done
  2989.2 92.4 %reduce-scatter.42.cloned.1.call-done = bf16[2,512,1408]{1,2,0:T(8,128)(2,1)} async-done(((bf16[2,2048,1408]{1,2,0:T(8,128)(2,1)}), bf16[2,512,1408]{1,2,0:T(8,128)(2,1)}) %reduce-scatter.42.cloned.1.call-update) | async-done | bytes 2883600 | tf_op jit(solution)/shard_map/while/body/eval_jaxpr/reduce_scatter | solution.py:262
  3325.2 34.7 reduce-scatter.50.cloned.1.call-done
  3398.5 56.5 reduce-scatter.46.cloned.1.call-done
  3455.9 59.1 reduce-scatter.48.cloned.1.call-done
  3516.0 56.1 reduce-scatter.44.cloned.1.call-done
  3576.4 56.5 reduce-scatter.38.cloned.1.call-done
  3635.3 92.2 %reduce-scatter.42.cloned.1.call-done = bf16[2,512,1408]{1,2,0:T(8,128)(2,1)} async-done(((bf16[2,2048,1408]{1,2,0:T(8,128)(2,1)}), bf16[2,512,1408]{1,2,0:T(8,128)(2,1)}) %reduce-scatter.42.cloned.1.call-update) | async-done | bytes 2883600 | tf_op jit(solution)/shard_map/while/body/eval_jaxpr/reduce_scatter | solution.py:262
  3971.0 34.6 reduce-scatter.50.cloned.1.call-done
  4006.6 32.8 reduce-scatter.40.cloned.1.call-done
  4044.4 56.4 reduce-scatter.46.cloned.1.call-done
  4101.7 59.0 reduce-scatter.48.cloned.1.call-done
  4161.7 55.9 reduce-scatter.44.cloned.1.call-done
  4221.8 56.5 reduce-scatter.38.cloned.1.call-done
  4280.8 92.4 %reduce-scatter.42.cloned.1.call-done = bf16[2,512,1408]{1,2,0:T(8,128)(2,1)} async-done(((bf16[2,2048,1408]{1,2,0:T(8,128)(2,1)}), bf16[2,512,1408]{1,2,0:T(8,128)(2,1)}) %reduce-scatter.42.cloned.1.call-update) | async-done | bytes 2883600 | tf_op jit(solution)/shard_map/while/body/eval_jaxpr/reduce_scatter | solution.py:262
  4616.9 34.8 reduce-scatter.50.cloned.1.call-done
  4652.6 32.8 reduce-scatter.40.cloned.1.call-done
  4690.4 56.4 reduce-scatter.46.cloned.1.call-done
  4747.6 59.2 reduce-scatter.48.cloned.1.call-done
  4807.7 56.0 reduce-scatter.44.cloned.1.call-done
  4868.0 56.5 reduce-scatter.38.cloned.1.call-done
  4926.9 92.2 %reduce-scatter.42.cloned.1.call-done = bf16[2,512,1408]{1,2,0:T(8,128)(2,1)} async-done(((bf16[2,2048,1408]{1,2,0:T(8,128)(2,1)}), bf16[2,512,1408]{1,2,0:T(8,128)(2,1)}) %reduce-scatter.42.cloned.1.call-update) | async-done | bytes 2883600 | tf_op jit(solution)/shard_map/while/body/eval_jaxpr/reduce_scatter | solution.py:262
  5262.6 34.8 reduce-scatter.50.cloned.1.call-done
  5298.3 32.7 reduce-scatter.40.cloned.1.call-done
  5336.0 56.5 reduce-scatter.46.cloned.1.call-done
  5393.5 59.1 reduce-scatter.48.cloned.1.call-done
  5453.5 55.9 reduce-scatter.44.cloned.1.call-done
  5513.7 56.7 reduce-scatter.38.cloned.1.call-done
  5572.8 92.3 %reduce-scatter.42.cloned.1.call-done = bf16[2,512,1408]{1,2,0:T(8,128)(2,1)} async-done(((bf16[2,2048,1408]{1,2,0:T(8,128)(2,1)}), bf16[2,512,1408]{1,2,0:T(8,128)(2,1)}) %reduce-scatter.42.cloned.1.call-update) | async-done | bytes 2883600 | tf_op jit(solution)/shard_map/while/body/eval_jaxpr/reduce_scatter | solution.py:262
  5908.8 34.8 reduce-scatter.50.cloned.1.call-done
  5944.5 32.6 reduce-scatter.40.cloned.1.call-done
  5982.2 56.4 reduce-scatter.46.cloned.1.call-done
  6039.5 59.0 reduce-scatter.48.cloned.1.call-done
  6099.4 56.1 reduce-scatter.44.cloned.1.call-done
  6159.7 56.5 reduce-scatter.38.cloned.1.call-done
  6218.7 92.3 %reduce-scatter.42.cloned.1.call-done = bf16[2,512,1408]{1,2,0:T(8,128)(2,1)} async-done(((bf16[2,2048,1408]{1,2,0:T(8,128)(2,1)}), bf16[2,512,1408]{1,2,0:T(8,128)(2,1)}) %reduce-scatter.42.cloned.1.call-update) | async-done | bytes 2883600 | tf_op jit(solution)/shard_map/while/body/eval_jaxpr/reduce_scatter | solution.py:262
  6554.5 34.7 reduce-scatter.50.cloned.1.call-done
  6590.1 32.7 reduce-scatter.40.cloned.1.call-done
  6627.8 56.4 reduce-scatter.46.cloned.1.call-done
  6685.1 59.2 reduce-scatter.48.cloned.1.call-done
  6745.2 55.9 reduce-scatter.44.cloned.1.call-done
  6805.4 56.7 reduce-scatter.38.cloned.1.call-done
  6864.5 92.4 %reduce-scatter.42.cloned.1.call-done = bf16[2,512,1408]{1,2,0:T(8,128)(2,1)} async-done(((bf16[2,2048,1408]{1,2,0:T(8,128)(2,1)}), bf16[2,512,1408]{1,2,0:T(8,128)(2,1)}) %reduce-scatter.42.cloned.1.call-update) | async-done | bytes 2883600 | tf_op jit(solution)/shard_map/while/body/eval_jaxpr/reduce_scatter | solution.py:262
  7200.4 34.7 reduce-scatter.50.cloned.1.call-done
  7236.0 32.6 reduce-scatter.40.cloned.1.call-done
  7273.6 56.4 reduce-scatter.46.cloned.1.call-done
  7330.9 59.2 reduce-scatter.48.cloned.1.call-done
  7391.0 55.9 reduce-scatter.44.cloned.1.call-done
  7451.2 56.7 reduce-scatter.38.cloned.1.call-done
  7510.3 92.4 %reduce-scatter.42.cloned.1.call-done = bf16[2,512,1408]{1,2,0:T(8,128)(2,1)} async-done(((bf16[2,2048,1408]{1,2,0:T(8,128)(2,1)}), bf16[2,512,1408]{1,2,0:T(8,128)(2,1)}) %reduce-scatter.42.cloned.1.call-update) | async-done | bytes 2883600 | tf_op jit(solution)/shard_map/while/body/eval_jaxpr/reduce_scatter | solution.py:262
  (2121 shorter events, 4098.6 us)
Async XLA Ops:
  1982.2 87.5 %reduce-scatter.50.cloned.1.call-start = ((), (), s32[]{:S(2)}) async-start(), calls=%async_computation.31 | async-start | bytes 1114112 | tf_op jit(solution)/shard_map/while
  1984.1 119.3 %reduce-scatter.40.cloned.1.call-start = ((), (), s32[]{:S(2)}) async-start(), calls=%async_computation.26 | async-start | bytes 2621440 | tf_op jit(solution)/shard_map/while/body/eval_jaxpr/reduce_scatter | solution.py:259
  1987.2 177.7 %reduce-scatter.46.cloned.1.call-start = ((), (), s32[]{:S(2)}) async-start(), calls=%async_computation.29 | async-start | bytes 1114112 | tf_op jit(solution)/shard_map/while
  2012.5 212.2 %reduce-scatter.48.cloned.1.call-start = ((), (), s32[]{:S(2)}) async-start(), calls=%async_computation.30 | async-start | bytes 1114112 | tf_op jit(solution)/shard_map/while
  2014.0 267.7 %reduce-scatter.44.cloned.1.call-start = ((), (), s32[]{:S(2)}) async-start(), calls=%async_computation.28 | async-start | bytes 7208960 | tf_op jit(solution)/shard_map/while/body/eval_jaxpr/reduce_scatter | solution.py:265
  2020.2 322.3 %reduce-scatter.38.cloned.1.call-start = ((), (), s32[]{:S(2)}) async-start(), calls=%async_computation.25 | async-start | bytes 7864320 | tf_op jit(solution)/shard_map/while/body/eval_jaxpr/reduce_scatter | solution.py:256
  2026.2 411.0 %reduce-scatter.42.cloned.1.call-start = ((), (), s32[]{:S(2)}) async-start(), calls=%async_computation.27 | async-start | bytes 14417920 | tf_op jit(solution)/shard_map/while/body/eval_jaxpr/reduce_scatter | solution.py:262
  2626.4 87.3 %reduce-scatter.50.cloned.1.call-start = ((), (), s32[]{:S(2)}) async-start(), calls=%async_computation.31 | async-start | bytes 1114112 | tf_op jit(solution)/shard_map/while
  2628.2 119.2 %reduce-scatter.40.cloned.1.call-start = ((), (), s32[]{:S(2)}) async-start(), calls=%async_computation.26 | async-start | bytes 2621440 | tf_op jit(solution)/shard_map/while/body/eval_jaxpr/reduce_scatter | solution.py:259
  2631.3 177.5 %reduce-scatter.46.cloned.1.call-start = ((), (), s32[]{:S(2)}) async-start(), calls=%async_computation.29 | async-start | bytes 1114112 | tf_op jit(solution)/shard_map/while
  2656.6 212.2 %reduce-scatter.48.cloned.1.call-start = ((), (), s32[]{:S(2)}) async-start(), calls=%async_computation.30 | async-start | bytes 1114112 | tf_op jit(solution)/shard_map/while
  2658.1 267.7 %reduce-scatter.44.cloned.1.call-start = ((), (), s32[]{:S(2)}) async-start(), calls=%async_computation.28 | async-start | bytes 7208960 | tf_op jit(solution)/shard_map/while/body/eval_jaxpr/reduce_scatter | solution.py:265
  2664.3 322.4 %reduce-scatter.38.cloned.1.call-start = ((), (), s32[]{:S(2)}) async-start(), calls=%async_computation.25 | async-start | bytes 7864320 | tf_op jit(solution)/shard_map/while/body/eval_jaxpr/reduce_scatter | solution.py:256
  2670.3 411.3 %reduce-scatter.42.cloned.1.call-start = ((), (), s32[]{:S(2)}) async-start(), calls=%async_computation.27 | async-start | bytes 14417920 | tf_op jit(solution)/shard_map/while/body/eval_jaxpr/reduce_scatter | solution.py:262
  3272.6 87.3 %reduce-scatter.50.cloned.1.call-start = ((), (), s32[]{:S(2)}) async-start(), calls=%async_computation.31 | async-start | bytes 1114112 | tf_op jit(solution)/shard_map/while
  3274.4 119.0 %reduce-scatter.40.cloned.1.call-start = ((), (), s32[]{:S(2)}) async-start(), calls=%async_computation.26 | async-start | bytes 2621440 | tf_op jit(solution)/shard_map/while/body/eval_jaxpr/reduce_scatter | solution.py:259
  3277.5 177.5 %reduce-scatter.46.cloned.1.call-start = ((), (), s32[]{:S(2)}) async-start(), calls=%async_computation.29 | async-start | bytes 1114112 | tf_op jit(solution)/shard_map/while
  3302.9 212.2 %reduce-scatter.48.cloned.1.call-start = ((), (), s32[]{:S(2)}) async-start(), calls=%async_computation.30 | async-start | bytes 1114112 | tf_op jit(solution)/shard_map/while
  3304.3 267.8 %reduce-scatter.44.cloned.1.call-start = ((), (), s32[]{:S(2)}) async-start(), calls=%async_computation.28 | async-start | bytes 7208960 | tf_op jit(solution)/shard_map/while/body/eval_jaxpr/reduce_scatter | solution.py:265
  3310.6 322.3 %reduce-scatter.38.cloned.1.call-start = ((), (), s32[]{:S(2)}) async-start(), calls=%async_computation.25 | async-start | bytes 7864320 | tf_op jit(solution)/shard_map/while/body/eval_jaxpr/reduce_scatter | solution.py:256
  3316.5 411.0 %reduce-scatter.42.cloned.1.call-start = ((), (), s32[]{:S(2)}) async-start(), calls=%async_computation.27 | async-start | bytes 14417920 | tf_op jit(solution)/shard_map/while/body/eval_jaxpr/reduce_scatter | solution.py:262
  3918.4 87.3 %reduce-scatter.50.cloned.1.call-start = ((), (), s32[]{:S(2)}) async-start(), calls=%async_computation.31 | async-start | bytes 1114112 | tf_op jit(solution)/shard_map/while
  3920.2 119.1 %reduce-scatter.40.cloned.1.call-start = ((), (), s32[]{:S(2)}) async-start(), calls=%async_computation.26 | async-start | bytes 2621440 | tf_op jit(solution)/shard_map/while/body/eval_jaxpr/reduce_scatter | solution.py:259
  3923.3 177.5 %reduce-scatter.46.cloned.1.call-start = ((), (), s32[]{:S(2)}) async-start(), calls=%async_computation.29 | async-start | bytes 1114112 | tf_op jit(solution)/shard_map/while
  3948.7 212.1 %reduce-scatter.48.cloned.1.call-start = ((), (), s32[]{:S(2)}) async-start(), calls=%async_computation.30 | async-start | bytes 1114112 | tf_op jit(solution)/shard_map/while
  3950.1 267.4 %reduce-scatter.44.cloned.1.call-start = ((), (), s32[]{:S(2)}) async-start(), calls=%async_computation.28 | async-start | bytes 7208960 | tf_op jit(solution)/shard_map/while/body/eval_jaxpr/reduce_scatter | solution.py:265
  3956.4 322.0 %reduce-scatter.38.cloned.1.call-start = ((), (), s32[]{:S(2)}) async-start(), calls=%async_computation.25 | async-start | bytes 7864320 | tf_op jit(solution)/shard_map/while/body/eval_jaxpr/reduce_scatter | solution.py:256
  3962.3 410.9 %reduce-scatter.42.cloned.1.call-start = ((), (), s32[]{:S(2)}) async-start(), calls=%async_computation.27 | async-start | bytes 14417920 | tf_op jit(solution)/shard_map/while/body/eval_jaxpr/reduce_scatter | solution.py:262
  4511.3 80.3 %reduce-scatter.36.cloned.1.call-start = ((), (), s32[]{:S(2)}) async-start(), calls=%async_computation.24 | async-start | bytes 1310720 | tf_op jit(solution)/shard_map/while/body/eval_jaxpr/reduce_scatter | solution.py:230
  4564.2 87.5 %reduce-scatter.50.cloned.1.call-start = ((), (), s32[]{:S(2)}) async-start(), calls=%async_computation.31 | async-start | bytes 1114112 | tf_op jit(solution)/shard_map/while
  4566.0 119.3 %reduce-scatter.40.cloned.1.call-start = ((), (), s32[]{:S(2)}) async-start(), calls=%async_computation.26 | async-start | bytes 2621440 | tf_op jit(solution)/shard_map/while/body/eval_jaxpr/reduce_scatter | solution.py:259
  4569.1 177.6 %reduce-scatter.46.cloned.1.call-start = ((), (), s32[]{:S(2)}) async-start(), calls=%async_computation.29 | async-start | bytes 1114112 | tf_op jit(solution)/shard_map/while
  4594.5 212.3 %reduce-scatter.48.cloned.1.call-start = ((), (), s32[]{:S(2)}) async-start(), calls=%async_computation.30 | async-start | bytes 1114112 | tf_op jit(solution)/shard_map/while
  4595.9 267.7 %reduce-scatter.44.cloned.1.call-start = ((), (), s32[]{:S(2)}) async-start(), calls=%async_computation.28 | async-start | bytes 7208960 | tf_op jit(solution)/shard_map/while/body/eval_jaxpr/reduce_scatter | solution.py:265
  4602.2 322.3 %reduce-scatter.38.cloned.1.call-start = ((), (), s32[]{:S(2)}) async-start(), calls=%async_computation.25 | async-start | bytes 7864320 | tf_op jit(solution)/shard_map/while/body/eval_jaxpr/reduce_scatter | solution.py:256
  4608.1 411.0 %reduce-scatter.42.cloned.1.call-start = ((), (), s32[]{:S(2)}) async-start(), calls=%async_computation.27 | async-start | bytes 14417920 | tf_op jit(solution)/shard_map/while/body/eval_jaxpr/reduce_scatter | solution.py:262
  5210.0 87.5 %reduce-scatter.50.cloned.1.call-start = ((), (), s32[]{:S(2)}) async-start(), calls=%async_computation.31 | async-start | bytes 1114112 | tf_op jit(solution)/shard_map/while
  5211.8 119.2 %reduce-scatter.40.cloned.1.call-start = ((), (), s32[]{:S(2)}) async-start(), calls=%async_computation.26 | async-start | bytes 2621440 | tf_op jit(solution)/shard_map/while/body/eval_jaxpr/reduce_scatter | solution.py:259
  5214.9 177.7 %reduce-scatter.46.cloned.1.call-start = ((), (), s32[]{:S(2)}) async-start(), calls=%async_computation.29 | async-start | bytes 1114112 | tf_op jit(solution)/shard_map/while
  5240.2 212.4 %reduce-scatter.48.cloned.1.call-start = ((), (), s32[]{:S(2)}) async-start(), calls=%async_computation.30 | async-start | bytes 1114112 | tf_op jit(solution)/shard_map/while
  5241.7 267.8 %reduce-scatter.44.cloned.1.call-start = ((), (), s32[]{:S(2)}) async-start(), calls=%async_computation.28 | async-start | bytes 7208960 | tf_op jit(solution)/shard_map/while/body/eval_jaxpr/reduce_scatter | solution.py:265
  5247.9 322.5 %reduce-scatter.38.cloned.1.call-start = ((), (), s32[]{:S(2)}) async-start(), calls=%async_computation.25 | async-start | bytes 7864320 | tf_op jit(solution)/shard_map/while/body/eval_jaxpr/reduce_scatter | solution.py:256
  5253.9 411.2 %reduce-scatter.42.cloned.1.call-start = ((), (), s32[]{:S(2)}) async-start(), calls=%async_computation.27 | async-start | bytes 14417920 | tf_op jit(solution)/shard_map/while/body/eval_jaxpr/reduce_scatter | solution.py:262
  5856.1 87.5 %reduce-scatter.50.cloned.1.call-start = ((), (), s32[]{:S(2)}) async-start(), calls=%async_computation.31 | async-start | bytes 1114112 | tf_op jit(solution)/shard_map/while
  5858.0 119.2 %reduce-scatter.40.cloned.1.call-start = ((), (), s32[]{:S(2)}) async-start(), calls=%async_computation.26 | async-start | bytes 2621440 | tf_op jit(solution)/shard_map/while/body/eval_jaxpr/reduce_scatter | solution.py:259
  5861.0 177.5 %reduce-scatter.46.cloned.1.call-start = ((), (), s32[]{:S(2)}) async-start(), calls=%async_computation.29 | async-start | bytes 1114112 | tf_op jit(solution)/shard_map/while
  5886.4 212.0 %reduce-scatter.48.cloned.1.call-start = ((), (), s32[]{:S(2)}) async-start(), calls=%async_computation.30 | async-start | bytes 1114112 | tf_op jit(solution)/shard_map/while
  5887.9 267.6 %reduce-scatter.44.cloned.1.call-start = ((), (), s32[]{:S(2)}) async-start(), calls=%async_computation.28 | async-start | bytes 7208960 | tf_op jit(solution)/shard_map/while/body/eval_jaxpr/reduce_scatter | solution.py:265
  5894.1 322.1 %reduce-scatter.38.cloned.1.call-start = ((), (), s32[]{:S(2)}) async-start(), calls=%async_computation.25 | async-start | bytes 7864320 | tf_op jit(solution)/shard_map/while/body/eval_jaxpr/reduce_scatter | solution.py:256
  5900.1 411.0 %reduce-scatter.42.cloned.1.call-start = ((), (), s32[]{:S(2)}) async-start(), calls=%async_computation.27 | async-start | bytes 14417920 | tf_op jit(solution)/shard_map/while/body/eval_jaxpr/reduce_scatter | solution.py:262
  6501.9 87.3 %reduce-scatter.50.cloned.1.call-start = ((), (), s32[]{:S(2)}) async-start(), calls=%async_computation.31 | async-start | bytes 1114112 | tf_op jit(solution)/shard_map/while
  6503.7 119.1 %reduce-scatter.40.cloned.1.call-start = ((), (), s32[]{:S(2)}) async-start(), calls=%async_computation.26 | async-start | bytes 2621440 | tf_op jit(solution)/shard_map/while/body/eval_jaxpr/reduce_scatter | solution.py:259
  6506.8 177.4 %reduce-scatter.46.cloned.1.call-start = ((), (), s32[]{:S(2)}) async-start(), calls=%async_computation.29 | async-start | bytes 1114112 | tf_op jit(solution)/shard_map/while
  6532.1 212.1 %reduce-scatter.48.cloned.1.call-start = ((), (), s32[]{:S(2)}) async-start(), calls=%async_computation.30 | async-start | bytes 1114112 | tf_op jit(solution)/shard_map/while
  6533.6 267.5 %reduce-scatter.44.cloned.1.call-start = ((), (), s32[]{:S(2)}) async-start(), calls=%async_computation.28 | async-start | bytes 7208960 | tf_op jit(solution)/shard_map/while/body/eval_jaxpr/reduce_scatter | solution.py:265
  6539.9 322.2 %reduce-scatter.38.cloned.1.call-start = ((), (), s32[]{:S(2)}) async-start(), calls=%async_computation.25 | async-start | bytes 7864320 | tf_op jit(solution)/shard_map/while/body/eval_jaxpr/reduce_scatter | solution.py:256
  6545.8 411.1 %reduce-scatter.42.cloned.1.call-start = ((), (), s32[]{:S(2)}) async-start(), calls=%async_computation.27 | async-start | bytes 14417920 | tf_op jit(solution)/shard_map/while/body/eval_jaxpr/reduce_scatter | solution.py:262
  7147.8 87.3 %reduce-scatter.50.cloned.1.call-start = ((), (), s32[]{:S(2)}) async-start(), calls=%async_computation.31 | async-start | bytes 1114112 | tf_op jit(solution)/shard_map/while
  7149.6 119.0 %reduce-scatter.40.cloned.1.call-start = ((), (), s32[]{:S(2)}) async-start(), calls=%async_computation.26 | async-start | bytes 2621440 | tf_op jit(solution)/shard_map/while/body/eval_jaxpr/reduce_scatter | solution.py:259
  7152.7 177.3 %reduce-scatter.46.cloned.1.call-start = ((), (), s32[]{:S(2)}) async-start(), calls=%async_computation.29 | async-start | bytes 1114112 | tf_op jit(solution)/shard_map/while
  7178.0 212.1 %reduce-scatter.48.cloned.1.call-start = ((), (), s32[]{:S(2)}) async-start(), calls=%async_computation.30 | async-start | bytes 1114112 | tf_op jit(solution)/shard_map/while
  7179.5 267.5 %reduce-scatter.44.cloned.1.call-start = ((), (), s32[]{:S(2)}) async-start(), calls=%async_computation.28 | async-start | bytes 7208960 | tf_op jit(solution)/shard_map/while/body/eval_jaxpr/reduce_scatter | solution.py:265
  7185.7 322.1 %reduce-scatter.38.cloned.1.call-start = ((), (), s32[]{:S(2)}) async-start(), calls=%async_computation.25 | async-start | bytes 7864320 | tf_op jit(solution)/shard_map/while/body/eval_jaxpr/reduce_scatter | solution.py:256
  7191.7 411.0 %reduce-scatter.42.cloned.1.call-start = ((), (), s32[]{:S(2)}) async-start(), calls=%async_computation.27 | async-start | bytes 14417920 | tf_op jit(solution)/shard_map/while/body/eval_jaxpr/reduce_scatter | solution.py:262
  (417 other events, 13973.5 us)
Sparse Core Ops, SparseCore 0:
  25.1 29.8 all-gather.10
  2013.6 56.0 reduce-scatter.49
  2073.0 30.3 reduce-scatter.39
  2107.3 57.4 reduce-scatter.45
  2168.3 56.3 reduce-scatter.47
  2227.8 53.8 reduce-scatter.43
  2284.1 58.3 reduce-scatter.37
  2345.0 92.1 reduce-scatter.41
  2657.6 56.0 reduce-scatter.49
  2716.9 30.4 reduce-scatter.39
  2751.3 57.4 reduce-scatter.45
  2812.4 56.3 reduce-scatter.47
  2871.9 53.8 reduce-scatter.43
  2928.4 58.3 reduce-scatter.37
  2989.3 92.1 reduce-scatter.41
  3303.8 56.0 reduce-scatter.49
  3363.0 30.3 reduce-scatter.39
  3397.5 57.4 reduce-scatter.45
  3458.6 56.3 reduce-scatter.47
  3518.2 53.8 reduce-scatter.43
  3574.5 58.3 reduce-scatter.37
  3635.3 92.1 reduce-scatter.41
  3949.6 56.0 reduce-scatter.49
  4008.9 30.3 reduce-scatter.39
  4043.4 57.3 reduce-scatter.45
  4104.3 56.4 reduce-scatter.47
  4163.7 53.8 reduce-scatter.43
  4220.0 58.3 reduce-scatter.37
  4280.9 92.1 reduce-scatter.41
  4595.6 56.0 reduce-scatter.49
  4654.9 30.3 reduce-scatter.39
  4689.3 57.4 reduce-scatter.45
  4750.4 56.3 reduce-scatter.47
  4809.8 53.8 reduce-scatter.43
  4866.1 58.3 reduce-scatter.37
  4926.9 92.1 reduce-scatter.41
  5241.3 56.0 reduce-scatter.49
  5300.5 30.4 reduce-scatter.39
  5335.1 57.4 reduce-scatter.45
  5396.2 56.3 reduce-scatter.47
  5455.6 53.8 reduce-scatter.43
  5512.0 58.3 reduce-scatter.37
  5572.8 92.2 reduce-scatter.41
  5887.5 56.0 reduce-scatter.49
  5946.7 30.3 reduce-scatter.39
  5981.1 57.4 reduce-scatter.45
  6042.0 56.3 reduce-scatter.47
  6101.5 53.8 reduce-scatter.43
  6157.9 58.3 reduce-scatter.37
  6218.8 92.1 reduce-scatter.41
  6533.1 56.0 reduce-scatter.49
  6592.3 30.4 reduce-scatter.39
  6626.7 57.4 reduce-scatter.45
  6687.8 56.3 reduce-scatter.47
  6747.2 53.8 reduce-scatter.43
  6803.7 58.3 reduce-scatter.37
  6864.7 92.1 reduce-scatter.41
  7179.0 56.0 reduce-scatter.49
  7238.2 30.3 reduce-scatter.39
  7272.5 57.4 reduce-scatter.45
  7333.6 56.3 reduce-scatter.47
  7393.0 53.8 reduce-scatter.43
  7449.5 58.3 reduce-scatter.37
  7510.5 92.1 reduce-scatter.41
  (107 shorter events, 2641.6 us)
where the time goes:
time: 7650 us; the launch traced here: 7630 us
  waiting for transfers between devices  5830 us (76%)
  matrix products  857 us (11%)
  other arithmetic  487 us (6%)
  local copies, waits for them, and re-layouts  334 us (4%)
    while x198, waiting for transfers between devices  1360 us
    reduce_scatter x9, waiting for transfers between devices, spread(): lax.psum_scatter(gu_term.astype(jnp.bfloat16), 'ctx', scatter_dimension=1...  831 us
    reduce_scatter x9, waiting for transfers between devices, spread(): lax.psum_scatter(qkv_term.astype(jnp.bfloat16), 'ctx', scatter_dimension=...  510 us
    reduce_scatter x9, waiting for transfers between devices, spread(): lax.psum_scatter(down_term.astype(jnp.bfloat16), 'ctx', scatter_dimension...  504 us
    reduce_scatter x9, waiting for transfers between devices, spread(): lax.psum_scatter(out_term.astype(jnp.bfloat16), 'ctx', scatter_dimension=...  294 us
    all_gather x9, waiting for transfers between devices, forward_layer(): normed_all = lax.all_gather(normed, 'tp', axis=0, tiled=True)  249 us
    reduce_scatter x9, waiting for transfers between devices, forward_layer(): lax.psum_scatter(jnp.einsum('rse,ed->rsd', piece, w_out, preferred_elemen...  245 us
    all_gather x9, waiting for transfers between devices, backward_layer(): lax.all_gather(grad_out.astype(jnp.bfloat16), 'tp', axis=0, tiled=True)  243 us
  transfers between devices with their start and end apart: 189, of which 180 were waited for; matrix products, arithmetic and copies ran while one was open for 11% of the time, Pallas kernels for 0%

commit v1 on v0

--- a/solution.py
+++ b/solution.py
@@ -1,10 +1,422 @@
+import functools
+
 import jax
 import jax.numpy as jnp
 from jax import lax
+from jax.experimental import pallas as pl
+from jax.experimental.pallas import tpu as pltpu
 from jax.sharding import PartitionSpec as P
 
 HEAD_WIDTH = 64
 ROT = 16
+
+
+def pair_routes(ctx_count):
+    core = [(i, i ^ 1) for i in range(ctx_count)]
+    across = [(i, (i + 2) % 4) for i in range(ctx_count)]
+    return core, across
+
+
+def ln_stats(stream):
+    mean = jnp.mean(stream, axis=-1, keepdims=True)
+    centre = stream - mean
+    inv_std = lax.rsqrt(jnp.mean(centre * centre, axis=-1, keepdims=True) + 1e-05)
+    return centre, inv_std
+
+
+def ln(stream, gain_vec, shift_vec):
+    centre, inv_std = ln_stats(stream)
+    return (centre * inv_std * gain_vec + shift_vec).astype(jnp.bfloat16)
+
+
+def ln_back(stream, grad_in, gain_vec):
+    centre, inv_std = ln_stats(stream)
+    unit = centre * inv_std
+    scaled = grad_in * gain_vec
+    result = inv_std * (
+        scaled
+        - jnp.mean(scaled, axis=-1, keepdims=True)
+        - unit * jnp.mean(scaled * unit, axis=-1, keepdims=True)
+    )
+    return result, jnp.sum(grad_in * unit, axis=0), jnp.sum(grad_in, axis=0)
+
+
+def rot_tables(pos_row):
+    half = ROT // 2
+    freqs = 10000.0 ** (-jnp.arange(half, dtype=jnp.float32) * 2.0 / ROT)
+    angles = pos_row.astype(jnp.float32)[:, None] * freqs
+    cosine, sine = jnp.cos(angles), jnp.sin(angles)
+    rows = pos_row.shape[0]
+    rest = HEAD_WIDTH - ROT
+    zeros = jnp.zeros((rows, half), jnp.float32)
+    cos_head = jnp.concatenate([cosine, cosine, jnp.ones((rows, rest), jnp.float32)], 1)
+    low_head = jnp.concatenate([-sine, zeros, jnp.zeros((rows, rest), jnp.float32)], 1)
+    high_head = jnp.concatenate([zeros, sine, jnp.zeros((rows, rest), jnp.float32)], 1)
+    return tuple(jnp.concatenate([t, t], 1) for t in (cos_head, low_head, high_head))
+
+
+def dot_t(a, b):
+    return lax.dot_general(a, b, (((1,), (1,)), ((), ())), preferred_element_type=jnp.float32)
+
+
+def dot_0(a, b):
+    return lax.dot_general(a, b, (((0,), (0,)), ((), ())), preferred_element_type=jnp.float32)
+
+
+def dot_n(a, b):
+    return lax.dot_general(a, b, (((1,), (0,)), ((), ())), preferred_element_type=jnp.float32)
+
+
+def chunked(x, chunk):
+    half = x.shape[0] // 2
+    pieces = []
+    for i in range(half // chunk):
+        pieces.append(x[i * chunk : (i + 1) * chunk])
+        pieces.append(x[half + i * chunk : half + (i + 1) * chunk])
+    return jnp.concatenate(pieces, axis=0)
+
+
+def attn_fwd_kernel(heads, chunk, mixed, bias, cos_t, low_t, high_t, pos_c, pos_r, qkv, out):
+    rows = mixed.shape[0]
+    half = rows // 2
+    width = heads * HEAD_WIDTH
+    half_rot = ROT // 2
+    cosine, low, high = cos_t[...], low_t[...], high_t[...]
+    for pair in range(heads // 2):
+        parts = []
+        for c in range(3):
+            at = c * width + pair * 128
+            x = mixed[:, at : at + 128] + bias[0, :, at : at + 128]
+            if c < 2:
+                x = x * cosine + pltpu.roll(x, 128 - half_rot, 1) * low + pltpu.roll(x, half_rot, 1) * high
+            x = x.astype(jnp.bfloat16)
+            qkv[:, at : at + 128] = x
+            parts.append(chunked(x, chunk))
+        query, key, value = parts
+        query = query * jnp.bfloat16(HEAD_WIDTH ** (-0.5))
+        for i in range(half // chunk):
+            end = 2 * chunk * (i + 1)
+            begin = end - 2 * chunk
+            allowed = pos_r[:, begin:end] <= pos_c[begin:end, :]
+            halves = []
+            for h in range(2):
+                lanes = slice(h * HEAD_WIDTH, (h + 1) * HEAD_WIDTH)
+                q_h = query[begin:end, lanes]
+                score = dot_t(q_h, key[:end, lanes])
+                last = jnp.where(allowed, score[:, begin:], -1e30)
+                score = last if i == 0 else jnp.concatenate([score[:, :begin], last], axis=1)
+                prob = jnp.exp(score - jnp.max(score, axis=1, keepdims=True))
+                total = jnp.sum(prob, axis=1, keepdims=True)
+                mixed_values = dot_n(prob.astype(jnp.bfloat16), value[:end, lanes])
+                halves.append(mixed_values / total)
+            done = jnp.concatenate(halves, axis=1).astype(jnp.bfloat16)
+            lanes = slice(pair * 128, pair * 128 + 128)
+            out[i * chunk : (i + 1) * chunk, lanes] = done[:chunk]
+            out[half + i * chunk : half + (i + 1) * chunk, lanes] = done[chunk:]
+
+
+def attn_bwd_kernel(heads, chunk, qkv, ctx, cos_t, low_t, high_t, pos_c, pos_r, grad, bias_grad, dk_s, dv_s):
+    rows = qkv.shape[0]
+    half = rows // 2
+    width = heads * HEAD_WIDTH
+    half_rot = ROT // 2
+    cosine, low, high = cos_t[...], low_t[...], high_t[...]
+    scale = HEAD_WIDTH ** (-0.5)
+
+    def finish(c, pair, x):
+        at = c * width + pair * 128
+        if c < 2:
+            x = x * scale
+            x = x * cosine + pltpu.roll(x * high, 128 - half_rot, 1) + pltpu.roll(x * low, half_rot, 1)
+        x = x.astype(jnp.bfloat16)
+        grad[:, at : at + 128] = x
+        bias_grad[0, :, at : at + 128] = jnp.sum(x.astype(jnp.float32), axis=0, keepdims=True)
+
+    def unchunked(x):
+        steps = half // chunk
+        own = [x[2 * i * chunk : (2 * i + 1) * chunk] for i in range(steps)]
+        other = [x[(2 * i + 1) * chunk : (2 * i + 2) * chunk] for i in range(steps)]
+        return jnp.concatenate(own + other, axis=0)
+
+    for pair in range(heads // 2):
+        lanes2 = slice(pair * 128, pair * 128 + 128)
+        query, key, value = (
+            chunked(qkv[:, c * width + pair * 128 : c * width + pair * 128 + 128], chunk) for c in range(3)
+        )
+        query_s = query * jnp.bfloat16(scale)
+        ctx_grad = chunked(ctx[:, lanes2], chunk)
+        dk_s[...] = jnp.zeros_like(dk_s)
+        dv_s[...] = jnp.zeros_like(dv_s)
+        dq_parts = []
+        for i in range(half // chunk):
+            end = 2 * chunk * (i + 1)
+            begin = end - 2 * chunk
+            allowed = pos_c[begin:end, :] <= pos_r[:, begin:end]
+            dq_h, dk_h, dv_h = [], [], []
+            for h in range(2):
+                lanes = slice(h * HEAD_WIDTH, (h + 1) * HEAD_WIDTH)
+                score = dot_t(key[:end, lanes], query_s[begin:end, lanes])
+                last = jnp.where(allowed, score[begin:, :], -1e30)
+                score = last if i == 0 else jnp.concatenate([score[:begin, :], last], axis=0)
+                prob = jnp.exp(score - jnp.max(score, axis=0, keepdims=True))
+                prob = prob * (1.0 / jnp.sum(prob, axis=0, keepdims=True))
+                grad_h = ctx_grad[begin:end, lanes]
+                dv_h.append(dot_n(prob.astype(jnp.bfloat16), grad_h))
+                prob_grad = dot_t(value[:end, lanes], grad_h)
+                delta = jnp.sum(prob * prob_grad, axis=0, keepdims=True)
+                score_grad = (prob * (prob_grad - delta)).astype(jnp.bfloat16)
+                dk_h.append(dot_n(score_grad, query[begin:end, lanes]))
+                dq_h.append(dot_0(score_grad, key[:end, lanes]))
+            dk_s[:end, :] += jnp.concatenate(dk_h, axis=1)
+            dv_s[:end, :] += jnp.concatenate(dv_h, axis=1)
+            dq_parts.append(jnp.concatenate(dq_h, axis=1))
+        finish(0, pair, unchunked(jnp.concatenate(dq_parts, axis=0)))
+        finish(1, pair, unchunked(dk_s[...]))
+        finish(2, pair, unchunked(dv_s[...]))
+
+
+VMEM_LIMIT = 56 * 1024 * 1024
+
+
+def attn_fwd(mixed, bias, context, groups, chunk):
+    rows, columns = mixed.shape
+    block = columns // groups
+    heads = block // (3 * HEAD_WIDTH)
+    cos_t, low_t, high_t, pos_c, pos_r = context
+    whole = lambda shape: pl.BlockSpec(shape, lambda g: (0, 0))
+    return pl.pallas_call(
+        functools.partial(attn_fwd_kernel, heads, chunk),
+        grid=(groups,),
+        in_specs=[
+            pl.BlockSpec((rows, block), lambda g: (0, g)),
+            pl.BlockSpec((1, 1, block), lambda g: (g, 0, 0)),
+            whole((rows, 128)),
+            whole((rows, 128)),
+            whole((rows, 128)),
+            whole((rows, 1)),
+            whole((1, rows)),
+        ],
+        out_specs=[
+            pl.BlockSpec((rows, block), lambda g: (0, g)),
+            pl.BlockSpec((rows, block // 3), lambda g: (0, g)),
+        ],
+        out_shape=[
+            jax.ShapeDtypeStruct((rows, columns), jnp.bfloat16),
+            jax.ShapeDtypeStruct((rows, columns // 3), jnp.bfloat16),
+        ],
+        compiler_params=pltpu.CompilerParams(vmem_limit_bytes=VMEM_LIMIT),
+        cost_estimate=pl.CostEstimate(
+            flops=3 * rows * rows * columns // 3 * 4,
+            bytes_accessed=rows * columns * 7,
+            transcendentals=rows * rows * columns // (3 * HEAD_WIDTH),
+        ),
+    )(mixed, bias.reshape(groups, 1, block), cos_t, low_t, high_t, pos_c, pos_r)
+
+
+def attn_bwd(qkv, ctx_grad, context, groups, chunk):
+    rows, columns = qkv.shape
+    block = columns // groups
+    heads = block // (3 * HEAD_WIDTH)
+    cos_t, low_t, high_t, pos_c, pos_r = context
+    whole = lambda shape: pl.BlockSpec(shape, lambda g: (0, 0))
+    return pl.pallas_call(
+        functools.partial(attn_bwd_kernel, heads, chunk),
+        grid=(groups,),
+        in_specs=[
+            pl.BlockSpec((rows, block), lambda g: (0, g)),
+            pl.BlockSpec((rows, block // 3), lambda g: (0, g)),
+            whole((rows, 128)),
+            whole((rows, 128)),
+            whole((rows, 128)),
+            whole((rows, 1)),
+            whole((1, rows)),
+        ],
+        out_specs=[
+            pl.BlockSpec((rows, block), lambda g: (0, g)),
+            pl.BlockSpec((1, 1, block), lambda g: (g, 0, 0)),
+        ],
+        out_shape=[
+            jax.ShapeDtypeStruct((rows, columns), jnp.bfloat16),
+            jax.ShapeDtypeStruct((groups, 1, block), jnp.float32),
+        ],
+        scratch_shapes=[pltpu.VMEM((rows, 128), jnp.float32), pltpu.VMEM((rows, 128), jnp.float32)],
+        compiler_params=pltpu.CompilerParams(vmem_limit_bytes=VMEM_LIMIT),
+        cost_estimate=pl.CostEstimate(
+            flops=7 * rows * rows * columns // 3 * 4,
+            bytes_accessed=rows * columns * 5,
+            transcendentals=rows * rows * columns // (3 * HEAD_WIDTH),
+        ),
+    )(qkv, ctx_grad, cos_t, low_t, high_t, pos_c, pos_r)
+
+
+def bulk_device(
+    tokens_in,
+    cotangent,
+    plan,
+    positions,
+    norm_gain,
+    norm_shift,
+    w_qkv,
+    b_qkv,
+    w_out,
+    w_gate_up,
+    down_weight,
+):
+    tp_count = lax.axis_size("tp")
+    ctx_count = lax.axis_size("ctx")
+    section_index = lax.axis_index("section")
+    ctx_index = lax.axis_index("ctx")
+    side, core = ctx_index // 2, ctx_index % 2
+    core_route, across_route = pair_routes(ctx_count)
+    micro_count, slice_len, _, width = tokens_in.shape
+    gain, shift = norm_gain[0], norm_shift[0]
+    piece = slice_len // 2
+    rows = micro_count * slice_len * 2
+    own_rows = rows // 2
+    half_width = width // 2
+    columns = w_qkv.shape[3] // 2
+    hidden = w_gate_up.shape[3] // 2
+    first = section_index == 0
+
+    ordered = jnp.stack(
+        [lax.dynamic_index_in_dim(tokens_in, plan[m], 0, keepdims=False)[:, 0] for m in range(micro_count)]
+    )
+    fresh = jnp.where(first, ordered, cotangent[:, :, 0])
+    fresh = fresh.reshape(ctx_count // 2, tp_count, 2, piece, width).transpose(0, 2, 1, 3, 4)
+    fresh = fresh.reshape(ctx_count * tp_count, piece, width)
+    inbound = lax.all_to_all(fresh, ("ctx", "tp"), 0, 0, tiled=True).reshape(own_rows, width)
+
+    pos = positions.reshape(-1, 2, piece)
+    pos = jnp.concatenate(
+        [
+            lax.dynamic_index_in_dim(pos, core, 1, False).reshape(-1),
+            lax.dynamic_index_in_dim(pos, 1 - core, 1, False).reshape(-1),
+        ]
+    )
+    chunk = min(128, own_rows)
+    chunk_pos = chunked(pos, chunk)
+    context = (*rot_tables(pos), chunk_pos[:, None], chunk_pos[None, :])
+
+    def gathered(block):
+        own = lax.all_gather(block, "tp", axis=0, tiled=True)
+        other = lax.ppermute(own, "ctx", across_route)
+        return jnp.where(
+            side == 0, jnp.concatenate([own, other], axis=1), jnp.concatenate([other, own], axis=1)
+        )
+
+    d_from = side * half_width
+    qkv_block = lax.dynamic_slice(w_qkv[0], (0, d_from, core * columns), (3, half_width, columns))
+    qkv_block = qkv_block.transpose(0, 2, 1).reshape(3 * columns, half_width)
+    out_block = lax.dynamic_slice(w_out[0], (core * columns, d_from), (columns, half_width))
+    gu_block = lax.dynamic_slice(w_gate_up[0], (0, d_from, core * hidden), (2, half_width, hidden))
+    gu_block = gu_block.transpose(0, 2, 1)
+    down_block = lax.dynamic_slice(down_weight[0], (core * hidden, d_from), (hidden, half_width))
+    wt_qkv = gathered(qkv_block)
+    wt_out = gathered(out_block)
+    wt_gu = jnp.concatenate([gathered(gu_block[0]), gathered(gu_block[1])], axis=0)
+    wt_down = gathered(down_block)
+    bias_all = lax.all_gather(b_qkv[0], "tp", axis=0)
+    bias = lax.dynamic_slice_in_dim(bias_all, core * columns, columns, 2).reshape(tp_count, 3 * columns)
+    ff = wt_down.shape[0]
+
+    def both(own):
+        return jnp.concatenate([own, lax.ppermute(own, "ctx", core_route)], axis=0)
+
+    def summed(a, weight):
+        other = dot_n(a[own_rows:], weight).astype(jnp.bfloat16)
+        arriving = lax.ppermute(other, "ctx", core_route)
+        return dot_n(a[:own_rows], weight) + arriving.astype(jnp.float32)
+
+    def forward(stream):
+        normed = both(ln(stream, gain[0], shift[0]))
+        mixed = dot_t(normed, wt_qkv)
+        qkv, attended = attn_fwd(mixed, bias, context, tp_count, chunk)
+        hidden_state = stream + summed(attended, wt_out)
+        normed_two = both(ln(hidden_state, gain[1], shift[1]))
+        gate_up = dot_t(normed_two, wt_gu)
+        gate, up = gate_up[:, :ff], gate_up[:, ff:]
+        activation = (jax.nn.silu(gate) * up).astype(jnp.bfloat16)
+        out = (hidden_state + summed(activation, wt_down)).astype(jnp.bfloat16)
+        return out, (stream, normed, qkv, attended, hidden_state, normed_two, gate_up, activation)
+
+    def backward(grad_out, stored):
+        stream, normed, qkv, attended, hidden_state, normed_two, gate_up, activation = stored
+        mlp_grad = both(grad_out)
+        act_grad = dot_t(mlp_grad, wt_down)
+        gate, up = gate_up[:, :ff], gate_up[:, ff:]
+        sigma = jax.nn.sigmoid(gate)
+        gu_grad = jnp.concatenate(
+            [act_grad * up * sigma * (1.0 + gate * (1.0 - sigma)), act_grad * gate * sigma], axis=1
+        ).astype(jnp.bfloat16)
+        two_grad = summed(gu_grad, wt_gu)
+        result, gain_two, shift_two = ln_back(hidden_state, two_grad, gain[1])
+        hidden_grad = grad_out.astype(jnp.float32) + result
+        attn_grad = both(hidden_grad.astype(jnp.bfloat16))
+        ctx_grad = dot_t(attn_grad, wt_out).astype(jnp.bfloat16)
+        qkv_grad, bias_grad = attn_bwd(qkv, ctx_grad, context, tp_count, chunk)
+        one_grad = summed(qkv_grad, wt_qkv)
+        result, gain_one, shift_one = ln_back(stream, one_grad, gain[0])
+        input_grad = (hidden_grad + result).astype(jnp.bfloat16)
+        small = (jnp.stack([gain_one, gain_two]), jnp.stack([shift_one, shift_two]), bias_grad)
+        pairs = ((activation, mlp_grad), (gu_grad, normed_two), (attended, attn_grad), (qkv_grad, normed))
+        return input_grad, small, pairs
+
+    sent, _ = forward(inbound.astype(jnp.float32))
+    arriving = lax.ppermute(sent, "section", [(0, 1)])
+    final_out, stored = forward(jnp.where(first, inbound, arriving).astype(jnp.float32))
+    sent_back, _, _ = backward(inbound, stored)
+    arriving_back = lax.ppermute(sent_back, "section", [(1, 0)])
+    grad_out = jnp.where(first, arriving_back, inbound)
+    input_grad, small, pairs = backward(grad_out, stored)
+
+    def weight_grad(pair):
+        left, right = pair
+        far = lax.dynamic_slice_in_dim(right, (1 - side) * half_width, half_width, 1)
+        near = lax.dynamic_slice_in_dim(right, side * half_width, half_width, 1)
+        arriving = lax.ppermute(dot_0(left, far).astype(jnp.bfloat16), "ctx", across_route)
+        total = (dot_0(left, near) + arriving.astype(jnp.float32)).astype(jnp.bfloat16)
+        return lax.psum_scatter(total, "tp", scatter_dimension=0, tiled=True)
+
+    def settled(term):
+        share = half_width // 2
+        away = lax.dynamic_slice_in_dim(term, (1 - core) * share, share, term.ndim - 1)
+        kept = lax.dynamic_slice_in_dim(term, core * share, share, term.ndim - 1)
+        got = lax.ppermute(away, "ctx", core_route)
+        axis = term.ndim - 2
+        return jnp.where(
+            core == 0, jnp.concatenate([kept, got], axis), jnp.concatenate([got, kept], axis)
+        ).astype(jnp.float32)
+
+    act_pair, gu_pair, out_pair, qkv_pair = pairs
+    grad_down = settled(weight_grad(act_pair))
+    gu_left, gu_right = gu_pair
+    grad_gate = settled(weight_grad((gu_left[:, :ff], gu_right)))
+    grad_up = settled(weight_grad((gu_left[:, ff:], gu_right)))
+    grad_out_w = settled(weight_grad(out_pair))
+    grad_qkv = settled(weight_grad(qkv_pair).reshape(3, columns, half_width))
+
+    gain_terms, shift_terms, bias_terms = small
+    bias_terms = bias_terms.reshape(tp_count, 3, columns).transpose(1, 0, 2)[:, :, None]
+    bias_full = jnp.where(
+        (jnp.arange(2) == core)[None, None, :, None], bias_terms, 0.0
+    ).reshape(3, tp_count * 2 * columns)
+    vectors = jnp.concatenate([gain_terms, shift_terms, bias_full], axis=0)
+    vectors = lax.psum_scatter(vectors, ("ctx", "tp"), scatter_dimension=1, tiled=True)
+
+    ends = jnp.where(first, input_grad, final_out).reshape(ctx_count * tp_count, piece, width)
+    ends = lax.all_to_all(ends, ("ctx", "tp"), 0, 0, tiled=True)
+    ends = ends.reshape(ctx_count // 2, 2, tp_count, piece, width).transpose(0, 2, 1, 3, 4)
+    ends = ends.reshape(micro_count, slice_len, 1, width)
+    return (
+        ends[None],
+        vectors[None, :2],
+        vectors[None, 2:4],
+        vectors[None, 4:],
+        grad_qkv.transpose(0, 2, 1)[None],
+        grad_out_w[None],
+        jnp.stack([grad_gate.T, grad_up.T])[None],
+        grad_down[None],
+    )
 
 
 def passed_along(block, axis, distance):
@@ -277,7 +689,7 @@
     return (tuple(scattered), gain_part, shift_part, bias_part)
 
 
-def per_device(
+def stepwise_device(
     tokens_in,
     cotangent,
     plan,
@@ -375,6 +787,13 @@
     )
 
 
+def per_device(*arrays):
+    chips = lax.axis_size("ctx") // 2 * lax.axis_size("tp")
+    if lax.axis_size("section") == 2 and lax.axis_size("ctx") == 4 and arrays[0].shape[0] == chips:
+        return bulk_device(*arrays)
+    return stepwise_device(*arrays)
+
+
 def solution(mesh):
     placed = (
         P(None, ("ctx", "tp"), None, None),

time: 7650 us -> 2090 us (0.27)
  waiting for transfers between devices: 5830 us -> 1130 us
  other arithmetic: 487 us -> 81.6 us
  matrix products: 857 us -> 527 us
  local copies, waits for them, and re-layouts: 334 us -> 68.5 us
  Pallas kernels: 0 us -> 203 us
    reduce_scatter x90 -> x6, waiting for transfers between devices: 3300 us -> 0.05 us  [the longest x5 0.05 us: weight_grad(): return lax.psum_scatter(total, 'tp', scatter_dimension=0, tiled=True)]
    while x198 -> x0, waiting for transfers between devices: 1360 us -> none
    all_gather x54 -> x5, waiting for transfers between devices: 1110 us -> 378 us  [gathered(): own = lax.all_gather(block, 'tp', axis=0, tiled=True)]
    ppermute x18 -> x33, waiting for transfers between devices: 66.4 us -> 658 us  [the longest x5 421 us: weight_grad(): lax.ppermute(dot_0(left, far).astype(jnp.bfloat16), 'ctx', across_route)]
    dot_general x171 -> x34, matrix products: 857 us -> 527 us  [the longest x16 247 us: dot_n(): lax.dot_general(a, b, (((1,), (0,)), ((), ())), preferred_element_type=jn...]
    pallas_call x0 -> x4, Pallas kernels: none -> 203 us  [the longest x2 126 us: attn_bwd(): pl.pallas_call(functools.partial(attn_bwd_kernel, heads, chunk), grid=(gr...]
    add x63 -> x0, other arithmetic: 143 us -> none  [backward_step(): running = jax.tree.map(jnp.add, running, terms)]
    while x632 -> x0, local copies, waits for them, and re-layouts: 140 us -> none
  transfers between devices with their start and end apart: 189 -> 46, of which waited for: 180 -> 24; matrix products, arithmetic and copies ran while one was open for 11% -> 21% of each run, Pallas kernels for 0% -> 5%
where the time goes in v1:
time: 2090 us
  waiting for transfers between devices  1130 us (54%)
  matrix products  527 us (25%)
  Pallas kernels  203 us (10%)
  other arithmetic  81.6 us (4%)
  local copies, waits for them, and re-layouts  68.5 us (3%)
  starting transfers between devices  33.3 us (2%)
  between operations  30.5 us (1%)
    ppermute x5, waiting for transfers between devices, weight_grad(): lax.ppermute(dot_0(left, far).astype(jnp.bfloat16), 'ctx', across_route)  421 us
    all_gather x5, waiting for transfers between devices, gathered(): own = lax.all_gather(block, 'tp', axis=0, tiled=True)  378 us
    dot_general x16, matrix products, dot_n(): lax.dot_general(a, b, (((1,), (0,)), ((), ())), preferred_element_type=jn...  247 us
    dot_general x8, matrix products, dot_t(): lax.dot_general(a, b, (((1,), (1,)), ((), ())), preferred_element_type=jn...  186 us
    pallas_call x2, Pallas kernels, attn_bwd(): pl.pallas_call(functools.partial(attn_bwd_kernel, heads, chunk), grid=(gr...  126 us
    ppermute x5, waiting for transfers between devices, gathered(): other = lax.ppermute(own, 'ctx', across_route)  102 us
    dot_general x10, matrix products, dot_0(): lax.dot_general(a, b, (((0,), (0,)), ((), ())), preferred_element_type=jn...  94.9 us
    all_to_all x1, waiting for transfers between devices, bulk_device(): ends = lax.all_to_all(ends, ('ctx', 'tp'), 0, 0, tiled=True)  91.5 us
  transfers between devices with their start and end apart: 46, of which 24 were waited for; matrix products, arithmetic and copies ran while one was open for 21% of the time, Pallas kernels for 5%

profile of v1, /device:TPU:0, one launch (start us, length us, event | category | flops | bytes accessed | tf_op | source)
XLA Modules:
  0.0 2086.7 jit_solution(6836160284583283045)
XLA Ops:
  13.7 5.5 constant_dynamic-slice_fusion.9
  19.2 4.6 copy.70
  47.9 7.5 all-to-all-start
  55.5 120.0 %all-gather.10.cloned.1.call-done = bf16[3072,1024]{1,0:T(8,128)(2,1)} async-done(((bf16[768,1024]{1,0:T(8,128)(2,1)}), bf16[3072,1024]{1,0:T(8,128)(2,1)}) %all-gather.10.cloned.1.call-update) | async-done | bytes 6291472 | tf_op jit(solution)/shard_map/all_gather | solution.py:301
  196.6 13.8 all_gather.19
  212.8 8.9 all-gather.12.cloned.1.call-done
  223.2 106.1 %all-gather.14.cloned.1.call-done = bf16[1,2816,1024]{2,1,0:T(8,128)(2,1)} async-done(((bf16[1,704,1024]{2,1,0:T(8,128)(2,1)}), bf16[1,2816,1024]{2,1,0:T(8,128)(2,1)}) %all-gather.14.cloned.1.call-update) | async-done | bytes 5767184 | tf_op jit(solution)/shard_map/all_gather | solution.py:301
  330.8 22.3 %fusion.43.mixed = f32[1024,3072]{1,0:T(8,128)} fusion(bf16[512,2048]{1,0:T(8,128)(2,1)} %collective-permute-done, bf16[512,2048]{1,0:T(8,128)(2,1)} %fusion.42, bf16[3072,1024]{1,0:T(8,128)(2,1)} %collective-permute-done.1, bf16[3072,1024]{1,0:T(8,128)(2,1)} %all-gather.10.cloned.1.call-done, pred[]{:T(512)S(6)} %eq.30), kind=kOutput, calls=%fused_computation.96 | convolution fusion | flops 12949913600 | bytes 29360128 | tf_op jit(solution)/shard_map/dot_general | solution.py:59
  353.1 38.9 %shard_map.170 = (bf16[1024,3072]{1,0:T(8,128)(2,1)}, bf16[1024,1024]{1,0:T(8,128)(2,1)}) custom-call(f32[1024,3072]{1,0:T(8,128)} %fusion.43.mixed, f32[4,1,768]{2,1,0:T(1,128)} %reshape_reshape.5.bias, f32[1024,128]{1,0:T(8,128)} %concatenate.169.cos_t, f32[1024,128]{1,0:T(8,128)} %concatenate.170.low_t, f32[1024,128]{1,0:T(8,128)} %concatenate.171.high_t, ...), custom_call_target="tpu_custom_call" | custom-call | flops 12884901888 | bytes 22020096 | tf_op jit(solution)/shard_map/pallas_call | solution.py:187
  392.0 6.3 convolution_convert_fusion.5
  398.3 37.5 %all-gather.16.cloned.1.call-done = bf16[1,2816,1024]{2,1,0:T(8,128)(2,1)} async-done(((bf16[1,704,1024]{2,1,0:T(8,128)(2,1)}), bf16[1,2816,1024]{2,1,0:T(8,128)(2,1)}) %all-gather.16.cloned.1.call-update) | async-done | bytes 5767184 | tf_op jit(solution)/shard_map/all_gather | solution.py:301
  437.3 105.6 %all-gather.18.cloned.1.call-done = bf16[1,2816,1024]{2,1,0:T(8,128)(2,1)} async-done(((bf16[1,704,1024]{2,1,0:T(8,128)(2,1)}), bf16[1,2816,1024]{2,1,0:T(8,128)(2,1)}) %all-gather.18.cloned.1.call-update) | async-done | bytes 5767184 | tf_op jit(solution)/shard_map/all_gather | solution.py:301
  544.3 7.4 fusion.163
  553.7 15.5 maximum_select_fusion.1
  569.2 37.2 %collective-permute-done.6 = bf16[2816,1024]{1,0:T(8,128)(2,1)} collective-permute-done((bf16[2816,1024]{1,0:T(8,128)(2,1)}, bf16[2816,1024]{1,0:T(8,128)(2,1)}, u32[]{:S(2)}, u32[]{:S(2)}) %collective-permute-start.6) | collective-permute-done | bytes 5767200 | tf_op jit(solution)/shard_map/ppermute | solution.py:302
  606.3 12.1 maximum_select_fusion.2
  618.4 34.0 %fusion.47 = f32[1024,5632]{1,0:T(8,128)} fusion(bf16[512,2048]{1,0:T(8,128)(2,1)} %collective-permute-done.4, bf16[512,2048]{1,0:T(8,128)(2,1)} %copy-done.16, bf16[2816,2048]{1,0:T(8,128)(2,1)} %maximum_select_fusion.2, bf16[2816,2048]{1,0:T(8,128)(2,1)} %maximum_select_fusion.1), kind=kOutput, calls=%fused_computation.101 | convolution fusion | flops 23676846080 | bytes 50331648 | tf_op jit(solution)/shard_map/dot_general | solution.py:59
  652.4 11.6 fusion
  664.0 65.1 %collective-permute-done.7 = bf16[2816,1024]{1,0:T(8,128)(2,1)} collective-permute-done((bf16[2816,1024]{1,0:T(8,128)(2,1)}, bf16[2816,1024]{1,0:T(8,128)(2,1)}, u32[]{:S(2)}, u32[]{:S(2)}) %collective-permute-start.7) | collective-permute-done | bytes 5767200 | tf_op jit(solution)/shard_map/ppermute | solution.py:302
  729.0 16.0 convolution_convert_fusion.7
  749.4 18.6 add_convert_fusion.7
  771.6 45.3 %collective-permute-done.9 = bf16[512,2048]{1,0:T(8,128)(2,1)S(1)} collective-permute-done((bf16[512,2048]{1,0:T(8,128)(2,1)}, bf16[512,2048]{1,0:T(8,128)(2,1)S(1)}, u32[]{:S(2)}, u32[]{:S(2)}) %collective-permute-start.9) | collective-permute-done | bytes 2097184 | tf_op jit(solution)/shard_map/ppermute | solution.py:365
  821.4 4.3 collective-permute-done.10
  825.6 22.7 %fusion.38.mixed = f32[1024,3072]{1,0:T(8,128)} fusion(bf16[512,2048]{1,0:T(8,128)(2,1)} %collective-permute-done.10, bf16[512,2048]{1,0:T(8,128)(2,1)} %copy-done.11, bf16[3072,1024]{1,0:T(8,128)(2,1)} %collective-permute-done.1, bf16[3072,1024]{1,0:T(8,128)(2,1)} %all-gather.10.cloned.1.call-done, pred[]{:T(512)S(6)} %eq.30), kind=kOutput, calls=%fused_computation.91 | convolution fusion | flops 12949913600 | bytes 29360128 | tf_op jit(solution)/shard_map/dot_general | solution.py:59
  848.3 38.8 %shard_map.171 = (bf16[1024,3072]{1,0:T(8,128)(2,1)}, bf16[1024,1024]{1,0:T(8,128)(2,1)}) custom-call(f32[1024,3072]{1,0:T(8,128)} %fusion.38.mixed, f32[4,1,768]{2,1,0:T(1,128)} %reshape_reshape.5.bias, f32[1024,128]{1,0:T(8,128)} %concatenate.169.cos_t, f32[1024,128]{1,0:T(8,128)} %concatenate.170.low_t, f32[1024,128]{1,0:T(8,128)} %concatenate.171.high_t, ...), custom_call_target="tpu_custom_call" | custom-call | flops 12884901888 | bytes 22020096 | tf_op jit(solution)/shard_map/pallas_call | solution.py:187
  887.2 5.1 convolution_convert_fusion.4
  896.5 5.3 fusion.164
  908.1 33.7 %fusion.37 = f32[1024,5632]{1,0:T(8,128)} fusion(bf16[512,2048]{1,0:T(8,128)(2,1)} %collective-permute-done.13, bf16[512,2048]{1,0:T(8,128)(2,1)} %copy-done.13, bf16[2816,2048]{1,0:T(8,128)(2,1)} %maximum_select_fusion.2, bf16[2816,2048]{1,0:T(8,128)(2,1)} %maximum_select_fusion.1), kind=kOutput, calls=%fused_computation.90 | convolution fusion | flops 23676846080 | bytes 50331648 | tf_op jit(solution)/shard_map/dot_general | solution.py:59
  941.8 27.0 %multiply_convert_fusion.4 = (bf16[1024,2816]{1,0:T(8,128)(2,1)}, bf16[1024,2816]{1,0:T(8,128)(2,1)}) fusion(f32[1024,5632]{1,0:T(8,128)} %fusion.37, bf16[2816,1024]{1,0:T(8,128)(2,1)} %collective-permute-done.7, bf16[2816,1024]{1,0:T(8,128)(2,1)} %bitcast.175, pred[]{:T(512)S(6)} %eq.30, bf16[512,2048]{1,0:T(8,128)(2,1)} %collective-permute-done.12, ...), kind=kOutput, calls=%fused_computation.19 | convolution fusion | flops 11908939776 | bytes 50331648 | tf_op jit(solution)/shard_map/dot_general | solution.py:59
  968.8 17.2 fusion.81
  990.3 22.3 %fusion.154 = (f32[512]{0:T(512)S(1)}, f32[512]{0:T(512)S(1)}, f32[512,2048]{1,0:T(8,128)}) fusion(f32[512]{0:T(512)S(1)} %add_rsqrt_fusion.1, f32[512,2048]{1,0:T(8,128)} %copy-done.2, f32[512]{0:T(512)S(1)} %broadcast_multiply_fusion.9, f32[2048]{0:T(1024)S(1)} %bitcast.146, bf16[512,2048]{1,0:T(8,128)(2,1)} %collective-permute-done.14, ...), kind=kOutput, calls=%fused_computation.267 | convolution fusion | flops 11877220352 | bytes 45105152 | tf_op jit(solution)/shard_map/dot_general | solution.py:67
  1012.6 4.4 fusion.156
  1021.3 8.2 fusion.108.ctx
  1029.4 63.0 %shard_map.172 = (bf16[1024,3072]{1,0:T(8,128)(2,1)}, f32[4,1,768]{2,1,0:T(1,128)}) custom-call(bf16[1024,3072]{1,0:T(8,128)(2,1)} %get-tuple-element.16.qkv, bf16[1024,1024]{1,0:T(8,128)(2,1)} %fusion.108.ctx, f32[1024,128]{1,0:T(8,128)} %concatenate.169.cos_t, f32[1024,128]{1,0:T(8,128)} %concatenate.170.low_t, f32[1024,128]{1,0:T(8,128)} %concatenate.171.high_t, ...), custom_call_target="tpu_custom_call" | custom-call | flops 30064771072 | bytes 15728640 | tf_op jit(solution)/shard_map/pallas_call | solution.py:222
  1092.4 15.5 fusion.75
  1112.4 16.5 fusion.153
  1131.8 48.3 %collective-permute-done.17 = bf16[512,2048]{1,0:T(8,128)(2,1)S(1)} collective-permute-done((bf16[512,2048]{1,0:T(8,128)(2,1)S(1)}, bf16[512,2048]{1,0:T(8,128)(2,1)S(1)}, u32[]{:S(2)}, u32[]{:S(2)}) %collective-permute-start.17) | collective-permute-done | bytes 2097184 | tf_op jit(solution)/shard_map/ppermute | solution.py:368
  1181.7 4.5 collective-permute-done.18
  1186.2 30.0 %multiply_convert_fusion.2 = (bf16[1024,2816]{1,0:T(8,128)(2,1)}, bf16[1024,2816]{1,0:T(8,128)(2,1)}, bf16[1024,2816]{1,0:T(8,128)(2,1)}) fusion(f32[1024,5632]{1,0:T(8,128)} %fusion.37, bf16[2816,1024]{1,0:T(8,128)(2,1)} %collective-permute-done.7, bf16[2816,1024]{1,0:T(8,128)(2,1)} %bitcast.176, pred[]{:T(512)S(6)} %eq.30, ...), kind=kOutput, calls=%fused_computation.17 | convolution fusion | flops 11917590528 | bytes 56098816 | tf_op jit(solution)/shard_map/dot_general | solution.py:59
  1216.2 9.3 convolution_convert_fusion.2
  1227.1 18.0 fusion.82
  1245.0 106.8 %collective-permute-done.27 = bf16[2816,1024]{1,0:T(8,128)(2,1)S(1)} collective-permute-done((bf16[2816,1024]{1,0:T(8,128)(2,1)S(1)}, bf16[2816,1024]{1,0:T(8,128)(2,1)S(1)}, u32[]{:S(2)}, u32[]{:S(2)}) %collective-permute-start.27) | collective-permute-done | bytes 5767200 | tf_op jit(solution)/shard_map/ppermute | solution.py:376
  1351.9 11.1 add_convert_fusion.3
  1363.7 24.0 %multiply_reduce_fusion = (f32[2048]{0:T(1024)}, f32[512]{0:T(512)S(1)}, f32[512]{0:T(512)S(1)}, f32[2048]{0:T(1024)}, f32[512,2048]{1,0:T(8,128)}) fusion(f32[512]{0:T(512)S(1)} %copy-done.35, f32[512,2048]{1,0:T(8,128)} %copy-done.2, f32[512]{0:T(512)S(1)} %copy-done.29, f32[2048]{0:T(1024)S(1)} %bitcast.147, ...), kind=kOutput, calls=%fused_computation.114 | convolution fusion | flops 11880361984 | bytes 45121536 | tf_op jit(solution)/shard_map/dot_general | solution.py:67
  1387.7 6.3 fusion.155
  1394.0 11.3 convolution_convert_fusion.1
  1410.0 167.1 %collective-permute-done.25 = bf16[1024,1024]{1,0:T(8,128)(2,1)S(1)} collective-permute-done((bf16[1024,1024]{1,0:T(8,128)(2,1)S(1)}, bf16[1024,1024]{1,0:T(8,128)(2,1)S(1)}, u32[]{:S(2)}, u32[]{:S(2)}) %collective-permute-start.25) | collective-permute-done | bytes 2097184 | tf_op jit(solution)/shard_map/ppermute | solution.py:376
  1581.0 12.2 add_convert_fusion.2
  1593.3 11.2 convolution_convert_fusion
  1605.8 8.2 fusion.111.ctx
  1614.0 62.8 %shard_map.173 = (bf16[1024,3072]{1,0:T(8,128)(2,1)}, f32[4,1,768]{2,1,0:T(1,128)}) custom-call(bf16[1024,3072]{1,0:T(8,128)(2,1)} %get-tuple-element.16.qkv, bf16[1024,1024]{1,0:T(8,128)(2,1)} %fusion.111.ctx, f32[1024,128]{1,0:T(8,128)} %concatenate.169.cos_t, f32[1024,128]{1,0:T(8,128)} %concatenate.170.low_t, f32[1024,128]{1,0:T(8,128)} %concatenate.171.high_t, ...), custom_call_target="tpu_custom_call" | custom-call | flops 30064771072 | bytes 15728640 | tf_op jit(solution)/shard_map/pallas_call | solution.py:222
  1676.8 16.6 fusion.78
  1693.7 4.3 collective-permute-done.21
  1698.0 19.1 fusion.31
  1717.9 12.4 collective-permute-done.31
  1730.3 11.9 add_convert_fusion.1
  1742.3 10.8 convolution_convert_fusion.3
  1754.6 134.4 %collective-permute-done.23 = bf16[3072,1024]{1,0:T(8,128)(2,1)S(1)} collective-permute-done((bf16[3072,1024]{1,0:T(8,128)(2,1)S(1)}, bf16[3072,1024]{1,0:T(8,128)(2,1)S(1)}, u32[]{:S(2)}, u32[]{:S(2)}) %collective-permute-start.23) | collective-permute-done | bytes 6291488 | tf_op jit(solution)/shard_map/ppermute | solution.py:376
  1889.1 10.8 add_convert_fusion
  1899.9 17.3 convolution_convert_fusion.6
  1917.2 4.5 collective-permute-done.22
  1921.7 21.5 %fusion.88 = bf16[512,2048]{1,0:T(8,128)(2,1)} fusion(f32[512,2048]{1,0:T(8,128)} %get-tuple-element.65, bf16[512,2048]{1,0:T(8,128)(2,1)S(1)} %copy-done.6, f32[512,2048]{1,0:T(8,128)} %get-tuple-element.121, f32[512]{0:T(512)S(1)} %broadcast_multiply_fusion.1, f32[512]{0:T(512)S(1)} %broadcast_multiply_fusion.2, f32[512]{0:T(512)S(1)} %copy-done.38, ...), kind=kOutput, calls=%fused_computation.154 | convolution fusion | flops 5973213184 | bytes 33308674 | tf_op jit(solution)/shard_map/dot_general | solution.py:67
  1956.3 91.5 %all-to-all-done.1 = bf16[16,32,2048]{2,1,0:T(8,128)(2,1)S(1)} async-done(((bf16[16,32,2048]{2,1,0:T(8,128)(2,1)}), bf16[16,32,2048]{2,1,0:T(8,128)(2,1)S(1)}, u32[]{:S(2)}, u32[]{:S(2)}) %all-to-all-start.1) | async-done | bytes 2097184 | tf_op jit(solution)/shard_map/all_to_all | solution.py:407
  2065.2 6.3 copy.79
  (311 shorter events, 140.0 us)
Async XLA Ops:
  7.2 168.3 %all-gather.10.cloned.1.call-start = ((), (), s32[]{:S(2)}) async-start(), calls=%async_computation.8 | async-start | bytes 7864320 | tf_op jit(solution)/shard_map/all_gather | solution.py:301
  12.7 209.0 %all-gather.12.cloned.1.call-start = ((), (), s32[]{:S(2)}) async-start(), calls=%async_computation.15 | async-start | bytes 2621440 | tf_op jit(solution)/shard_map/all_gather | solution.py:301
  13.6 315.7 %all-gather.14.cloned.1.call-start = ((), (), s32[]{:S(2)}) async-start(), calls=%async_computation.16 | async-start | bytes 7208960 | tf_op jit(solution)/shard_map/all_gather | solution.py:301
  27.9 407.9 %all-gather.16.cloned.1.call-start = ((), (), s32[]{:S(2)}) async-start(), calls=%async_computation.17 | async-start | bytes 7208960 | tf_op jit(solution)/shard_map/all_gather | solution.py:301
  46.3 130.7 %copy-start.39 = (f32[1,2,2048]{2,1,0:T(2,128)S(1)}, f32[1,2,2048]{2,1,0:T(2,128)}, u32[]{:S(2)}) copy-start(f32[1,2,2048]{2,1,0:T(2,128)} %param.15) | copy-start | bytes 49156
  46.4 130.7 %copy-start.40 = (f32[1,2,2048]{2,1,0:T(2,128)S(1)}, f32[1,2,2048]{2,1,0:T(2,128)}, u32[]{:S(2)}) copy-start(f32[1,2,2048]{2,1,0:T(2,128)} %param.16) | copy-start | bytes 49156
  47.9 129.2 %all-to-all-start = ((bf16[16,32,2048]{2,1,0:T(8,128)(2,1)}), bf16[16,32,2048]{2,1,0:T(8,128)(2,1)S(1)}, u32[]{:S(2)}, u32[]{:S(2)}) async-start(bf16[16,32,2048]{2,1,0:T(8,128)(2,1)} %bitcast.131), calls=%async_computation | async-start | bytes 4194304 | tf_op jit(solution)/shard_map/all_to_all | solution.py:287
  55.4 487.4 %all-gather.18.cloned.1.call-start = ((), (), s32[]{:S(2)}) async-start(), calls=%async_computation.18 | async-start | bytes 7208960 | tf_op jit(solution)/shard_map/all_gather | solution.py:301
  175.5 155.3 %collective-permute-start.1 = (bf16[3072,1024]{1,0:T(8,128)(2,1)}, bf16[3072,1024]{1,0:T(8,128)(2,1)}, u32[]{:S(2)}, u32[]{:S(2)}) collective-permute-start(bf16[3072,1024]{1,0:T(8,128)(2,1)} %all-gather.10.cloned.1.call-done), channel_id=1, source_target_pairs={{0,8},{4,12},{8,0},{12,4},{1,9},{5,13},{9,1},{13,5},{2,10},{6,14},... | collective-permute-start | bytes 18874376 | tf_op jit(solution)/shard_map/ppermute | solution.py:302
  177.0 375.2 %copy-start.17 = (f32[1,1,2048]{2,1,0:T(1,128)}, f32[1,1,2048]{2,1,0:T(1,128)S(1)}, u32[]{:S(2)}) copy-start(f32[1,1,2048]{2,1,0:T(1,128)S(1)} %get-tuple-element.90) | copy-start | bytes 24580
  177.1 375.2 %copy-start.24 = (f32[1,1,2048]{2,1,0:T(1,128)}, f32[1,1,2048]{2,1,0:T(1,128)S(1)}, u32[]{:S(2)}) copy-start(f32[1,1,2048]{2,1,0:T(1,128)S(1)} %get-tuple-element.92) | copy-start | bytes 24580
  180.5 150.3 %collective-permute-start = (bf16[512,2048]{1,0:T(8,128)(2,1)}, bf16[512,2048]{1,0:T(8,128)(2,1)}, u32[]{:S(2)}, u32[]{:S(2)}) collective-permute-start(bf16[512,2048]{1,0:T(8,128)(2,1)} %fusion.42), channel_id=1, source_target_pairs={{0,4},{4,0},{8,12},{12,8},{1,5},{5,1},{9,13},{13,9},{2,6},{6,2},{1... | collective-permute-start | bytes 6291464 | tf_op jit(solution)/shard_map/ppermute | solution.py:323
  183.2 1763.8 %reduce-scatter.13.cloned.1.call-start = ((), (), s32[]{:S(2)}) async-start(), calls=%async_computation.12 | async-start | bytes 7208960 | tf_op jit(solution)/shard_map/reduce_scatter | solution.py:378
  221.7 170.2 %collective-permute-start.2 = (bf16[1024,1024]{1,0:T(8,128)(2,1)}, bf16[1024,1024]{1,0:T(8,128)(2,1)}, u32[]{:S(2)}, u32[]{:S(2)}) collective-permute-start(bf16[1024,1024]{1,0:T(8,128)(2,1)} %bitcast.179), channel_id=1, source_target_pairs={{0,8},{4,12},{8,0},{12,4},{1,9},{5,13},{9,1},{13,5},{2,10},{6,14},... | collective-permute-start | bytes 6291464 | tf_op jit(solution)/shard_map/ppermute | solution.py:302
  329.3 224.4 %collective-permute-start.5 = (bf16[2816,1024]{1,0:T(8,128)(2,1)}, bf16[2816,1024]{1,0:T(8,128)(2,1)}, u32[]{:S(2)}, u32[]{:S(2)}) collective-permute-start(bf16[2816,1024]{1,0:T(8,128)(2,1)} %bitcast.133), channel_id=1, source_target_pairs={{0,8},{4,12},{8,0},{12,4},{1,9},{5,13},{9,1},{13,5},{2,10},{6,14},... | collective-permute-start | bytes 17301512 | tf_op jit(solution)/shard_map/ppermute | solution.py:302
  353.1 38.9 %copy-start.47 = (bf16[1,1024,1024]{2,1,0:T(8,128)(2,1)S(1)}, bf16[1,1024,1024]{2,1,0:T(8,128)(2,1)}, u32[]{:S(2)}) copy-start(bf16[1,1024,1024]{2,1,0:T(8,128)(2,1)} %all-gather.12.cloned.1.call-done) | copy-start | bytes 6291460
  398.3 146.0 %collective-permute-start.3 = (bf16[512,2048]{1,0:T(8,128)(2,1)}, bf16[512,2048]{1,0:T(8,128)(2,1)}, u32[]{:S(2)}, u32[]{:S(2)}) collective-permute-start(bf16[512,2048]{1,0:T(8,128)(2,1)} %convolution_convert_fusion.5), channel_id=1, source_target_pairs={{0,4},{4,0},{8,12},{12,8},{1,5},{5,1},{9,13},{13,9},{2,6},{6,2},{1... | collective-permute-start | bytes 6291464 | tf_op jit(solution)/shard_map/ppermute | solution.py:327
  435.8 170.5 %collective-permute-start.6 = (bf16[2816,1024]{1,0:T(8,128)(2,1)}, bf16[2816,1024]{1,0:T(8,128)(2,1)}, u32[]{:S(2)}, u32[]{:S(2)}) collective-permute-start(bf16[2816,1024]{1,0:T(8,128)(2,1)} %bitcast.135), channel_id=1, source_target_pairs={{0,8},{4,12},{8,0},{12,4},{1,9},{5,13},{9,1},{13,5},{2,10},{6,14},... | collective-permute-start | bytes 17301512 | tf_op jit(solution)/shard_map/ppermute | solution.py:302
  542.8 186.2 %collective-permute-start.7 = (bf16[2816,1024]{1,0:T(8,128)(2,1)}, bf16[2816,1024]{1,0:T(8,128)(2,1)}, u32[]{:S(2)}, u32[]{:S(2)}) collective-permute-start(bf16[2816,1024]{1,0:T(8,128)(2,1)} %bitcast.172), channel_id=1, source_target_pairs={{0,8},{4,12},{8,0},{12,4},{1,9},{5,13},{9,1},{13,5},{2,10},{6,14},... | collective-permute-start | bytes 17301512 | tf_op jit(solution)/shard_map/ppermute | solution.py:302
  552.3 54.0 %slice-start = ((s8[5767168]{0:T(1024)(128)(4,1)}), s8[4194304]{0:T(1024)(128)(4,1)S(1)}, s32[]{:S(2)}) async-start(s8[5767168]{0:T(1024)(128)(4,1)} %bitcast.136), calls=%async_computation.19 | async-start | bytes 8388608
  553.7 52.6 %slice-start.1 = ((s8[5767168]{0:T(1024)(128)(4,1)}), s8[1572864]{0:T(1024)(128)(4,1)S(1)}, s32[]{:S(2)}) async-start(s8[5767168]{0:T(1024)(128)(4,1)} %bitcast.136), calls=%async_computation.20 | async-start | bytes 3145728
  553.7 64.7 %collective-permute-start.4 = (bf16[512,2048]{1,0:T(8,128)(2,1)S(1)}, bf16[512,2048]{1,0:T(8,128)(2,1)}, u32[]{:S(2)}, u32[]{:S(2)}) collective-permute-start(bf16[512,2048]{1,0:T(8,128)(2,1)S(1)} %add_convert_fusion.8), channel_id=1, source_target_pairs={{0,4},{4,0},{8,12},{12,8},{1,5},{5,1},{9,13},{13,9},{2,6},{6,2},{1... | collective-permute-start | bytes 6291464 | tf_op jit(solution)/shard_map/ppermute | solution.py:323
  745.1 4.4 collective-permute-start.8
  768.0 51.2 %copy-start.21 = (f32[1,1,2048]{2,1,0:T(1,128)S(1)}, f32[1,1,2048]{2,1,0:T(1,128)}, u32[]{:S(2)}) copy-start(f32[1,1,2048]{2,1,0:T(1,128)} %copy-done.20) | copy-start | bytes 24580
  768.0 51.2 %copy-start.27 = (f32[1,1,2048]{2,1,0:T(1,128)S(1)}, f32[1,1,2048]{2,1,0:T(1,128)}, u32[]{:S(2)}) copy-start(f32[1,1,2048]{2,1,0:T(1,128)} %copy-done.26) | copy-start | bytes 24580
  768.0 49.0 %collective-permute-start.9 = (bf16[512,2048]{1,0:T(8,128)(2,1)}, bf16[512,2048]{1,0:T(8,128)(2,1)S(1)}, u32[]{:S(2)}, u32[]{:S(2)}) collective-permute-start(bf16[512,2048]{1,0:T(8,128)(2,1)} %add_convert_fusion.7), channel_id=1, source_target_pairs={{0,16},{1,17},{2,18},{3,19},{4,20},{5,21},{6,22},{7,23},{8,24},{9,... | collective-permute-start | bytes 6291464 | tf_op jit(solution)/shard_map/ppermute | solution.py:365
  821.4 4.3 collective-permute-start.10
  848.3 38.8 %copy-start.48 = (bf16[1,1024,1024]{2,1,0:T(8,128)(2,1)S(1)}, bf16[1,1024,1024]{2,1,0:T(8,128)(2,1)}, u32[]{:S(2)}) copy-start(bf16[1,1024,1024]{2,1,0:T(8,128)(2,1)} %all-gather.12.cloned.1.call-done) | copy-start | bytes 6291460
  892.3 4.2 collective-permute-start.11
  901.8 110.8 %copy-start.28 = (f32[512]{0:T(512)}, f32[512]{0:T(512)S(1)}, u32[]{:S(2)}) copy-start(f32[512]{0:T(512)S(1)} %broadcast_multiply_fusion.9) | copy-start | bytes 6148
  902.6 110.0 %copy-start.34 = (f32[512]{0:T(512)}, f32[512]{0:T(512)S(1)}, u32[]{:S(2)}) copy-start(f32[512]{0:T(512)S(1)} %add_rsqrt_fusion.1) | copy-start | bytes 6148
  903.8 4.3 collective-permute-start.13
  905.1 36.7 %collective-permute-start.12 = (bf16[512,2048]{1,0:T(8,128)(2,1)S(1)}, bf16[512,2048]{1,0:T(8,128)(2,1)}, u32[]{:S(2)}, u32[]{:S(2)}) collective-permute-start(bf16[512,2048]{1,0:T(8,128)(2,1)S(1)} %bitcast.127), channel_id=1, source_target_pairs={{0,4},{4,0},{8,12},{12,8},{1,5},{5,1},{9,13},{13,9},{2,6},{6,2},{1... | collective-permute-start | bytes 6291464 | tf_op jit(solution)/shard_map/ppermute | solution.py:323
  985.9 4.4 collective-permute-start.14
  1017.0 4.2 collective-permute-start.15
  1108.0 4.4 collective-permute-start.16
  1130.5 49.6 %collective-permute-start.17 = (bf16[512,2048]{1,0:T(8,128)(2,1)S(1)}, bf16[512,2048]{1,0:T(8,128)(2,1)S(1)}, u32[]{:S(2)}, u32[]{:S(2)}) collective-permute-start(bf16[512,2048]{1,0:T(8,128)(2,1)S(1)} %fusion.25), channel_id=1, source_target_pairs={{16,0},{17,1},{18,2},{19,3},{20,4},{21,5},{22,6},{23,7},{24,8},{25... | collective-permute-start | bytes 6291464 | tf_op jit(solution)/shard_map/ppermute | solution.py:368
  1181.7 4.5 collective-permute-start.18
  1181.7 34.5 %copy-start.14 = (bf16[512,2048]{1,0:T(8,128)(2,1)S(1)}, bf16[512,2048]{1,0:T(8,128)(2,1)}, u32[]{:S(2)}) copy-start(bf16[512,2048]{1,0:T(8,128)(2,1)} %copy-done.13) | copy-start | bytes 6291460
  1225.5 126.4 %collective-permute-start.27 = (bf16[2816,1024]{1,0:T(8,128)(2,1)S(1)}, bf16[2816,1024]{1,0:T(8,128)(2,1)S(1)}, u32[]{:S(2)}, u32[]{:S(2)}) collective-permute-start(bf16[2816,1024]{1,0:T(8,128)(2,1)S(1)} %convolution_convert_fusion.2), channel_id=1, source_target_pairs={{0,8},{4,12},{8,0},{12,4},{1,9},{5,13},{9,1},{13,5},{2,10},{6,14},... | collective-permute-start | bytes 17301512 | tf_op jit(solution)/shard_map/ppermute | solution.py:376
  1245.0 118.2 %collective-permute-start.19 = (bf16[512,2048]{1,0:T(8,128)(2,1)}, bf16[512,2048]{1,0:T(8,128)(2,1)}, u32[]{:S(2)}, u32[]{:S(2)}) collective-permute-start(bf16[512,2048]{1,0:T(8,128)(2,1)} %fusion.82), channel_id=1, source_target_pairs={{0,4},{4,0},{8,12},{12,8},{1,5},{5,1},{9,13},{13,9},{2,6},{6,2},{1... | collective-permute-start | bytes 6291464 | tf_op jit(solution)/shard_map/ppermute | solution.py:327
  1363.0 586.5 %reduce-scatter.11.cloned.1.call-start = ((), (), s32[]{:S(2)}) async-start(), calls=%async_computation.11 | async-start | bytes 2621440 | tf_op jit(solution)/shard_map/reduce_scatter | solution.py:378
  1394.0 12.9 collective-permute-start.20
  1405.4 175.6 %collective-permute-start.29 = (bf16[2816,1024]{1,0:T(8,128)(2,1)}, bf16[2816,1024]{1,0:T(8,128)(2,1)}, u32[]{:S(2)}, u32[]{:S(2)}) collective-permute-start(bf16[2816,1024]{1,0:T(8,128)(2,1)} %convolution_convert_fusion.1), channel_id=1, source_target_pairs={{0,8},{4,12},{8,0},{12,4},{1,9},{5,13},{9,1},{13,5},{2,10},{6,14},... | collective-permute-start | bytes 17301512 | tf_op jit(solution)/shard_map/ppermute | solution.py:376
  1407.0 170.2 %copy-start.51 = (bf16[512,2048]{1,0:T(8,128)(2,1)}, bf16[512,2048]{1,0:T(8,128)(2,1)S(1)}, u32[]{:S(2)}) copy-start(bf16[512,2048]{1,0:T(8,128)(2,1)S(1)} %collective-permute-done.20) | copy-start | bytes 6291460
  1409.4 167.7 %collective-permute-start.25 = (bf16[1024,1024]{1,0:T(8,128)(2,1)S(1)}, bf16[1024,1024]{1,0:T(8,128)(2,1)S(1)}, u32[]{:S(2)}, u32[]{:S(2)}) collective-permute-start(bf16[1024,1024]{1,0:T(8,128)(2,1)S(1)} %fusion.105), channel_id=1, source_target_pairs={{0,8},{4,12},{8,0},{12,4},{1,9},{5,13},{9,1},{13,5},{2,10},{6,14},... | collective-permute-start | bytes 6291464 | tf_op jit(solution)/shard_map/ppermute | solution.py:376
  1581.0 370.0 %reduce-scatter.15.cloned.1.call-start = ((), (), s32[]{:S(2)}) async-start(), calls=%async_computation.13 | async-start | bytes 7208960 | tf_op jit(solution)/shard_map/reduce_scatter | solution.py:378
  1593.3 360.4 %reduce-scatter.7.cloned.1.call-start = ((), (), s32[]{:S(2)}) async-start(), calls=%async_computation.9 | async-start | bytes 69632 | tf_op jit(solution)/shard_map/reduce_scatter | solution.py:404
  1604.6 125.7 %collective-permute-start.31 = (bf16[2816,1024]{1,0:T(8,128)(2,1)}, bf16[2816,1024]{1,0:T(8,128)(2,1)}, u32[]{:S(2)}, u32[]{:S(2)}) collective-permute-start(bf16[2816,1024]{1,0:T(8,128)(2,1)} %convolution_convert_fusion), channel_id=1, source_target_pairs={{0,8},{4,12},{8,0},{12,4},{1,9},{5,13},{9,1},{13,5},{2,10},{6,14},... | collective-permute-start | bytes 17301512 | tf_op jit(solution)/shard_map/ppermute | solution.py:376
  1676.8 21.2 %copy-start.6 = (bf16[512,2048]{1,0:T(8,128)(2,1)S(1)}, bf16[512,2048]{1,0:T(8,128)(2,1)}, u32[]{:S(2)}) copy-start(bf16[512,2048]{1,0:T(8,128)(2,1)} %copy-done.3) | copy-start | bytes 6291460
  1693.4 4.5 collective-permute-start.21
  1693.6 23.4 %copy-start.42 = (f32[2048]{0:T(1024)S(1)}, f32[2048]{0:T(1024)}, u32[]{:S(2)}) copy-start(f32[2048]{0:T(1024)} %get-tuple-element.52) | copy-start | bytes 24580
  1693.7 23.4 %copy-start.43 = (f32[2048]{0:T(1024)S(1)}, f32[2048]{0:T(1024)}, u32[]{:S(2)}) copy-start(f32[2048]{0:T(1024)} %get-tuple-element.58) | copy-start | bytes 24580
  1717.8 333.8 %reduce-scatter.17.cloned.1.call-start = ((), (), s32[]{:S(2)}) async-start(), calls=%async_computation.14 | async-start | bytes 7208960 | tf_op jit(solution)/shard_map/reduce_scatter | solution.py:378
  1742.2 313.8 %reduce-scatter.9.cloned.1.call-start = ((), (), s32[]{:S(2)}) async-start(), calls=%async_computation.10 | async-start | bytes 7864320 | tf_op jit(solution)/shard_map/reduce_scatter | solution.py:378
  1742.3 146.8 %copy-start.12 = (bf16[512,2048]{1,0:T(8,128)(2,1)S(1)}, bf16[512,2048]{1,0:T(8,128)(2,1)}, u32[]{:S(2)}) copy-start(bf16[512,2048]{1,0:T(8,128)(2,1)} %copy-done.11) | copy-start | bytes 6291460
  1753.0 136.0 %collective-permute-start.23 = (bf16[3072,1024]{1,0:T(8,128)(2,1)S(1)}, bf16[3072,1024]{1,0:T(8,128)(2,1)S(1)}, u32[]{:S(2)}, u32[]{:S(2)}) collective-permute-start(bf16[3072,1024]{1,0:T(8,128)(2,1)S(1)} %convolution_convert_fusion.3), channel_id=1, source_target_pairs={{0,8},{4,12},{8,0},{12,4},{1,9},{5,13},{9,1},{13,5},{2,10},{6,14},... | collective-permute-start | bytes 18874376 | tf_op jit(solution)/shard_map/ppermute | solution.py:376
  1917.2 4.5 collective-permute-start.22
  1943.2 104.6 %all-to-all-start.1 = ((bf16[16,32,2048]{2,1,0:T(8,128)(2,1)}), bf16[16,32,2048]{2,1,0:T(8,128)(2,1)S(1)}, u32[]{:S(2)}, u32[]{:S(2)}) async-start(bf16[16,32,2048]{2,1,0:T(8,128)(2,1)} %bitcast.142), calls=%async_computation.1 | async-start | bytes 4194304 | tf_op jit(solution)/shard_map/all_to_all | solution.py:407
  1949.3 104.9 %collective-permute-start.28 = (bf16[704,512]{1,0:T(8,128)(2,1)}, bf16[704,512]{1,0:T(8,128)(2,1)}, u32[]{:S(2)}, u32[]{:S(2)}) collective-permute-start(bf16[704,512]{1,0:T(8,128)(2,1)} %get-tuple-element.82), channel_id=1, source_target_pairs={{0,4},{4,0},{8,12},{12,8},{1,5},{5,1},{9,13},{13,9},{2,6},{6,2},{1... | collective-permute-start | bytes 2162696 | tf_op jit(solution)/shard_map/ppermute | solution.py:384
  1950.6 98.8 %collective-permute-start.26 = (bf16[256,512]{1,0:T(8,128)(2,1)S(1)}, bf16[256,512]{1,0:T(8,128)(2,1)}, u32[]{:S(2)}, u32[]{:S(2)}) collective-permute-start(bf16[256,512]{1,0:T(8,128)(2,1)S(1)} %get-tuple-element.86), channel_id=1, source_target_pairs={{0,4},{4,0},{8,12},{12,8},{1,5},{5,1},{9,13},{13,9},{2,6},{6,2},{1... | collective-permute-start | bytes 786440 | tf_op jit(solution)/shard_map/ppermute | solution.py:384
  1953.4 106.6 %collective-permute-start.30 = (bf16[704,512]{1,0:T(8,128)(2,1)}, bf16[704,512]{1,0:T(8,128)(2,1)}, u32[]{:S(2)}, u32[]{:S(2)}) collective-permute-start(bf16[704,512]{1,0:T(8,128)(2,1)} %get-tuple-element.84), channel_id=1, source_target_pairs={{0,4},{4,0},{8,12},{12,8},{1,5},{5,1},{9,13},{13,9},{2,6},{6,2},{1... | collective-permute-start | bytes 2162696 | tf_op jit(solution)/shard_map/ppermute | solution.py:384
  2054.2 17.3 collective-permute-start.32
  2059.5 16.9 collective-permute-start.24
  (39 other events, 341.9 us)
Sparse Core Ops, SparseCore 0:
  12.8 162.6 all-gather.9
  177.1 44.5 all-gather.11
  223.9 105.4 all-gather.13
  330.8 104.9 all-gather.15
  437.8 104.9 all-gather.17
  1363.2 99.5 reduce-scatter.12
  1581.1 41.1 reduce-scatter.10
  1625.2 101.5 reduce-scatter.14
  1731.1 52.7 reduce-scatter.6
  1786.1 101.2 reduce-scatter.16
  1900.0 140.2 reduce-scatter.8

commit v2 on v1

--- a/solution.py
+++ b/solution.py
@@ -297,85 +297,242 @@
     chunk_pos = chunked(pos, chunk)
     context = (*rot_tables(pos), chunk_pos[:, None], chunk_pos[None, :])
 
-    def gathered(block):
+    tp_index = lax.axis_index("tp")
+
+    def turned_by_tp(shards, axis=0):
+        count = shards.shape[axis] // tp_count
+        twice = jnp.concatenate([shards, shards], axis=axis)
+        start = lax.rem(tp_count - tp_index, tp_count) * count
+        return lax.dynamic_slice_in_dim(twice, start, tp_count * count, axis)
+
+    def after(x, *others):
+        return lax.optimization_barrier((x, *others))[0]
+
+    own_parts, across_parts = [], []
+
+    def gathered(block_of):
+        block, held = block_of(side), block_of(1 - side)
+        count = block.shape[0]
+        step = len(own_parts)
+        if step == 2:
+            block = after(block, own_parts[0], across_parts[0], inbound)
+        elif step > 2:
+            block = after(block, own_parts[step - 2], across_parts[step - 3])
         own = lax.all_gather(block, "tp", axis=0, tiled=True)
-        other = lax.ppermute(own, "ctx", across_route)
+        wanted = [
+            lax.dynamic_slice_in_dim(own, lax.rem(tp_index + p, tp_count) * count, count, 0)
+            for p in range(1, tp_count)
+        ]
+        arriving = lax.ppermute(jnp.concatenate(wanted, axis=0), "ctx", across_route)
+        own_parts.append(own)
+        across_parts.append(arriving)
+        other = turned_by_tp(jnp.concatenate([held, arriving], axis=0))
         return jnp.where(
             side == 0, jnp.concatenate([own, other], axis=1), jnp.concatenate([other, own], axis=1)
         )
 
-    d_from = side * half_width
-    qkv_block = lax.dynamic_slice(w_qkv[0], (0, d_from, core * columns), (3, half_width, columns))
-    qkv_block = qkv_block.transpose(0, 2, 1).reshape(3 * columns, half_width)
-    out_block = lax.dynamic_slice(w_out[0], (core * columns, d_from), (columns, half_width))
-    gu_block = lax.dynamic_slice(w_gate_up[0], (0, d_from, core * hidden), (2, half_width, hidden))
-    gu_block = gu_block.transpose(0, 2, 1)
-    down_block = lax.dynamic_slice(down_weight[0], (core * hidden, d_from), (hidden, half_width))
+    def qkv_block(half):
+        block = lax.dynamic_slice(w_qkv[0], (0, half * half_width, core * columns), (3, half_width, columns))
+        return block.transpose(0, 2, 1).reshape(3 * columns, half_width)
+
+    def out_block(half):
+        return lax.dynamic_slice(w_out[0], (core * columns, half * half_width), (columns, half_width))
+
+    def gu_block(which, half):
+        block = lax.dynamic_slice(
+            w_gate_up[0], (which, half * half_width, core * hidden), (1, half_width, hidden)
+        )
+        return block[0].T
+
+    def down_block(part, half):
+        start = core * hidden + part * (hidden // 2)
+        return lax.dynamic_slice(down_weight[0], (start, half * half_width), (hidden // 2, half_width))
+
+    wt_out = gathered(out_block)
     wt_qkv = gathered(qkv_block)
-    wt_out = gathered(out_block)
-    wt_gu = jnp.concatenate([gathered(gu_block[0]), gathered(gu_block[1])], axis=0)
-    wt_down = gathered(down_block)
-    bias_all = lax.all_gather(b_qkv[0], "tp", axis=0)
-    bias = lax.dynamic_slice_in_dim(bias_all, core * columns, columns, 2).reshape(tp_count, 3 * columns)
+    wt_gu = jnp.concatenate([gathered(functools.partial(gu_block, w)) for w in range(2)], axis=0)
+    wt_down = jnp.concatenate(
+        [
+            gathered(functools.partial(down_block, part)).reshape(tp_count, hidden // 2, width)
+            for part in range(2)
+        ],
+        axis=1,
+    ).reshape(tp_count * hidden, width)
+    bias_own = lax.dynamic_slice_in_dim(b_qkv[0], core * columns, columns, 1).reshape(1, 3 * columns)
+    bias = [bias_own]
+    for p in range(1, tp_count):
+        ring = [((i + p) % tp_count, i) for i in range(tp_count)]
+        bias.append(lax.ppermute(bias_own, "tp", ring))
+    bias = turned_by_tp(jnp.concatenate(bias, axis=0))
     ff = wt_down.shape[0]
 
     def both(own):
         return jnp.concatenate([own, lax.ppermute(own, "ctx", core_route)], axis=0)
 
-    def summed(a, weight):
-        other = dot_n(a[own_rows:], weight).astype(jnp.bfloat16)
-        arriving = lax.ppermute(other, "ctx", core_route)
-        return dot_n(a[:own_rows], weight) + arriving.astype(jnp.float32)
+    def summed(a, weight, parts=1):
+        step = own_rows // parts
+        spans = [slice(i * step, (i + 1) * step) for i in range(parts)]
+        others = [dot_n(a[own_rows:][span], weight).astype(jnp.bfloat16) for span in spans]
+        arriving = [lax.ppermute(other, "ctx", core_route) for other in others]
+        own = [dot_n(a[:own_rows][span], weight) for span in spans]
+        return [x + y.astype(jnp.float32) for x, y in zip(own, arriving)]
+
+    def split(x, parts):
+        step = x.shape[0] // parts
+        return [x[i * step : (i + 1) * step] for i in range(parts)]
+
+    def over_x(parts, route):
+        return jnp.concatenate([lax.ppermute(part, "section", route) for part in parts], axis=0)
 
     def forward(stream):
         normed = both(ln(stream, gain[0], shift[0]))
         mixed = dot_t(normed, wt_qkv)
         qkv, attended = attn_fwd(mixed, bias, context, tp_count, chunk)
-        hidden_state = stream + summed(attended, wt_out)
+        hidden_state = stream + summed(attended, wt_out)[0]
         normed_two = both(ln(hidden_state, gain[1], shift[1]))
         gate_up = dot_t(normed_two, wt_gu)
         gate, up = gate_up[:, :ff], gate_up[:, ff:]
         activation = (jax.nn.silu(gate) * up).astype(jnp.bfloat16)
-        out = (hidden_state + summed(activation, wt_down)).astype(jnp.bfloat16)
+        out = [
+            (x + y).astype(jnp.bfloat16)
+            for x, y in zip(split(hidden_state, 2), summed(activation, wt_down, 2))
+        ]
         return out, (stream, normed, qkv, attended, hidden_state, normed_two, gate_up, activation)
+
+    def far_near(right):
+        far = lax.dynamic_slice_in_dim(right, (1 - side) * half_width, half_width, 1)
+        near = lax.dynamic_slice_in_dim(right, side * half_width, half_width, 1)
+        return far, near
+
+    def far_term(left, right):
+        return dot_0(left, far_near(right)[0]).astype(jnp.bfloat16)
+
+    def near_total(left, right, arriving, *others):
+        near = far_near(right)[1]
+        if others:
+            near = after(near, *others)
+        return (dot_0(left, near) + arriving.astype(jnp.float32)).astype(jnp.bfloat16)
+
+    def across(term, *others):
+        return lax.ppermute(after(term, *others) if others else term, "ctx", across_route)
+
+    def over_tp(term):
+        return lax.psum_scatter(term, "tp", scatter_dimension=0, tiled=True)
+
+    together = lax.optimization_barrier
+
+    def part_of(x, i, parts, axis):
+        shard = x.shape[axis] // tp_count
+        step = shard // parts
+        return jnp.concatenate(
+            [
+                lax.slice_in_dim(x, z * shard + i * step, z * shard + (i + 1) * step, axis=axis)
+                for z in range(tp_count)
+            ],
+            axis=axis,
+        )
+
+    def mlp_back(act_grad, gate_up):
+        gate, up = gate_up[:, :ff], gate_up[:, ff:]
+        sigma = jax.nn.sigmoid(gate)
+        gate_grad = (act_grad * up * sigma * (1.0 + gate * (1.0 - sigma))).astype(jnp.bfloat16)
+        up_grad = (act_grad * gate * sigma).astype(jnp.bfloat16)
+        return gate_grad, up_grad, jnp.concatenate([gate_grad, up_grad], axis=1)
 
     def backward(grad_out, stored):
         stream, normed, qkv, attended, hidden_state, normed_two, gate_up, activation = stored
+        gu_grad = mlp_back(dot_t(both(grad_out), wt_down), gate_up)[2]
+        result = ln_back(hidden_state, summed(gu_grad, wt_gu)[0], gain[1])[0]
+        hidden_grad = grad_out.astype(jnp.float32) + result
+        ctx_grad = dot_t(both(hidden_grad.astype(jnp.bfloat16)), wt_out).astype(jnp.bfloat16)
+        qkv_grad, _ = attn_bwd(qkv, ctx_grad, context, tp_count, chunk)
+        one_grad = jnp.concatenate(summed(qkv_grad, wt_qkv, 2), axis=0)
+        result = ln_back(stream, one_grad, gain[0])[0]
+        return split((hidden_grad + result).astype(jnp.bfloat16), 2)
+
+    def last_backward(grad_out, stored, final_out):
+        stream, normed, qkv, attended, hidden_state, normed_two, gate_up, activation, act_a, act_b = stored
+        grad_f32 = grad_out.astype(jnp.float32)
         mlp_grad = both(grad_out)
-        act_grad = dot_t(mlp_grad, wt_down)
-        gate, up = gate_up[:, :ff], gate_up[:, ff:]
-        sigma = jax.nn.sigmoid(gate)
-        gu_grad = jnp.concatenate(
-            [act_grad * up * sigma * (1.0 + gate * (1.0 - sigma)), act_grad * gate * sigma], axis=1
-        ).astype(jnp.bfloat16)
-        two_grad = summed(gu_grad, wt_gu)
+        far_a, far_b = far_term(act_a, mlp_grad), far_term(act_b, mlp_grad)
+
+        mlp_in, far_a, far_b = together((mlp_grad, far_a, far_b))
+        arriving = across(far_a)
+        gate_grad, up_grad, gu_grad = mlp_back(dot_t(mlp_in, wt_down), gate_up)
+
+        arriving, far_b, gate_grad, up_grad, act_a = together((arriving, far_b, gate_grad, up_grad, act_a))
+        arriving_b = across(far_b)
+        sum_a = over_tp(near_total(act_a, mlp_grad, arriving))
+        gu_grad = jnp.concatenate([gate_grad, up_grad], axis=1)
+        two_other = dot_n(gu_grad[own_rows:], wt_gu).astype(jnp.bfloat16)
+        far_gate = far_term(gate_grad, normed_two)
+
+        arriving_b, far_gate, gu_grad, two_other, act_b, up_grad = together(
+            (arriving_b, far_gate, gu_grad, two_other, act_b, up_grad)
+        )
+        arriving_gate = across(far_gate)
+        sum_b = over_tp(near_total(act_b, mlp_grad, arriving_b))
+        two_grad = dot_n(gu_grad[:own_rows], wt_gu) + lax.ppermute(two_other, "ctx", core_route).astype(jnp.float32)
         result, gain_two, shift_two = ln_back(hidden_state, two_grad, gain[1])
-        hidden_grad = grad_out.astype(jnp.float32) + result
+        hidden_grad = grad_f32 + result
         attn_grad = both(hidden_grad.astype(jnp.bfloat16))
+        far_up = far_term(up_grad, normed_two)
+
+        arriving_gate, far_up, gate_grad, attn_grad, hidden_grad = together(
+            (arriving_gate, far_up, gate_grad, attn_grad, hidden_grad)
+        )
+        far_up_a, far_up_b = split(far_up, 2)
+        arriving = across(far_up_a)
+        sum_gate = over_tp(near_total(gate_grad, normed_two, arriving_gate))
         ctx_grad = dot_t(attn_grad, wt_out).astype(jnp.bfloat16)
+
+        arriving, far_up_b, ctx_grad = together((arriving, far_up_b, ctx_grad))
+        arriving_up = jnp.concatenate([arriving, across(far_up_b)], axis=0)
         qkv_grad, bias_grad = attn_bwd(qkv, ctx_grad, context, tp_count, chunk)
-        one_grad = summed(qkv_grad, wt_qkv)
+        qkv_a, qkv_b = (part_of(qkv_grad, i, 2, 1) for i in range(2))
+        far_a = far_term(qkv_a, normed)
+
+        arriving_up, far_a, qkv_a, qkv_b, qkv_grad, up_grad, attn_grad = together(
+            (arriving_up, far_a, qkv_a, qkv_b, qkv_grad, up_grad, attn_grad)
+        )
+        arriving = across(far_a)
+        sum_up = over_tp(near_total(up_grad, normed_two, arriving_up))
+        one_other = dot_n(qkv_grad[own_rows:], wt_qkv).astype(jnp.bfloat16)
+        far_b = far_term(qkv_b, normed)
+
+        arriving, far_b, one_other, qkv_grad, qkv_a, qkv_b = together(
+            (arriving, far_b, one_other, qkv_grad, qkv_a, qkv_b)
+        )
+        arriving_b = across(far_b)
+        sum_qkv_a = over_tp(near_total(qkv_a, normed, arriving))
+        one_grad = dot_n(qkv_grad[:own_rows], wt_qkv) + lax.ppermute(one_other, "ctx", core_route).astype(jnp.float32)
         result, gain_one, shift_one = ln_back(stream, one_grad, gain[0])
         input_grad = (hidden_grad + result).astype(jnp.bfloat16)
+        ends = jnp.where(first, input_grad, final_out)
+        far_out = far_term(attended, attn_grad)
+
+        arriving_b, far_out, ends, qkv_b = together((arriving_b, far_out, ends, qkv_b))
+        arriving_out = across(far_out)
+        ends = lax.all_to_all(
+            ends.reshape(ctx_count * tp_count, piece, width), ("ctx", "tp"), 0, 0, tiled=True
+        )
+        sum_qkv_b = over_tp(near_total(qkv_b, normed, arriving_b))
+        sum_out = over_tp(near_total(attended, attn_grad, arriving_out))
         small = (jnp.stack([gain_one, gain_two]), jnp.stack([shift_one, shift_two]), bias_grad)
-        pairs = ((activation, mlp_grad), (gu_grad, normed_two), (attended, attn_grad), (qkv_grad, normed))
-        return input_grad, small, pairs
+        sum_down = jnp.concatenate([sum_a, sum_b], axis=0)
+        sum_qkv = jnp.concatenate([sum_qkv_a, sum_qkv_b], axis=0)
+        return ends, small, (sum_down, sum_gate, sum_up, sum_out, sum_qkv)
 
     sent, _ = forward(inbound.astype(jnp.float32))
-    arriving = lax.ppermute(sent, "section", [(0, 1)])
+    arriving = over_x(sent, [(0, 1)])
     final_out, stored = forward(jnp.where(first, inbound, arriving).astype(jnp.float32))
-    sent_back, _, _ = backward(inbound, stored)
-    arriving_back = lax.ppermute(sent_back, "section", [(1, 0)])
+    arriving_back = over_x(backward(inbound, stored), [(1, 0)])
+    halves = tuple(part_of(stored[-1], i, 2, 1) for i in range(2))
+    arriving_back, final_out, *halves = together((arriving_back, jnp.concatenate(final_out, axis=0), *halves))
+    stored = (*stored, *halves)
     grad_out = jnp.where(first, arriving_back, inbound)
-    input_grad, small, pairs = backward(grad_out, stored)
-
-    def weight_grad(pair):
-        left, right = pair
-        far = lax.dynamic_slice_in_dim(right, (1 - side) * half_width, half_width, 1)
-        near = lax.dynamic_slice_in_dim(right, side * half_width, half_width, 1)
-        arriving = lax.ppermute(dot_0(left, far).astype(jnp.bfloat16), "ctx", across_route)
-        total = (dot_0(left, near) + arriving.astype(jnp.float32)).astype(jnp.bfloat16)
-        return lax.psum_scatter(total, "tp", scatter_dimension=0, tiled=True)
+    ends, small, sums = last_backward(grad_out, stored, final_out)
+    down_sum, gate_sum, up_sum, out_sum, qkv_sum = sums
 
     def settled(term):
         share = half_width // 2
@@ -387,13 +544,11 @@
             core == 0, jnp.concatenate([kept, got], axis), jnp.concatenate([got, kept], axis)
         ).astype(jnp.float32)
 
-    act_pair, gu_pair, out_pair, qkv_pair = pairs
-    grad_down = settled(weight_grad(act_pair))
-    gu_left, gu_right = gu_pair
-    grad_gate = settled(weight_grad((gu_left[:, :ff], gu_right)))
-    grad_up = settled(weight_grad((gu_left[:, ff:], gu_right)))
-    grad_out_w = settled(weight_grad(out_pair))
-    grad_qkv = settled(weight_grad(qkv_pair).reshape(3, columns, half_width))
+    grad_down = settled(down_sum)
+    grad_gate = settled(gate_sum)
+    grad_up = settled(up_sum)
+    grad_out_w = settled(out_sum)
+    grad_qkv = settled(qkv_sum.reshape(3, columns, half_width))
 
     gain_terms, shift_terms, bias_terms = small
     bias_terms = bias_terms.reshape(tp_count, 3, columns).transpose(1, 0, 2)[:, :, None]
@@ -401,10 +556,10 @@
         (jnp.arange(2) == core)[None, None, :, None], bias_terms, 0.0
     ).reshape(3, tp_count * 2 * columns)
     vectors = jnp.concatenate([gain_terms, shift_terms, bias_full], axis=0)
-    vectors = lax.psum_scatter(vectors, ("ctx", "tp"), scatter_dimension=1, tiled=True)
-
-    ends = jnp.where(first, input_grad, final_out).reshape(ctx_count * tp_count, piece, width)
-    ends = lax.all_to_all(ends, ("ctx", "tp"), 0, 0, tiled=True)
+    share = width // (ctx_count * tp_count)
+    vectors = vectors.reshape(-1, ctx_count * tp_count, share).transpose(1, 0, 2)
+    vectors = jnp.sum(lax.all_to_all(vectors, ("ctx", "tp"), 0, 0, tiled=True), axis=0).reshape(-1, share)
+
     ends = ends.reshape(ctx_count // 2, 2, tp_count, piece, width).transpose(0, 2, 1, 3, 4)
     ends = ends.reshape(micro_count, slice_len, 1, width)
     return (

time: 2090 us -> 1900 us (0.909)
  waiting for transfers between devices: 1130 us -> 748 us
  other arithmetic: 81.6 us -> 166 us
  local copies, waits for them, and re-layouts: 68.5 us -> 133 us
  blocking collectives: 13.8 us -> 47.4 us
    ppermute x20 -> x32, waiting for transfers between devices: 642 us -> 375 us  [the longest x8 283 us: across(): lax.ppermute(after(term, *others) if others else term, 'ctx', across_route)]
    all_gather x5 -> x6, waiting for transfers between devices: 378 us -> 254 us  [gathered(): own = lax.all_gather(block, 'tp', axis=0, tiled=True)]
    concatenate x0 -> x21, other arithmetic: none -> 83.1 us  [the longest x5 48.9 us: turned_by_tp(): twice = jnp.concatenate([shards, shards], axis=axis)]
    all_to_all x0 -> x1, blocking collectives: none -> 47.4 us  [bulk_device(): lax.all_to_all(vectors, ('ctx', 'tp'), 0, 0, tiled=True)]
    all_to_all x1, waiting for transfers between devices: 0.01 us -> 42.6 us  [bulk_device(): lax.all_to_all(fresh, ('ctx', 'tp'), 0, 0, tiled=True)]
    all_to_all x1, waiting for transfers between devices: 91.5 us -> 64.4 us  [last_backward(): lax.all_to_all(ends.reshape(ctx_count * tp_count, piece, width), ('ctx',...]
    dynamic_slice x7 -> x18, local copies, waits for them, and re-layouts: 19.1 us -> 44.6 us  [the longest x5 19.5 us: gu_block(): lax.dynamic_slice(w_gate_up[0], (which, half * half_width, core * hidden)...]
    dot_general x10 -> x14, matrix products: 94.9 us -> 106 us  [dot_0(): lax.dot_general(a, b, (((0,), (0,)), ((), ())), preferred_element_type=jn...]
  transfers between devices with their start and end apart: 46 -> 60, of which waited for: 24 -> 26; matrix products, arithmetic and copies ran while one was open for 21% -> 36% of each run, Pallas kernels for 5% -> 9%
where the time goes in v2:
time: 1900 us
  waiting for transfers between devices  748 us (39%)
  matrix products  522 us (27%)
  Pallas kernels  204 us (11%)
  other arithmetic  166 us (9%)
  local copies, waits for them, and re-layouts  133 us (7%)
  blocking collectives  47.4 us (2%)
  starting transfers between devices  44.7 us (2%)
  between operations  31.3 us (2%)
    ppermute x8, waiting for transfers between devices, across(): lax.ppermute(after(term, *others) if others else term, 'ctx', across_route)  283 us
    all_gather x6, waiting for transfers between devices, gathered(): own = lax.all_gather(block, 'tp', axis=0, tiled=True)  254 us
    dot_general x22, matrix products, dot_n(): lax.dot_general(a, b, (((1,), (0,)), ((), ())), preferred_element_type=jn...  239 us
    dot_general x8, matrix products, dot_t(): lax.dot_general(a, b, (((1,), (1,)), ((), ())), preferred_element_type=jn...  178 us
    pallas_call x2, Pallas kernels, attn_bwd(): pl.pallas_call(functools.partial(attn_bwd_kernel, heads, chunk), grid=(gr...  126 us
    dot_general x14, matrix products, dot_0(): lax.dot_general(a, b, (((0,), (0,)), ((), ())), preferred_element_type=jn...  106 us
    ppermute x4, waiting for transfers between devices, over_x(): lax.ppermute(part, 'section', route)  79.1 us
    pallas_call x2, Pallas kernels, attn_fwd(): pl.pallas_call(functools.partial(attn_fwd_kernel, heads, chunk), grid=(gr...  78 us
  transfers between devices with their start and end apart: 60, of which 26 were waited for; matrix products, arithmetic and copies ran while one was open for 36% of the time, Pallas kernels for 9%

profile of v2, /device:TPU:0, one launch (start us, length us, event | category | flops | bytes accessed | tf_op | source)
XLA Modules:
  0.0 1897.1 jit_solution(17418470246756368456)
XLA Ops:
  40.1 7.4 all-to-all-start
  47.5 29.3 %all-gather.18.cloned.1.call-done = bf16[1,1024,1024]{2,1,0:T(8,128)(2,1)} async-done(((bf16[1,256,1024]{2,1,0:T(8,128)(2,1)}), bf16[1,1024,1024]{2,1,0:T(8,128)(2,1)}) %all-gather.18.cloned.1.call-update) | async-done | bytes 2097168 | tf_op jit(solution)/shard_map/all_gather | solution.py:321
  81.1 9.5 constant_dynamic-slice_fusion.22
  93.2 42.6 %all-to-all-done = bf16[16,32,2048]{2,1,0:T(8,128)(2,1)S(1)} async-done(((bf16[16,32,2048]{2,1,0:T(8,128)(2,1)}), bf16[16,32,2048]{2,1,0:T(8,128)(2,1)S(1)}, u32[]{:S(2)}, u32[]{:S(2)}) %all-to-all-start) | async-done | bytes 2097184 | tf_op jit(solution)/shard_map/all_to_all | solution.py:287
  139.1 65.9 %all-gather.8.cloned.1.call-done = bf16[3072,1024]{1,0:T(8,128)(2,1)} async-done(((bf16[768,1024]{1,0:T(8,128)(2,1)}), bf16[3072,1024]{1,0:T(8,128)(2,1)}) %all-gather.8.cloned.1.call-update) | async-done | bytes 6291472 | tf_op jit(solution)/shard_map/all_gather | solution.py:321
  244.1 68.1 %all-gather.10.cloned.1.call-done = bf16[2816,1024]{1,0:T(8,128)(2,1)} async-done(((bf16[704,1024]{1,0:T(8,128)(2,1)}), bf16[2816,1024]{1,0:T(8,128)(2,1)}) %all-gather.10.cloned.1.call-update) | async-done | bytes 5767184 | tf_op jit(solution)/shard_map/all_gather | solution.py:321
  319.2 11.4 fusion.3
  330.5 21.9 %fusion.50.mixed = f32[1024,3072]{1,0:T(8,128)} fusion(bf16[512,2048]{1,0:T(8,128)(2,1)} %collective-permute-done, bf16[512,2048]{1,0:T(8,128)(2,1)} %fusion.49, bf16[3072,1024]{1,0:T(8,128)(2,1)} %fusion.3, bf16[3072,1024]{1,0:T(8,128)(2,1)} %all-gather.8.cloned.1.call-done, pred[]{:T(512)S(6)} %eq.31), kind=kOutput, calls=%fused_computation.123 | convolution fusion | flops 12949913600 | bytes 29360128 | tf_op jit(solution)/shard_map/dot_general | solution.py:59
  352.4 39.3 %shard_map.170 = (bf16[1024,3072]{1,0:T(8,128)(2,1)}, bf16[1024,1024]{1,0:T(8,128)(2,1)}) custom-call(f32[1024,3072]{1,0:T(8,128)} %fusion.50.mixed, f32[4,1,768]{2,1,0:T(1,128)} %reshape.425.bias, f32[1024,128]{1,0:T(8,128)} %concatenate.290.cos_t, f32[1024,128]{1,0:T(8,128)} %concatenate.291.low_t, f32[1024,128]{1,0:T(8,128)} %concatenate.292.high_t, ...), custom_call_target="tpu_custom_call" | custom-call | flops 12884901888 | bytes 22020096 | tf_op jit(solution)/shard_map/pallas_call | solution.py:187
  402.5 9.7 fusion.195
  428.3 12.1 fusion.12
  440.4 7.0 maximum_select_fusion.1
  447.4 30.7 %all-gather.14.cloned.1.call-done = bf16[1408,1024]{1,0:T(8,128)(2,1)} async-done(((bf16[352,1024]{1,0:T(8,128)(2,1)}), bf16[1408,1024]{1,0:T(8,128)(2,1)}) %all-gather.14.cloned.1.call-update) | async-done | bytes 2883600 | tf_op jit(solution)/shard_map/all_gather | solution.py:321
  482.8 54.6 %all-gather.16.cloned.1.call-done = bf16[1408,1024]{1,0:T(8,128)(2,1)} async-done(((bf16[352,1024]{1,0:T(8,128)(2,1)}), bf16[1408,1024]{1,0:T(8,128)(2,1)}) %all-gather.16.cloned.1.call-update) | async-done | bytes 2883600 | tf_op jit(solution)/shard_map/all_gather | solution.py:321
  542.2 11.9 fusion.9
  554.1 7.0 maximum_select_fusion.2
  561.2 34.3 %fusion.54 = f32[1024,5632]{1,0:T(8,128)} fusion(bf16[512,2048]{1,0:T(8,128)(2,1)} %collective-permute-done.7, bf16[512,2048]{1,0:T(8,128)(2,1)} %add_convert_fusion.8, bf16[2816,2048]{1,0:T(8,128)(2,1)} %maximum_select_fusion.2, bf16[2816,2048]{1,0:T(8,128)(2,1)} %maximum_select_fusion.1), kind=kOutput, calls=%fused_computation.132 | convolution fusion | flops 23676846080 | bytes 50331648 | tf_op jit(solution)/shard_map/dot_general | solution.py:59
  595.4 9.4 fusion
  604.9 7.5 collective-permute-done.11
  612.4 8.2 fusion.85
  625.9 9.0 pad_maximum_fusion.1
  653.1 18.8 collective-permute-done.13
  672.0 21.5 %collective-permute-done.15 = bf16[256,2048]{1,0:T(8,128)(2,1)S(1)} collective-permute-done((bf16[256,2048]{1,0:T(8,128)(2,1)S(1)}, bf16[256,2048]{1,0:T(8,128)(2,1)S(1)}, u32[]{:S(2)}, u32[]{:S(2)}) %collective-permute-start.15) | collective-permute-done | bytes 1048608 | tf_op jit(solution)/shard_map/ppermute | solution.py:385
  707.6 22.2 %fusion.45.mixed = f32[1024,3072]{1,0:T(8,128)} fusion(bf16[512,2048]{1,0:T(8,128)(2,1)} %collective-permute-done.16, bf16[512,2048]{1,0:T(8,128)(2,1)} %copy-done.38, bf16[3072,1024]{1,0:T(8,128)(2,1)} %fusion.3, bf16[3072,1024]{1,0:T(8,128)(2,1)} %all-gather.8.cloned.1.call-done, pred[]{:T(512)S(6)} %eq.31), kind=kOutput, calls=%fused_computation.118 | convolution fusion | flops 12949913600 | bytes 29360128 | tf_op jit(solution)/shard_map/dot_general | solution.py:59
  729.8 38.7 %shard_map.171 = (bf16[1024,3072]{1,0:T(8,128)(2,1)}, bf16[1024,1024]{1,0:T(8,128)(2,1)}) custom-call(f32[1024,3072]{1,0:T(8,128)} %fusion.45.mixed, f32[4,1,768]{2,1,0:T(1,128)} %reshape.425.bias, f32[1024,128]{1,0:T(8,128)} %concatenate.290.cos_t, f32[1024,128]{1,0:T(8,128)} %concatenate.291.low_t, f32[1024,128]{1,0:T(8,128)} %concatenate.292.high_t, ...), custom_call_target="tpu_custom_call" | custom-call | flops 12884901888 | bytes 22020096 | tf_op jit(solution)/shard_map/pallas_call | solution.py:187
  787.8 33.8 %fusion.44 = f32[1024,5632]{1,0:T(8,128)} fusion(bf16[512,2048]{1,0:T(8,128)(2,1)} %collective-permute-done.19, bf16[512,2048]{1,0:T(8,128)(2,1)} %copy-done.42, bf16[2816,2048]{1,0:T(8,128)(2,1)} %maximum_select_fusion.2, bf16[2816,2048]{1,0:T(8,128)(2,1)} %maximum_select_fusion.1), kind=kOutput, calls=%fused_computation.117 | convolution fusion | flops 23676846080 | bytes 50331648 | tf_op jit(solution)/shard_map/dot_general | solution.py:59
  821.6 26.8 %multiply_convert_fusion.4 = (bf16[1024,2816]{1,0:T(8,128)(2,1)}, bf16[1024,2816]{1,0:T(8,128)(2,1)}, bf16[1024,2816]{1,0:T(8,128)(2,1)}) fusion(f32[1024,5632]{1,0:T(8,128)} %fusion.44, bf16[2816,2048]{1,0:T(8,128)(2,1)} %bitcast.194, bf16[512,2048]{1,0:T(8,128)(2,1)} %collective-permute-done.18, bf16[512,2048]{1,0:T(8,128)(2,1)S(1)} %bitcast.183), kind=kOutput, calls=%fused_computation.27 | convolution fusion | flops 11865686016 | bytes 56098816 | tf_op jit(solution)/shard_map/dot_general | solution.py:59
  848.5 17.1 fusion.79
  865.8 8.8 convolution_convert_fusion.8
  875.0 22.1 %fusion.183 = (f32[512]{0:T(512)S(1)}, f32[512]{0:T(512)S(1)}, f32[512,2048]{1,0:T(8,128)}) fusion(f32[512]{0:T(512)S(1)} %add_rsqrt_fusion.2, f32[512,2048]{1,0:T(8,128)} %copy-done.4, f32[512]{0:T(512)S(1)} %broadcast_multiply_fusion.10, f32[2048]{0:T(1024)S(1)} %bitcast.242, bf16[512,2048]{1,0:T(8,128)(2,1)} %collective-permute-done.20, ...), kind=kOutput, calls=%fused_computation.367 | convolution fusion | flops 11877220352 | bytes 45105152 | tf_op jit(solution)/shard_map/dot_general | solution.py:67
  903.4 8.9 convolution_convert_fusion.9
  928.1 9.8 fusion.100
  937.9 8.2 fusion.111.ctx
  946.2 63.1 %shard_map.172 = (bf16[1024,3072]{1,0:T(8,128)(2,1)}, f32[4,1,768]{2,1,0:T(1,128)}) custom-call(bf16[1024,3072]{1,0:T(8,128)(2,1)} %get-tuple-element.67.qkv, bf16[1024,1024]{1,0:T(8,128)(2,1)} %fusion.111.ctx, f32[1024,128]{1,0:T(8,128)} %concatenate.290.cos_t, f32[1024,128]{1,0:T(8,128)} %concatenate.291.low_t, f32[1024,128]{1,0:T(8,128)} %concatenate.292.high_t, ...), custom_call_target="tpu_custom_call" | custom-call | flops 30064771072 | bytes 15728640 | tf_op jit(solution)/shard_map/pallas_call | solution.py:222
  1009.3 13.7 convolution_convert_fusion.12
  1023.2 13.7 convolution_convert_fusion.13
  1037.3 12.5 convert_add_fusion.5
  1049.8 12.7 convert_add_fusion.6
  1074.1 8.1 fusion.101
  1083.6 16.8 collective-permute-done.25
  1100.5 22.0 %collective-permute-done.24 = bf16[256,2048]{1,0:T(8,128)(2,1)S(1)} collective-permute-done((bf16[256,2048]{1,0:T(8,128)(2,1)S(1)}, bf16[256,2048]{1,0:T(8,128)(2,1)S(1)}, u32[]{:S(2)}, u32[]{:S(2)}) %collective-permute-start.24) | collective-permute-done | bytes 1048608 | tf_op jit(solution)/shard_map/ppermute | solution.py:385
  1140.6 24.6 %multiply_convert_fusion = (bf16[1024,2816]{1,0:T(8,128)(2,1)}, bf16[1024,2816]{1,0:T(8,128)(2,1)}) fusion(f32[1024,5632]{1,0:T(8,128)} %fusion.44, bf16[1024,2048]{1,0:T(8,128)(2,1)} %pad_maximum_fusion.7, bf16[2816,2048]{1,0:T(8,128)(2,1)} %bitcast.199), kind=kOutput, calls=%fused_computation.23 | convolution fusion | flops 11848646656 | bytes 50331648 | tf_op jit(solution)/shard_map/dot_general | solution.py:59
  1165.2 38.7 %collective-permute-done.29 = bf16[1408,1024]{1,0:T(8,128)(2,1)} collective-permute-done((bf16[1408,1024]{1,0:T(8,128)(2,1)}, bf16[1408,1024]{1,0:T(8,128)(2,1)}, u32[]{:S(2)}, u32[]{:S(2)}) %collective-permute-start.29) | collective-permute-done | bytes 2883616 | tf_op jit(solution)/shard_map/ppermute | solution.py:417
  1217.1 12.0 convolution_convert_fusion.1
  1234.8 19.2 %fusion.80 = bf16[512,2048]{1,0:T(8,128)(2,1)} fusion(bf16[1024,5632]{1,0:T(8,128)(2,1)} %constant_dynamic-update-slice_fusion.3, bf16[2816,2048]{1,0:T(8,128)(2,1)} %maximum_select_fusion.2, bf16[2816,2048]{1,0:T(8,128)(2,1)} %maximum_select_fusion.1), kind=kOutput, calls=%fused_computation.175 | convolution fusion | flops 11858345984 | bytes 30932992 | tf_op jit(solution)/shard_map/dot_general | solution.py:67
  1254.0 13.9 collective-permute-done.30
  1269.4 7.8 add_convert_fusion.4
  1277.4 20.4 %multiply_reduce_fusion = (f32[2048]{0:T(1024)}, f32[512]{0:T(512)S(1)}, f32[512]{0:T(512)S(1)}, f32[2048]{0:T(1024)}, f32[512,2048]{1,0:T(8,128)S(1)}) fusion(f32[512]{0:T(512)S(1)} %copy-done.76, f32[512,2048]{1,0:T(8,128)} %copy-done.4, f32[512]{0:T(512)S(1)} %copy-done.67, f32[2048]{0:T(1024)S(1)} %bitcast.243, ...), kind=kOutput, calls=%fused_computation.147 | convolution fusion | flops 11868827648 | bytes 39354368 | tf_op jit(solution)/shard_map/dot_general | solution.py:67
  1301.2 11.1 convolution_convert_fusion
  1314.8 80.1 %collective-permute-done.31 = bf16[2816,1024]{1,0:T(8,128)(2,1)} collective-permute-done((bf16[2816,1024]{1,0:T(8,128)(2,1)}, bf16[2816,1024]{1,0:T(8,128)(2,1)}, u32[]{:S(2)}, u32[]{:S(2)}) %collective-permute-start.31) | collective-permute-done | bytes 5767200 | tf_op jit(solution)/shard_map/ppermute | solution.py:417
  1395.0 10.3 add_convert_fusion.1
  1417.2 55.7 %collective-permute-done.34 = bf16[1408,1024]{1,0:T(8,128)(2,1)S(1)} collective-permute-done((bf16[1408,1024]{1,0:T(8,128)(2,1)S(1)}, bf16[1408,1024]{1,0:T(8,128)(2,1)S(1)}, u32[]{:S(2)}, u32[]{:S(2)}) %collective-permute-start.34) | collective-permute-done | bytes 2883616 | tf_op jit(solution)/shard_map/ppermute | solution.py:417
  1476.1 63.0 %shard_map.173 = (bf16[1024,3072]{1,0:T(8,128)(2,1)}, f32[4,1,768]{2,1,0:T(1,128)}) custom-call(bf16[1024,3072]{1,0:T(8,128)(2,1)} %get-tuple-element.67.qkv, bf16[1024,1024]{1,0:T(8,128)(2,1)} %convolution_convert_fusion.14.ctx, f32[1024,128]{1,0:T(8,128)} %concatenate.290.cos_t, f32[1024,128]{1,0:T(8,128)} %concatenate.291.low_t, ...), custom_call_target="tpu_custom_call" | custom-call | flops 30064771072 | bytes 15728640 | tf_op jit(solution)/shard_map/pallas_call | solution.py:222
  1545.9 7.8 convolution_convert_fusion.3
  1557.1 9.8 add_convert_fusion
  1567.5 6.4 convolution_convert_fusion.2
  1573.9 16.8 fusion.76
  1590.7 45.2 %collective-permute-done.36 = bf16[1536,1024]{1,0:T(8,128)(2,1)S(1)} collective-permute-done((bf16[1536,1024]{1,0:T(8,128)(2,1)}, bf16[1536,1024]{1,0:T(8,128)(2,1)S(1)}, u32[]{:S(2)}, u32[]{:S(2)}) %collective-permute-start.36) | collective-permute-done | bytes 3145760 | tf_op jit(solution)/shard_map/ppermute | solution.py:417
  1648.9 17.7 fusion.43
  1669.8 49.3 %collective-permute-done.37 = bf16[1536,1024]{1,0:T(8,128)(2,1)} collective-permute-done((bf16[1536,1024]{1,0:T(8,128)(2,1)}, bf16[1536,1024]{1,0:T(8,128)(2,1)}, u32[]{:S(2)}, u32[]{:S(2)}) %collective-permute-start.37) | collective-permute-done | bytes 3145760 | tf_op jit(solution)/shard_map/ppermute | solution.py:417
  1719.1 6.6 add_convert_fusion.2
  1726.6 47.4 %all_to_all.15 = f32[16,7,128]{2,1,0:T(8,128)} all-to-all(f32[16,7,128]{2,1,0:T(8,128)S(1)} %copy.94), channel_id=1, replica_groups=mesh['section'=2,'ctx'=4,'tp'=4] {'ctx','tp'}, dimensions={0} | all-to-all | bytes 114688 | tf_op jit(solution)/shard_map/all_to_all | solution.py:561
  1778.0 6.6 add_convert_fusion.6
  1801.5 64.4 %all-to-all-done.1 = bf16[16,32,2048]{2,1,0:T(8,128)(2,1)S(1)} async-done(((bf16[16,32,2048]{2,1,0:T(8,128)(2,1)}), bf16[16,32,2048]{2,1,0:T(8,128)(2,1)S(1)}, u32[]{:S(2)}, u32[]{:S(2)}) %all-to-all-start.1) | async-done | bytes 2097184 | tf_op jit(solution)/shard_map/all_to_all | solution.py:516
  (499 shorter events, 334.8 us)
Async XLA Ops:
  7.2 198.0 %copy-start = (f32[1,3,512]{2,0,1:T(1,128)S(1)}, f32[1,3,512]{2,0,1:T(1,128)}, u32[]{:S(2)}) copy-start(f32[1,3,512]{2,0,1:T(1,128)} %param.18) | copy-start | bytes 18436
  7.2 69.7 %all-gather.18.cloned.1.call-start = ((), (), s32[]{:S(2)}) async-start(), calls=%async_computation.22 | async-start | bytes 2621440 | tf_op jit(solution)/shard_map/all_gather | solution.py:321
  9.5 195.5 %all-gather.8.cloned.1.call-start = ((), (), s32[]{:S(2)}) async-start(), calls=%async_computation.10 | async-start | bytes 7864320 | tf_op jit(solution)/shard_map/all_gather | solution.py:321
  40.1 95.8 %all-to-all-start = ((bf16[16,32,2048]{2,1,0:T(8,128)(2,1)}), bf16[16,32,2048]{2,1,0:T(8,128)(2,1)S(1)}, u32[]{:S(2)}, u32[]{:S(2)}) async-start(bf16[16,32,2048]{2,1,0:T(8,128)(2,1)} %bitcast.205), calls=%async_computation | async-start | bytes 4194304 | tf_op jit(solution)/shard_map/all_to_all | solution.py:287
  47.4 264.7 %all-gather.10.cloned.1.call-start = ((), (), s32[]{:S(2)}) async-start(), calls=%async_computation.11 | async-start | bytes 7208960 | tf_op jit(solution)/shard_map/all_gather | solution.py:321
  79.6 56.2 %collective-permute-start.5 = (bf16[768,1024]{1,0:T(8,128)(2,1)}, bf16[768,1024]{1,0:T(8,128)(2,1)}, u32[]{:S(2)}, u32[]{:S(2)}) collective-permute-start(bf16[768,1024]{1,0:T(8,128)(2,1)} %pad_maximum_fusion.23), channel_id=1, source_target_pairs={{0,8},{4,12},{8,0},{12,4},{1,9},{5,13},{9,1},{13,5},{2,10},{6,14},... | collective-permute-start | bytes 4718600 | tf_op jit(solution)/shard_map/ppermute | solution.py:326
  90.6 117.4 %copy-start.83 = (s32[1,1024]{1,0:T(1,128)S(1)}, s32[1,1024]{1,0:T(1,128)}, u32[]{:S(2)}) copy-start(s32[1,1024]{1,0:T(1,128)} %param.14) | copy-start | bytes 12292
  135.8 761.2 %copy-start.2 = (bf16[16,32,2048]{2,1,0:T(8,128)(2,1)}, bf16[16,32,2048]{2,1,0:T(8,128)(2,1)S(1)}, u32[]{:S(2)}) copy-start(bf16[16,32,2048]{2,1,0:T(8,128)(2,1)S(1)} %all-to-all-done) | copy-start | bytes 6291460
  135.8 282.8 %all-gather.12.cloned.1.call-start = ((), (), s32[]{:S(2)}) async-start(), calls=%async_computation.12 | async-start | bytes 7208960 | tf_op jit(solution)/shard_map/all_gather | solution.py:321
  205.1 273.0 %all-gather.14.cloned.1.call-start = ((), (), s32[]{:S(2)}) async-start(), calls=%async_computation.13 | async-start | bytes 3604480 | tf_op jit(solution)/shard_map/all_gather | solution.py:321
  205.2 32.9 %collective-permute-start.2 = (f32[1,768]{1,0:T(1,128)S(1)}, f32[1,768]{1,0:T(1,128)S(1)}, u32[]{:S(2)}, u32[]{:S(2)}) collective-permute-start(f32[1,768]{1,0:T(1,128)S(1)} %bitcast.255), channel_id=1, source_target_pairs={{1,0},{2,1},{3,2},{0,3},{5,4},{6,5},{7,6},{4,7},{9,8},{10,9},{11,1... | collective-permute-start | bytes 9224 | tf_op jit(solution)/shard_map/ppermute | solution.py:365
  206.4 31.7 %collective-permute-start.3 = (f32[1,768]{1,0:T(1,128)S(1)}, f32[1,768]{1,0:T(1,128)S(1)}, u32[]{:S(2)}, u32[]{:S(2)}) collective-permute-start(f32[1,768]{1,0:T(1,128)S(1)} %bitcast.256), channel_id=1, source_target_pairs={{2,0},{3,1},{0,2},{1,3},{6,4},{7,5},{4,6},{5,7},{10,8},{11,9},{8,1... | collective-permute-start | bytes 9224 | tf_op jit(solution)/shard_map/ppermute | solution.py:365
  206.4 31.7 %collective-permute-start.4 = (f32[1,768]{1,0:T(1,128)S(1)}, f32[1,768]{1,0:T(1,128)S(1)}, u32[]{:S(2)}, u32[]{:S(2)}) collective-permute-start(f32[1,768]{1,0:T(1,128)S(1)} %bitcast.257), channel_id=1, source_target_pairs={{3,0},{0,1},{1,2},{2,3},{7,4},{4,5},{5,6},{6,7},{11,8},{8,9},{9,10... | collective-permute-start | bytes 9224 | tf_op jit(solution)/shard_map/ppermute | solution.py:365
  215.4 103.5 %collective-permute-start.1 = (bf16[2304,1024]{1,0:T(8,128)(2,1)}, bf16[2304,1024]{1,0:T(8,128)(2,1)}, u32[]{:S(2)}, u32[]{:S(2)}) collective-permute-start(bf16[2304,1024]{1,0:T(8,128)(2,1)} %pad_maximum_fusion.8), channel_id=1, source_target_pairs={{0,8},{4,12},{8,0},{12,4},{1,9},{5,13},{9,1},{13,5},{2,10},{6,14},... | collective-permute-start | bytes 14155784 | tf_op jit(solution)/shard_map/ppermute | solution.py:326
  222.2 203.9 %copy-start.55 = (f32[1,1,2048]{2,1,0:T(1,128)}, f32[1,1,2048]{2,1,0:T(1,128)S(1)}, u32[]{:S(2)}) copy-start(f32[1,1,2048]{2,1,0:T(1,128)S(1)} %get-tuple-element.242) | copy-start | bytes 24580
  225.7 104.8 %collective-permute-start = (bf16[512,2048]{1,0:T(8,128)(2,1)}, bf16[512,2048]{1,0:T(8,128)(2,1)}, u32[]{:S(2)}, u32[]{:S(2)}) collective-permute-start(bf16[512,2048]{1,0:T(8,128)(2,1)} %fusion.49), channel_id=1, source_target_pairs={{0,4},{4,0},{8,12},{12,8},{1,5},{5,1},{9,13},{13,9},{2,6},{6,2},{1... | collective-permute-start | bytes 6291464 | tf_op jit(solution)/shard_map/ppermute | solution.py:370
  317.1 95.7 %collective-permute-start.8 = (bf16[2112,1024]{1,0:T(8,128)(2,1)}, bf16[2112,1024]{1,0:T(8,128)(2,1)}, u32[]{:S(2)}, u32[]{:S(2)}) collective-permute-start(bf16[2112,1024]{1,0:T(8,128)(2,1)} %pad_maximum_fusion.9), channel_id=1, source_target_pairs={{0,8},{4,12},{8,0},{12,4},{1,9},{5,13},{9,1},{13,5},{2,10},{6,14},... | collective-permute-start | bytes 12976136 | tf_op jit(solution)/shard_map/ppermute | solution.py:326
  318.9 218.6 %all-gather.16.cloned.1.call-start = ((), (), s32[]{:S(2)}) async-start(), calls=%async_computation.14 | async-start | bytes 3604480 | tf_op jit(solution)/shard_map/all_gather | solution.py:321
  398.0 4.5 collective-permute-start.6
  418.6 1366.1 %reduce-scatter.18.cloned.1.call-start = ((), (), s32[]{:S(2)}) async-start(), calls=%async_computation.20 | async-start | bytes 3604480 | tf_op jit(solution)/shard_map/reduce_scatter | solution.py:420
  424.1 118.1 %collective-permute-start.9 = (bf16[2112,1024]{1,0:T(8,128)(2,1)}, bf16[2112,1024]{1,0:T(8,128)(2,1)}, u32[]{:S(2)}, u32[]{:S(2)}) collective-permute-start(bf16[2112,1024]{1,0:T(8,128)(2,1)} %pad_maximum_fusion.10), channel_id=1, source_target_pairs={{0,8},{4,12},{8,0},{12,4},{1,9},{5,13},{9,1},{13,5},{2,10},{6,14},... | collective-permute-start | bytes 12976136 | tf_op jit(solution)/shard_map/ppermute | solution.py:326
  428.2 132.9 %collective-permute-start.7 = (bf16[512,2048]{1,0:T(8,128)(2,1)}, bf16[512,2048]{1,0:T(8,128)(2,1)}, u32[]{:S(2)}, u32[]{:S(2)}) collective-permute-start(bf16[512,2048]{1,0:T(8,128)(2,1)} %add_convert_fusion.8), channel_id=1, source_target_pairs={{0,4},{4,0},{8,12},{12,8},{1,5},{5,1},{9,13},{13,9},{2,6},{6,2},{1... | collective-permute-start | bytes 6291464 | tf_op jit(solution)/shard_map/ppermute | solution.py:370
  481.4 123.5 %collective-permute-start.10 = (bf16[1056,1024]{1,0:T(8,128)(2,1)}, bf16[1056,1024]{1,0:T(8,128)(2,1)}, u32[]{:S(2)}, u32[]{:S(2)}) collective-permute-start(bf16[1056,1024]{1,0:T(8,128)(2,1)} %pad_maximum_fusion.19), channel_id=1, source_target_pairs={{0,8},{4,12},{8,0},{12,4},{1,9},{5,13},{9,1},{13,5},{2,10},{6,14},... | collective-permute-start | bytes 6488072 | tf_op jit(solution)/shard_map/ppermute | solution.py:326
  540.7 71.7 %collective-permute-start.11 = (bf16[1056,1024]{1,0:T(8,128)(2,1)}, bf16[1056,1024]{1,0:T(8,128)(2,1)}, u32[]{:S(2)}, u32[]{:S(2)}) collective-permute-start(bf16[1056,1024]{1,0:T(8,128)(2,1)} %pad_maximum_fusion.20), channel_id=1, source_target_pairs={{0,8},{4,12},{8,0},{12,4},{1,9},{5,13},{9,1},{13,5},{2,10},{6,14},... | collective-permute-start | bytes 6488072 | tf_op jit(solution)/shard_map/ppermute | solution.py:326
  638.0 3.8 collective-permute-start.12
  641.2 7.3 collective-permute-start.14
  645.1 26.9 %collective-permute-start.13 = (bf16[256,2048]{1,0:T(8,128)(2,1)S(1)}, bf16[256,2048]{1,0:T(8,128)(2,1)S(1)}, u32[]{:S(2)}, u32[]{:S(2)}) collective-permute-start(bf16[256,2048]{1,0:T(8,128)(2,1)S(1)} %fusion.103), channel_id=1, source_target_pairs={{0,16},{1,17},{2,18},{3,19},{4,20},{5,21},{6,22},{7,23},{8,24},{9,... | collective-permute-start | bytes 3145736 | tf_op jit(solution)/shard_map/ppermute | solution.py:385
  651.8 41.7 %collective-permute-start.15 = (bf16[256,2048]{1,0:T(8,128)(2,1)S(1)}, bf16[256,2048]{1,0:T(8,128)(2,1)S(1)}, u32[]{:S(2)}, u32[]{:S(2)}) collective-permute-start(bf16[256,2048]{1,0:T(8,128)(2,1)S(1)} %fusion.102), channel_id=1, source_target_pairs={{0,16},{1,17},{2,18},{3,19},{4,20},{5,21},{6,22},{7,23},{8,24},{9,... | collective-permute-start | bytes 3145736 | tf_op jit(solution)/shard_map/ppermute | solution.py:385
  703.3 4.3 collective-permute-start.16
  774.2 4.2 collective-permute-start.17
  783.5 4.3 collective-permute-start.19
  784.8 36.8 %collective-permute-start.18 = (bf16[512,2048]{1,0:T(8,128)(2,1)S(1)}, bf16[512,2048]{1,0:T(8,128)(2,1)}, u32[]{:S(2)}, u32[]{:S(2)}) collective-permute-start(bf16[512,2048]{1,0:T(8,128)(2,1)S(1)} %bitcast.182), channel_id=1, source_target_pairs={{0,4},{4,0},{8,12},{12,8},{1,5},{5,1},{9,13},{13,9},{2,6},{6,2},{1... | collective-permute-start | bytes 6291464 | tf_op jit(solution)/shard_map/ppermute | solution.py:370
  865.5 9.4 collective-permute-start.20
  874.6 53.5 %collective-permute-start.27 = (bf16[256,2048]{1,0:T(8,128)(2,1)}, bf16[256,2048]{1,0:T(8,128)(2,1)}, u32[]{:S(2)}, u32[]{:S(2)}) collective-permute-start(bf16[256,2048]{1,0:T(8,128)(2,1)} %convolution_convert_fusion.8), channel_id=1, source_target_pairs={{0,4},{4,0},{8,12},{12,8},{1,5},{5,1},{9,13},{13,9},{2,6},{6,2},{1... | collective-permute-start | bytes 3145736 | tf_op jit(solution)/shard_map/ppermute | solution.py:376
  903.2 34.7 %collective-permute-start.21 = (bf16[512,2048]{1,0:T(8,128)(2,1)}, bf16[512,2048]{1,0:T(8,128)(2,1)}, u32[]{:S(2)}, u32[]{:S(2)}) collective-permute-start(bf16[512,2048]{1,0:T(8,128)(2,1)} %get-tuple-element.166), channel_id=1, source_target_pairs={{0,4},{4,0},{8,12},{12,8},{1,5},{5,1},{9,13},{13,9},{2,6},{6,2},{1... | collective-permute-start | bytes 6291464 | tf_op jit(solution)/shard_map/ppermute | solution.py:370
  912.3 161.7 %collective-permute-start.26 = (bf16[256,2048]{1,0:T(8,128)(2,1)}, bf16[256,2048]{1,0:T(8,128)(2,1)}, u32[]{:S(2)}, u32[]{:S(2)}) collective-permute-start(bf16[256,2048]{1,0:T(8,128)(2,1)} %convolution_convert_fusion.9), channel_id=1, source_target_pairs={{0,4},{4,0},{8,12},{12,8},{1,5},{5,1},{9,13},{13,9},{2,6},{6,2},{1... | collective-permute-start | bytes 3145736 | tf_op jit(solution)/shard_map/ppermute | solution.py:376
  1023.0 14.3 collective-permute-start.23
  1036.9 12.9 collective-permute-start.22
  1071.0 29.4 %collective-permute-start.25 = (bf16[256,2048]{1,0:T(8,128)(2,1)S(1)}, bf16[256,2048]{1,0:T(8,128)(2,1)S(1)}, u32[]{:S(2)}, u32[]{:S(2)}) collective-permute-start(bf16[256,2048]{1,0:T(8,128)(2,1)S(1)} %get-tuple-element.223), channel_id=1, source_target_pairs={{16,0},{17,1},{18,2},{19,3},{20,4},{21,5},{22,6},{23,7},{24,8},{25... | collective-permute-start | bytes 3145736 | tf_op jit(solution)/shard_map/ppermute | solution.py:385
  1072.6 49.8 %collective-permute-start.24 = (bf16[256,2048]{1,0:T(8,128)(2,1)S(1)}, bf16[256,2048]{1,0:T(8,128)(2,1)S(1)}, u32[]{:S(2)}, u32[]{:S(2)}) collective-permute-start(bf16[256,2048]{1,0:T(8,128)(2,1)S(1)} %get-tuple-element.222), channel_id=1, source_target_pairs={{16,0},{17,1},{18,2},{19,3},{20,4},{21,5},{22,6},{23,7},{24,8},{25... | collective-permute-start | bytes 3145736 | tf_op jit(solution)/shard_map/ppermute | solution.py:385
  1123.1 4.2 collective-permute-start.28
  1139.1 64.8 %collective-permute-start.29 = (bf16[1408,1024]{1,0:T(8,128)(2,1)}, bf16[1408,1024]{1,0:T(8,128)(2,1)}, u32[]{:S(2)}, u32[]{:S(2)}) collective-permute-start(bf16[1408,1024]{1,0:T(8,128)(2,1)} %convolution_convert_fusion.5), channel_id=1, source_target_pairs={{0,8},{4,12},{8,0},{12,4},{1,9},{5,13},{9,1},{13,5},{2,10},{6,14},... | collective-permute-start | bytes 8650760 | tf_op jit(solution)/shard_map/ppermute | solution.py:417
  1203.9 64.0 %collective-permute-start.30 = (bf16[1408,1024]{1,0:T(8,128)(2,1)}, bf16[1408,1024]{1,0:T(8,128)(2,1)}, u32[]{:S(2)}, u32[]{:S(2)}) collective-permute-start(bf16[1408,1024]{1,0:T(8,128)(2,1)} %convolution_convert_fusion.4), channel_id=1, source_target_pairs={{0,8},{4,12},{8,0},{12,4},{1,9},{5,13},{9,1},{13,5},{2,10},{6,14},... | collective-permute-start | bytes 8650760 | tf_op jit(solution)/shard_map/ppermute | solution.py:417
  1217.1 568.9 %reduce-scatter.20.cloned.1.call-start = ((), (), s32[]{:S(2)}) async-start(), calls=%async_computation.21 | async-start | bytes 3604480 | tf_op jit(solution)/shard_map/reduce_scatter | solution.py:420
  1267.9 9.4 collective-permute-start.32
  1267.9 127.0 %collective-permute-start.31 = (bf16[2816,1024]{1,0:T(8,128)(2,1)}, bf16[2816,1024]{1,0:T(8,128)(2,1)}, u32[]{:S(2)}, u32[]{:S(2)}) collective-permute-start(bf16[2816,1024]{1,0:T(8,128)(2,1)} %convolution_convert_fusion.1), channel_id=1, source_target_pairs={{0,8},{4,12},{8,0},{12,4},{1,9},{5,13},{9,1},{13,5},{2,10},{6,14},... | collective-permute-start | bytes 17301512 | tf_op jit(solution)/shard_map/ppermute | solution.py:417
  1277.3 511.3 %reduce-scatter.14.cloned.1.call-start = ((), (), s32[]{:S(2)}) async-start(), calls=%async_computation.18 | async-start | bytes 7208960 | tf_op jit(solution)/shard_map/reduce_scatter | solution.py:420
  1301.0 11.3 collective-permute-start.33
  1405.3 390.7 %reduce-scatter.16.cloned.1.call-start = ((), (), s32[]{:S(2)}) async-start(), calls=%async_computation.19 | async-start | bytes 7208960 | tf_op jit(solution)/shard_map/reduce_scatter | solution.py:420
  1408.8 64.2 %collective-permute-start.34 = (bf16[1408,1024]{1,0:T(8,128)(2,1)S(1)}, bf16[1408,1024]{1,0:T(8,128)(2,1)S(1)}, u32[]{:S(2)}, u32[]{:S(2)}) collective-permute-start(bf16[1408,1024]{1,0:T(8,128)(2,1)S(1)} %get-tuple-element.195), channel_id=1, source_target_pairs={{0,8},{4,12},{8,0},{12,4},{1,9},{5,13},{9,1},{13,5},{2,10},{6,14},... | collective-permute-start | bytes 8650760 | tf_op jit(solution)/shard_map/ppermute | solution.py:417
  1474.6 79.1 %collective-permute-start.35 = (bf16[1408,1024]{1,0:T(8,128)(2,1)S(1)}, bf16[1408,1024]{1,0:T(8,128)(2,1)}, u32[]{:S(2)}, u32[]{:S(2)}) collective-permute-start(bf16[1408,1024]{1,0:T(8,128)(2,1)S(1)} %get-tuple-element.85), channel_id=1, source_target_pairs={{0,8},{4,12},{8,0},{12,4},{1,9},{5,13},{9,1},{13,5},{2,10},{6,14},... | collective-permute-start | bytes 8650760 | tf_op jit(solution)/shard_map/ppermute | solution.py:417
  1566.9 300.6 %reduce-scatter.8.cloned.1.call-start = ((), (), s32[]{:S(2)}) async-start(), calls=%async_computation.15 | async-start | bytes 3932160 | tf_op jit(solution)/shard_map/reduce_scatter | solution.py:420
  1566.9 69.0 %collective-permute-start.36 = (bf16[1536,1024]{1,0:T(8,128)(2,1)}, bf16[1536,1024]{1,0:T(8,128)(2,1)S(1)}, u32[]{:S(2)}, u32[]{:S(2)}) collective-permute-start(bf16[1536,1024]{1,0:T(8,128)(2,1)} %convolution_convert_fusion.3), channel_id=1, source_target_pairs={{0,8},{4,12},{8,0},{12,4},{1,9},{5,13},{9,1},{13,5},{2,10},{6,14},... | collective-permute-start | bytes 9437192 | tf_op jit(solution)/shard_map/ppermute | solution.py:417
  1635.9 13.0 collective-permute-start.38
  1642.2 225.2 %reduce-scatter.10.cloned.1.call-start = ((), (), s32[]{:S(2)}) async-start(), calls=%async_computation.16 | async-start | bytes 3932160 | tf_op jit(solution)/shard_map/reduce_scatter | solution.py:420
  1648.3 70.8 %collective-permute-start.37 = (bf16[1536,1024]{1,0:T(8,128)(2,1)}, bf16[1536,1024]{1,0:T(8,128)(2,1)}, u32[]{:S(2)}, u32[]{:S(2)}) collective-permute-start(bf16[1536,1024]{1,0:T(8,128)(2,1)} %convolution_convert_fusion.2), channel_id=1, source_target_pairs={{0,8},{4,12},{8,0},{12,4},{1,9},{5,13},{9,1},{13,5},{2,10},{6,14},... | collective-permute-start | bytes 9437192 | tf_op jit(solution)/shard_map/ppermute | solution.py:417
  1725.7 52.3 %collective-permute-start.40 = (bf16[1024,1024]{1,0:T(8,128)(2,1)}, bf16[1024,1024]{1,0:T(8,128)(2,1)}, u32[]{:S(2)}, u32[]{:S(2)}) collective-permute-start(bf16[1024,1024]{1,0:T(8,128)(2,1)} %fusion.108), channel_id=1, source_target_pairs={{0,8},{4,12},{8,0},{12,4},{1,9},{5,13},{9,1},{13,5},{2,10},{6,14},... | collective-permute-start | bytes 6291464 | tf_op jit(solution)/shard_map/ppermute | solution.py:417
  1774.0 92.0 %all-to-all-start.1 = ((bf16[16,32,2048]{2,1,0:T(8,128)(2,1)}), bf16[16,32,2048]{2,1,0:T(8,128)(2,1)S(1)}, u32[]{:S(2)}, u32[]{:S(2)}) async-start(bf16[16,32,2048]{2,1,0:T(8,128)(2,1)} %bitcast.58), calls=%async_computation.1 | async-start | bytes 4194304 | tf_op jit(solution)/shard_map/all_to_all | solution.py:516
  1777.7 95.6 %reduce-scatter.12.cloned.1.call-start = ((), (), s32[]{:S(2)}) async-start(), calls=%async_computation.17 | async-start | bytes 2621440 | tf_op jit(solution)/shard_map/reduce_scatter | solution.py:420
  1788.3 2.8 collective-permute-start.44
  1790.9 8.4 collective-permute-start.42
  1798.4 72.7 %collective-permute-start.43 = (bf16[704,512]{1,0:T(8,128)(2,1)}, bf16[704,512]{1,0:T(8,128)(2,1)}, u32[]{:S(2)}, u32[]{:S(2)}) collective-permute-start(bf16[704,512]{1,0:T(8,128)(2,1)} %get-tuple-element.236), channel_id=1, source_target_pairs={{0,4},{4,0},{8,12},{12,8},{1,5},{5,1},{9,13},{13,9},{2,6},{6,2},{1... | collective-permute-start | bytes 2162696 | tf_op jit(solution)/shard_map/ppermute | solution.py:541
  1871.1 15.4 collective-permute-start.39
  1874.4 10.0 collective-permute-start.41
  (96 other events, 1770.4 us)
Sparse Core Ops, SparseCore 0:
  10.2 66.6 all-gather.17
  79.0 126.0 all-gather.7
  206.7 105.4 all-gather.9
  313.6 104.9 all-gather.11
  420.6 57.4 all-gather.13
  479.5 57.8 all-gather.15
  1217.2 52.7 reduce-scatter.17
  1277.4 52.5 reduce-scatter.19
  1405.4 99.5 reduce-scatter.13
  1567.0 98.6 reduce-scatter.15
  1668.0 60.7 reduce-scatter.7
  1731.5 67.8 reduce-scatter.9
  1801.7 65.7 reduce-scatter.11

commit v3 on v2

--- a/solution.py
+++ b/solution.py
@@ -344,20 +344,19 @@
         )
         return block[0].T
 
-    def down_block(part, half):
-        start = core * hidden + part * (hidden // 2)
-        return lax.dynamic_slice(down_weight[0], (start, half * half_width), (hidden // 2, half_width))
+    def down_block(half):
+        return lax.dynamic_slice(down_weight[0], (core * hidden, half * half_width), (hidden // 2, half_width))
+
+    def by_parts(weight):
+        return weight.reshape(tp_count, 2, hidden // 2, width).swapaxes(0, 1).reshape(-1, width)
 
     wt_out = gathered(out_block)
     wt_qkv = gathered(qkv_block)
-    wt_gu = jnp.concatenate([gathered(functools.partial(gu_block, w)) for w in range(2)], axis=0)
-    wt_down = jnp.concatenate(
-        [
-            gathered(functools.partial(down_block, part)).reshape(tp_count, hidden // 2, width)
-            for part in range(2)
-        ],
-        axis=1,
-    ).reshape(tp_count * hidden, width)
+    wt_gu = jnp.concatenate([by_parts(gathered(functools.partial(gu_block, w))) for w in range(2)], axis=0)
+    down_first = gathered(down_block)
+    down_last = lax.dynamic_slice_in_dim(down_weight[0], core * hidden + hidden // 2, hidden // 2, 0)
+    down_last = lax.all_gather(after(down_last, across_parts[2]), "tp", axis=0, tiled=True)
+    wt_down = jnp.concatenate([down_first, down_last], axis=0)
     bias_own = lax.dynamic_slice_in_dim(b_qkv[0], core * columns, columns, 1).reshape(1, 3 * columns)
     bias = [bias_own]
     for p in range(1, tp_count):
@@ -439,39 +438,41 @@
         up_grad = (act_grad * gate * sigma).astype(jnp.bfloat16)
         return gate_grad, up_grad, jnp.concatenate([gate_grad, up_grad], axis=1)
 
-    def backward(grad_out, stored):
+    def backward(grad_out, stored, wait):
         stream, normed, qkv, attended, hidden_state, normed_two, gate_up, activation = stored
         gu_grad = mlp_back(dot_t(both(grad_out), wt_down), gate_up)[2]
         result = ln_back(hidden_state, summed(gu_grad, wt_gu)[0], gain[1])[0]
         hidden_grad = grad_out.astype(jnp.float32) + result
         ctx_grad = dot_t(both(hidden_grad.astype(jnp.bfloat16)), wt_out).astype(jnp.bfloat16)
-        qkv_grad, _ = attn_bwd(qkv, ctx_grad, context, tp_count, chunk)
-        one_grad = jnp.concatenate(summed(qkv_grad, wt_qkv, 2), axis=0)
-        result = ln_back(stream, one_grad, gain[0])[0]
-        return split((hidden_grad + result).astype(jnp.bfloat16), 2)
-
-    def last_backward(grad_out, stored, final_out):
-        stream, normed, qkv, attended, hidden_state, normed_two, gate_up, activation, act_a, act_b = stored
+        qkv_grad, _ = attn_bwd(qkv, after(ctx_grad, wait), context, tp_count, chunk)
+        one_grad = summed(qkv_grad, wt_qkv, 2)
+        return [
+            (z + ln_back(x, y, gain[0])[0]).astype(jnp.bfloat16)
+            for x, y, z in zip(split(stream, 2), one_grad, split(hidden_grad, 2))
+        ]
+
+    def last_backward(grad_out, stored, final_out, act_both):
+        stream, normed, qkv, attended, hidden_state, normed_two, gate_up, _ = stored
         grad_f32 = grad_out.astype(jnp.float32)
+        far_grad, near_grad = far_near(grad_out)
+        grad_across = both(across(far_grad))
         mlp_grad = both(grad_out)
-        far_a, far_b = far_term(act_a, mlp_grad), far_term(act_b, mlp_grad)
-
-        mlp_in, far_a, far_b = together((mlp_grad, far_a, far_b))
-        arriving = across(far_a)
-        gate_grad, up_grad, gu_grad = mlp_back(dot_t(mlp_in, wt_down), gate_up)
-
-        arriving, far_b, gate_grad, up_grad, act_a = together((arriving, far_b, gate_grad, up_grad, act_a))
-        arriving_b = across(far_b)
-        sum_a = over_tp(near_total(act_a, mlp_grad, arriving))
-        gu_grad = jnp.concatenate([gate_grad, up_grad], axis=1)
+        gate_grad, up_grad, gu_grad = mlp_back(dot_t(mlp_grad, wt_down), gate_up)
+        far_gate = far_term(gate_grad, normed_two)
+
+        grad_across, far_gate, gate_grad, up_grad, gu_grad = together(
+            (grad_across, far_gate, gate_grad, up_grad, gu_grad)
+        )
+        far_gate_a, far_gate_b = split(far_gate, 2)
+        arriving = across(far_gate_a)
+        down_total = dot_0(act_both, jnp.concatenate([both(near_grad), grad_across], axis=0)).astype(jnp.bfloat16)
         two_other = dot_n(gu_grad[own_rows:], wt_gu).astype(jnp.bfloat16)
-        far_gate = far_term(gate_grad, normed_two)
-
-        arriving_b, far_gate, gu_grad, two_other, act_b, up_grad = together(
-            (arriving_b, far_gate, gu_grad, two_other, act_b, up_grad)
-        )
-        arriving_gate = across(far_gate)
-        sum_b = over_tp(near_total(act_b, mlp_grad, arriving_b))
+
+        arriving, far_gate_b, two_other, gu_grad, down_total = together(
+            (arriving, far_gate_b, two_other, gu_grad, down_total)
+        )
+        arriving_gate = jnp.concatenate([arriving, across(far_gate_b)], axis=0)
+        sums_down = [over_tp(x) for x in split(down_total, 2)]
         two_grad = dot_n(gu_grad[:own_rows], wt_gu) + lax.ppermute(two_other, "ctx", core_route).astype(jnp.float32)
         result, gain_two, shift_two = ln_back(hidden_state, two_grad, gain[1])
         hidden_grad = grad_f32 + result
@@ -483,7 +484,8 @@
         )
         far_up_a, far_up_b = split(far_up, 2)
         arriving = across(far_up_a)
-        sum_gate = over_tp(near_total(gate_grad, normed_two, arriving_gate))
+        gate_total = near_total(gate_grad, normed_two, arriving_gate)
+        sums_gate = [over_tp(x) for x in split(gate_total, 2)]
         ctx_grad = dot_t(attn_grad, wt_out).astype(jnp.bfloat16)
 
         arriving, far_up_b, ctx_grad = together((arriving, far_up_b, ctx_grad))
@@ -496,7 +498,8 @@
             (arriving_up, far_a, qkv_a, qkv_b, qkv_grad, up_grad, attn_grad)
         )
         arriving = across(far_a)
-        sum_up = over_tp(near_total(up_grad, normed_two, arriving_up))
+        up_total = near_total(up_grad, normed_two, arriving_up)
+        sums_up = [over_tp(x) for x in split(up_total, 2)]
         one_other = dot_n(qkv_grad[own_rows:], wt_qkv).astype(jnp.bfloat16)
         far_b = far_term(qkv_b, normed)
 
@@ -517,21 +520,21 @@
             ends.reshape(ctx_count * tp_count, piece, width), ("ctx", "tp"), 0, 0, tiled=True
         )
         sum_qkv_b = over_tp(near_total(qkv_b, normed, arriving_b))
-        sum_out = over_tp(near_total(attended, attn_grad, arriving_out))
+        sum_out = over_tp(near_total(attended, after(attn_grad, ends), arriving_out))
         small = (jnp.stack([gain_one, gain_two]), jnp.stack([shift_one, shift_two]), bias_grad)
-        sum_down = jnp.concatenate([sum_a, sum_b], axis=0)
-        sum_qkv = jnp.concatenate([sum_qkv_a, sum_qkv_b], axis=0)
-        return ends, small, (sum_down, sum_gate, sum_up, sum_out, sum_qkv)
+        sums = (jnp.concatenate(x, axis=0) for x in (sums_down, sums_gate, sums_up))
+        return ends, small, (*sums, sum_out, jnp.concatenate([sum_qkv_a, sum_qkv_b], axis=0))
 
     sent, _ = forward(inbound.astype(jnp.float32))
     arriving = over_x(sent, [(0, 1)])
     final_out, stored = forward(jnp.where(first, inbound, arriving).astype(jnp.float32))
-    arriving_back = over_x(backward(inbound, stored), [(1, 0)])
-    halves = tuple(part_of(stored[-1], i, 2, 1) for i in range(2))
-    arriving_back, final_out, *halves = together((arriving_back, jnp.concatenate(final_out, axis=0), *halves))
-    stored = (*stored, *halves)
+    act_across = across(stored[7])
+    arriving_back = over_x(backward(inbound, stored, act_across), [(1, 0)])
+    arriving_back, final_out, act_both = together(
+        (arriving_back, jnp.concatenate(final_out, axis=0), jnp.concatenate([stored[7], act_across], axis=0))
+    )
     grad_out = jnp.where(first, arriving_back, inbound)
-    ends, small, sums = last_backward(grad_out, stored, final_out)
+    ends, small, sums = last_backward(grad_out, stored, final_out, act_both)
     down_sum, gate_sum, up_sum, out_sum, qkv_sum = sums
 
     def settled(term):
@@ -557,7 +560,7 @@
     ).reshape(3, tp_count * 2 * columns)
     vectors = jnp.concatenate([gain_terms, shift_terms, bias_full], axis=0)
     share = width // (ctx_count * tp_count)
-    vectors = vectors.reshape(-1, ctx_count * tp_count, share).transpose(1, 0, 2)
+    vectors = after(vectors, ends).reshape(-1, ctx_count * tp_count, share).transpose(1, 0, 2)
     vectors = jnp.sum(lax.all_to_all(vectors, ("ctx", "tp"), 0, 0, tiled=True), axis=0).reshape(-1, share)
 
     ends = ends.reshape(ctx_count // 2, 2, tp_count, piece, width).transpose(0, 2, 1, 3, 4)

time: 1900 us -> 2000 us (1.053)
  waiting for transfers between devices: 748 us -> 885 us
  blocking collectives: 47.4 us -> 0 us
    ppermute x6 -> x5, waiting for transfers between devices: 8.38 us -> 146 us  [gathered(): lax.ppermute(jnp.concatenate(wanted, axis=0), 'ctx', across_route)]
    all_to_all x1 -> x0, blocking collectives: 47.4 us -> none  [bulk_device(): lax.all_to_all(vectors, ('ctx', 'tp'), 0, 0, tiled=True)]
    all_gather x6 -> x5, waiting for transfers between devices: 254 us -> 226 us  [gathered(): own = lax.all_gather(block, 'tp', axis=0, tiled=True)]
    all_to_all x1, waiting for transfers between devices: 64.4 us -> 90.1 us  [last_backward(): lax.all_to_all(ends.reshape(ctx_count * tp_count, piece, width), ('ctx',...]
    dot_general x14 -> x11, matrix products: 106 us -> 92 us  [dot_0(): lax.dot_general(a, b, (((0,), (0,)), ((), ())), preferred_element_type=jn...]
    concatenate x5 -> x4, other arithmetic: 48.9 us -> 39.5 us  [turned_by_tp(): twice = jnp.concatenate([shards, shards], axis=axis)]
    ppermute x8 -> x9, waiting for transfers between devices: 283 us -> 284 us  [across(): lax.ppermute(after(term, *others) if others else term, 'ctx', across_route)]
  transfers between devices with their start and end apart: 60 -> 65, of which waited for: 26 -> 27; matrix products, arithmetic and copies ran while one was open for 36% -> 34% of each run, Pallas kernels for 9% -> 5%
where the time goes in v3:
time: 2000 us; the launch traced here: 1990 us
  waiting for transfers between devices  885 us (44%)
  matrix products  513 us (26%)
  Pallas kernels  204 us (10%)
  other arithmetic  169 us (8%)
  local copies, waits for them, and re-layouts  141 us (7%)
  starting transfers between devices  50.9 us (3%)
  between operations  31.3 us (2%)
    ppermute x9, waiting for transfers between devices, across(): lax.ppermute(after(term, *others) if others else term, 'ctx', across_route)  284 us
    dot_general x22, matrix products, dot_n(): lax.dot_general(a, b, (((1,), (0,)), ((), ())), preferred_element_type=jn...  240 us
    all_gather x5, waiting for transfers between devices, gathered(): own = lax.all_gather(block, 'tp', axis=0, tiled=True)  226 us
    dot_general x8, matrix products, dot_t(): lax.dot_general(a, b, (((1,), (1,)), ((), ())), preferred_element_type=jn...  181 us
    ppermute x5, waiting for transfers between devices, gathered(): lax.ppermute(jnp.concatenate(wanted, axis=0), 'ctx', across_route)  146 us
    pallas_call x2, Pallas kernels, attn_bwd(): pl.pallas_call(functools.partial(attn_bwd_kernel, heads, chunk), grid=(gr...  126 us
    dot_general x11, matrix products, dot_0(): lax.dot_general(a, b, (((0,), (0,)), ((), ())), preferred_element_type=jn...  92 us
    all_to_all x1, waiting for transfers between devices, last_backward(): lax.all_to_all(ends.reshape(ctx_count * tp_count, piece, width), ('ctx',...  90.1 us
  transfers between devices with their start and end apart: 65, of which 27 were waited for; matrix products, arithmetic and copies ran while one was open for 34% of the time, Pallas kernels for 5%

profile of v3, /device:TPU:0, one launch (start us, length us, event | category | flops | bytes accessed | tf_op | source)
XLA Modules:
  0.0 1994.2 jit_solution(12269209977266260817)
XLA Ops:
  39.9 7.4 all-to-all-start
  47.4 29.5 %all-gather.18.cloned.1.call-done = bf16[1,1024,1024]{2,1,0:T(8,128)(2,1)} async-done(((bf16[1,256,1024]{2,1,0:T(8,128)(2,1)}), bf16[1,1024,1024]{2,1,0:T(8,128)(2,1)}) %all-gather.18.cloned.1.call-update) | async-done | bytes 2097168 | tf_op jit(solution)/shard_map/all_gather | solution.py:321
  81.2 9.6 constant_dynamic-slice_fusion.21
  93.4 42.5 %all-to-all-done = bf16[16,32,2048]{2,1,0:T(8,128)(2,1)S(1)} async-done(((bf16[16,32,2048]{2,1,0:T(8,128)(2,1)}), bf16[16,32,2048]{2,1,0:T(8,128)(2,1)S(1)}, u32[]{:S(2)}, u32[]{:S(2)}) %all-to-all-start) | async-done | bytes 2097184 | tf_op jit(solution)/shard_map/all_to_all | solution.py:287
  139.2 65.9 %all-gather.8.cloned.1.call-done = bf16[3072,1024]{1,0:T(8,128)(2,1)} async-done(((bf16[768,1024]{1,0:T(8,128)(2,1)}), bf16[3072,1024]{1,0:T(8,128)(2,1)}) %all-gather.8.cloned.1.call-update) | async-done | bytes 6291472 | tf_op jit(solution)/shard_map/all_gather | solution.py:321
  244.1 68.1 %all-gather.10.cloned.1.call-done = bf16[2816,1024]{1,0:T(8,128)(2,1)} async-done(((bf16[704,1024]{1,0:T(8,128)(2,1)}), bf16[2816,1024]{1,0:T(8,128)(2,1)}) %all-gather.10.cloned.1.call-update) | async-done | bytes 5767184 | tf_op jit(solution)/shard_map/all_gather | solution.py:321
  318.3 11.3 fusion.5
  329.5 22.0 %fusion.31.mixed = f32[1024,3072]{1,0:T(8,128)} fusion(bf16[512,2048]{1,0:T(8,128)(2,1)} %collective-permute-done, bf16[512,2048]{1,0:T(8,128)(2,1)} %fusion.30, bf16[3072,1024]{1,0:T(8,128)(2,1)} %fusion.5, bf16[3072,1024]{1,0:T(8,128)(2,1)} %all-gather.8.cloned.1.call-done, pred[]{:T(512)S(6)} %eq.30), kind=kOutput, calls=%fused_computation.94 | convolution fusion | flops 12949913600 | bytes 29360128 | tf_op jit(solution)/shard_map/dot_general | solution.py:59
  351.6 39.3 %shard_map.170 = (bf16[1024,3072]{1,0:T(8,128)(2,1)}, bf16[1024,1024]{1,0:T(8,128)(2,1)}) custom-call(f32[1024,3072]{1,0:T(8,128)} %fusion.31.mixed, f32[4,1,768]{2,1,0:T(1,128)} %reshape.423.bias, f32[1024,128]{1,0:T(8,128)} %concatenate.274.cos_t, f32[1024,128]{1,0:T(8,128)} %concatenate.275.low_t, f32[1024,128]{1,0:T(8,128)} %concatenate.276.high_t, ...), custom_call_target="tpu_custom_call" | custom-call | flops 12884901888 | bytes 22020096 | tf_op jit(solution)/shard_map/pallas_call | solution.py:187
  390.9 6.5 convolution_convert_fusion.6
  409.0 9.6 all-gather.12.cloned.1.call-done
  425.3 52.8 %all-gather.14.cloned.1.call-done = bf16[1408,1024]{1,0:T(8,128)(2,1)} async-done(((bf16[352,1024]{1,0:T(8,128)(2,1)}), bf16[1408,1024]{1,0:T(8,128)(2,1)}) %all-gather.14.cloned.1.call-update) | async-done | bytes 2883600 | tf_op jit(solution)/shard_map/all_gather | solution.py:321
  496.3 138.5 %collective-permute-done.10 = bf16[1056,1024]{1,0:T(8,128)(2,1)} collective-permute-done((bf16[1056,1024]{1,0:T(8,128)(2,1)}, bf16[1056,1024]{1,0:T(8,128)(2,1)}, u32[]{:S(2)}, u32[]{:S(2)}) %collective-permute-start.10) | collective-permute-done | bytes 2162720 | tf_op jit(solution)/shard_map/ppermute | solution.py:326
  643.9 18.1 fusion.11
  682.4 34.2 %fusion.35 = f32[1024,5632]{1,0:T(8,128)} fusion(bf16[512,2048]{1,0:T(8,128)(2,1)} %collective-permute-done.7, bf16[512,2048]{1,0:T(8,128)(2,1)} %add_convert_fusion.8, bf16[2816,2048]{1,0:T(8,128)(2,1)} %bitcast.180, bf16[2816,2048]{1,0:T(8,128)(2,1)} %bitcast.186), kind=kOutput, calls=%fused_computation.103 | convolution fusion | flops 23676846080 | bytes 50331648 | tf_op jit(solution)/shard_map/dot_general | solution.py:59
  716.6 11.6 fusion
  728.2 6.6 convolution_convert_fusion.10
  736.3 6.9 convolution_convert_fusion.9
  755.8 17.6 collective-permute-done.12
  773.5 22.1 %collective-permute-done.14 = bf16[256,2048]{1,0:T(8,128)(2,1)S(1)} collective-permute-done((bf16[256,2048]{1,0:T(8,128)(2,1)}, bf16[256,2048]{1,0:T(8,128)(2,1)S(1)}, u32[]{:S(2)}, u32[]{:S(2)}) %collective-permute-start.14) | collective-permute-done | bytes 1048608 | tf_op jit(solution)/shard_map/ppermute | solution.py:384
  807.1 21.8 %fusion.26.mixed = f32[1024,3072]{1,0:T(8,128)} fusion(bf16[512,2048]{1,0:T(8,128)(2,1)} %collective-permute-done.15, bf16[512,2048]{1,0:T(8,128)(2,1)} %copy-done.38, bf16[3072,1024]{1,0:T(8,128)(2,1)} %fusion.5, bf16[3072,1024]{1,0:T(8,128)(2,1)} %all-gather.8.cloned.1.call-done, pred[]{:T(512)S(6)} %eq.30), kind=kOutput, calls=%fused_computation.89 | convolution fusion | flops 12949913600 | bytes 29360128 | tf_op jit(solution)/shard_map/dot_general | solution.py:59
  828.9 38.9 %shard_map.171 = (bf16[1024,3072]{1,0:T(8,128)(2,1)}, bf16[1024,1024]{1,0:T(8,128)(2,1)}) custom-call(f32[1024,3072]{1,0:T(8,128)} %fusion.26.mixed, f32[4,1,768]{2,1,0:T(1,128)} %reshape.423.bias, f32[1024,128]{1,0:T(8,128)} %concatenate.274.cos_t, f32[1024,128]{1,0:T(8,128)} %concatenate.275.low_t, f32[1024,128]{1,0:T(8,128)} %concatenate.276.high_t, ...), custom_call_target="tpu_custom_call" | custom-call | flops 12884901888 | bytes 22020096 | tf_op jit(solution)/shard_map/pallas_call | solution.py:187
  887.0 34.1 %fusion.25 = f32[1024,5632]{1,0:T(8,128)} fusion(bf16[512,2048]{1,0:T(8,128)(2,1)} %collective-permute-done.18, bf16[512,2048]{1,0:T(8,128)(2,1)} %copy-done.42, bf16[2816,2048]{1,0:T(8,128)(2,1)} %bitcast.181, bf16[2816,2048]{1,0:T(8,128)(2,1)} %bitcast.187), kind=kOutput, calls=%fused_computation.88 | convolution fusion | flops 23676846080 | bytes 50331648 | tf_op jit(solution)/shard_map/dot_general | solution.py:59
  921.0 26.1 %multiply_convert_fusion.3 = (bf16[1024,2816]{1,0:T(8,128)(2,1)}, bf16[1024,2816]{1,0:T(8,128)(2,1)}, bf16[1024,2816]{1,0:T(8,128)(2,1)}) fusion(f32[1024,5632]{1,0:T(8,128)} %fusion.25, bf16[1408,2048]{1,0:T(8,128)(2,1)} %all-gather.16.cloned.1.call-done, bf16[1408,2048]{1,0:T(8,128)(2,1)} %maximum_select_fusion.3, ...), kind=kOutput, calls=%fused_computation.30 | convolution fusion | flops 11888754688 | bytes 56098816 | tf_op jit(solution)/shard_map/dot_general | solution.py:59
  947.1 17.4 fusion.70
  967.4 7.9 convolution_convert_fusion.7
  981.4 21.9 %fusion.132 = (f32[512]{0:T(512)S(1)}, f32[512]{0:T(512)S(1)}, f32[512,2048]{1,0:T(8,128)}) fusion(f32[2048]{0:T(1024)S(1)} %bitcast.225, bf16[512,2048]{1,0:T(8,128)(2,1)} %collective-permute-done.19, f32[512]{0:T(512)S(1)} %add_rsqrt_fusion.2, f32[512,2048]{1,0:T(8,128)} %copy-done.7, f32[512]{0:T(512)S(1)} %broadcast_multiply_fusion.8, ...), kind=kOutput, calls=%fused_computation.244 | convolution fusion | flops 11877220352 | bytes 45105152 | tf_op jit(solution)/shard_map/dot_general | solution.py:67
  1003.4 6.5 fusion.166
  1009.9 7.6 fusion.83
  1024.8 7.6 fusion.96.ctx
  1032.4 60.4 %collective-permute-done.21 = bf16[1024,2816]{1,0:T(8,128)(2,1)} collective-permute-done((bf16[1024,2816]{1,0:T(8,128)(2,1)}, bf16[1024,2816]{1,0:T(8,128)(2,1)}, u32[]{:S(2)}, u32[]{:S(2)}) %collective-permute-start.21) | collective-permute-done | bytes 5767200 | tf_op jit(solution)/shard_map/ppermute | solution.py:416
  1092.8 63.2 %shard_map.172 = (bf16[1024,3072]{1,0:T(8,128)(2,1)}, f32[4,1,768]{2,1,0:T(1,128)}) custom-call(bf16[1024,3072]{1,0:T(8,128)(2,1)} %get-tuple-element.65.qkv, bf16[1024,1024]{1,0:T(8,128)(2,1)} %fusion.96.ctx, f32[1024,128]{1,0:T(8,128)} %concatenate.274.cos_t, f32[1024,128]{1,0:T(8,128)} %concatenate.275.low_t, f32[1024,128]{1,0:T(8,128)} %concatenate.276.high_t, ...), custom_call_target="tpu_custom_call" | custom-call | flops 30064771072 | bytes 15728640 | tf_op jit(solution)/shard_map/pallas_call | solution.py:222
  1156.0 13.7 convolution_convert_fusion.11
  1169.7 13.7 convolution_convert_fusion.12
  1184.0 13.9 add_multiply_fusion.1
  1198.0 16.9 multiply_reduce_fusion.11
  1224.1 11.0 pad_maximum_fusion.2
  1235.1 15.5 collective-permute-done.25
  1250.7 21.9 %collective-permute-done.23 = bf16[256,2048]{1,0:T(8,128)(2,1)S(1)} collective-permute-done((bf16[256,2048]{1,0:T(8,128)(2,1)S(1)}, bf16[256,2048]{1,0:T(8,128)(2,1)S(1)}, u32[]{:S(2)}, u32[]{:S(2)}) %collective-permute-start.23) | collective-permute-done | bytes 1048608 | tf_op jit(solution)/shard_map/ppermute | solution.py:384
  1275.2 23.9 %collective-permute-done.28 = bf16[512,1024]{1,0:T(8,128)(2,1)S(1)} collective-permute-done((bf16[512,1024]{1,0:T(8,128)(2,1)S(1)}, bf16[512,1024]{1,0:T(8,128)(2,1)S(1)}, u32[]{:S(2)}, u32[]{:S(2)}) %collective-permute-start.28) | collective-permute-done | bytes 1048608 | tf_op jit(solution)/shard_map/ppermute | solution.py:416
  1299.1 24.2 %multiply_convert_fusion = (bf16[1024,2816]{1,0:T(8,128)(2,1)}, bf16[1024,2816]{1,0:T(8,128)(2,1)}) fusion(f32[1024,5632]{1,0:T(8,128)} %fusion.25, bf16[1408,2048]{1,0:T(8,128)(2,1)} %all-gather.16.cloned.1.call-done, bf16[1408,2048]{1,0:T(8,128)(2,1)} %maximum_select_fusion.3, bf16[512,2048]{1,0:T(8,128)(2,1)} %collective-permute-done.30, ...), kind=kOutput, calls=%fused_computation.27 | convolution fusion | flops 11880103936 | bytes 50331648 | tf_op jit(solution)/shard_map/dot_general | solution.py:59
  1323.3 9.6 convolution_convert_fusion.2
  1332.9 7.0 pad_maximum_fusion.3
  1347.3 19.6 fusion.67
  1366.8 16.0 convolution_convert_fusion.1
  1382.8 28.2 %collective-permute-done.31 = bf16[1408,1024]{1,0:T(8,128)(2,1)} collective-permute-done((bf16[1408,1024]{1,0:T(8,128)(2,1)}, bf16[1408,1024]{1,0:T(8,128)(2,1)}, u32[]{:S(2)}, u32[]{:S(2)}) %collective-permute-start.31) | collective-permute-done | bytes 2883616 | tf_op jit(solution)/shard_map/ppermute | solution.py:416
  1418.8 20.2 %multiply_reduce_fusion = (f32[2048]{0:T(1024)}, f32[512]{0:T(512)S(1)}, f32[512]{0:T(512)S(1)}, f32[2048]{0:T(1024)}, f32[512,2048]{1,0:T(8,128)S(1)}) fusion(f32[512]{0:T(512)S(1)} %copy-done.67, f32[512,2048]{1,0:T(8,128)} %copy-done.7, f32[512]{0:T(512)S(1)} %copy-done.64, f32[2048]{0:T(1024)S(1)} %bitcast.227, ...), kind=kOutput, calls=%fused_computation.126 | convolution fusion | flops 11868827648 | bytes 39354368 | tf_op jit(solution)/shard_map/dot_general | solution.py:67
  1442.4 10.9 convolution_convert_fusion
  1453.3 26.2 %collective-permute-done.33 = bf16[1408,1024]{1,0:T(8,128)(2,1)} collective-permute-done((bf16[1408,1024]{1,0:T(8,128)(2,1)}, bf16[1408,1024]{1,0:T(8,128)(2,1)}, u32[]{:S(2)}, u32[]{:S(2)}) %collective-permute-start.33) | collective-permute-done | bytes 2883616 | tf_op jit(solution)/shard_map/ppermute | solution.py:416
  1485.3 9.4 add_convert_fusion.1
  1505.4 10.6 convolution_convert_fusion.13.ctx
  1516.0 52.1 %collective-permute-done.36 = bf16[1408,1024]{1,0:T(8,128)(2,1)S(1)} collective-permute-done((bf16[1408,1024]{1,0:T(8,128)(2,1)}, bf16[1408,1024]{1,0:T(8,128)(2,1)S(1)}, u32[]{:S(2)}, u32[]{:S(2)}) %collective-permute-start.36) | collective-permute-done | bytes 2883616 | tf_op jit(solution)/shard_map/ppermute | solution.py:416
  1569.6 62.9 %shard_map.173 = (bf16[1024,3072]{1,0:T(8,128)(2,1)}, f32[4,1,768]{2,1,0:T(1,128)}) custom-call(bf16[1024,3072]{1,0:T(8,128)(2,1)} %get-tuple-element.65.qkv, bf16[1024,1024]{1,0:T(8,128)(2,1)} %convolution_convert_fusion.13.ctx, f32[1024,128]{1,0:T(8,128)} %concatenate.274.cos_t, f32[1024,128]{1,0:T(8,128)} %concatenate.275.low_t, ...), custom_call_target="tpu_custom_call" | custom-call | flops 30064771072 | bytes 15728640 | tf_op jit(solution)/shard_map/pallas_call | solution.py:222
  1639.6 7.7 convolution_convert_fusion.4
  1650.7 8.2 add_convert_fusion
  1663.4 6.6 convolution_convert_fusion.3
  1670.0 16.8 fusion.64
  1686.8 44.8 %collective-permute-done.38 = bf16[1536,1024]{1,0:T(8,128)(2,1)S(1)} collective-permute-done((bf16[1536,1024]{1,0:T(8,128)(2,1)}, bf16[1536,1024]{1,0:T(8,128)(2,1)S(1)}, u32[]{:S(2)}, u32[]{:S(2)}) %collective-permute-start.38) | collective-permute-done | bytes 3145760 | tf_op jit(solution)/shard_map/ppermute | solution.py:416
  1731.6 6.2 add_convert_fusion.3
  1744.9 18.2 multiply_reduce_fusion.1
  1766.3 48.5 %collective-permute-done.39 = bf16[1536,1024]{1,0:T(8,128)(2,1)} collective-permute-done((bf16[1536,1024]{1,0:T(8,128)(2,1)}, bf16[1536,1024]{1,0:T(8,128)(2,1)}, u32[]{:S(2)}, u32[]{:S(2)}) %collective-permute-start.39) | collective-permute-done | bytes 3145760 | tf_op jit(solution)/shard_map/ppermute | solution.py:416
  1814.8 6.6 add_convert_fusion.2
  1828.7 90.1 %all-to-all-done.1 = bf16[16,32,2048]{2,1,0:T(8,128)(2,1)S(1)} async-done(((bf16[16,32,2048]{2,1,0:T(8,128)(2,1)}), bf16[16,32,2048]{2,1,0:T(8,128)(2,1)S(1)}, u32[]{:S(2)}, u32[]{:S(2)}) %all-to-all-start.1) | async-done | bytes 2097184 | tf_op jit(solution)/shard_map/all_to_all | solution.py:519
  1966.9 6.2 copy.87
  (524 shorter events, 342.3 us)
Async XLA Ops:
  7.2 69.7 %all-gather.18.cloned.1.call-start = ((), (), s32[]{:S(2)}) async-start(), calls=%async_computation.26 | async-start | bytes 2621440 | tf_op jit(solution)/shard_map/all_gather | solution.py:321
  9.5 195.6 %all-gather.8.cloned.1.call-start = ((), (), s32[]{:S(2)}) async-start(), calls=%async_computation.12 | async-start | bytes 7864320 | tf_op jit(solution)/shard_map/all_gather | solution.py:321
  39.9 95.9 %all-to-all-start = ((bf16[16,32,2048]{2,1,0:T(8,128)(2,1)}), bf16[16,32,2048]{2,1,0:T(8,128)(2,1)S(1)}, u32[]{:S(2)}, u32[]{:S(2)}) async-start(bf16[16,32,2048]{2,1,0:T(8,128)(2,1)} %bitcast.193), calls=%async_computation | async-start | bytes 4194304 | tf_op jit(solution)/shard_map/all_to_all | solution.py:287
  47.3 264.9 %all-gather.10.cloned.1.call-start = ((), (), s32[]{:S(2)}) async-start(), calls=%async_computation.13 | async-start | bytes 7208960 | tf_op jit(solution)/shard_map/all_gather | solution.py:321
  79.7 56.2 %collective-permute-start.5 = (bf16[768,1024]{1,0:T(8,128)(2,1)}, bf16[768,1024]{1,0:T(8,128)(2,1)}, u32[]{:S(2)}, u32[]{:S(2)}) collective-permute-start(bf16[768,1024]{1,0:T(8,128)(2,1)} %pad_maximum_fusion.24), channel_id=1, source_target_pairs={{0,8},{4,12},{8,0},{12,4},{1,9},{5,13},{9,1},{13,5},{2,10},{6,14},... | collective-permute-start | bytes 4718600 | tf_op jit(solution)/shard_map/ppermute | solution.py:326
  135.9 282.7 %all-gather.12.cloned.1.call-start = ((), (), s32[]{:S(2)}) async-start(), calls=%async_computation.14 | async-start | bytes 7208960 | tf_op jit(solution)/shard_map/all_gather | solution.py:321
  205.1 273.0 %all-gather.14.cloned.1.call-start = ((), (), s32[]{:S(2)}) async-start(), calls=%async_computation.15 | async-start | bytes 3604480 | tf_op jit(solution)/shard_map/all_gather | solution.py:321
  205.2 32.8 %collective-permute-start.2 = (f32[1,768]{1,0:T(1,128)S(1)}, f32[1,768]{1,0:T(1,128)S(1)}, u32[]{:S(2)}, u32[]{:S(2)}) collective-permute-start(f32[1,768]{1,0:T(1,128)S(1)} %bitcast.244), channel_id=1, source_target_pairs={{1,0},{2,1},{3,2},{0,3},{5,4},{6,5},{7,6},{4,7},{9,8},{10,9},{11,1... | collective-permute-start | bytes 9224 | tf_op jit(solution)/shard_map/ppermute | solution.py:364
  206.4 31.7 %collective-permute-start.3 = (f32[1,768]{1,0:T(1,128)S(1)}, f32[1,768]{1,0:T(1,128)S(1)}, u32[]{:S(2)}, u32[]{:S(2)}) collective-permute-start(f32[1,768]{1,0:T(1,128)S(1)} %bitcast.245), channel_id=1, source_target_pairs={{2,0},{3,1},{0,2},{1,3},{6,4},{7,5},{4,6},{5,7},{10,8},{11,9},{8,1... | collective-permute-start | bytes 9224 | tf_op jit(solution)/shard_map/ppermute | solution.py:364
  206.4 31.7 %collective-permute-start.4 = (f32[1,768]{1,0:T(1,128)S(1)}, f32[1,768]{1,0:T(1,128)S(1)}, u32[]{:S(2)}, u32[]{:S(2)}) collective-permute-start(f32[1,768]{1,0:T(1,128)S(1)} %bitcast.246), channel_id=1, source_target_pairs={{3,0},{0,1},{1,2},{2,3},{7,4},{4,5},{5,6},{6,7},{11,8},{8,9},{9,10... | collective-permute-start | bytes 9224 | tf_op jit(solution)/shard_map/ppermute | solution.py:364
  214.4 103.5 %collective-permute-start.1 = (bf16[2304,1024]{1,0:T(8,128)(2,1)}, bf16[2304,1024]{1,0:T(8,128)(2,1)}, u32[]{:S(2)}, u32[]{:S(2)}) collective-permute-start(bf16[2304,1024]{1,0:T(8,128)(2,1)} %pad_maximum_fusion.10), channel_id=1, source_target_pairs={{0,8},{4,12},{8,0},{12,4},{1,9},{5,13},{9,1},{13,5},{2,10},{6,14},... | collective-permute-start | bytes 14155784 | tf_op jit(solution)/shard_map/ppermute | solution.py:326
  220.1 109.5 %collective-permute-start = (bf16[512,2048]{1,0:T(8,128)(2,1)}, bf16[512,2048]{1,0:T(8,128)(2,1)}, u32[]{:S(2)}, u32[]{:S(2)}) collective-permute-start(bf16[512,2048]{1,0:T(8,128)(2,1)} %fusion.30), channel_id=1, source_target_pairs={{0,4},{4,0},{8,12},{12,8},{1,5},{5,1},{9,13},{13,9},{2,6},{6,2},{1... | collective-permute-start | bytes 6291464 | tf_op jit(solution)/shard_map/ppermute | solution.py:369
  318.0 410.2 %all-gather.16.cloned.1.call-start = ((), (), s32[]{:S(2)}) async-start(), calls=%async_computation.16 | async-start | bytes 7208960 | tf_op jit(solution)/shard_map/all_gather | solution.py:358
  397.4 85.6 %collective-permute-start.6 = (bf16[512,2048]{1,0:T(8,128)(2,1)}, bf16[512,2048]{1,0:T(8,128)(2,1)}, u32[]{:S(2)}, u32[]{:S(2)}) collective-permute-start(bf16[512,2048]{1,0:T(8,128)(2,1)} %convolution_convert_fusion.6), channel_id=1, source_target_pairs={{0,4},{4,0},{8,12},{12,8},{1,5},{5,1},{9,13},{13,9},{2,6},{6,2},{1... | collective-permute-start | bytes 6291464 | tf_op jit(solution)/shard_map/ppermute | solution.py:375
  399.7 96.5 %collective-permute-start.8 = (bf16[2112,1024]{1,0:T(8,128)(2,1)}, bf16[2112,1024]{1,0:T(8,128)(2,1)}, u32[]{:S(2)}, u32[]{:S(2)}) collective-permute-start(bf16[2112,1024]{1,0:T(8,128)(2,1)} %pad_maximum_fusion.11), channel_id=1, source_target_pairs={{0,8},{4,12},{8,0},{12,4},{1,9},{5,13},{9,1},{13,5},{2,10},{6,14},... | collective-permute-start | bytes 12976136 | tf_op jit(solution)/shard_map/ppermute | solution.py:326
  423.8 220.1 %collective-permute-start.9 = (bf16[2112,1024]{1,0:T(8,128)(2,1)}, bf16[2112,1024]{1,0:T(8,128)(2,1)}, u32[]{:S(2)}, u32[]{:S(2)}) collective-permute-start(bf16[2112,1024]{1,0:T(8,128)(2,1)} %pad_maximum_fusion.12), channel_id=1, source_target_pairs={{0,8},{4,12},{8,0},{12,4},{1,9},{5,13},{9,1},{13,5},{2,10},{6,14},... | collective-permute-start | bytes 12976136 | tf_op jit(solution)/shard_map/ppermute | solution.py:326
  481.5 153.3 %collective-permute-start.10 = (bf16[1056,1024]{1,0:T(8,128)(2,1)}, bf16[1056,1024]{1,0:T(8,128)(2,1)}, u32[]{:S(2)}, u32[]{:S(2)}) collective-permute-start(bf16[1056,1024]{1,0:T(8,128)(2,1)} %pad_maximum_fusion.20), channel_id=1, source_target_pairs={{0,8},{4,12},{8,0},{12,4},{1,9},{5,13},{9,1},{13,5},{2,10},{6,14},... | collective-permute-start | bytes 6488072 | tf_op jit(solution)/shard_map/ppermute | solution.py:326
  490.3 192.1 %collective-permute-start.7 = (bf16[512,2048]{1,0:T(8,128)(2,1)}, bf16[512,2048]{1,0:T(8,128)(2,1)}, u32[]{:S(2)}, u32[]{:S(2)}) collective-permute-start(bf16[512,2048]{1,0:T(8,128)(2,1)} %add_convert_fusion.8), channel_id=1, source_target_pairs={{0,4},{4,0},{8,12},{12,8},{1,5},{5,1},{9,13},{13,9},{2,6},{6,2},{1... | collective-permute-start | bytes 6291464 | tf_op jit(solution)/shard_map/ppermute | solution.py:369
  496.3 1431.1 %reduce-scatter.24.cloned.1.call-start = ((), (), s32[]{:S(2)}) async-start(), calls=%async_computation.24 | async-start | bytes 3604480 | tf_op jit(solution)/shard_map/reduce_scatter | solution.py:419
  734.8 8.3 collective-permute-start.11
  743.2 6.8 collective-permute-start.13
  746.6 26.8 %collective-permute-start.12 = (bf16[256,2048]{1,0:T(8,128)(2,1)S(1)}, bf16[256,2048]{1,0:T(8,128)(2,1)S(1)}, u32[]{:S(2)}, u32[]{:S(2)}) collective-permute-start(bf16[256,2048]{1,0:T(8,128)(2,1)S(1)} %fusion.88), channel_id=1, source_target_pairs={{0,16},{1,17},{2,18},{3,19},{4,20},{5,21},{6,22},{7,23},{8,24},{9,... | collective-permute-start | bytes 3145736 | tf_op jit(solution)/shard_map/ppermute | solution.py:384
  754.3 41.2 %collective-permute-start.14 = (bf16[256,2048]{1,0:T(8,128)(2,1)}, bf16[256,2048]{1,0:T(8,128)(2,1)S(1)}, u32[]{:S(2)}, u32[]{:S(2)}) collective-permute-start(bf16[256,2048]{1,0:T(8,128)(2,1)} %fusion.87), channel_id=1, source_target_pairs={{0,16},{1,17},{2,18},{3,19},{4,20},{5,21},{6,22},{7,23},{8,24},{9,... | collective-permute-start | bytes 3145736 | tf_op jit(solution)/shard_map/ppermute | solution.py:384
  802.8 4.3 collective-permute-start.15
  873.2 4.2 collective-permute-start.16
  882.7 4.3 collective-permute-start.18
  882.8 38.2 %collective-permute-start.17 = (bf16[512,2048]{1,0:T(8,128)(2,1)S(1)}, bf16[512,2048]{1,0:T(8,128)(2,1)}, u32[]{:S(2)}, u32[]{:S(2)}) collective-permute-start(bf16[512,2048]{1,0:T(8,128)(2,1)S(1)} %bitcast.168), channel_id=1, source_target_pairs={{0,4},{4,0},{8,12},{12,8},{1,5},{5,1},{9,13},{13,9},{2,6},{6,2},{1... | collective-permute-start | bytes 6291464 | tf_op jit(solution)/shard_map/ppermute | solution.py:369
  964.5 16.9 collective-permute-start.19
  965.8 126.9 %collective-permute-start.21 = (bf16[1024,2816]{1,0:T(8,128)(2,1)}, bf16[1024,2816]{1,0:T(8,128)(2,1)}, u32[]{:S(2)}, u32[]{:S(2)}) collective-permute-start(bf16[1024,2816]{1,0:T(8,128)(2,1)} %get-tuple-element.170), channel_id=1, source_target_pairs={{0,8},{4,12},{8,0},{12,4},{1,9},{5,13},{9,1},{13,5},{2,10},{6,14},... | collective-permute-start | bytes 17301512 | tf_op jit(solution)/shard_map/ppermute | solution.py:416
  975.3 34.6 %collective-permute-start.27 = (bf16[256,2048]{1,0:T(8,128)(2,1)}, bf16[256,2048]{1,0:T(8,128)(2,1)}, u32[]{:S(2)}, u32[]{:S(2)}) collective-permute-start(bf16[256,2048]{1,0:T(8,128)(2,1)} %convolution_convert_fusion.7), channel_id=1, source_target_pairs={{0,4},{4,0},{8,12},{12,8},{1,5},{5,1},{9,13},{13,9},{2,6},{6,2},{1... | collective-permute-start | bytes 3145736 | tf_op jit(solution)/shard_map/ppermute | solution.py:375
  980.9 36.6 %collective-permute-start.26 = (bf16[256,2048]{1,0:T(8,128)(2,1)}, bf16[256,2048]{1,0:T(8,128)(2,1)}, u32[]{:S(2)}, u32[]{:S(2)}) collective-permute-start(bf16[256,2048]{1,0:T(8,128)(2,1)} %convolution_convert_fusion.8), channel_id=1, source_target_pairs={{0,4},{4,0},{8,12},{12,8},{1,5},{5,1},{9,13},{13,9},{2,6},{6,2},{1... | collective-permute-start | bytes 3145736 | tf_op jit(solution)/shard_map/ppermute | solution.py:375
  1009.8 14.9 collective-permute-start.20
  1169.7 14.3 collective-permute-start.24
  1183.5 14.5 collective-permute-start.22
  1219.8 30.8 %collective-permute-start.25 = (bf16[256,2048]{1,0:T(8,128)(2,1)S(1)}, bf16[256,2048]{1,0:T(8,128)(2,1)S(1)}, u32[]{:S(2)}, u32[]{:S(2)}) collective-permute-start(bf16[256,2048]{1,0:T(8,128)(2,1)S(1)} %get-tuple-element.176), channel_id=1, source_target_pairs={{16,0},{17,1},{18,2},{19,3},{20,4},{21,5},{22,6},{23,7},{24,8},{25... | collective-permute-start | bytes 3145736 | tf_op jit(solution)/shard_map/ppermute | solution.py:384
  1221.3 51.2 %collective-permute-start.23 = (bf16[256,2048]{1,0:T(8,128)(2,1)S(1)}, bf16[256,2048]{1,0:T(8,128)(2,1)S(1)}, u32[]{:S(2)}, u32[]{:S(2)}) collective-permute-start(bf16[256,2048]{1,0:T(8,128)(2,1)S(1)} %get-tuple-element.175), channel_id=1, source_target_pairs={{16,0},{17,1},{18,2},{19,3},{20,4},{21,5},{22,6},{23,7},{24,8},{25... | collective-permute-start | bytes 3145736 | tf_op jit(solution)/shard_map/ppermute | solution.py:384
  1273.2 25.9 %collective-permute-start.30 = (bf16[512,2048]{1,0:T(8,128)(2,1)S(1)}, bf16[512,2048]{1,0:T(8,128)(2,1)}, u32[]{:S(2)}, u32[]{:S(2)}) collective-permute-start(bf16[512,2048]{1,0:T(8,128)(2,1)S(1)} %broadcast_select_fusion.1), channel_id=1, source_target_pairs={{0,4},{4,0},{8,12},{12,8},{1,5},{5,1},{9,13},{13,9},{2,6},{6,2},{1... | collective-permute-start | bytes 6291464 | tf_op jit(solution)/shard_map/ppermute | solution.py:369
  1273.5 25.6 %collective-permute-start.28 = (bf16[512,1024]{1,0:T(8,128)(2,1)S(1)}, bf16[512,1024]{1,0:T(8,128)(2,1)S(1)}, u32[]{:S(2)}, u32[]{:S(2)}) collective-permute-start(bf16[512,1024]{1,0:T(8,128)(2,1)S(1)} %get-tuple-element.212), channel_id=1, source_target_pairs={{0,8},{4,12},{8,0},{12,4},{1,9},{5,13},{9,1},{13,5},{2,10},{6,14},... | collective-permute-start | bytes 3145736 | tf_op jit(solution)/shard_map/ppermute | solution.py:416
  1275.0 91.9 %collective-permute-start.32 = (bf16[512,1024]{1,0:T(8,128)(2,1)S(1)}, bf16[512,1024]{1,0:T(8,128)(2,1)}, u32[]{:S(2)}, u32[]{:S(2)}) collective-permute-start(bf16[512,1024]{1,0:T(8,128)(2,1)S(1)} %get-tuple-element.211), channel_id=1, source_target_pairs={{0,4},{4,0},{8,12},{12,8},{1,5},{5,1},{9,13},{13,9},{2,6},{6,2},{1... | collective-permute-start | bytes 3145736 | tf_op jit(solution)/shard_map/ppermute | solution.py:369
  1299.1 40.8 %collective-permute-start.29 = (bf16[512,1024]{1,0:T(8,128)(2,1)S(1)}, bf16[512,1024]{1,0:T(8,128)(2,1)}, u32[]{:S(2)}, u32[]{:S(2)}) collective-permute-start(bf16[512,1024]{1,0:T(8,128)(2,1)S(1)} %collective-permute-done.28), channel_id=1, source_target_pairs={{0,4},{4,0},{8,12},{12,8},{1,5},{5,1},{9,13},{13,9},{2,6},{6,2},{1... | collective-permute-start | bytes 3145736 | tf_op jit(solution)/shard_map/ppermute | solution.py:369
  1345.8 65.2 %collective-permute-start.31 = (bf16[1408,1024]{1,0:T(8,128)(2,1)}, bf16[1408,1024]{1,0:T(8,128)(2,1)}, u32[]{:S(2)}, u32[]{:S(2)}) collective-permute-start(bf16[1408,1024]{1,0:T(8,128)(2,1)} %get-tuple-element.199), channel_id=1, source_target_pairs={{0,8},{4,12},{8,0},{12,4},{1,9},{5,13},{9,1},{13,5},{2,10},{6,14},... | collective-permute-start | bytes 8650760 | tf_op jit(solution)/shard_map/ppermute | solution.py:416
  1414.1 514.4 %reduce-scatter.26.cloned.1.call-start = ((), (), s32[]{:S(2)}) async-start(), calls=%async_computation.25 | async-start | bytes 3604480 | tf_op jit(solution)/shard_map/reduce_scatter | solution.py:419
  1414.2 4.6 collective-permute-start.34
  1414.3 65.2 %collective-permute-start.33 = (bf16[1408,1024]{1,0:T(8,128)(2,1)}, bf16[1408,1024]{1,0:T(8,128)(2,1)}, u32[]{:S(2)}, u32[]{:S(2)}) collective-permute-start(bf16[1408,1024]{1,0:T(8,128)(2,1)} %get-tuple-element.74), channel_id=1, source_target_pairs={{0,8},{4,12},{8,0},{12,4},{1,9},{5,13},{9,1},{13,5},{2,10},{6,14},... | collective-permute-start | bytes 8650760 | tf_op jit(solution)/shard_map/ppermute | solution.py:416
  1415.8 522.3 %reduce-scatter.16.cloned.1.call-start = ((), (), s32[]{:S(2)}) async-start(), calls=%async_computation.20 | async-start | bytes 3604480 | tf_op jit(solution)/shard_map/reduce_scatter | solution.py:419
  1442.2 40.6 %collective-permute-start.35 = (bf16[512,2048]{1,0:T(8,128)(2,1)S(1)}, bf16[512,2048]{1,0:T(8,128)(2,1)S(1)}, u32[]{:S(2)}, u32[]{:S(2)}) collective-permute-start(bf16[512,2048]{1,0:T(8,128)(2,1)S(1)} %get-tuple-element.160), channel_id=1, source_target_pairs={{0,4},{4,0},{8,12},{12,8},{1,5},{5,1},{9,13},{13,9},{2,6},{6,2},{1... | collective-permute-start | bytes 6291464 | tf_op jit(solution)/shard_map/ppermute | solution.py:369
  1497.9 441.4 %reduce-scatter.18.cloned.1.call-start = ((), (), s32[]{:S(2)}) async-start(), calls=%async_computation.21 | async-start | bytes 3604480 | tf_op jit(solution)/shard_map/reduce_scatter | solution.py:419
  1503.9 64.3 %collective-permute-start.36 = (bf16[1408,1024]{1,0:T(8,128)(2,1)}, bf16[1408,1024]{1,0:T(8,128)(2,1)S(1)}, u32[]{:S(2)}, u32[]{:S(2)}) collective-permute-start(bf16[1408,1024]{1,0:T(8,128)(2,1)} %get-tuple-element.197), channel_id=1, source_target_pairs={{0,8},{4,12},{8,0},{12,4},{1,9},{5,13},{9,1},{13,5},{2,10},{6,14},... | collective-permute-start | bytes 8650760 | tf_op jit(solution)/shard_map/ppermute | solution.py:416
  1505.4 436.5 %reduce-scatter.20.cloned.1.call-start = ((), (), s32[]{:S(2)}) async-start(), calls=%async_computation.22 | async-start | bytes 3604480 | tf_op jit(solution)/shard_map/reduce_scatter | solution.py:419
  1568.2 79.1 %collective-permute-start.37 = (bf16[1408,1024]{1,0:T(8,128)(2,1)}, bf16[1408,1024]{1,0:T(8,128)(2,1)}, u32[]{:S(2)}, u32[]{:S(2)}) collective-permute-start(bf16[1408,1024]{1,0:T(8,128)(2,1)} %get-tuple-element.82), channel_id=1, source_target_pairs={{0,8},{4,12},{8,0},{12,4},{1,9},{5,13},{9,1},{13,5},{2,10},{6,14},... | collective-permute-start | bytes 8650760 | tf_op jit(solution)/shard_map/ppermute | solution.py:416
  1662.0 281.0 %reduce-scatter.22.cloned.1.call-start = ((), (), s32[]{:S(2)}) async-start(), calls=%async_computation.23 | async-start | bytes 3604480 | tf_op jit(solution)/shard_map/reduce_scatter | solution.py:419
  1662.6 287.3 %reduce-scatter.10.cloned.1.call-start = ((), (), s32[]{:S(2)}) async-start(), calls=%async_computation.17 | async-start | bytes 3932160 | tf_op jit(solution)/shard_map/reduce_scatter | solution.py:419
  1662.7 68.9 %collective-permute-start.38 = (bf16[1536,1024]{1,0:T(8,128)(2,1)}, bf16[1536,1024]{1,0:T(8,128)(2,1)S(1)}, u32[]{:S(2)}, u32[]{:S(2)}) collective-permute-start(bf16[1536,1024]{1,0:T(8,128)(2,1)} %convolution_convert_fusion.4), channel_id=1, source_target_pairs={{0,8},{4,12},{8,0},{12,4},{1,9},{5,13},{9,1},{13,5},{2,10},{6,14},... | collective-permute-start | bytes 9437192 | tf_op jit(solution)/shard_map/ppermute | solution.py:416
  1731.5 13.3 collective-permute-start.40
  1737.8 212.1 %reduce-scatter.12.cloned.1.call-start = ((), (), s32[]{:S(2)}) async-start(), calls=%async_computation.18 | async-start | bytes 3932160 | tf_op jit(solution)/shard_map/reduce_scatter | solution.py:419
  1743.9 70.9 %collective-permute-start.39 = (bf16[1536,1024]{1,0:T(8,128)(2,1)}, bf16[1536,1024]{1,0:T(8,128)(2,1)}, u32[]{:S(2)}, u32[]{:S(2)}) collective-permute-start(bf16[1536,1024]{1,0:T(8,128)(2,1)} %convolution_convert_fusion.3), channel_id=1, source_target_pairs={{0,8},{4,12},{8,0},{12,4},{1,9},{5,13},{9,1},{13,5},{2,10},{6,14},... | collective-permute-start | bytes 9437192 | tf_op jit(solution)/shard_map/ppermute | solution.py:416
  1821.4 97.4 %all-to-all-start.1 = ((bf16[16,32,2048]{2,1,0:T(8,128)(2,1)}), bf16[16,32,2048]{2,1,0:T(8,128)(2,1)S(1)}, u32[]{:S(2)}, u32[]{:S(2)}) async-start(bf16[16,32,2048]{2,1,0:T(8,128)(2,1)} %bitcast.59), calls=%async_computation.1 | async-start | bytes 4194304 | tf_op jit(solution)/shard_map/all_to_all | solution.py:519
  1826.4 153.3 %reduce-scatter.14.cloned.1.call-start = ((), (), s32[]{:S(2)}) async-start(), calls=%async_computation.19 | async-start | bytes 2621440 | tf_op jit(solution)/shard_map/reduce_scatter | solution.py:419
  1826.7 96.8 %collective-permute-start.42 = (bf16[1024,1024]{1,0:T(8,128)(2,1)}, bf16[1024,1024]{1,0:T(8,128)(2,1)}, u32[]{:S(2)}, u32[]{:S(2)}) collective-permute-start(bf16[1024,1024]{1,0:T(8,128)(2,1)} %fusion.93), channel_id=1, source_target_pairs={{0,8},{4,12},{8,0},{12,4},{1,9},{5,13},{9,1},{13,5},{2,10},{6,14},... | collective-permute-start | bytes 6291464 | tf_op jit(solution)/shard_map/ppermute | solution.py:416
  1941.7 4.9 collective-permute-start.44
  1945.6 9.6 collective-permute-start.45
  1955.1 27.2 %collective-permute-start.41 = (bf16[3,256,512]{1,2,0:T(8,128)(2,1)}, bf16[3,256,512]{1,2,0:T(8,128)(2,1)}, u32[]{:S(2)}, u32[]{:S(2)}) collective-permute-start(bf16[3,256,512]{1,2,0:T(8,128)(2,1)} %copy.91), channel_id=1, source_target_pairs={{0,4},{4,0},{8,12},{12,8},{1,5},{5,1},{9,13},{13,9},{2,6},{6,2},{1... | collective-permute-start | bytes 2359304 | tf_op jit(solution)/shard_map/ppermute | solution.py:544
  1958.5 16.1 all-to-all-start.2
  1980.8 5.2 collective-permute-start.43
  (105 other events, 3104.7 us)
Sparse Core Ops, SparseCore 0:
  10.2 66.7 all-gather.17
  79.1 125.9 all-gather.7
  206.7 105.4 all-gather.9
  313.6 104.9 all-gather.11
  420.6 57.4 all-gather.13
  496.4 107.1 all-gather.15
  1414.3 55.7 reduce-scatter.23
  1472.4 56.0 reduce-scatter.25
  1530.8 56.0 reduce-scatter.15
  1589.0 56.0 reduce-scatter.17
  1662.2 55.0 reduce-scatter.19
  1719.4 56.0 reduce-scatter.21
  1778.4 65.6 reduce-scatter.9
  1846.8 83.1 reduce-scatter.11
  1932.1 47.5 reduce-scatter.13

commit v4 on v2

--- a/solution.py
+++ b/solution.py
@@ -242,9 +242,9 @@
         scratch_shapes=[pltpu.VMEM((rows, 128), jnp.float32), pltpu.VMEM((rows, 128), jnp.float32)],
         compiler_params=pltpu.CompilerParams(vmem_limit_bytes=VMEM_LIMIT),
         cost_estimate=pl.CostEstimate(
-            flops=7 * rows * rows * columns // 3 * 4,
-            bytes_accessed=rows * columns * 5,
-            transcendentals=rows * rows * columns // (3 * HEAD_WIDTH),
+            flops=rows * columns,
+            bytes_accessed=rows * columns,
+            transcendentals=0,
         ),
     )(qkv, ctx_grad, cos_t, low_t, high_t, pos_c, pos_r)
 
@@ -437,101 +437,107 @@
         sigma = jax.nn.sigmoid(gate)
         gate_grad = (act_grad * up * sigma * (1.0 + gate * (1.0 - sigma))).astype(jnp.bfloat16)
         up_grad = (act_grad * gate * sigma).astype(jnp.bfloat16)
-        return gate_grad, up_grad, jnp.concatenate([gate_grad, up_grad], axis=1)
-
-    def backward(grad_out, stored):
+        return gate_grad, up_grad
+
+    def two_dot(gate_grad, up_grad):
+        return dot_n(jnp.concatenate([gate_grad, up_grad], axis=1), wt_gu)
+
+    def from_core(term):
+        return lax.ppermute(term.astype(jnp.bfloat16), "ctx", core_route).astype(jnp.float32)
+
+    def backward(grad_out, stored, wait):
         stream, normed, qkv, attended, hidden_state, normed_two, gate_up, activation = stored
-        gu_grad = mlp_back(dot_t(both(grad_out), wt_down), gate_up)[2]
-        result = ln_back(hidden_state, summed(gu_grad, wt_gu)[0], gain[1])[0]
-        hidden_grad = grad_out.astype(jnp.float32) + result
+        gate_grad, up_grad = mlp_back(dot_t(both(grad_out), wt_down), gate_up)
+        gu_grad = jnp.concatenate([gate_grad, up_grad], axis=1)
+        two_grad = summed(gu_grad, wt_gu)[0]
+        hidden_grad = grad_out.astype(jnp.float32) + ln_back(hidden_state, two_grad, gain[1])[0]
         ctx_grad = dot_t(both(hidden_grad.astype(jnp.bfloat16)), wt_out).astype(jnp.bfloat16)
         qkv_grad, _ = attn_bwd(qkv, ctx_grad, context, tp_count, chunk)
-        one_grad = jnp.concatenate(summed(qkv_grad, wt_qkv, 2), axis=0)
-        result = ln_back(stream, one_grad, gain[0])[0]
-        return split((hidden_grad + result).astype(jnp.bfloat16), 2)
-
-    def last_backward(grad_out, stored, final_out):
-        stream, normed, qkv, attended, hidden_state, normed_two, gate_up, activation, act_a, act_b = stored
+        one_grad = summed(after(qkv_grad, wait), wt_qkv, 2)
+        return [
+            (z + ln_back(x, y, gain[0])[0]).astype(jnp.bfloat16)
+            for x, y, z in zip(split(stream, 2), one_grad, split(hidden_grad, 2))
+        ]
+
+    def last_backward(grad_out, stored, final_out, act_both):
+        stream, normed, qkv, attended, hidden_state, normed_two, gate_up, _ = stored
         grad_f32 = grad_out.astype(jnp.float32)
+        far_grad, near_grad = far_near(grad_out)
+        grad_across = across(far_grad)
         mlp_grad = both(grad_out)
-        far_a, far_b = far_term(act_a, mlp_grad), far_term(act_b, mlp_grad)
-
-        mlp_in, far_a, far_b = together((mlp_grad, far_a, far_b))
-        arriving = across(far_a)
-        gate_grad, up_grad, gu_grad = mlp_back(dot_t(mlp_in, wt_down), gate_up)
-
-        arriving, far_b, gate_grad, up_grad, act_a = together((arriving, far_b, gate_grad, up_grad, act_a))
-        arriving_b = across(far_b)
-        sum_a = over_tp(near_total(act_a, mlp_grad, arriving))
-        gu_grad = jnp.concatenate([gate_grad, up_grad], axis=1)
-        two_other = dot_n(gu_grad[own_rows:], wt_gu).astype(jnp.bfloat16)
+        gate_grad, up_grad = mlp_back(dot_t(mlp_grad, wt_down), gate_up)
         far_gate = far_term(gate_grad, normed_two)
 
-        arriving_b, far_gate, gu_grad, two_other, act_b, up_grad = together(
-            (arriving_b, far_gate, gu_grad, two_other, act_b, up_grad)
+        grad_across, far_gate, gate_grad, up_grad = together((grad_across, far_gate, gate_grad, up_grad))
+        arriving_gate = across(far_gate)
+        grad_both = jnp.concatenate([both(near_grad), both(grad_across)], axis=0)
+        down_total = dot_0(act_both, grad_both).astype(jnp.bfloat16)
+        down_total, gate_other, up_other = together((down_total, gate_grad[own_rows:], up_grad[own_rows:]))
+        sum_down = over_tp(down_total)
+        arriving = from_core(two_dot(gate_other, up_other))
+        two_grad = two_dot(gate_grad[:own_rows], up_grad[:own_rows]) + arriving
+        far_up_a, far_up_b = (far_term(x, normed_two) for x in jnp.split(up_grad, 2, axis=1))
+
+        arriving_gate, far_up_a, far_up_b, gate_grad, two_grad = together(
+            (arriving_gate, far_up_a, far_up_b, gate_grad, two_grad)
         )
-        arriving_gate = across(far_gate)
-        sum_b = over_tp(near_total(act_b, mlp_grad, arriving_b))
-        two_grad = dot_n(gu_grad[:own_rows], wt_gu) + lax.ppermute(two_other, "ctx", core_route).astype(jnp.float32)
+        arriving = across(far_up_a)
+        gate_total = near_total(gate_grad, normed_two, arriving_gate)
+        gate_total, two_grad = together((gate_total, two_grad))
+        sum_gate = over_tp(gate_total)
         result, gain_two, shift_two = ln_back(hidden_state, two_grad, gain[1])
         hidden_grad = grad_f32 + result
         attn_grad = both(hidden_grad.astype(jnp.bfloat16))
-        far_up = far_term(up_grad, normed_two)
-
-        arriving_gate, far_up, gate_grad, attn_grad, hidden_grad = together(
-            (arriving_gate, far_up, gate_grad, attn_grad, hidden_grad)
-        )
-        far_up_a, far_up_b = split(far_up, 2)
-        arriving = across(far_up_a)
-        sum_gate = over_tp(near_total(gate_grad, normed_two, arriving_gate))
         ctx_grad = dot_t(attn_grad, wt_out).astype(jnp.bfloat16)
 
         arriving, far_up_b, ctx_grad = together((arriving, far_up_b, ctx_grad))
         arriving_up = jnp.concatenate([arriving, across(far_up_b)], axis=0)
         qkv_grad, bias_grad = attn_bwd(qkv, ctx_grad, context, tp_count, chunk)
+        far_out = far_term(attended, attn_grad)
+
+        arriving_up, far_out, qkv_grad, up_grad, attn_grad = together(
+            (arriving_up, far_out, qkv_grad, up_grad, attn_grad)
+        )
+        arriving_out = across(far_out)
+        sum_up = over_tp(near_total(up_grad, normed_two, arriving_up))
         qkv_a, qkv_b = (part_of(qkv_grad, i, 2, 1) for i in range(2))
         far_a = far_term(qkv_a, normed)
 
-        arriving_up, far_a, qkv_a, qkv_b, qkv_grad, up_grad, attn_grad = together(
-            (arriving_up, far_a, qkv_a, qkv_b, qkv_grad, up_grad, attn_grad)
+        arriving_out, far_a, qkv_a, qkv_b, qkv_grad, attn_grad = together(
+            (arriving_out, far_a, qkv_a, qkv_b, qkv_grad, attn_grad)
         )
         arriving = across(far_a)
-        sum_up = over_tp(near_total(up_grad, normed_two, arriving_up))
-        one_other = dot_n(qkv_grad[own_rows:], wt_qkv).astype(jnp.bfloat16)
+        sum_out = over_tp(near_total(attended, attn_grad, arriving_out))
+        one_grad = summed(qkv_grad, wt_qkv)[0]
         far_b = far_term(qkv_b, normed)
 
-        arriving, far_b, one_other, qkv_grad, qkv_a, qkv_b = together(
-            (arriving, far_b, one_other, qkv_grad, qkv_a, qkv_b)
-        )
+        arriving, far_b, one_grad, qkv_a, qkv_b = together((arriving, far_b, one_grad, qkv_a, qkv_b))
         arriving_b = across(far_b)
         sum_qkv_a = over_tp(near_total(qkv_a, normed, arriving))
-        one_grad = dot_n(qkv_grad[:own_rows], wt_qkv) + lax.ppermute(one_other, "ctx", core_route).astype(jnp.float32)
         result, gain_one, shift_one = ln_back(stream, one_grad, gain[0])
         input_grad = (hidden_grad + result).astype(jnp.bfloat16)
         ends = jnp.where(first, input_grad, final_out)
-        far_out = far_term(attended, attn_grad)
-
-        arriving_b, far_out, ends, qkv_b = together((arriving_b, far_out, ends, qkv_b))
-        arriving_out = across(far_out)
+
+        arriving_b, ends, qkv_b = together((arriving_b, ends, qkv_b))
         ends = lax.all_to_all(
             ends.reshape(ctx_count * tp_count, piece, width), ("ctx", "tp"), 0, 0, tiled=True
         )
         sum_qkv_b = over_tp(near_total(qkv_b, normed, arriving_b))
-        sum_out = over_tp(near_total(attended, attn_grad, arriving_out))
         small = (jnp.stack([gain_one, gain_two]), jnp.stack([shift_one, shift_two]), bias_grad)
-        sum_down = jnp.concatenate([sum_a, sum_b], axis=0)
         sum_qkv = jnp.concatenate([sum_qkv_a, sum_qkv_b], axis=0)
+
         return ends, small, (sum_down, sum_gate, sum_up, sum_out, sum_qkv)
 
     sent, _ = forward(inbound.astype(jnp.float32))
     arriving = over_x(sent, [(0, 1)])
     final_out, stored = forward(jnp.where(first, inbound, arriving).astype(jnp.float32))
-    arriving_back = over_x(backward(inbound, stored), [(1, 0)])
-    halves = tuple(part_of(stored[-1], i, 2, 1) for i in range(2))
-    arriving_back, final_out, *halves = together((arriving_back, jnp.concatenate(final_out, axis=0), *halves))
-    stored = (*stored, *halves)
+    act_across = across(stored[7])
+    arriving_back = over_x(backward(inbound, stored, act_across), [(1, 0)])
+    arriving_back, final_out, act_both = together(
+        (arriving_back, jnp.concatenate(final_out, axis=0), jnp.concatenate([stored[7], act_across], axis=0))
+    )
     grad_out = jnp.where(first, arriving_back, inbound)
-    ends, small, sums = last_backward(grad_out, stored, final_out)
+    ends, small, sums = last_backward(grad_out, stored, final_out, act_both)
     down_sum, gate_sum, up_sum, out_sum, qkv_sum = sums
 
     def settled(term):
@@ -557,7 +563,7 @@
     ).reshape(3, tp_count * 2 * columns)
     vectors = jnp.concatenate([gain_terms, shift_terms, bias_full], axis=0)
     share = width // (ctx_count * tp_count)
-    vectors = vectors.reshape(-1, ctx_count * tp_count, share).transpose(1, 0, 2)
+    vectors = after(vectors, ends).reshape(-1, ctx_count * tp_count, share).transpose(1, 0, 2)
     vectors = jnp.sum(lax.all_to_all(vectors, ("ctx", "tp"), 0, 0, tiled=True), axis=0).reshape(-1, share)
 
     ends = ends.reshape(ctx_count // 2, 2, tp_count, piece, width).transpose(0, 2, 1, 3, 4)

time: 1900 us -> 1840 us (0.968)
  blocking collectives: 47.4 us -> 0 us
  other arithmetic: 166 us -> 194 us
  waiting for transfers between devices: 748 us -> 720 us
    reduce_scatter x7 -> x6, waiting for transfers between devices: 0.07 us -> 63.8 us  [over_tp(): return lax.psum_scatter(term, 'tp', scatter_dimension=0, tiled=True)]
    all_to_all x1, waiting for transfers between devices: 64.4 us -> 1.26 us  [last_backward(): lax.all_to_all(ends.reshape(ctx_count * tp_count, piece, width), ('ctx',...]
    all_to_all x1 -> x0, blocking collectives: 47.4 us -> none  [bulk_device(): lax.all_to_all(vectors, ('ctx', 'tp'), 0, 0, tiled=True)]
    ppermute x8, waiting for transfers between devices: 283 us -> 260 us  [across(): lax.ppermute(after(term, *others) if others else term, 'ctx', across_route)]
    dot_general x14 -> x12, matrix products: 106 us -> 99 us  [dot_0(): lax.dot_general(a, b, (((0,), (0,)), ((), ())), preferred_element_type=jn...]
  transfers between devices with their start and end apart: 60 -> 62, of which waited for: 26 -> 26; matrix products, arithmetic and copies ran while one was open for 36% -> 35% of each run, Pallas kernels for 9% -> 9%
where the time goes in v4:
time: 1840 us; the launch traced here: 1830 us
  waiting for transfers between devices  720 us (39%)
  matrix products  509 us (28%)
  Pallas kernels  204 us (11%)
  other arithmetic  194 us (11%)
  local copies, waits for them, and re-layouts  118 us (6%)
  starting transfers between devices  57.7 us (3%)
  between operations  31.5 us (2%)
    ppermute x8, waiting for transfers between devices, across(): lax.ppermute(after(term, *others) if others else term, 'ctx', across_route)  260 us
    all_gather x6, waiting for transfers between devices, gathered(): own = lax.all_gather(block, 'tp', axis=0, tiled=True)  255 us
    dot_general x22, matrix products, dot_n(): lax.dot_general(a, b, (((1,), (0,)), ((), ())), preferred_element_type=jn...  234 us
    dot_general x8, matrix products, dot_t(): lax.dot_general(a, b, (((1,), (1,)), ((), ())), preferred_element_type=jn...  176 us
    pallas_call x2, Pallas kernels, attn_bwd(): pl.pallas_call(functools.partial(attn_bwd_kernel, heads, chunk), grid=(gr...  126 us
    dot_general x12, matrix products, dot_0(): lax.dot_general(a, b, (((0,), (0,)), ((), ())), preferred_element_type=jn...  99 us
    ppermute x4, waiting for transfers between devices, over_x(): lax.ppermute(part, 'section', route)  78 us
    pallas_call x2, Pallas kernels, attn_fwd(): pl.pallas_call(functools.partial(attn_fwd_kernel, heads, chunk), grid=(gr...  77.9 us
  transfers between devices with their start and end apart: 62, of which 26 were waited for; matrix products, arithmetic and copies ran while one was open for 35% of the time, Pallas kernels for 9%

profile of v4, /device:TPU:0, one launch (start us, length us, event | category | flops | bytes accessed | tf_op | source)
XLA Modules:
  0.0 1834.0 jit_solution(14581017316265444469)
XLA Ops:
  40.6 7.4 all-to-all-start
  48.1 28.6 %all-gather.18.cloned.1.call-done = bf16[1,1024,1024]{2,1,0:T(8,128)(2,1)} async-done(((bf16[1,256,1024]{2,1,0:T(8,128)(2,1)}), bf16[1,1024,1024]{2,1,0:T(8,128)(2,1)}) %all-gather.18.cloned.1.call-update) | async-done | bytes 2097168 | tf_op jit(solution)/shard_map/all_gather | solution.py:321
  80.8 9.6 constant_dynamic-slice_fusion.24
  93.0 42.6 %all-to-all-done = bf16[16,32,2048]{2,1,0:T(8,128)(2,1)S(1)} async-done(((bf16[16,32,2048]{2,1,0:T(8,128)(2,1)}), bf16[16,32,2048]{2,1,0:T(8,128)(2,1)S(1)}, u32[]{:S(2)}, u32[]{:S(2)}) %all-to-all-start) | async-done | bytes 2097184 | tf_op jit(solution)/shard_map/all_to_all | solution.py:287
  138.2 66.9 %all-gather.8.cloned.1.call-done = bf16[3072,1024]{1,0:T(8,128)(2,1)} async-done(((bf16[768,1024]{1,0:T(8,128)(2,1)}), bf16[3072,1024]{1,0:T(8,128)(2,1)}) %all-gather.8.cloned.1.call-update) | async-done | bytes 6291472 | tf_op jit(solution)/shard_map/all_gather | solution.py:321
  244.1 68.1 %all-gather.10.cloned.1.call-done = bf16[2816,1024]{1,0:T(8,128)(2,1)} async-done(((bf16[704,1024]{1,0:T(8,128)(2,1)}), bf16[2816,1024]{1,0:T(8,128)(2,1)}) %all-gather.10.cloned.1.call-update) | async-done | bytes 5767184 | tf_op jit(solution)/shard_map/all_gather | solution.py:321
  319.1 11.4 fusion.3
  330.6 22.3 %fusion.33.mixed = f32[1024,3072]{1,0:T(8,128)} fusion(bf16[512,2048]{1,0:T(8,128)(2,1)} %collective-permute-done, bf16[512,2048]{1,0:T(8,128)(2,1)} %fusion.32, bf16[3072,1024]{1,0:T(8,128)(2,1)} %fusion.3, bf16[3072,1024]{1,0:T(8,128)(2,1)} %all-gather.8.cloned.1.call-done, pred[]{:T(512)S(6)} %eq.31), kind=kOutput, calls=%fused_computation.101 | convolution fusion | flops 12949913600 | bytes 29360128 | tf_op jit(solution)/shard_map/dot_general | solution.py:59
  352.9 39.2 %shard_map.170 = (bf16[1024,3072]{1,0:T(8,128)(2,1)}, bf16[1024,1024]{1,0:T(8,128)(2,1)}) custom-call(f32[1024,3072]{1,0:T(8,128)} %fusion.33.mixed, f32[4,1,768]{2,1,0:T(1,128)} %reshape.421.bias, f32[1024,128]{1,0:T(8,128)} %concatenate.276.cos_t, f32[1024,128]{1,0:T(8,128)} %concatenate.277.low_t, f32[1024,128]{1,0:T(8,128)} %concatenate.278.high_t, ...), custom_call_target="tpu_custom_call" | custom-call | flops 12884901888 | bytes 22020096 | tf_op jit(solution)/shard_map/pallas_call | solution.py:187
  392.1 6.3 convolution_convert_fusion.7
  402.9 9.8 fusion.186
  428.3 12.1 fusion.12
  440.4 7.0 maximum_select_fusion.1
  447.5 30.7 %all-gather.14.cloned.1.call-done = bf16[1408,1024]{1,0:T(8,128)(2,1)} async-done(((bf16[352,1024]{1,0:T(8,128)(2,1)}), bf16[1408,1024]{1,0:T(8,128)(2,1)}) %all-gather.14.cloned.1.call-update) | async-done | bytes 2883600 | tf_op jit(solution)/shard_map/all_gather | solution.py:321
  482.9 54.6 %all-gather.16.cloned.1.call-done = bf16[1408,1024]{1,0:T(8,128)(2,1)} async-done(((bf16[352,1024]{1,0:T(8,128)(2,1)}), bf16[1408,1024]{1,0:T(8,128)(2,1)}) %all-gather.16.cloned.1.call-update) | async-done | bytes 2883600 | tf_op jit(solution)/shard_map/all_gather | solution.py:321
  542.2 11.9 fusion.9
  554.1 7.1 maximum_select_fusion.2
  561.2 34.2 %fusion.37 = f32[1024,5632]{1,0:T(8,128)} fusion(bf16[512,2048]{1,0:T(8,128)(2,1)} %collective-permute-done.7, bf16[512,2048]{1,0:T(8,128)(2,1)} %add_convert_fusion.8, bf16[2816,2048]{1,0:T(8,128)(2,1)} %maximum_select_fusion.2, bf16[2816,2048]{1,0:T(8,128)(2,1)} %maximum_select_fusion.1), kind=kOutput, calls=%fused_computation.110 | convolution fusion | flops 23676846080 | bytes 50331648 | tf_op jit(solution)/shard_map/dot_general | solution.py:59
  595.4 9.4 fusion
  604.9 7.6 collective-permute-done.11
  612.4 8.2 fusion.79
  625.9 9.0 pad_maximum_fusion.1
  653.1 18.8 %collective-permute-done.13 = bf16[256,2048]{1,0:T(8,128)(2,1)S(1)} collective-permute-done((bf16[256,2048]{1,0:T(8,128)(2,1)S(1)}, bf16[256,2048]{1,0:T(8,128)(2,1)S(1)}, u32[]{:S(2)}, u32[]{:S(2)}) %collective-permute-start.13) | collective-permute-done | bytes 1048608 | tf_op jit(solution)/shard_map/ppermute | solution.py:385
  672.0 21.5 %collective-permute-done.15 = bf16[256,2048]{1,0:T(8,128)(2,1)S(1)} collective-permute-done((bf16[256,2048]{1,0:T(8,128)(2,1)S(1)}, bf16[256,2048]{1,0:T(8,128)(2,1)S(1)}, u32[]{:S(2)}, u32[]{:S(2)}) %collective-permute-start.15) | collective-permute-done | bytes 1048608 | tf_op jit(solution)/shard_map/ppermute | solution.py:385
  704.9 22.5 %fusion.28.mixed = f32[1024,3072]{1,0:T(8,128)} fusion(bf16[512,2048]{1,0:T(8,128)(2,1)} %collective-permute-done.16, bf16[512,2048]{1,0:T(8,128)(2,1)} %copy-done.34, bf16[3072,1024]{1,0:T(8,128)(2,1)} %fusion.3, bf16[3072,1024]{1,0:T(8,128)(2,1)} %all-gather.8.cloned.1.call-done, pred[]{:T(512)S(6)} %eq.31), kind=kOutput, calls=%fused_computation.96 | convolution fusion | flops 12949913600 | bytes 29360128 | tf_op jit(solution)/shard_map/dot_general | solution.py:59
  727.4 38.7 %shard_map.171 = (bf16[1024,3072]{1,0:T(8,128)(2,1)}, bf16[1024,1024]{1,0:T(8,128)(2,1)}) custom-call(f32[1024,3072]{1,0:T(8,128)} %fusion.28.mixed, f32[4,1,768]{2,1,0:T(1,128)} %reshape.421.bias, f32[1024,128]{1,0:T(8,128)} %concatenate.276.cos_t, f32[1024,128]{1,0:T(8,128)} %concatenate.277.low_t, f32[1024,128]{1,0:T(8,128)} %concatenate.278.high_t, ...), custom_call_target="tpu_custom_call" | custom-call | flops 12884901888 | bytes 22020096 | tf_op jit(solution)/shard_map/pallas_call | solution.py:187
  785.7 34.0 %fusion.27 = f32[1024,5632]{1,0:T(8,128)} fusion(bf16[512,2048]{1,0:T(8,128)(2,1)} %collective-permute-done.19, bf16[512,2048]{1,0:T(8,128)(2,1)} %copy-done.18, bf16[2816,2048]{1,0:T(8,128)(2,1)} %maximum_select_fusion.2, bf16[2816,2048]{1,0:T(8,128)(2,1)} %maximum_select_fusion.1), kind=kOutput, calls=%fused_computation.95 | convolution fusion | flops 23676846080 | bytes 50331648 | tf_op jit(solution)/shard_map/dot_general | solution.py:59
  819.7 26.4 %multiply_convert_fusion.4 = (bf16[1024,2816]{1,0:T(8,128)(2,1)}, bf16[1024,2816]{1,0:T(8,128)(2,1)}, bf16[1024,2816]{1,0:T(8,128)(2,1)}) fusion(f32[1024,5632]{1,0:T(8,128)} %fusion.27, bf16[2816,2048]{1,0:T(8,128)(2,1)} %bitcast.190, bf16[512,2048]{1,0:T(8,128)(2,1)} %collective-permute-done.18, bf16[512,2048]{1,0:T(8,128)(2,1)S(1)} %bitcast.177), kind=kOutput, calls=%fused_computation.28 | convolution fusion | flops 11865686016 | bytes 56098816 | tf_op jit(solution)/shard_map/dot_general | solution.py:59
  846.1 17.5 fusion.76
  865.4 9.5 convolution_convert_fusion.8
  881.0 21.8 %fusion.175 = (f32[512]{0:T(512)S(1)}, f32[512]{0:T(512)S(1)}, f32[512,2048]{1,0:T(8,128)}) fusion(f32[512]{0:T(512)S(1)} %add_rsqrt_fusion.2, f32[512,2048]{1,0:T(8,128)} %copy-done.2, f32[512]{0:T(512)S(1)} %broadcast_multiply_fusion.8, f32[2048]{0:T(1024)S(1)} %bitcast.245, bf16[512,2048]{1,0:T(8,128)(2,1)} %collective-permute-done.20, ...), kind=kOutput, calls=%fused_computation.376 | convolution fusion | flops 11877220352 | bytes 45105152 | tf_op jit(solution)/shard_map/dot_general | solution.py:67
  908.7 8.2 fusion.99
  928.7 62.7 %shard_map.172 = (bf16[1024,3072]{1,0:T(8,128)(2,1)}, f32[4,1,768]{2,1,0:T(1,128)}) custom-call(bf16[1024,3072]{1,0:T(8,128)(2,1)} %get-tuple-element.65.qkv, bf16[1024,1024]{1,0:T(8,128)(2,1)} %fusion.110.ctx, f32[1024,128]{1,0:T(8,128)} %concatenate.276.cos_t, f32[1024,128]{1,0:T(8,128)} %concatenate.277.low_t, f32[1024,128]{1,0:T(8,128)} %concatenate.278.high_t, ...), custom_call_target="tpu_custom_call" | custom-call | flops 3145728 | bytes 3145728 | tf_op jit(solution)/shard_map/pallas_call | solution.py:222
  991.4 12.7 convolution_convert_fusion.12
  1004.8 12.7 convolution_convert_fusion.13
  1017.6 14.2 fusion.86
  1031.8 15.3 multiply_reduce_fusion.11
  1056.7 11.4 pad_maximum_fusion.2
  1068.0 15.4 collective-permute-done.26
  1083.4 22.3 %collective-permute-done.24 = bf16[256,2048]{1,0:T(8,128)(2,1)S(1)} collective-permute-done((bf16[256,2048]{1,0:T(8,128)(2,1)S(1)}, bf16[256,2048]{1,0:T(8,128)(2,1)S(1)}, u32[]{:S(2)}, u32[]{:S(2)}) %collective-permute-start.24) | collective-permute-done | bytes 1048608 | tf_op jit(solution)/shard_map/ppermute | solution.py:385
  1110.8 24.5 %multiply_convert_fusion = (bf16[1024,2816]{1,0:T(8,128)(2,1)}, bf16[1024,2816]{1,0:T(8,128)(2,1)}) fusion(f32[1024,5632]{1,0:T(8,128)} %fusion.27, bf16[2816,2048]{1,0:T(8,128)(2,1)} %bitcast.193, bf16[512,2048]{1,0:T(8,128)(2,1)} %collective-permute-done.30, bf16[512,2048]{1,0:T(8,128)(2,1)} %copy-done.9), kind=kOutput, calls=%fused_computation.24 | convolution fusion | flops 11857035264 | bytes 50331648 | tf_op jit(solution)/shard_map/dot_general | solution.py:59
  1135.2 10.9 convolution_convert_fusion.1
  1156.5 15.9 convolution_convert_fusion
  1174.2 19.2 %fusion.73 = bf16[512,2048]{1,0:T(8,128)(2,1)} fusion(bf16[512,2816]{1,0:T(8,128)(2,1)} %get-tuple-element.75, bf16[512,2816]{1,0:T(8,128)(2,1)} %get-tuple-element.74, bf16[2816,2048]{1,0:T(8,128)(2,1)} %maximum_select_fusion.2, bf16[2816,2048]{1,0:T(8,128)(2,1)} %maximum_select_fusion.1), kind=kOutput, calls=%fused_computation.166 | convolution fusion | flops 11869880320 | bytes 30932992 | tf_op jit(solution)/shard_map/dot_general | solution.py:67
  1193.7 6.6 convolution_convert_fusion.5
  1200.3 6.5 convolution_convert_fusion.4
  1206.8 22.6 %convert_add_fusion.3 = f32[512,2048]{1,0:T(8,128)} fusion(bf16[512,2048]{1,0:T(8,128)(2,1)S(1)} %collective-permute-done.34, bf16[512,2816]{1,0:T(8,128)(2,1)} %get-tuple-element.192, bf16[512,2816]{1,0:T(8,128)(2,1)} %get-tuple-element.190, bf16[2816,2048]{1,0:T(8,128)(2,1)} %maximum_select_fusion.2, bf16[2816,2048]{1,0:T(8,128)(2,1)S(1)} %bitcast.185), kind=kOutput, calls=%fused_computation.141 | convolution fusion | flops 11870928896 | bytes 35127296 | tf_op jit(solution)/shard_map/dot_general | solution.py:67
  1229.3 70.2 %collective-permute-done.31 = bf16[2816,1024]{1,0:T(8,128)(2,1)} collective-permute-done((bf16[2816,1024]{1,0:T(8,128)(2,1)}, bf16[2816,1024]{1,0:T(8,128)(2,1)}, u32[]{:S(2)}, u32[]{:S(2)}) %collective-permute-start.31) | collective-permute-done | bytes 5767200 | tf_op jit(solution)/shard_map/ppermute | solution.py:417
  1299.6 12.2 add_convert_fusion.1
  1333.2 54.9 %collective-permute-done.35 = bf16[1408,1024]{1,0:T(8,128)(2,1)S(1)} collective-permute-done((bf16[1408,1024]{1,0:T(8,128)(2,1)S(1)}, bf16[1408,1024]{1,0:T(8,128)(2,1)S(1)}, u32[]{:S(2)}, u32[]{:S(2)}) %collective-permute-start.35) | collective-permute-done | bytes 2883616 | tf_op jit(solution)/shard_map/ppermute | solution.py:417
  1396.0 63.1 %shard_map.173 = (bf16[1024,3072]{1,0:T(8,128)(2,1)}, f32[4,1,768]{2,1,0:T(1,128)}) custom-call(bf16[1024,3072]{1,0:T(8,128)(2,1)} %get-tuple-element.65.qkv, bf16[1024,1024]{1,0:T(8,128)(2,1)} %convolution_convert_fusion.14.ctx, f32[1024,128]{1,0:T(8,128)} %concatenate.276.cos_t, f32[1024,128]{1,0:T(8,128)} %concatenate.277.low_t, ...), custom_call_target="tpu_custom_call" | custom-call | flops 3145728 | bytes 3145728 | tf_op jit(solution)/shard_map/pallas_call | solution.py:222
  1464.3 10.2 add_convert_fusion
  1483.8 7.2 convolution_convert_fusion.3
  1491.0 31.0 %collective-permute-done.38 = bf16[1024,1024]{1,0:T(8,128)(2,1)S(1)} collective-permute-done((bf16[1024,1024]{1,0:T(8,128)(2,1)}, bf16[1024,1024]{1,0:T(8,128)(2,1)S(1)}, u32[]{:S(2)}, u32[]{:S(2)}) %collective-permute-start.38) | collective-permute-done | bytes 2097184 | tf_op jit(solution)/shard_map/ppermute | solution.py:417
  1522.0 13.6 fusion.70
  1535.6 6.2 add_convert_fusion.4
  1542.5 7.3 convolution_convert_fusion.2
  1549.8 17.8 convert_add_fusion.2
  1567.6 45.1 %collective-permute-done.39 = bf16[1536,1024]{1,0:T(8,128)(2,1)S(1)} collective-permute-done((bf16[1536,1024]{1,0:T(8,128)(2,1)}, bf16[1536,1024]{1,0:T(8,128)(2,1)S(1)}, u32[]{:S(2)}, u32[]{:S(2)}) %collective-permute-start.39) | collective-permute-done | bytes 3145760 | tf_op jit(solution)/shard_map/ppermute | solution.py:417
  1612.7 6.2 add_convert_fusion.3
  1630.4 58.6 %collective-permute-done.41 = bf16[1536,1024]{1,0:T(8,128)(2,1)S(1)} collective-permute-done((bf16[1536,1024]{1,0:T(8,128)(2,1)}, bf16[1536,1024]{1,0:T(8,128)(2,1)S(1)}, u32[]{:S(2)}, u32[]{:S(2)}) %collective-permute-start.41) | collective-permute-done | bytes 3145760 | tf_op jit(solution)/shard_map/ppermute | solution.py:417
  1721.6 63.8 %reduce-scatter.9.cloned.1.call-done = bf16[384,1024]{1,0:T(8,128)(2,1)} async-done(((bf16[1536,1024]{1,0:T(8,128)(2,1)}), bf16[384,1024]{1,0:T(8,128)(2,1)}) %reduce-scatter.9.cloned.1.call-update) | async-done | bytes 786448 | tf_op jit(solution)/shard_map/reduce_scatter | solution.py:420
  1795.3 13.8 all-to-all-start.2
  1813.3 6.2 copy.77
  (508 shorter events, 319.6 us)
Async XLA Ops:
  7.2 198.1 %copy-start = (f32[1,3,512]{2,0,1:T(1,128)S(1)}, f32[1,3,512]{2,0,1:T(1,128)}, u32[]{:S(2)}) copy-start(f32[1,3,512]{2,0,1:T(1,128)} %param.18) | copy-start | bytes 18436
  7.2 69.5 %all-gather.18.cloned.1.call-start = ((), (), s32[]{:S(2)}) async-start(), calls=%async_computation.20 | async-start | bytes 2621440 | tf_op jit(solution)/shard_map/all_gather | solution.py:321
  9.5 195.6 %all-gather.8.cloned.1.call-start = ((), (), s32[]{:S(2)}) async-start(), calls=%async_computation.9 | async-start | bytes 7864320 | tf_op jit(solution)/shard_map/all_gather | solution.py:321
  40.6 94.9 %all-to-all-start = ((bf16[16,32,2048]{2,1,0:T(8,128)(2,1)}), bf16[16,32,2048]{2,1,0:T(8,128)(2,1)S(1)}, u32[]{:S(2)}, u32[]{:S(2)}) async-start(bf16[16,32,2048]{2,1,0:T(8,128)(2,1)} %bitcast.207), calls=%async_computation | async-start | bytes 4194304 | tf_op jit(solution)/shard_map/all_to_all | solution.py:287
  48.0 264.1 %all-gather.10.cloned.1.call-start = ((), (), s32[]{:S(2)}) async-start(), calls=%async_computation.10 | async-start | bytes 7208960 | tf_op jit(solution)/shard_map/all_gather | solution.py:321
  79.4 56.2 %collective-permute-start.5 = (bf16[768,1024]{1,0:T(8,128)(2,1)}, bf16[768,1024]{1,0:T(8,128)(2,1)}, u32[]{:S(2)}, u32[]{:S(2)}) collective-permute-start(bf16[768,1024]{1,0:T(8,128)(2,1)} %pad_maximum_fusion.22), channel_id=1, source_target_pairs={{0,8},{4,12},{8,0},{12,4},{1,9},{5,13},{9,1},{13,5},{2,10},{6,14},... | collective-permute-start | bytes 4718600 | tf_op jit(solution)/shard_map/ppermute | solution.py:326
  135.6 283.0 %all-gather.12.cloned.1.call-start = ((), (), s32[]{:S(2)}) async-start(), calls=%async_computation.11 | async-start | bytes 7208960 | tf_op jit(solution)/shard_map/all_gather | solution.py:321
  205.2 273.0 %all-gather.14.cloned.1.call-start = ((), (), s32[]{:S(2)}) async-start(), calls=%async_computation.12 | async-start | bytes 3604480 | tf_op jit(solution)/shard_map/all_gather | solution.py:321
  205.2 32.7 %collective-permute-start.2 = (f32[1,768]{1,0:T(1,128)S(1)}, f32[1,768]{1,0:T(1,128)S(1)}, u32[]{:S(2)}, u32[]{:S(2)}) collective-permute-start(f32[1,768]{1,0:T(1,128)S(1)} %bitcast.266), channel_id=1, source_target_pairs={{1,0},{2,1},{3,2},{0,3},{5,4},{6,5},{7,6},{4,7},{9,8},{10,9},{11,1... | collective-permute-start | bytes 9224 | tf_op jit(solution)/shard_map/ppermute | solution.py:365
  206.4 31.6 %collective-permute-start.3 = (f32[1,768]{1,0:T(1,128)S(1)}, f32[1,768]{1,0:T(1,128)S(1)}, u32[]{:S(2)}, u32[]{:S(2)}) collective-permute-start(f32[1,768]{1,0:T(1,128)S(1)} %bitcast.267), channel_id=1, source_target_pairs={{2,0},{3,1},{0,2},{1,3},{6,4},{7,5},{4,6},{5,7},{10,8},{11,9},{8,1... | collective-permute-start | bytes 9224 | tf_op jit(solution)/shard_map/ppermute | solution.py:365
  206.4 31.6 %collective-permute-start.4 = (f32[1,768]{1,0:T(1,128)S(1)}, f32[1,768]{1,0:T(1,128)S(1)}, u32[]{:S(2)}, u32[]{:S(2)}) collective-permute-start(f32[1,768]{1,0:T(1,128)S(1)} %bitcast.268), channel_id=1, source_target_pairs={{3,0},{0,1},{1,2},{2,3},{7,4},{4,5},{5,6},{6,7},{11,8},{8,9},{9,10... | collective-permute-start | bytes 9224 | tf_op jit(solution)/shard_map/ppermute | solution.py:365
  215.4 103.5 %collective-permute-start.1 = (bf16[2304,1024]{1,0:T(8,128)(2,1)}, bf16[2304,1024]{1,0:T(8,128)(2,1)}, u32[]{:S(2)}, u32[]{:S(2)}) collective-permute-start(bf16[2304,1024]{1,0:T(8,128)(2,1)} %pad_maximum_fusion.9), channel_id=1, source_target_pairs={{0,8},{4,12},{8,0},{12,4},{1,9},{5,13},{9,1},{13,5},{2,10},{6,14},... | collective-permute-start | bytes 14155784 | tf_op jit(solution)/shard_map/ppermute | solution.py:326
  222.2 204.0 %copy-start.47 = (f32[1,1,2048]{2,1,0:T(1,128)}, f32[1,1,2048]{2,1,0:T(1,128)S(1)}, u32[]{:S(2)}) copy-start(f32[1,1,2048]{2,1,0:T(1,128)S(1)} %get-tuple-element.230) | copy-start | bytes 24580
  225.6 105.0 %collective-permute-start = (bf16[512,2048]{1,0:T(8,128)(2,1)}, bf16[512,2048]{1,0:T(8,128)(2,1)}, u32[]{:S(2)}, u32[]{:S(2)}) collective-permute-start(bf16[512,2048]{1,0:T(8,128)(2,1)} %fusion.32), channel_id=1, source_target_pairs={{0,4},{4,0},{8,12},{12,8},{1,5},{5,1},{9,13},{13,9},{2,6},{6,2},{1... | collective-permute-start | bytes 6291464 | tf_op jit(solution)/shard_map/ppermute | solution.py:370
  317.2 95.7 %collective-permute-start.8 = (bf16[2112,1024]{1,0:T(8,128)(2,1)}, bf16[2112,1024]{1,0:T(8,128)(2,1)}, u32[]{:S(2)}, u32[]{:S(2)}) collective-permute-start(bf16[2112,1024]{1,0:T(8,128)(2,1)} %pad_maximum_fusion.10), channel_id=1, source_target_pairs={{0,8},{4,12},{8,0},{12,4},{1,9},{5,13},{9,1},{13,5},{2,10},{6,14},... | collective-permute-start | bytes 12976136 | tf_op jit(solution)/shard_map/ppermute | solution.py:326
  318.9 218.6 %all-gather.16.cloned.1.call-start = ((), (), s32[]{:S(2)}) async-start(), calls=%async_computation.13 | async-start | bytes 3604480 | tf_op jit(solution)/shard_map/all_gather | solution.py:321
  398.4 4.5 collective-permute-start.6
  418.7 1280.5 %reduce-scatter.17.cloned.1.call-start = ((), (), s32[]{:S(2)}) async-start(), calls=%async_computation.19 | async-start | bytes 7208960 | tf_op jit(solution)/shard_map/reduce_scatter | solution.py:420
  424.1 118.1 %collective-permute-start.9 = (bf16[2112,1024]{1,0:T(8,128)(2,1)}, bf16[2112,1024]{1,0:T(8,128)(2,1)}, u32[]{:S(2)}, u32[]{:S(2)}) collective-permute-start(bf16[2112,1024]{1,0:T(8,128)(2,1)} %pad_maximum_fusion.11), channel_id=1, source_target_pairs={{0,8},{4,12},{8,0},{12,4},{1,9},{5,13},{9,1},{13,5},{2,10},{6,14},... | collective-permute-start | bytes 12976136 | tf_op jit(solution)/shard_map/ppermute | solution.py:326
  428.3 132.9 %collective-permute-start.7 = (bf16[512,2048]{1,0:T(8,128)(2,1)}, bf16[512,2048]{1,0:T(8,128)(2,1)}, u32[]{:S(2)}, u32[]{:S(2)}) collective-permute-start(bf16[512,2048]{1,0:T(8,128)(2,1)} %add_convert_fusion.8), channel_id=1, source_target_pairs={{0,4},{4,0},{8,12},{12,8},{1,5},{5,1},{9,13},{13,9},{2,6},{6,2},{1... | collective-permute-start | bytes 6291464 | tf_op jit(solution)/shard_map/ppermute | solution.py:370
  481.4 123.5 %collective-permute-start.10 = (bf16[1056,1024]{1,0:T(8,128)(2,1)}, bf16[1056,1024]{1,0:T(8,128)(2,1)}, u32[]{:S(2)}, u32[]{:S(2)}) collective-permute-start(bf16[1056,1024]{1,0:T(8,128)(2,1)} %pad_maximum_fusion.18), channel_id=1, source_target_pairs={{0,8},{4,12},{8,0},{12,4},{1,9},{5,13},{9,1},{13,5},{2,10},{6,14},... | collective-permute-start | bytes 6488072 | tf_op jit(solution)/shard_map/ppermute | solution.py:326
  540.7 71.7 %collective-permute-start.11 = (bf16[1056,1024]{1,0:T(8,128)(2,1)}, bf16[1056,1024]{1,0:T(8,128)(2,1)}, u32[]{:S(2)}, u32[]{:S(2)}) collective-permute-start(bf16[1056,1024]{1,0:T(8,128)(2,1)} %pad_maximum_fusion.19), channel_id=1, source_target_pairs={{0,8},{4,12},{8,0},{12,4},{1,9},{5,13},{9,1},{13,5},{2,10},{6,14},... | collective-permute-start | bytes 6488072 | tf_op jit(solution)/shard_map/ppermute | solution.py:326
  638.0 3.8 collective-permute-start.12
  641.3 7.3 collective-permute-start.14
  645.1 26.9 %collective-permute-start.13 = (bf16[256,2048]{1,0:T(8,128)(2,1)S(1)}, bf16[256,2048]{1,0:T(8,128)(2,1)S(1)}, u32[]{:S(2)}, u32[]{:S(2)}) collective-permute-start(bf16[256,2048]{1,0:T(8,128)(2,1)S(1)} %fusion.104), channel_id=1, source_target_pairs={{0,16},{1,17},{2,18},{3,19},{4,20},{5,21},{6,22},{7,23},{8,24},{9,... | collective-permute-start | bytes 3145736 | tf_op jit(solution)/shard_map/ppermute | solution.py:385
  651.8 41.7 %collective-permute-start.15 = (bf16[256,2048]{1,0:T(8,128)(2,1)S(1)}, bf16[256,2048]{1,0:T(8,128)(2,1)S(1)}, u32[]{:S(2)}, u32[]{:S(2)}) collective-permute-start(bf16[256,2048]{1,0:T(8,128)(2,1)S(1)} %fusion.103), channel_id=1, source_target_pairs={{0,16},{1,17},{2,18},{3,19},{4,20},{5,21},{6,22},{7,23},{8,24},{9,... | collective-permute-start | bytes 3145736 | tf_op jit(solution)/shard_map/ppermute | solution.py:385
  700.6 4.3 collective-permute-start.16
  772.2 4.2 collective-permute-start.17
  781.4 4.3 collective-permute-start.19
  781.6 38.1 %collective-permute-start.18 = (bf16[512,2048]{1,0:T(8,128)(2,1)S(1)}, bf16[512,2048]{1,0:T(8,128)(2,1)}, u32[]{:S(2)}, u32[]{:S(2)}) collective-permute-start(bf16[512,2048]{1,0:T(8,128)(2,1)S(1)} %bitcast.176), channel_id=1, source_target_pairs={{0,4},{4,0},{8,12},{12,8},{1,5},{5,1},{9,13},{13,9},{2,6},{6,2},{1... | collective-permute-start | bytes 6291464 | tf_op jit(solution)/shard_map/ppermute | solution.py:370
  863.6 17.4 collective-permute-start.20
  863.8 127.6 %collective-permute-start.22 = (bf16[1024,2816]{1,0:T(8,128)(2,1)}, bf16[1024,2816]{1,0:T(8,128)(2,1)}, u32[]{:S(2)}, u32[]{:S(2)}) collective-permute-start(bf16[1024,2816]{1,0:T(8,128)(2,1)} %get-tuple-element.170), channel_id=1, source_target_pairs={{0,8},{4,12},{8,0},{12,4},{1,9},{5,13},{9,1},{13,5},{2,10},{6,14},... | collective-permute-start | bytes 17301512 | tf_op jit(solution)/shard_map/ppermute | solution.py:417
  874.9 33.8 %collective-permute-start.28 = (bf16[256,2048]{1,0:T(8,128)(2,1)}, bf16[256,2048]{1,0:T(8,128)(2,1)}, u32[]{:S(2)}, u32[]{:S(2)}) collective-permute-start(bf16[256,2048]{1,0:T(8,128)(2,1)} %convolution_convert_fusion.8), channel_id=1, source_target_pairs={{0,4},{4,0},{8,12},{12,8},{1,5},{5,1},{9,13},{13,9},{2,6},{6,2},{1... | collective-permute-start | bytes 3145736 | tf_op jit(solution)/shard_map/ppermute | solution.py:376
  880.5 36.5 %collective-permute-start.27 = (bf16[256,2048]{1,0:T(8,128)(2,1)}, bf16[256,2048]{1,0:T(8,128)(2,1)}, u32[]{:S(2)}, u32[]{:S(2)}) collective-permute-start(bf16[256,2048]{1,0:T(8,128)(2,1)} %convolution_convert_fusion.9), channel_id=1, source_target_pairs={{0,4},{4,0},{8,12},{12,8},{1,5},{5,1},{9,13},{13,9},{2,6},{6,2},{1... | collective-permute-start | bytes 3145736 | tf_op jit(solution)/shard_map/ppermute | solution.py:376
  908.6 14.2 collective-permute-start.21
  1004.1 13.5 collective-permute-start.25
  1017.5 14.3 collective-permute-start.23
  1052.6 30.8 %collective-permute-start.26 = (bf16[256,2048]{1,0:T(8,128)(2,1)S(1)}, bf16[256,2048]{1,0:T(8,128)(2,1)S(1)}, u32[]{:S(2)}, u32[]{:S(2)}) collective-permute-start(bf16[256,2048]{1,0:T(8,128)(2,1)S(1)} %get-tuple-element.176), channel_id=1, source_target_pairs={{16,0},{17,1},{18,2},{19,3},{20,4},{21,5},{22,6},{23,7},{24,8},{25... | collective-permute-start | bytes 3145736 | tf_op jit(solution)/shard_map/ppermute | solution.py:385
  1053.9 51.8 %collective-permute-start.24 = (bf16[256,2048]{1,0:T(8,128)(2,1)S(1)}, bf16[256,2048]{1,0:T(8,128)(2,1)S(1)}, u32[]{:S(2)}, u32[]{:S(2)}) collective-permute-start(bf16[256,2048]{1,0:T(8,128)(2,1)S(1)} %get-tuple-element.175), channel_id=1, source_target_pairs={{16,0},{17,1},{18,2},{19,3},{20,4},{21,5},{22,6},{23,7},{24,8},{25... | collective-permute-start | bytes 3145736 | tf_op jit(solution)/shard_map/ppermute | solution.py:385
  1106.4 4.4 collective-permute-start.30
  1110.5 35.7 %collective-permute-start.29 = (bf16[512,1024]{1,0:T(8,128)(2,1)}, bf16[512,1024]{1,0:T(8,128)(2,1)}, u32[]{:S(2)}, u32[]{:S(2)}) collective-permute-start(bf16[512,1024]{1,0:T(8,128)(2,1)} %get-tuple-element.211), channel_id=1, source_target_pairs={{0,8},{4,12},{8,0},{12,4},{1,9},{5,13},{9,1},{13,5},{2,10},{6,14},... | collective-permute-start | bytes 3145736 | tf_op jit(solution)/shard_map/ppermute | solution.py:417
  1110.8 43.3 %collective-permute-start.32 = (bf16[512,1024]{1,0:T(8,128)(2,1)S(1)}, bf16[512,1024]{1,0:T(8,128)(2,1)}, u32[]{:S(2)}, u32[]{:S(2)}) collective-permute-start(bf16[512,1024]{1,0:T(8,128)(2,1)S(1)} %get-tuple-element.210), channel_id=1, source_target_pairs={{0,4},{4,0},{8,12},{12,8},{1,5},{5,1},{9,13},{13,9},{2,6},{6,2},{1... | collective-permute-start | bytes 3145736 | tf_op jit(solution)/shard_map/ppermute | solution.py:370
  1146.2 7.9 collective-permute-start.33
  1172.4 534.1 %reduce-scatter.13.cloned.1.call-start = ((), (), s32[]{:S(2)}) async-start(), calls=%async_computation.17 | async-start | bytes 7208960 | tf_op jit(solution)/shard_map/reduce_scatter | solution.py:420
  1172.4 127.2 %collective-permute-start.31 = (bf16[2816,1024]{1,0:T(8,128)(2,1)}, bf16[2816,1024]{1,0:T(8,128)(2,1)}, u32[]{:S(2)}, u32[]{:S(2)}) collective-permute-start(bf16[2816,1024]{1,0:T(8,128)(2,1)} %convolution_convert_fusion.1), channel_id=1, source_target_pairs={{0,8},{4,12},{8,0},{12,4},{1,9},{5,13},{9,1},{13,5},{2,10},{6,14},... | collective-permute-start | bytes 17301512 | tf_op jit(solution)/shard_map/ppermute | solution.py:417
  1193.4 13.3 collective-permute-start.34
  1311.8 402.2 %reduce-scatter.15.cloned.1.call-start = ((), (), s32[]{:S(2)}) async-start(), calls=%async_computation.18 | async-start | bytes 7208960 | tf_op jit(solution)/shard_map/reduce_scatter | solution.py:420
  1323.2 4.2 collective-permute-start.36
  1323.2 64.9 %collective-permute-start.35 = (bf16[1408,1024]{1,0:T(8,128)(2,1)S(1)}, bf16[1408,1024]{1,0:T(8,128)(2,1)S(1)}, u32[]{:S(2)}, u32[]{:S(2)}) collective-permute-start(bf16[1408,1024]{1,0:T(8,128)(2,1)S(1)} %copy-done.74), channel_id=1, source_target_pairs={{0,8},{4,12},{8,0},{12,4},{1,9},{5,13},{9,1},{13,5},{2,10},{6,14},... | collective-permute-start | bytes 8650760 | tf_op jit(solution)/shard_map/ppermute | solution.py:417
  1388.1 71.0 %collective-permute-start.37 = (bf16[1408,1024]{1,0:T(8,128)(2,1)}, bf16[1408,1024]{1,0:T(8,128)(2,1)}, u32[]{:S(2)}, u32[]{:S(2)}) collective-permute-start(bf16[1408,1024]{1,0:T(8,128)(2,1)} %convolution_convert_fusion.4), channel_id=1, source_target_pairs={{0,8},{4,12},{8,0},{12,4},{1,9},{5,13},{9,1},{13,5},{2,10},{6,14},... | collective-permute-start | bytes 8650760 | tf_op jit(solution)/shard_map/ppermute | solution.py:417
  1474.5 242.5 %reduce-scatter.11.cloned.1.call-start = ((), (), s32[]{:S(2)}) async-start(), calls=%async_computation.16 | async-start | bytes 2621440 | tf_op jit(solution)/shard_map/reduce_scatter | solution.py:420
  1474.6 47.4 %collective-permute-start.38 = (bf16[1024,1024]{1,0:T(8,128)(2,1)}, bf16[1024,1024]{1,0:T(8,128)(2,1)S(1)}, u32[]{:S(2)}, u32[]{:S(2)}) collective-permute-start(bf16[1024,1024]{1,0:T(8,128)(2,1)} %fusion.107), channel_id=1, source_target_pairs={{0,8},{4,12},{8,0},{12,4},{1,9},{5,13},{9,1},{13,5},{2,10},{6,14},... | collective-permute-start | bytes 6291464 | tf_op jit(solution)/shard_map/ppermute | solution.py:417
  1535.6 14.2 collective-permute-start.40
  1541.8 179.8 %reduce-scatter.7.cloned.1.call-start = ((), (), s32[]{:S(2)}) async-start(), calls=%async_computation.14 | async-start | bytes 3932160 | tf_op jit(solution)/shard_map/reduce_scatter | solution.py:420
  1542.1 70.6 %collective-permute-start.39 = (bf16[1536,1024]{1,0:T(8,128)(2,1)}, bf16[1536,1024]{1,0:T(8,128)(2,1)S(1)}, u32[]{:S(2)}, u32[]{:S(2)}) collective-permute-start(bf16[1536,1024]{1,0:T(8,128)(2,1)} %convolution_convert_fusion.3), channel_id=1, source_target_pairs={{0,8},{4,12},{8,0},{12,4},{1,9},{5,13},{9,1},{13,5},{2,10},{6,14},... | collective-permute-start | bytes 9437192 | tf_op jit(solution)/shard_map/ppermute | solution.py:417
  1619.0 166.5 %reduce-scatter.9.cloned.1.call-start = ((), (), s32[]{:S(2)}) async-start(), calls=%async_computation.15 | async-start | bytes 3932160 | tf_op jit(solution)/shard_map/reduce_scatter | solution.py:420
  1619.0 69.9 %collective-permute-start.41 = (bf16[1536,1024]{1,0:T(8,128)(2,1)}, bf16[1536,1024]{1,0:T(8,128)(2,1)S(1)}, u32[]{:S(2)}, u32[]{:S(2)}) collective-permute-start(bf16[1536,1024]{1,0:T(8,128)(2,1)} %convolution_convert_fusion.2), channel_id=1, source_target_pairs={{0,8},{4,12},{8,0},{12,4},{1,9},{5,13},{9,1},{13,5},{2,10},{6,14},... | collective-permute-start | bytes 9437192 | tf_op jit(solution)/shard_map/ppermute | solution.py:417
  1695.2 100.1 %all-to-all-start.1 = ((bf16[16,32,2048]{2,1,0:T(8,128)(2,1)}), bf16[16,32,2048]{2,1,0:T(8,128)(2,1)S(1)}, u32[]{:S(2)}, u32[]{:S(2)}) async-start(bf16[16,32,2048]{2,1,0:T(8,128)(2,1)} %bitcast.57), calls=%async_computation.1 | async-start | bytes 4194304 | tf_op jit(solution)/shard_map/all_to_all | solution.py:522
  1701.5 9.1 collective-permute-start.46
  1709.1 9.1 collective-permute-start.44
  1716.6 74.0 %collective-permute-start.45 = (bf16[704,512]{1,0:T(8,128)(2,1)}, bf16[704,512]{1,0:T(8,128)(2,1)}, u32[]{:S(2)}, u32[]{:S(2)}) collective-permute-start(bf16[704,512]{1,0:T(8,128)(2,1)} %get-tuple-element.224), channel_id=1, source_target_pairs={{0,4},{4,0},{8,12},{12,8},{1,5},{5,1},{9,13},{13,9},{2,6},{6,2},{1... | collective-permute-start | bytes 2162696 | tf_op jit(solution)/shard_map/ppermute | solution.py:547
  1718.0 2.4 collective-permute-start.43
  1790.6 32.8 %collective-permute-start.42 = (bf16[3,256,512]{1,2,0:T(8,128)(2,1)}, bf16[3,256,512]{1,2,0:T(8,128)(2,1)}, u32[]{:S(2)}, u32[]{:S(2)}) collective-permute-start(bf16[3,256,512]{1,2,0:T(8,128)(2,1)} %copy.81), channel_id=1, source_target_pairs={{0,4},{4,0},{8,12},{12,8},{1,5},{5,1},{9,13},{13,9},{2,6},{6,2},{1... | collective-permute-start | bytes 2359304 | tf_op jit(solution)/shard_map/ppermute | solution.py:547
  1795.3 25.8 %all-to-all-start.2 = ((f32[16,7,128]{2,1,0:T(8,128)}), f32[16,7,128]{2,1,0:T(8,128)}, u32[]{:S(2)}, u32[]{:S(2)}) async-start(f32[16,7,128]{2,1,0:T(8,128)} %bitcast.235), calls=%async_computation.2 | async-start | bytes 131072 | tf_op jit(solution)/shard_map/all_to_all | solution.py:567
  (101 other events, 1782.6 us)
Sparse Core Ops, SparseCore 0:
  10.2 66.4 all-gather.17
  78.8 126.2 all-gather.7
  206.7 105.3 all-gather.9
  313.6 104.9 all-gather.11
  420.6 57.4 all-gather.13
  479.6 57.8 all-gather.15
  1172.5 100.0 reduce-scatter.16
  1311.9 99.8 reduce-scatter.12
  1474.6 98.8 reduce-scatter.14
  1575.6 44.3 reduce-scatter.10
  1622.5 59.5 reduce-scatter.6
  1695.3 90.1 reduce-scatter.8

commit v5 on v4

--- a/solution.py
+++ b/solution.py
@@ -384,7 +384,7 @@
     def over_x(parts, route):
         return jnp.concatenate([lax.ppermute(part, "section", route) for part in parts], axis=0)
 
-    def forward(stream):
+    def forward(stream, parts):
         normed = both(ln(stream, gain[0], shift[0]))
         mixed = dot_t(normed, wt_qkv)
         qkv, attended = attn_fwd(mixed, bias, context, tp_count, chunk)
@@ -395,7 +395,7 @@
         activation = (jax.nn.silu(gate) * up).astype(jnp.bfloat16)
         out = [
             (x + y).astype(jnp.bfloat16)
-            for x, y in zip(split(hidden_state, 2), summed(activation, wt_down, 2))
+            for x, y in zip(split(hidden_state, parts), summed(activation, wt_down, parts))
         ]
         return out, (stream, normed, qkv, attended, hidden_state, normed_two, gate_up, activation)
 
@@ -453,92 +453,8 @@
         hidden_grad = grad_out.astype(jnp.float32) + ln_back(hidden_state, two_grad, gain[1])[0]
         ctx_grad = dot_t(both(hidden_grad.astype(jnp.bfloat16)), wt_out).astype(jnp.bfloat16)
         qkv_grad, _ = attn_bwd(qkv, ctx_grad, context, tp_count, chunk)
-        one_grad = summed(after(qkv_grad, wait), wt_qkv, 2)
-        return [
-            (z + ln_back(x, y, gain[0])[0]).astype(jnp.bfloat16)
-            for x, y, z in zip(split(stream, 2), one_grad, split(hidden_grad, 2))
-        ]
-
-    def last_backward(grad_out, stored, final_out, act_both):
-        stream, normed, qkv, attended, hidden_state, normed_two, gate_up, _ = stored
-        grad_f32 = grad_out.astype(jnp.float32)
-        far_grad, near_grad = far_near(grad_out)
-        grad_across = across(far_grad)
-        mlp_grad = both(grad_out)
-        gate_grad, up_grad = mlp_back(dot_t(mlp_grad, wt_down), gate_up)
-        far_gate = far_term(gate_grad, normed_two)
-
-        grad_across, far_gate, gate_grad, up_grad = together((grad_across, far_gate, gate_grad, up_grad))
-        arriving_gate = across(far_gate)
-        grad_both = jnp.concatenate([both(near_grad), both(grad_across)], axis=0)
-        down_total = dot_0(act_both, grad_both).astype(jnp.bfloat16)
-        down_total, gate_other, up_other = together((down_total, gate_grad[own_rows:], up_grad[own_rows:]))
-        sum_down = over_tp(down_total)
-        arriving = from_core(two_dot(gate_other, up_other))
-        two_grad = two_dot(gate_grad[:own_rows], up_grad[:own_rows]) + arriving
-        far_up_a, far_up_b = (far_term(x, normed_two) for x in jnp.split(up_grad, 2, axis=1))
-
-        arriving_gate, far_up_a, far_up_b, gate_grad, two_grad = together(
-            (arriving_gate, far_up_a, far_up_b, gate_grad, two_grad)
-        )
-        arriving = across(far_up_a)
-        gate_total = near_total(gate_grad, normed_two, arriving_gate)
-        gate_total, two_grad = together((gate_total, two_grad))
-        sum_gate = over_tp(gate_total)
-        result, gain_two, shift_two = ln_back(hidden_state, two_grad, gain[1])
-        hidden_grad = grad_f32 + result
-        attn_grad = both(hidden_grad.astype(jnp.bfloat16))
-        ctx_grad = dot_t(attn_grad, wt_out).astype(jnp.bfloat16)
-
-        arriving, far_up_b, ctx_grad = together((arriving, far_up_b, ctx_grad))
-        arriving_up = jnp.concatenate([arriving, across(far_up_b)], axis=0)
-        qkv_grad, bias_grad = attn_bwd(qkv, ctx_grad, context, tp_count, chunk)
-        far_out = far_term(attended, attn_grad)
-
-        arriving_up, far_out, qkv_grad, up_grad, attn_grad = together(
-            (arriving_up, far_out, qkv_grad, up_grad, attn_grad)
-        )
-        arriving_out = across(far_out)
-        sum_up = over_tp(near_total(up_grad, normed_two, arriving_up))
-        qkv_a, qkv_b = (part_of(qkv_grad, i, 2, 1) for i in range(2))
-        far_a = far_term(qkv_a, normed)
-
-        arriving_out, far_a, qkv_a, qkv_b, qkv_grad, attn_grad = together(
-            (arriving_out, far_a, qkv_a, qkv_b, qkv_grad, attn_grad)
-        )
-        arriving = across(far_a)
-        sum_out = over_tp(near_total(attended, attn_grad, arriving_out))
-        one_grad = summed(qkv_grad, wt_qkv)[0]
-        far_b = far_term(qkv_b, normed)
-
-        arriving, far_b, one_grad, qkv_a, qkv_b = together((arriving, far_b, one_grad, qkv_a, qkv_b))
-        arriving_b = across(far_b)
-        sum_qkv_a = over_tp(near_total(qkv_a, normed, arriving))
-        result, gain_one, shift_one = ln_back(stream, one_grad, gain[0])
-        input_grad = (hidden_grad + result).astype(jnp.bfloat16)
-        ends = jnp.where(first, input_grad, final_out)
-
-        arriving_b, ends, qkv_b = together((arriving_b, ends, qkv_b))
-        ends = lax.all_to_all(
-            ends.reshape(ctx_count * tp_count, piece, width), ("ctx", "tp"), 0, 0, tiled=True
-        )
-        sum_qkv_b = over_tp(near_total(qkv_b, normed, arriving_b))
-        small = (jnp.stack([gain_one, gain_two]), jnp.stack([shift_one, shift_two]), bias_grad)
-        sum_qkv = jnp.concatenate([sum_qkv_a, sum_qkv_b], axis=0)
-
-        return ends, small, (sum_down, sum_gate, sum_up, sum_out, sum_qkv)
-
-    sent, _ = forward(inbound.astype(jnp.float32))
-    arriving = over_x(sent, [(0, 1)])
-    final_out, stored = forward(jnp.where(first, inbound, arriving).astype(jnp.float32))
-    act_across = across(stored[7])
-    arriving_back = over_x(backward(inbound, stored, act_across), [(1, 0)])
-    arriving_back, final_out, act_both = together(
-        (arriving_back, jnp.concatenate(final_out, axis=0), jnp.concatenate([stored[7], act_across], axis=0))
-    )
-    grad_out = jnp.where(first, arriving_back, inbound)
-    ends, small, sums = last_backward(grad_out, stored, final_out, act_both)
-    down_sum, gate_sum, up_sum, out_sum, qkv_sum = sums
+        one_grad = summed(after(qkv_grad, wait), wt_qkv)[0]
+        return (hidden_grad + ln_back(stream, one_grad, gain[0])[0]).astype(jnp.bfloat16)
 
     def settled(term):
         share = half_width // 2
@@ -550,21 +466,102 @@
             core == 0, jnp.concatenate([kept, got], axis), jnp.concatenate([got, kept], axis)
         ).astype(jnp.float32)
 
-    grad_down = settled(down_sum)
-    grad_gate = settled(gate_sum)
-    grad_up = settled(up_sum)
-    grad_out_w = settled(out_sum)
-    grad_qkv = settled(qkv_sum.reshape(3, columns, half_width))
-
-    gain_terms, shift_terms, bias_terms = small
-    bias_terms = bias_terms.reshape(tp_count, 3, columns).transpose(1, 0, 2)[:, :, None]
-    bias_full = jnp.where(
-        (jnp.arange(2) == core)[None, None, :, None], bias_terms, 0.0
-    ).reshape(3, tp_count * 2 * columns)
-    vectors = jnp.concatenate([gain_terms, shift_terms, bias_full], axis=0)
-    share = width // (ctx_count * tp_count)
-    vectors = after(vectors, ends).reshape(-1, ctx_count * tp_count, share).transpose(1, 0, 2)
-    vectors = jnp.sum(lax.all_to_all(vectors, ("ctx", "tp"), 0, 0, tiled=True), axis=0).reshape(-1, share)
+    def vector_sums(small):
+        gain_terms, shift_terms, bias_terms = small
+        bias_terms = bias_terms.reshape(tp_count, 3, columns).transpose(1, 0, 2)[:, :, None]
+        bias_full = jnp.where(
+            (jnp.arange(2) == core)[None, None, :, None], bias_terms, 0.0
+        ).reshape(3, tp_count * 2 * columns)
+        vectors = jnp.concatenate([gain_terms, shift_terms, bias_full], axis=0)
+        share = width // (ctx_count * tp_count)
+        vectors = vectors.reshape(-1, ctx_count * tp_count, share).transpose(1, 0, 2)
+        return jnp.sum(lax.all_to_all(vectors, ("ctx", "tp"), 0, 0, tiled=True), axis=0).reshape(-1, share)
+
+    def last_backward(grad_out, stored, final_out, act_both):
+        stream, normed, qkv, attended, hidden_state, normed_two, gate_up, _ = stored
+        grad_f32 = grad_out.astype(jnp.float32)
+        far_grad, near_grad = far_near(grad_out)
+        grad_across = across(far_grad)
+        mlp_grad = both(grad_out)
+        gate_grad, up_grad = mlp_back(dot_t(mlp_grad, wt_down), gate_up)
+        far_gate = far_term(gate_grad, normed_two)
+
+        grad_across, far_gate, gate_grad, up_grad = together((grad_across, far_gate, gate_grad, up_grad))
+        far_gate_a, far_gate_b = split(far_gate, 2)
+        arriving = across(far_gate_a)
+        gu_grad = jnp.concatenate([gate_grad, up_grad], axis=1)
+        grad_both = jnp.concatenate([both(near_grad), both(grad_across)], axis=0)
+        down_total = dot_0(act_both, grad_both).astype(jnp.bfloat16)
+        two_other = dot_n(gu_grad[own_rows:], wt_gu).astype(jnp.bfloat16)
+
+        arriving, far_gate_b, two_other, gu_grad, down_total, gate_grad, up_grad = together(
+            (arriving, far_gate_b, two_other, gu_grad, down_total, gate_grad, up_grad)
+        )
+        arriving_gate = jnp.concatenate([arriving, across(far_gate_b)], axis=0)
+        sum_down = over_tp(down_total)
+        two_grad = dot_n(gu_grad[:own_rows], wt_gu) + lax.ppermute(two_other, "ctx", core_route).astype(jnp.float32)
+        result, gain_two, shift_two = ln_back(hidden_state, two_grad, gain[1])
+        hidden_grad = grad_f32 + result
+        attn_grad = both(hidden_grad.astype(jnp.bfloat16))
+        far_up_a, far_up_b = (far_term(x, normed_two) for x in jnp.split(up_grad, 2, axis=1))
+
+        arriving_gate, far_up_a, far_up_b, gate_grad, attn_grad, hidden_grad = together(
+            (arriving_gate, far_up_a, far_up_b, gate_grad, attn_grad, hidden_grad)
+        )
+        arriving = across(far_up_a)
+        sum_gate = over_tp(near_total(gate_grad, normed_two, arriving_gate))
+        far_up_b = jnp.concatenate([far_up_b, far_term(attended, attn_grad)], axis=0)
+        ctx_grad = dot_t(attn_grad, wt_out).astype(jnp.bfloat16)
+
+        arriving, far_up_b, ctx_grad = together((arriving, far_up_b, ctx_grad))
+        arriving_b = across(far_up_b)
+        arriving_up = jnp.concatenate([arriving, arriving_b[: ff // 2]], axis=0)
+        arriving_out = arriving_b[ff // 2 :]
+        qkv_grad, bias_grad = attn_bwd(qkv, ctx_grad, context, tp_count, chunk)
+        qkv_a, qkv_b = (part_of(qkv_grad, i, 2, 1) for i in range(2))
+        far_a, far_b = far_term(qkv_a, normed), far_term(qkv_b, normed)
+
+        arriving_up, arriving_out, far_a, far_b, qkv_a, qkv_b, qkv_grad, up_grad, attn_grad = together(
+            (arriving_up, arriving_out, far_a, far_b, qkv_a, qkv_b, qkv_grad, up_grad, attn_grad)
+        )
+        arriving = across(far_a)
+        sum_up = over_tp(near_total(up_grad, normed_two, arriving_up))
+        out_total = near_total(attended, attn_grad, arriving_out)
+        one_other = dot_n(qkv_grad[own_rows:], wt_qkv).astype(jnp.bfloat16)
+
+        arriving, far_b, one_other, qkv_grad, qkv_a, qkv_b, out_total = together(
+            (arriving, far_b, one_other, qkv_grad, qkv_a, qkv_b, out_total)
+        )
+        arriving_b = across(far_b)
+        sum_out = over_tp(out_total)
+        sum_qkv_a = over_tp(near_total(qkv_a, normed, arriving))
+        one_grad = dot_n(qkv_grad[:own_rows], wt_qkv) + lax.ppermute(one_other, "ctx", core_route).astype(jnp.float32)
+        result, gain_one, shift_one = ln_back(stream, one_grad, gain[0])
+        input_grad = (hidden_grad + result).astype(jnp.bfloat16)
+        ends = jnp.where(first, input_grad, final_out)
+        small = vector_sums((jnp.stack([gain_one, gain_two]), jnp.stack([shift_one, shift_two]), bias_grad))
+        done = (settled(sum_down), jnp.stack([settled(sum_gate).T, settled(sum_up).T]))
+
+        arriving_b, ends, qkv_b, small, done = together((arriving_b, ends, qkv_b, small, done))
+        ends = lax.all_to_all(
+            ends.reshape(ctx_count * tp_count, piece, width), ("ctx", "tp"), 0, 0, tiled=True
+        )
+        sum_qkv_b = over_tp(near_total(qkv_b, normed, arriving_b))
+        sum_qkv = jnp.concatenate([sum_qkv_a, sum_qkv_b], axis=0)
+        grads = (*done, settled(sum_out), settled(sum_qkv.reshape(3, columns, half_width)))
+        return ends, small, grads
+
+    sent, _ = forward(inbound.astype(jnp.float32), 2)
+    arriving = over_x(sent, [(0, 1)])
+    final_out, stored = forward(jnp.where(first, inbound, arriving).astype(jnp.float32), 1)
+    act_across = across(stored[7])
+    arriving_back = over_x([backward(inbound, stored, act_across)], [(1, 0)])
+    arriving_back, final_out, act_both = together(
+        (arriving_back, final_out[0], jnp.concatenate([stored[7], act_across], axis=0))
+    )
+    grad_out = jnp.where(first, arriving_back, inbound)
+    ends, vectors, grads = last_backward(grad_out, stored, final_out, act_both)
+    grad_down, grad_gu, grad_out_w, grad_qkv = grads
 
     ends = ends.reshape(ctx_count // 2, 2, tp_count, piece, width).transpose(0, 2, 1, 3, 4)
     ends = ends.reshape(micro_count, slice_len, 1, width)
@@ -575,7 +572,7 @@
         vectors[None, 4:],
         grad_qkv.transpose(0, 2, 1)[None],
         grad_out_w[None],
-        jnp.stack([grad_gate.T, grad_up.T])[None],
+        grad_gu[None],
         grad_down[None],
     )
 

time: 1840 us -> 1810 us (0.984)
  matrix products: 509 us -> 478 us
  waiting for transfers between devices: 720 us -> 747 us
    reduce_scatter x6, waiting for transfers between devices: 63.8 us -> 139 us  [over_tp(): return lax.psum_scatter(term, 'tp', scatter_dimension=0, tiled=True)]
    ppermute x8, waiting for transfers between devices: 260 us -> 189 us  [across(): lax.ppermute(after(term, *others) if others else term, 'ctx', across_route)]
    dot_general x22 -> x18, matrix products: 234 us -> 207 us  [dot_n(): lax.dot_general(a, b, (((1,), (0,)), ((), ())), preferred_element_type=jn...]
    all_to_all x1, waiting for transfers between devices: 0.01 us -> 20.4 us  [vector_sums(): lax.all_to_all(vectors, ('ctx', 'tp'), 0, 0, tiled=True)]
    ppermute x4 -> x3, waiting for transfers between devices: 78 us -> 69.2 us  [over_x(): lax.ppermute(part, 'section', route)]
  transfers between devices with their start and end apart: 62 -> 59, of which waited for: 26 -> 31; matrix products, arithmetic and copies ran while one was open for 35% -> 35% of each run, Pallas kernels for 9% -> 9%
where the time goes in v5:
time: 1810 us; the launch traced here: 1800 us
  waiting for transfers between devices  747 us (41%)
  matrix products  478 us (26%)
  Pallas kernels  203 us (11%)
  other arithmetic  180 us (10%)
  local copies, waits for them, and re-layouts  121 us (7%)
  starting transfers between devices  44 us (2%)
  between operations  31.4 us (2%)
    all_gather x6, waiting for transfers between devices, gathered(): own = lax.all_gather(block, 'tp', axis=0, tiled=True)  255 us
    dot_general x18, matrix products, dot_n(): lax.dot_general(a, b, (((1,), (0,)), ((), ())), preferred_element_type=jn...  207 us
    ppermute x8, waiting for transfers between devices, across(): lax.ppermute(after(term, *others) if others else term, 'ctx', across_route)  189 us
    dot_general x8, matrix products, dot_t(): lax.dot_general(a, b, (((1,), (1,)), ((), ())), preferred_element_type=jn...  177 us
    reduce_scatter x6, waiting for transfers between devices, over_tp(): return lax.psum_scatter(term, 'tp', scatter_dimension=0, tiled=True)  139 us
    pallas_call x2, Pallas kernels, attn_bwd(): pl.pallas_call(functools.partial(attn_bwd_kernel, heads, chunk), grid=(gr...  125 us
    dot_general x12, matrix products, dot_0(): lax.dot_general(a, b, (((0,), (0,)), ((), ())), preferred_element_type=jn...  93.5 us
    pallas_call x2, Pallas kernels, attn_fwd(): pl.pallas_call(functools.partial(attn_fwd_kernel, heads, chunk), grid=(gr...  77.5 us
  transfers between devices with their start and end apart: 59, of which 31 were waited for; matrix products, arithmetic and copies ran while one was open for 35% of the time, Pallas kernels for 9%

profile of v5, /device:TPU:0, one launch (start us, length us, event | category | flops | bytes accessed | tf_op | source)
XLA Modules:
  0.0 1803.8 jit_solution(17504081864390912853)
XLA Ops:
  40.5 7.4 all-to-all-start
  48.0 28.6 %all-gather.18.cloned.1.call-done = bf16[1,1024,1024]{2,1,0:T(8,128)(2,1)} async-done(((bf16[1,256,1024]{2,1,0:T(8,128)(2,1)}), bf16[1,1024,1024]{2,1,0:T(8,128)(2,1)}) %all-gather.18.cloned.1.call-update) | async-done | bytes 2097168 | tf_op jit(solution)/shard_map/all_gather | solution.py:321
  80.9 9.6 constant_dynamic-slice_fusion.25
  93.1 42.5 %all-to-all-done = bf16[16,32,2048]{2,1,0:T(8,128)(2,1)S(1)} async-done(((bf16[16,32,2048]{2,1,0:T(8,128)(2,1)}), bf16[16,32,2048]{2,1,0:T(8,128)(2,1)S(1)}, u32[]{:S(2)}, u32[]{:S(2)}) %all-to-all-start) | async-done | bytes 2097184 | tf_op jit(solution)/shard_map/all_to_all | solution.py:287
  138.3 66.8 %all-gather.8.cloned.1.call-done = bf16[3072,1024]{1,0:T(8,128)(2,1)} async-done(((bf16[768,1024]{1,0:T(8,128)(2,1)}), bf16[3072,1024]{1,0:T(8,128)(2,1)}) %all-gather.8.cloned.1.call-update) | async-done | bytes 6291472 | tf_op jit(solution)/shard_map/all_gather | solution.py:321
  243.5 68.6 %all-gather.10.cloned.1.call-done = bf16[2816,1024]{1,0:T(8,128)(2,1)} async-done(((bf16[704,1024]{1,0:T(8,128)(2,1)}), bf16[2816,1024]{1,0:T(8,128)(2,1)}) %all-gather.10.cloned.1.call-update) | async-done | bytes 5767184 | tf_op jit(solution)/shard_map/all_gather | solution.py:321
  319.5 11.4 fusion.3
  331.0 21.9 %fusion.49.mixed = f32[1024,3072]{1,0:T(8,128)} fusion(bf16[512,2048]{1,0:T(8,128)(2,1)} %collective-permute-done, bf16[512,2048]{1,0:T(8,128)(2,1)} %fusion.48, bf16[3072,1024]{1,0:T(8,128)(2,1)} %fusion.3, bf16[3072,1024]{1,0:T(8,128)(2,1)} %all-gather.8.cloned.1.call-done, pred[]{:T(512)S(6)} %eq.31), kind=kOutput, calls=%fused_computation.118 | convolution fusion | flops 12949913600 | bytes 29360128 | tf_op jit(solution)/shard_map/dot_general | solution.py:59
  352.9 38.8 %shard_map.170 = (bf16[1024,3072]{1,0:T(8,128)(2,1)}, bf16[1024,1024]{1,0:T(8,128)(2,1)}) custom-call(f32[1024,3072]{1,0:T(8,128)} %fusion.49.mixed, f32[4,1,768]{2,1,0:T(1,128)} %reshape.344.bias, f32[1024,128]{1,0:T(8,128)} %concatenate.264.cos_t, f32[1024,128]{1,0:T(8,128)} %concatenate.265.low_t, f32[1024,128]{1,0:T(8,128)} %concatenate.266.high_t, ...), custom_call_target="tpu_custom_call" | custom-call | flops 12884901888 | bytes 22020096 | tf_op jit(solution)/shard_map/pallas_call | solution.py:187
  391.7 6.3 convolution_convert_fusion.7
  402.5 9.9 fusion.191
  428.3 12.1 fusion.12
  440.4 7.0 maximum_select_fusion.1
  447.5 30.7 %all-gather.14.cloned.1.call-done = bf16[1408,1024]{1,0:T(8,128)(2,1)} async-done(((bf16[352,1024]{1,0:T(8,128)(2,1)}), bf16[1408,1024]{1,0:T(8,128)(2,1)}) %all-gather.14.cloned.1.call-update) | async-done | bytes 2883600 | tf_op jit(solution)/shard_map/all_gather | solution.py:321
  482.8 54.6 %all-gather.16.cloned.1.call-done = bf16[1408,1024]{1,0:T(8,128)(2,1)} async-done(((bf16[352,1024]{1,0:T(8,128)(2,1)}), bf16[1408,1024]{1,0:T(8,128)(2,1)}) %all-gather.16.cloned.1.call-update) | async-done | bytes 2883600 | tf_op jit(solution)/shard_map/all_gather | solution.py:321
  542.2 11.9 fusion.9
  554.1 7.1 maximum_select_fusion.2
  561.2 34.2 %fusion.53 = f32[1024,5632]{1,0:T(8,128)} fusion(bf16[512,2048]{1,0:T(8,128)(2,1)} %collective-permute-done.7, bf16[512,2048]{1,0:T(8,128)(2,1)} %add_convert_fusion.7, bf16[2816,2048]{1,0:T(8,128)(2,1)} %maximum_select_fusion.2, bf16[2816,2048]{1,0:T(8,128)(2,1)} %maximum_select_fusion.1), kind=kOutput, calls=%fused_computation.127 | convolution fusion | flops 23676846080 | bytes 50331648 | tf_op jit(solution)/shard_map/dot_general | solution.py:59
  595.4 9.4 fusion
  604.8 7.6 collective-permute-done.11
  612.5 8.2 fusion.104
  625.9 9.0 pad_maximum_fusion.1
  653.2 18.8 %collective-permute-done.13 = bf16[256,2048]{1,0:T(8,128)(2,1)S(1)} collective-permute-done((bf16[256,2048]{1,0:T(8,128)(2,1)S(1)}, bf16[256,2048]{1,0:T(8,128)(2,1)S(1)}, u32[]{:S(2)}, u32[]{:S(2)}) %collective-permute-start.13) | collective-permute-done | bytes 1048608 | tf_op jit(solution)/shard_map/ppermute | solution.py:385
  672.1 21.5 %collective-permute-done.15 = bf16[256,2048]{1,0:T(8,128)(2,1)S(1)} collective-permute-done((bf16[256,2048]{1,0:T(8,128)(2,1)S(1)}, bf16[256,2048]{1,0:T(8,128)(2,1)S(1)}, u32[]{:S(2)}, u32[]{:S(2)}) %collective-permute-start.15) | collective-permute-done | bytes 1048608 | tf_op jit(solution)/shard_map/ppermute | solution.py:385
  705.0 22.2 %fusion.44.mixed = f32[1024,3072]{1,0:T(8,128)} fusion(bf16[512,2048]{1,0:T(8,128)(2,1)} %collective-permute-done.16, bf16[512,2048]{1,0:T(8,128)(2,1)} %copy-done.37, bf16[3072,1024]{1,0:T(8,128)(2,1)} %fusion.3, bf16[3072,1024]{1,0:T(8,128)(2,1)} %all-gather.8.cloned.1.call-done, pred[]{:T(512)S(6)} %eq.31), kind=kOutput, calls=%fused_computation.113 | convolution fusion | flops 12949913600 | bytes 29360128 | tf_op jit(solution)/shard_map/dot_general | solution.py:59
  727.2 38.7 %shard_map.171 = (bf16[1024,3072]{1,0:T(8,128)(2,1)}, bf16[1024,1024]{1,0:T(8,128)(2,1)}) custom-call(f32[1024,3072]{1,0:T(8,128)} %fusion.44.mixed, f32[4,1,768]{2,1,0:T(1,128)} %reshape.344.bias, f32[1024,128]{1,0:T(8,128)} %concatenate.264.cos_t, f32[1024,128]{1,0:T(8,128)} %concatenate.265.low_t, f32[1024,128]{1,0:T(8,128)} %concatenate.266.high_t, ...), custom_call_target="tpu_custom_call" | custom-call | flops 12884901888 | bytes 22020096 | tf_op jit(solution)/shard_map/pallas_call | solution.py:187
  785.2 33.7 %fusion.43 = f32[1024,5632]{1,0:T(8,128)} fusion(bf16[512,2048]{1,0:T(8,128)(2,1)} %collective-permute-done.19, bf16[512,2048]{1,0:T(8,128)(2,1)} %copy-done.16, bf16[2816,2048]{1,0:T(8,128)(2,1)} %maximum_select_fusion.2, bf16[2816,2048]{1,0:T(8,128)(2,1)} %maximum_select_fusion.1), kind=kOutput, calls=%fused_computation.112 | convolution fusion | flops 23676846080 | bytes 50331648 | tf_op jit(solution)/shard_map/dot_general | solution.py:59
  818.9 26.8 %multiply_convert_fusion.4 = (bf16[1024,2816]{1,0:T(8,128)(2,1)}, bf16[1024,2816]{1,0:T(8,128)(2,1)}, bf16[1024,2816]{1,0:T(8,128)(2,1)}) fusion(f32[1024,5632]{1,0:T(8,128)} %fusion.43, bf16[2816,2048]{1,0:T(8,128)(2,1)} %bitcast.183, bf16[512,2048]{1,0:T(8,128)(2,1)} %collective-permute-done.18, bf16[512,2048]{1,0:T(8,128)(2,1)S(1)} %bitcast.171), kind=kOutput, calls=%fused_computation.28 | convolution fusion | flops 11865686016 | bytes 56098816 | tf_op jit(solution)/shard_map/dot_general | solution.py:59
  845.7 17.1 fusion.98
  867.2 21.8 %fusion.181 = (f32[512]{0:T(512)S(1)}, f32[512]{0:T(512)S(1)}, f32[512,2048]{1,0:T(8,128)}) fusion(f32[512]{0:T(512)S(1)} %add_rsqrt_fusion.2, f32[512,2048]{1,0:T(8,128)} %copy-done.2, f32[512]{0:T(512)S(1)} %broadcast_multiply_fusion.10, f32[2048]{0:T(1024)S(1)} %bitcast.223, bf16[512,2048]{1,0:T(8,128)(2,1)} %collective-permute-done.20, ...), kind=kOutput, calls=%fused_computation.360 | convolution fusion | flops 11877220352 | bytes 45105152 | tf_op jit(solution)/shard_map/dot_general | solution.py:67
  903.5 62.7 %shard_map.172 = (bf16[1024,3072]{1,0:T(8,128)(2,1)}, f32[4,1,768]{2,1,0:T(1,128)}) custom-call(bf16[1024,3072]{1,0:T(8,128)(2,1)} %get-tuple-element.70.qkv, bf16[1024,1024]{1,0:T(8,128)(2,1)} %fusion.132.ctx, f32[1024,128]{1,0:T(8,128)} %concatenate.264.cos_t, f32[1024,128]{1,0:T(8,128)} %concatenate.265.low_t, f32[1024,128]{1,0:T(8,128)} %concatenate.266.high_t, ...), custom_call_target="tpu_custom_call" | custom-call | flops 3145728 | bytes 3145728 | tf_op jit(solution)/shard_map/pallas_call | solution.py:222
  966.2 23.7 %collective-permute-done.22 = bf16[1024,2816]{1,0:T(8,128)(2,1)} collective-permute-done((bf16[1024,2816]{1,0:T(8,128)(2,1)}, bf16[1024,2816]{1,0:T(8,128)(2,1)}, u32[]{:S(2)}, u32[]{:S(2)}) %collective-permute-start.22) | collective-permute-done | bytes 5767200 | tf_op jit(solution)/shard_map/ppermute | solution.py:417
  989.9 15.3 fusion.92
  1005.3 10.9 convolution_convert_fusion.8
  1016.6 16.4 fusion.180
  1035.9 11.6 add_convert_fusion.5
  1047.5 10.9 pad_maximum_fusion.2
  1058.5 28.9 %collective-permute-done.24 = bf16[512,2048]{1,0:T(8,128)(2,1)S(1)} collective-permute-done((bf16[512,2048]{1,0:T(8,128)(2,1)S(1)}, bf16[512,2048]{1,0:T(8,128)(2,1)S(1)}, u32[]{:S(2)}, u32[]{:S(2)}) %collective-permute-start.24) | collective-permute-done | bytes 2097184 | tf_op jit(solution)/shard_map/ppermute | solution.py:385
  1093.0 24.4 %multiply_convert_fusion = (bf16[1024,2816]{1,0:T(8,128)(2,1)}, bf16[1024,2816]{1,0:T(8,128)(2,1)}) fusion(f32[1024,5632]{1,0:T(8,128)} %fusion.43, bf16[2816,2048]{1,0:T(8,128)(2,1)} %bitcast.186, bf16[512,2048]{1,0:T(8,128)(2,1)} %collective-permute-done.27, bf16[512,2048]{1,0:T(8,128)(2,1)} %copy-done.6), kind=kOutput, calls=%fused_computation.24 | convolution fusion | flops 11857035264 | bytes 50331648 | tf_op jit(solution)/shard_map/dot_general | solution.py:59
  1117.4 9.1 convolution_convert_fusion.1
  1137.5 19.4 %fusion.99 = bf16[512,2048]{1,0:T(8,128)(2,1)} fusion(bf16[1024,5632]{1,0:T(8,128)(2,1)} %constant_dynamic-update-slice_fusion.3, bf16[2816,2048]{1,0:T(8,128)(2,1)} %maximum_select_fusion.2, bf16[2816,2048]{1,0:T(8,128)(2,1)} %maximum_select_fusion.1), kind=kOutput, calls=%fused_computation.186 | convolution fusion | flops 11858345984 | bytes 30932992 | tf_op jit(solution)/shard_map/dot_general | solution.py:67
  1156.9 17.3 convolution_convert_fusion
  1174.2 21.1 %collective-permute-done.28 = bf16[1408,1024]{1,0:T(8,128)(2,1)} collective-permute-done((bf16[1408,1024]{1,0:T(8,128)(2,1)}, bf16[1408,1024]{1,0:T(8,128)(2,1)}, u32[]{:S(2)}, u32[]{:S(2)}) %collective-permute-start.28) | collective-permute-done | bytes 2883616 | tf_op jit(solution)/shard_map/ppermute | solution.py:417
  1199.9 19.8 %multiply_reduce_fusion = (f32[2048]{0:T(1024)}, f32[512]{0:T(512)S(1)}, f32[512]{0:T(512)S(1)}, f32[2048]{0:T(1024)}, f32[512,2048]{1,0:T(8,128)S(1)}) fusion(f32[512]{0:T(512)S(1)} %copy-done.67, f32[512,2048]{1,0:T(8,128)} %copy-done.2, f32[512]{0:T(512)S(1)} %copy-done.57, f32[2048]{0:T(1024)S(1)} %bitcast.224, ...), kind=kOutput, calls=%fused_computation.151 | convolution fusion | flops 11868827648 | bytes 39354368 | tf_op jit(solution)/shard_map/dot_general | solution.py:67
  1223.2 6.5 convolution_convert_fusion.5
  1234.3 26.4 %collective-permute-done.31 = bf16[1408,1024]{1,0:T(8,128)(2,1)} collective-permute-done((bf16[1408,1024]{1,0:T(8,128)(2,1)}, bf16[1408,1024]{1,0:T(8,128)(2,1)}, u32[]{:S(2)}, u32[]{:S(2)}) %collective-permute-start.31) | collective-permute-done | bytes 2883616 | tf_op jit(solution)/shard_map/ppermute | solution.py:417
  1271.3 9.4 add_convert_fusion.1
  1289.2 8.1 convolution_convert_fusion.11.ctx
  1297.2 48.0 %collective-permute-done.34 = bf16[1408,1024]{1,0:T(8,128)(2,1)} collective-permute-done((bf16[1408,1024]{1,0:T(8,128)(2,1)}, bf16[1408,1024]{1,0:T(8,128)(2,1)}, u32[]{:S(2)}, u32[]{:S(2)}) %collective-permute-start.34) | collective-permute-done | bytes 2883616 | tf_op jit(solution)/shard_map/ppermute | solution.py:417
  1345.9 62.7 %shard_map.173 = (bf16[1024,3072]{1,0:T(8,128)(2,1)}, f32[4,1,768]{2,1,0:T(1,128)}) custom-call(bf16[1024,3072]{1,0:T(8,128)(2,1)} %get-tuple-element.70.qkv, bf16[1024,1024]{1,0:T(8,128)(2,1)} %convolution_convert_fusion.11.ctx, f32[1024,128]{1,0:T(8,128)} %concatenate.264.cos_t, f32[1024,128]{1,0:T(8,128)} %concatenate.265.low_t, ...), custom_call_target="tpu_custom_call" | custom-call | flops 3145728 | bytes 3145728 | tf_op jit(solution)/shard_map/pallas_call | solution.py:222
  1416.7 6.3 convolution_convert_fusion.3
  1423.0 6.3 convolution_convert_fusion.2
  1429.3 24.2 %collective-permute-done.35 = bf16[2432,1024]{1,0:T(8,128)(2,1)} collective-permute-done((bf16[2432,1024]{1,0:T(8,128)(2,1)S(1)}, bf16[2432,1024]{1,0:T(8,128)(2,1)}, u32[]{:S(2)}, u32[]{:S(2)}) %collective-permute-start.35) | collective-permute-done | bytes 4980768 | tf_op jit(solution)/shard_map/ppermute | solution.py:417
  1464.1 10.2 add_convert_fusion
  1476.4 17.0 fusion.95
  1497.3 45.2 %collective-permute-done.36 = bf16[1536,1024]{1,0:T(8,128)(2,1)} collective-permute-done((bf16[1536,1024]{1,0:T(8,128)(2,1)}, bf16[1536,1024]{1,0:T(8,128)(2,1)}, u32[]{:S(2)}, u32[]{:S(2)}) %collective-permute-start.36) | collective-permute-done | bytes 3145760 | tf_op jit(solution)/shard_map/ppermute | solution.py:417
  1548.9 8.7 add_convert_fusion.3
  1560.8 19.7 %fusion.40 = (f32[2048]{0:T(1024)S(1)}, f32[512]{0:T(512)}, f32[512]{0:T(512)}, f32[2048]{0:T(1024)S(1)}, f32[512,2048]{1,0:T(8,128)}) fusion(bf16[512,2048]{1,0:T(8,128)(2,1)S(1)} %copy-done.10, f32[512]{0:T(512)S(1)} %copy-done.65, f32[512]{0:T(512)S(1)} %copy-done.62, f32[2048]{0:T(1024)S(1)} %bitcast.229, ...), kind=kOutput, calls=%fused_computation.109 | convolution fusion | flops 6511651840 | bytes 24150016 | tf_op jit(solution)/shard_map/dot_general | solution.py:67
  1591.0 6.0 fusion.118
  1597.0 20.4 %all-to-all-done.1 = f32[16,7,128]{2,1,0:T(8,128)} async-done(((f32[16,7,128]{2,1,0:T(8,128)}), f32[16,7,128]{2,1,0:T(8,128)}, u32[]{:S(2)}, u32[]{:S(2)}) %all-to-all-start.1) | async-done | bytes 57376 | tf_op jit(solution)/shard_map/all_to_all | solution.py:478
  1625.1 6.6 add_convert_fusion.2
  1636.9 89.9 %reduce-scatter.15.cloned.1.call-done = bf16[384,1024]{1,0:T(8,128)(2,1)} async-done(((bf16[1536,1024]{1,0:T(8,128)(2,1)}), bf16[384,1024]{1,0:T(8,128)(2,1)}) %reduce-scatter.15.cloned.1.call-update) | async-done | bytes 786448 | tf_op jit(solution)/shard_map/reduce_scatter | solution.py:420
  1731.8 48.2 %reduce-scatter.17.cloned.1.call-done = bf16[256,1024]{1,0:T(8,128)(2,1)} async-done(((bf16[1024,1024]{1,0:T(8,128)(2,1)}), bf16[256,1024]{1,0:T(8,128)(2,1)}) %reduce-scatter.17.cloned.1.call-update) | async-done | bytes 524304 | tf_op jit(solution)/shard_map/reduce_scatter | solution.py:420
  1784.4 6.2 copy.97
  (468 shorter events, 300.3 us)
Async XLA Ops:
  7.2 198.0 %copy-start = (f32[1,3,512]{2,0,1:T(1,128)S(1)}, f32[1,3,512]{2,0,1:T(1,128)}, u32[]{:S(2)}) copy-start(f32[1,3,512]{2,0,1:T(1,128)} %param.18) | copy-start | bytes 18436
  7.2 69.5 %all-gather.18.cloned.1.call-start = ((), (), s32[]{:S(2)}) async-start(), calls=%async_computation.20 | async-start | bytes 2621440 | tf_op jit(solution)/shard_map/all_gather | solution.py:321
  9.5 195.6 %all-gather.8.cloned.1.call-start = ((), (), s32[]{:S(2)}) async-start(), calls=%async_computation.9 | async-start | bytes 7864320 | tf_op jit(solution)/shard_map/all_gather | solution.py:321
  40.5 95.1 %all-to-all-start = ((bf16[16,32,2048]{2,1,0:T(8,128)(2,1)}), bf16[16,32,2048]{2,1,0:T(8,128)(2,1)S(1)}, u32[]{:S(2)}, u32[]{:S(2)}) async-start(bf16[16,32,2048]{2,1,0:T(8,128)(2,1)} %bitcast.191), calls=%async_computation | async-start | bytes 4194304 | tf_op jit(solution)/shard_map/all_to_all | solution.py:287
  47.9 264.2 %all-gather.10.cloned.1.call-start = ((), (), s32[]{:S(2)}) async-start(), calls=%async_computation.10 | async-start | bytes 7208960 | tf_op jit(solution)/shard_map/all_gather | solution.py:321
  79.4 56.2 %collective-permute-start.5 = (bf16[768,1024]{1,0:T(8,128)(2,1)}, bf16[768,1024]{1,0:T(8,128)(2,1)}, u32[]{:S(2)}, u32[]{:S(2)}) collective-permute-start(bf16[768,1024]{1,0:T(8,128)(2,1)} %pad_maximum_fusion.22), channel_id=1, source_target_pairs={{0,8},{4,12},{8,0},{12,4},{1,9},{5,13},{9,1},{13,5},{2,10},{6,14},... | collective-permute-start | bytes 4718600 | tf_op jit(solution)/shard_map/ppermute | solution.py:326
  90.5 117.6 %copy-start.74 = (s32[1,1024]{1,0:T(1,128)S(1)}, s32[1,1024]{1,0:T(1,128)}, u32[]{:S(2)}) copy-start(s32[1,1024]{1,0:T(1,128)} %param.14) | copy-start | bytes 12292
  135.6 283.0 %all-gather.12.cloned.1.call-start = ((), (), s32[]{:S(2)}) async-start(), calls=%async_computation.11 | async-start | bytes 7208960 | tf_op jit(solution)/shard_map/all_gather | solution.py:321
  205.1 273.0 %all-gather.14.cloned.1.call-start = ((), (), s32[]{:S(2)}) async-start(), calls=%async_computation.12 | async-start | bytes 3604480 | tf_op jit(solution)/shard_map/all_gather | solution.py:321
  205.2 32.3 %collective-permute-start.2 = (f32[1,768]{1,0:T(1,128)S(1)}, f32[1,768]{1,0:T(1,128)S(1)}, u32[]{:S(2)}, u32[]{:S(2)}) collective-permute-start(f32[1,768]{1,0:T(1,128)S(1)} %bitcast.246), channel_id=1, source_target_pairs={{1,0},{2,1},{3,2},{0,3},{5,4},{6,5},{7,6},{4,7},{9,8},{10,9},{11,1... | collective-permute-start | bytes 9224 | tf_op jit(solution)/shard_map/ppermute | solution.py:365
  206.4 31.1 %collective-permute-start.3 = (f32[1,768]{1,0:T(1,128)S(1)}, f32[1,768]{1,0:T(1,128)S(1)}, u32[]{:S(2)}, u32[]{:S(2)}) collective-permute-start(f32[1,768]{1,0:T(1,128)S(1)} %bitcast.247), channel_id=1, source_target_pairs={{2,0},{3,1},{0,2},{1,3},{6,4},{7,5},{4,6},{5,7},{10,8},{11,9},{8,1... | collective-permute-start | bytes 9224 | tf_op jit(solution)/shard_map/ppermute | solution.py:365
  206.4 31.1 %collective-permute-start.4 = (f32[1,768]{1,0:T(1,128)S(1)}, f32[1,768]{1,0:T(1,128)S(1)}, u32[]{:S(2)}, u32[]{:S(2)}) collective-permute-start(f32[1,768]{1,0:T(1,128)S(1)} %bitcast.248), channel_id=1, source_target_pairs={{3,0},{0,1},{1,2},{2,3},{7,4},{4,5},{5,6},{6,7},{11,8},{8,9},{9,10... | collective-permute-start | bytes 9224 | tf_op jit(solution)/shard_map/ppermute | solution.py:365
  215.5 103.5 %collective-permute-start.1 = (bf16[2304,1024]{1,0:T(8,128)(2,1)}, bf16[2304,1024]{1,0:T(8,128)(2,1)}, u32[]{:S(2)}, u32[]{:S(2)}) collective-permute-start(bf16[2304,1024]{1,0:T(8,128)(2,1)} %pad_maximum_fusion.10), channel_id=1, source_target_pairs={{0,8},{4,12},{8,0},{12,4},{1,9},{5,13},{9,1},{13,5},{2,10},{6,14},... | collective-permute-start | bytes 14155784 | tf_op jit(solution)/shard_map/ppermute | solution.py:326
  221.7 204.5 %copy-start.52 = (f32[1,1,2048]{2,1,0:T(1,128)}, f32[1,1,2048]{2,1,0:T(1,128)S(1)}, u32[]{:S(2)}) copy-start(f32[1,1,2048]{2,1,0:T(1,128)S(1)} %get-tuple-element.240) | copy-start | bytes 24580
  221.7 204.4 %copy-start.44 = (f32[1,1,2048]{2,1,0:T(1,128)}, f32[1,1,2048]{2,1,0:T(1,128)S(1)}, u32[]{:S(2)}) copy-start(f32[1,1,2048]{2,1,0:T(1,128)S(1)} %get-tuple-element.238) | copy-start | bytes 24580
  225.2 105.8 %collective-permute-start = (bf16[512,2048]{1,0:T(8,128)(2,1)}, bf16[512,2048]{1,0:T(8,128)(2,1)}, u32[]{:S(2)}, u32[]{:S(2)}) collective-permute-start(bf16[512,2048]{1,0:T(8,128)(2,1)} %fusion.48), channel_id=1, source_target_pairs={{0,4},{4,0},{8,12},{12,8},{1,5},{5,1},{9,13},{13,9},{2,6},{6,2},{1... | collective-permute-start | bytes 6291464 | tf_op jit(solution)/shard_map/ppermute | solution.py:370
  317.2 95.7 %collective-permute-start.8 = (bf16[2112,1024]{1,0:T(8,128)(2,1)}, bf16[2112,1024]{1,0:T(8,128)(2,1)}, u32[]{:S(2)}, u32[]{:S(2)}) collective-permute-start(bf16[2112,1024]{1,0:T(8,128)(2,1)} %pad_maximum_fusion.11), channel_id=1, source_target_pairs={{0,8},{4,12},{8,0},{12,4},{1,9},{5,13},{9,1},{13,5},{2,10},{6,14},... | collective-permute-start | bytes 12976136 | tf_op jit(solution)/shard_map/ppermute | solution.py:326
  319.0 218.5 %all-gather.16.cloned.1.call-start = ((), (), s32[]{:S(2)}) async-start(), calls=%async_computation.13 | async-start | bytes 3604480 | tf_op jit(solution)/shard_map/all_gather | solution.py:321
  398.0 4.5 collective-permute-start.6
  418.6 1056.3 %reduce-scatter.7.cloned.1.call-start = ((), (), s32[]{:S(2)}) async-start(), calls=%async_computation.14 | async-start | bytes 7208960 | tf_op jit(solution)/shard_map/reduce_scatter | solution.py:420
  424.1 118.1 %collective-permute-start.9 = (bf16[2112,1024]{1,0:T(8,128)(2,1)}, bf16[2112,1024]{1,0:T(8,128)(2,1)}, u32[]{:S(2)}, u32[]{:S(2)}) collective-permute-start(bf16[2112,1024]{1,0:T(8,128)(2,1)} %pad_maximum_fusion.12), channel_id=1, source_target_pairs={{0,8},{4,12},{8,0},{12,4},{1,9},{5,13},{9,1},{13,5},{2,10},{6,14},... | collective-permute-start | bytes 12976136 | tf_op jit(solution)/shard_map/ppermute | solution.py:326
  428.3 132.9 %collective-permute-start.7 = (bf16[512,2048]{1,0:T(8,128)(2,1)}, bf16[512,2048]{1,0:T(8,128)(2,1)}, u32[]{:S(2)}, u32[]{:S(2)}) collective-permute-start(bf16[512,2048]{1,0:T(8,128)(2,1)} %add_convert_fusion.7), channel_id=1, source_target_pairs={{0,4},{4,0},{8,12},{12,8},{1,5},{5,1},{9,13},{13,9},{2,6},{6,2},{1... | collective-permute-start | bytes 6291464 | tf_op jit(solution)/shard_map/ppermute | solution.py:370
  481.4 123.5 %collective-permute-start.10 = (bf16[1056,1024]{1,0:T(8,128)(2,1)}, bf16[1056,1024]{1,0:T(8,128)(2,1)}, u32[]{:S(2)}, u32[]{:S(2)}) collective-permute-start(bf16[1056,1024]{1,0:T(8,128)(2,1)} %pad_maximum_fusion.20), channel_id=1, source_target_pairs={{0,8},{4,12},{8,0},{12,4},{1,9},{5,13},{9,1},{13,5},{2,10},{6,14},... | collective-permute-start | bytes 6488072 | tf_op jit(solution)/shard_map/ppermute | solution.py:326
  540.7 71.8 %collective-permute-start.11 = (bf16[1056,1024]{1,0:T(8,128)(2,1)}, bf16[1056,1024]{1,0:T(8,128)(2,1)}, u32[]{:S(2)}, u32[]{:S(2)}) collective-permute-start(bf16[1056,1024]{1,0:T(8,128)(2,1)} %pad_maximum_fusion.21), channel_id=1, source_target_pairs={{0,8},{4,12},{8,0},{12,4},{1,9},{5,13},{9,1},{13,5},{2,10},{6,14},... | collective-permute-start | bytes 6488072 | tf_op jit(solution)/shard_map/ppermute | solution.py:326
  638.1 3.8 collective-permute-start.12
  641.3 7.3 collective-permute-start.14
  645.1 26.9 %collective-permute-start.13 = (bf16[256,2048]{1,0:T(8,128)(2,1)S(1)}, bf16[256,2048]{1,0:T(8,128)(2,1)S(1)}, u32[]{:S(2)}, u32[]{:S(2)}) collective-permute-start(bf16[256,2048]{1,0:T(8,128)(2,1)S(1)} %fusion.124), channel_id=1, source_target_pairs={{0,16},{1,17},{2,18},{3,19},{4,20},{5,21},{6,22},{7,23},{8,24},{9,... | collective-permute-start | bytes 3145736 | tf_op jit(solution)/shard_map/ppermute | solution.py:385
  651.8 41.7 %collective-permute-start.15 = (bf16[256,2048]{1,0:T(8,128)(2,1)S(1)}, bf16[256,2048]{1,0:T(8,128)(2,1)S(1)}, u32[]{:S(2)}, u32[]{:S(2)}) collective-permute-start(bf16[256,2048]{1,0:T(8,128)(2,1)S(1)} %fusion.123), channel_id=1, source_target_pairs={{0,16},{1,17},{2,18},{3,19},{4,20},{5,21},{6,22},{7,23},{8,24},{9,... | collective-permute-start | bytes 3145736 | tf_op jit(solution)/shard_map/ppermute | solution.py:385
  700.7 4.3 collective-permute-start.16
  771.6 4.2 collective-permute-start.17
  778.9 110.0 %copy-start.56 = (f32[512]{0:T(512)}, f32[512]{0:T(512)S(1)}, u32[]{:S(2)}) copy-start(f32[512]{0:T(512)S(1)} %broadcast_multiply_fusion.10) | copy-start | bytes 6148
  780.9 4.3 collective-permute-start.19
  782.2 36.7 %collective-permute-start.18 = (bf16[512,2048]{1,0:T(8,128)(2,1)S(1)}, bf16[512,2048]{1,0:T(8,128)(2,1)}, u32[]{:S(2)}, u32[]{:S(2)}) collective-permute-start(bf16[512,2048]{1,0:T(8,128)(2,1)S(1)} %bitcast.170), channel_id=1, source_target_pairs={{0,4},{4,0},{8,12},{12,8},{1,5},{5,1},{9,13},{13,9},{2,6},{6,2},{1... | collective-permute-start | bytes 6291464 | tf_op jit(solution)/shard_map/ppermute | solution.py:370
  862.8 4.4 collective-permute-start.20
  863.0 126.9 %collective-permute-start.22 = (bf16[1024,2816]{1,0:T(8,128)(2,1)}, bf16[1024,2816]{1,0:T(8,128)(2,1)}, u32[]{:S(2)}, u32[]{:S(2)}) collective-permute-start(bf16[1024,2816]{1,0:T(8,128)(2,1)} %get-tuple-element.182), channel_id=1, source_target_pairs={{0,8},{4,12},{8,0},{12,4},{1,9},{5,13},{9,1},{13,5},{2,10},{6,14},... | collective-permute-start | bytes 17301512 | tf_op jit(solution)/shard_map/ppermute | solution.py:417
  893.4 4.2 collective-permute-start.21
  1005.2 11.4 collective-permute-start.23
  1016.2 19.7 %collective-permute-start.25 = (bf16[512,2048]{1,0:T(8,128)(2,1)}, bf16[512,2048]{1,0:T(8,128)(2,1)}, u32[]{:S(2)}, u32[]{:S(2)}) collective-permute-start(bf16[512,2048]{1,0:T(8,128)(2,1)} %convolution_convert_fusion.8), channel_id=1, source_target_pairs={{0,4},{4,0},{8,12},{12,8},{1,5},{5,1},{9,13},{13,9},{2,6},{6,2},{1... | collective-permute-start | bytes 6291464 | tf_op jit(solution)/shard_map/ppermute | solution.py:376
  1034.6 52.7 %collective-permute-start.24 = (bf16[512,2048]{1,0:T(8,128)(2,1)S(1)}, bf16[512,2048]{1,0:T(8,128)(2,1)S(1)}, u32[]{:S(2)}, u32[]{:S(2)}) collective-permute-start(bf16[512,2048]{1,0:T(8,128)(2,1)S(1)} %fusion.34), channel_id=1, source_target_pairs={{16,0},{17,1},{18,2},{19,3},{20,4},{21,5},{22,6},{23,7},{24,8},{25... | collective-permute-start | bytes 6291464 | tf_op jit(solution)/shard_map/ppermute | solution.py:385
  1087.8 5.1 collective-permute-start.27
  1091.5 35.0 %collective-permute-start.26 = (bf16[512,1024]{1,0:T(8,128)(2,1)}, bf16[512,1024]{1,0:T(8,128)(2,1)}, u32[]{:S(2)}, u32[]{:S(2)}) collective-permute-start(bf16[512,1024]{1,0:T(8,128)(2,1)} %get-tuple-element.219), channel_id=1, source_target_pairs={{0,8},{4,12},{8,0},{12,4},{1,9},{5,13},{9,1},{13,5},{2,10},{6,14},... | collective-permute-start | bytes 3145736 | tf_op jit(solution)/shard_map/ppermute | solution.py:417
  1093.0 63.9 %collective-permute-start.29 = (bf16[512,1024]{1,0:T(8,128)(2,1)S(1)}, bf16[512,1024]{1,0:T(8,128)(2,1)}, u32[]{:S(2)}, u32[]{:S(2)}) collective-permute-start(bf16[512,1024]{1,0:T(8,128)(2,1)S(1)} %get-tuple-element.218), channel_id=1, source_target_pairs={{0,4},{4,0},{8,12},{12,8},{1,5},{5,1},{9,13},{13,9},{2,6},{6,2},{1... | collective-permute-start | bytes 3145736 | tf_op jit(solution)/shard_map/ppermute | solution.py:370
  1130.1 65.2 %collective-permute-start.28 = (bf16[1408,1024]{1,0:T(8,128)(2,1)}, bf16[1408,1024]{1,0:T(8,128)(2,1)}, u32[]{:S(2)}, u32[]{:S(2)}) collective-permute-start(bf16[1408,1024]{1,0:T(8,128)(2,1)} %get-tuple-element.201), channel_id=1, source_target_pairs={{0,8},{4,12},{8,0},{12,4},{1,9},{5,13},{9,1},{13,5},{2,10},{6,14},... | collective-permute-start | bytes 8650760 | tf_op jit(solution)/shard_map/ppermute | solution.py:417
  1134.1 22.8 %collective-permute-start.30 = (bf16[512,1024]{1,0:T(8,128)(2,1)}, bf16[512,1024]{1,0:T(8,128)(2,1)S(1)}, u32[]{:S(2)}, u32[]{:S(2)}) collective-permute-start(bf16[512,1024]{1,0:T(8,128)(2,1)} %collective-permute-done.26), channel_id=1, source_target_pairs={{0,4},{4,0},{8,12},{12,8},{1,5},{5,1},{9,13},{13,9},{2,6},{6,2},{1... | collective-permute-start | bytes 3145736 | tf_op jit(solution)/shard_map/ppermute | solution.py:370
  1195.4 351.0 %reduce-scatter.9.cloned.1.call-start = ((), (), s32[]{:S(2)}) async-start(), calls=%async_computation.15 | async-start | bytes 7208960 | tf_op jit(solution)/shard_map/reduce_scatter | solution.py:420
  1195.4 4.4 collective-permute-start.32
  1195.5 65.2 %collective-permute-start.31 = (bf16[1408,1024]{1,0:T(8,128)(2,1)}, bf16[1408,1024]{1,0:T(8,128)(2,1)}, u32[]{:S(2)}, u32[]{:S(2)}) collective-permute-start(bf16[1408,1024]{1,0:T(8,128)(2,1)} %get-tuple-element.80), channel_id=1, source_target_pairs={{0,8},{4,12},{8,0},{12,4},{1,9},{5,13},{9,1},{13,5},{2,10},{6,14},... | collective-permute-start | bytes 8650760 | tf_op jit(solution)/shard_map/ppermute | solution.py:417
  1223.1 43.4 %collective-permute-start.33 = (bf16[512,2048]{1,0:T(8,128)(2,1)S(1)}, bf16[512,2048]{1,0:T(8,128)(2,1)S(1)}, u32[]{:S(2)}, u32[]{:S(2)}) collective-permute-start(bf16[512,2048]{1,0:T(8,128)(2,1)S(1)} %get-tuple-element.172), channel_id=1, source_target_pairs={{0,4},{4,0},{8,12},{12,8},{1,5},{5,1},{9,13},{13,9},{2,6},{6,2},{1... | collective-permute-start | bytes 6291464 | tf_op jit(solution)/shard_map/ppermute | solution.py:370
  1280.7 307.3 %reduce-scatter.11.cloned.1.call-start = ((), (), s32[]{:S(2)}) async-start(), calls=%async_computation.16 | async-start | bytes 7208960 | tf_op jit(solution)/shard_map/reduce_scatter | solution.py:420
  1280.8 64.5 %collective-permute-start.34 = (bf16[1408,1024]{1,0:T(8,128)(2,1)}, bf16[1408,1024]{1,0:T(8,128)(2,1)}, u32[]{:S(2)}, u32[]{:S(2)}) collective-permute-start(bf16[1408,1024]{1,0:T(8,128)(2,1)} %convolution_convert_fusion.5), channel_id=1, source_target_pairs={{0,8},{4,12},{8,0},{12,4},{1,9},{5,13},{9,1},{13,5},{2,10},{6,14},... | collective-permute-start | bytes 8650760 | tf_op jit(solution)/shard_map/ppermute | solution.py:417
  1345.3 108.3 %collective-permute-start.35 = (bf16[2432,1024]{1,0:T(8,128)(2,1)S(1)}, bf16[2432,1024]{1,0:T(8,128)(2,1)}, u32[]{:S(2)}, u32[]{:S(2)}) collective-permute-start(bf16[2432,1024]{1,0:T(8,128)(2,1)S(1)} %pad_maximum_fusion.9), channel_id=1, source_target_pairs={{0,8},{4,12},{8,0},{12,4},{1,9},{5,13},{9,1},{13,5},{2,10},{6,14},... | collective-permute-start | bytes 14942216 | tf_op jit(solution)/shard_map/ppermute | solution.py:417
  1474.2 162.7 %reduce-scatter.13.cloned.1.call-start = ((), (), s32[]{:S(2)}) async-start(), calls=%async_computation.17 | async-start | bytes 3932160 | tf_op jit(solution)/shard_map/reduce_scatter | solution.py:420
  1474.3 68.3 %collective-permute-start.36 = (bf16[1536,1024]{1,0:T(8,128)(2,1)}, bf16[1536,1024]{1,0:T(8,128)(2,1)}, u32[]{:S(2)}, u32[]{:S(2)}) collective-permute-start(bf16[1536,1024]{1,0:T(8,128)(2,1)} %convolution_convert_fusion.3), channel_id=1, source_target_pairs={{0,8},{4,12},{8,0},{12,4},{1,9},{5,13},{9,1},{13,5},{2,10},{6,14},... | collective-permute-start | bytes 9437192 | tf_op jit(solution)/shard_map/ppermute | solution.py:417
  1476.4 67.5 %collective-permute-start.39 = (bf16[704,512]{1,0:T(8,128)(2,1)S(1)}, bf16[704,512]{1,0:T(8,128)(2,1)S(1)}, u32[]{:S(2)}, u32[]{:S(2)}) collective-permute-start(bf16[704,512]{1,0:T(8,128)(2,1)S(1)} %get-tuple-element.232), channel_id=1, source_target_pairs={{0,4},{4,0},{8,12},{12,8},{1,5},{5,1},{9,13},{13,9},{2,6},{6,2},{1... | collective-permute-start | bytes 2162696 | tf_op jit(solution)/shard_map/ppermute | solution.py:463
  1542.6 18.2 %collective-permute-start.38 = (bf16[512,2048]{1,0:T(8,128)(2,1)}, bf16[512,2048]{1,0:T(8,128)(2,1)}, u32[]{:S(2)}, u32[]{:S(2)}) collective-permute-start(bf16[512,2048]{1,0:T(8,128)(2,1)} %fusion.95), channel_id=1, source_target_pairs={{0,4},{4,0},{8,12},{12,8},{1,5},{5,1},{9,13},{13,9},{2,6},{6,2},{1... | collective-permute-start | bytes 6291464 | tf_op jit(solution)/shard_map/ppermute | solution.py:538
  1545.9 77.9 %collective-permute-start.37 = (bf16[1536,1024]{1,0:T(8,128)(2,1)}, bf16[1536,1024]{1,0:T(8,128)(2,1)}, u32[]{:S(2)}, u32[]{:S(2)}) collective-permute-start(bf16[1536,1024]{1,0:T(8,128)(2,1)} %convolution_convert_fusion.2), channel_id=1, source_target_pairs={{0,8},{4,12},{8,0},{12,4},{1,9},{5,13},{9,1},{13,5},{2,10},{6,14},... | collective-permute-start | bytes 9437192 | tf_op jit(solution)/shard_map/ppermute | solution.py:417
  1548.7 9.0 collective-permute-start.40
  1581.3 36.1 %all-to-all-start.1 = ((f32[16,7,128]{2,1,0:T(8,128)}), f32[16,7,128]{2,1,0:T(8,128)}, u32[]{:S(2)}, u32[]{:S(2)}) async-start(f32[16,7,128]{2,1,0:T(8,128)} %copy.93), calls=%async_computation.1 | async-start | bytes 131072 | tf_op jit(solution)/shard_map/all_to_all | solution.py:478
  1585.4 141.4 %reduce-scatter.15.cloned.1.call-start = ((), (), s32[]{:S(2)}) async-start(), calls=%async_computation.18 | async-start | bytes 3932160 | tf_op jit(solution)/shard_map/reduce_scatter | solution.py:420
  1590.7 27.5 %collective-permute-start.41 = (bf16[704,512]{1,0:T(8,128)(2,1)}, bf16[704,512]{1,0:T(8,128)(2,1)}, u32[]{:S(2)}, u32[]{:S(2)}) collective-permute-start(bf16[704,512]{1,0:T(8,128)(2,1)} %get-tuple-element.230), channel_id=1, source_target_pairs={{0,4},{4,0},{8,12},{12,8},{1,5},{5,1},{9,13},{13,9},{2,6},{6,2},{1... | collective-permute-start | bytes 2162696 | tf_op jit(solution)/shard_map/ppermute | solution.py:463
  1631.7 148.3 %reduce-scatter.17.cloned.1.call-start = ((), (), s32[]{:S(2)}) async-start(), calls=%async_computation.19 | async-start | bytes 2621440 | tf_op jit(solution)/shard_map/reduce_scatter | solution.py:420
  1632.3 159.0 %all-to-all-start.2 = ((bf16[16,32,2048]{2,1,0:T(8,128)(2,1)}), bf16[16,32,2048]{2,1,0:T(8,128)(2,1)S(1)}, u32[]{:S(2)}, u32[]{:S(2)}) async-start(bf16[16,32,2048]{2,1,0:T(8,128)(2,1)} %bitcast.68), calls=%async_computation.5 | async-start | bytes 4194304 | tf_op jit(solution)/shard_map/all_to_all | solution.py:546
  1731.7 61.4 %collective-permute-start.42 = (bf16[3,256,512]{1,2,0:T(8,128)(2,1)}, bf16[3,256,512]{1,2,0:T(8,128)(2,1)}, u32[]{:S(2)}, u32[]{:S(2)}) collective-permute-start(bf16[3,256,512]{1,2,0:T(8,128)(2,1)} %copy.101), channel_id=1, source_target_pairs={{0,4},{4,0},{8,12},{12,8},{1,5},{5,1},{9,13},{13,9},{2,6},{6,2},{1... | collective-permute-start | bytes 2359304 | tf_op jit(solution)/shard_map/ppermute | solution.py:463
  1781.1 1.6 collective-permute-start.43
  (87 other events, 1095.0 us)
Sparse Core Ops, SparseCore 0:
  10.2 66.4 all-gather.17
  78.8 126.2 all-gather.7
  206.7 105.4 all-gather.9
  313.6 104.9 all-gather.11
  420.6 57.4 all-gather.13
  479.5 57.8 all-gather.15
  1195.5 98.6 reduce-scatter.6
  1296.4 102.7 reduce-scatter.8
  1474.4 98.5 reduce-scatter.10
  1575.1 61.7 reduce-scatter.12
  1639.8 86.9 reduce-scatter.14
  1729.0 50.9 reduce-scatter.16

commit v6 on v5

--- a/solution.py
+++ b/solution.py
@@ -76,7 +76,7 @@
     return jnp.concatenate(pieces, axis=0)
 
 
-def attn_fwd_kernel(heads, chunk, mixed, bias, cos_t, low_t, high_t, pos_c, pos_r, qkv, out):
+def attn_fwd_kernel(heads, chunk, mixed, bias, cos_t, low_t, high_t, pos_c, pos_r, qkv, out, lse):
     rows = mixed.shape[0]
     half = rows // 2
     width = heads * HEAD_WIDTH
@@ -105,8 +105,10 @@
                 score = dot_t(q_h, key[:end, lanes])
                 last = jnp.where(allowed, score[:, begin:], -1e30)
                 score = last if i == 0 else jnp.concatenate([score[:, :begin], last], axis=1)
-                prob = jnp.exp(score - jnp.max(score, axis=1, keepdims=True))
+                top = jnp.max(score, axis=1, keepdims=True)
+                prob = jnp.exp(score - top)
                 total = jnp.sum(prob, axis=1, keepdims=True)
+                lse[0, begin:end, 2 * pair + h : 2 * pair + h + 1] = top + jnp.log(total)
                 mixed_values = dot_n(prob.astype(jnp.bfloat16), value[:end, lanes])
                 halves.append(mixed_values / total)
             done = jnp.concatenate(halves, axis=1).astype(jnp.bfloat16)
@@ -115,7 +117,7 @@
             out[half + i * chunk : half + (i + 1) * chunk, lanes] = done[chunk:]
 
 
-def attn_bwd_kernel(heads, chunk, qkv, ctx, cos_t, low_t, high_t, pos_c, pos_r, grad, bias_grad, dk_s, dv_s):
+def attn_bwd_kernel(heads, chunk, qkv, lse, ctx, cos_t, low_t, high_t, pos_c, pos_r, grad, bias_grad, dk_s, dv_s):
     rows = qkv.shape[0]
     half = rows // 2
     width = heads * HEAD_WIDTH
@@ -158,8 +160,7 @@
                 score = dot_t(key[:end, lanes], query_s[begin:end, lanes])
                 last = jnp.where(allowed, score[begin:, :], -1e30)
                 score = last if i == 0 else jnp.concatenate([score[:begin, :], last], axis=0)
-                prob = jnp.exp(score - jnp.max(score, axis=0, keepdims=True))
-                prob = prob * (1.0 / jnp.sum(prob, axis=0, keepdims=True))
+                prob = jnp.exp(score - lse[0, 2 * pair + h : 2 * pair + h + 1, begin:end])
                 grad_h = ctx_grad[begin:end, lanes]
                 dv_h.append(dot_n(prob.astype(jnp.bfloat16), grad_h))
                 prob_grad = dot_t(value[:end, lanes], grad_h)
@@ -199,10 +200,12 @@
         out_specs=[
             pl.BlockSpec((rows, block), lambda g: (0, g)),
             pl.BlockSpec((rows, block // 3), lambda g: (0, g)),
+            pl.BlockSpec((1, rows, heads), lambda g: (g, 0, 0)),
         ],
         out_shape=[
             jax.ShapeDtypeStruct((rows, columns), jnp.bfloat16),
             jax.ShapeDtypeStruct((rows, columns // 3), jnp.bfloat16),
+            jax.ShapeDtypeStruct((groups, rows, heads), jnp.float32),
         ],
         compiler_params=pltpu.CompilerParams(vmem_limit_bytes=VMEM_LIMIT),
         cost_estimate=pl.CostEstimate(
@@ -213,7 +216,7 @@
     )(mixed, bias.reshape(groups, 1, block), cos_t, low_t, high_t, pos_c, pos_r)
 
 
-def attn_bwd(qkv, ctx_grad, context, groups, chunk):
+def attn_bwd(qkv, lse, ctx_grad, context, groups, chunk):
     rows, columns = qkv.shape
     block = columns // groups
     heads = block // (3 * HEAD_WIDTH)
@@ -224,6 +227,7 @@
         grid=(groups,),
         in_specs=[
             pl.BlockSpec((rows, block), lambda g: (0, g)),
+            pl.BlockSpec((1, heads, rows), lambda g: (g, 0, 0)),
             pl.BlockSpec((rows, block // 3), lambda g: (0, g)),
             whole((rows, 128)),
             whole((rows, 128)),
@@ -246,7 +250,7 @@
             bytes_accessed=rows * columns,
             transcendentals=0,
         ),
-    )(qkv, ctx_grad, cos_t, low_t, high_t, pos_c, pos_r)
+    )(qkv, lse.swapaxes(1, 2), ctx_grad, cos_t, low_t, high_t, pos_c, pos_r)
 
 
 def bulk_device(
@@ -387,7 +391,7 @@
     def forward(stream, parts):
         normed = both(ln(stream, gain[0], shift[0]))
         mixed = dot_t(normed, wt_qkv)
-        qkv, attended = attn_fwd(mixed, bias, context, tp_count, chunk)
+        qkv, attended, lse = attn_fwd(mixed, bias, context, tp_count, chunk)
         hidden_state = stream + summed(attended, wt_out)[0]
         normed_two = both(ln(hidden_state, gain[1], shift[1]))
         gate_up = dot_t(normed_two, wt_gu)
@@ -397,7 +401,7 @@
             (x + y).astype(jnp.bfloat16)
             for x, y in zip(split(hidden_state, parts), summed(activation, wt_down, parts))
         ]
-        return out, (stream, normed, qkv, attended, hidden_state, normed_two, gate_up, activation)
+        return out, (stream, normed, (qkv, lse), attended, hidden_state, normed_two, gate_up, activation)
 
     def far_near(right):
         far = lax.dynamic_slice_in_dim(right, (1 - side) * half_width, half_width, 1)
@@ -446,14 +450,15 @@
         return lax.ppermute(term.astype(jnp.bfloat16), "ctx", core_route).astype(jnp.float32)
 
     def backward(grad_out, stored, wait):
-        stream, normed, qkv, attended, hidden_state, normed_two, gate_up, activation = stored
+        stream, normed, (qkv, lse), attended, hidden_state, normed_two, gate_up, activation = stored
         gate_grad, up_grad = mlp_back(dot_t(both(grad_out), wt_down), gate_up)
         gu_grad = jnp.concatenate([gate_grad, up_grad], axis=1)
         two_grad = summed(gu_grad, wt_gu)[0]
         hidden_grad = grad_out.astype(jnp.float32) + ln_back(hidden_state, two_grad, gain[1])[0]
         ctx_grad = dot_t(both(hidden_grad.astype(jnp.bfloat16)), wt_out).astype(jnp.bfloat16)
-        qkv_grad, _ = attn_bwd(qkv, ctx_grad, context, tp_count, chunk)
-        one_grad = summed(after(qkv_grad, wait), wt_qkv)[0]
+        qkv_grad, _ = attn_bwd(qkv, lse, ctx_grad, context, tp_count, chunk)
+        one_other = from_core(dot_n(qkv_grad[own_rows:], wt_qkv))
+        one_grad = dot_n(after(qkv_grad[:own_rows], wait), wt_qkv) + one_other
         return (hidden_grad + ln_back(stream, one_grad, gain[0])[0]).astype(jnp.bfloat16)
 
     def settled(term):
@@ -478,7 +483,7 @@
         return jnp.sum(lax.all_to_all(vectors, ("ctx", "tp"), 0, 0, tiled=True), axis=0).reshape(-1, share)
 
     def last_backward(grad_out, stored, final_out, act_both):
-        stream, normed, qkv, attended, hidden_state, normed_two, gate_up, _ = stored
+        stream, normed, (qkv, lse), attended, hidden_state, normed_two, gate_up, _ = stored
         grad_f32 = grad_out.astype(jnp.float32)
         far_grad, near_grad = far_near(grad_out)
         grad_across = across(far_grad)
@@ -510,43 +515,44 @@
         )
         arriving = across(far_up_a)
         sum_gate = over_tp(near_total(gate_grad, normed_two, arriving_gate))
-        far_up_b = jnp.concatenate([far_up_b, far_term(attended, attn_grad)], axis=0)
         ctx_grad = dot_t(attn_grad, wt_out).astype(jnp.bfloat16)
 
         arriving, far_up_b, ctx_grad = together((arriving, far_up_b, ctx_grad))
-        arriving_b = across(far_up_b)
-        arriving_up = jnp.concatenate([arriving, arriving_b[: ff // 2]], axis=0)
-        arriving_out = arriving_b[ff // 2 :]
-        qkv_grad, bias_grad = attn_bwd(qkv, ctx_grad, context, tp_count, chunk)
+        arriving_up = jnp.concatenate([arriving, across(far_up_b)], axis=0)
+        qkv_grad, bias_grad = attn_bwd(qkv, lse, ctx_grad, context, tp_count, chunk)
         qkv_a, qkv_b = (part_of(qkv_grad, i, 2, 1) for i in range(2))
-        far_a, far_b = far_term(qkv_a, normed), far_term(qkv_b, normed)
-
-        arriving_up, arriving_out, far_a, far_b, qkv_a, qkv_b, qkv_grad, up_grad, attn_grad = together(
-            (arriving_up, arriving_out, far_a, far_b, qkv_a, qkv_b, qkv_grad, up_grad, attn_grad)
+        far_a = far_term(qkv_a, normed)
+
+        arriving_up, far_a, qkv_a, qkv_b, qkv_grad, up_grad, attn_grad = together(
+            (arriving_up, far_a, qkv_a, qkv_b, qkv_grad, up_grad, attn_grad)
         )
         arriving = across(far_a)
         sum_up = over_tp(near_total(up_grad, normed_two, arriving_up))
-        out_total = near_total(attended, attn_grad, arriving_out)
+        far_b = far_term(qkv_b, normed)
         one_other = dot_n(qkv_grad[own_rows:], wt_qkv).astype(jnp.bfloat16)
 
-        arriving, far_b, one_other, qkv_grad, qkv_a, qkv_b, out_total = together(
-            (arriving, far_b, one_other, qkv_grad, qkv_a, qkv_b, out_total)
+        arriving, far_b, one_other, qkv_grad, qkv_a, qkv_b, attn_grad = together(
+            (arriving, far_b, one_other, qkv_grad, qkv_a, qkv_b, attn_grad)
         )
         arriving_b = across(far_b)
-        sum_out = over_tp(out_total)
         sum_qkv_a = over_tp(near_total(qkv_a, normed, arriving))
         one_grad = dot_n(qkv_grad[:own_rows], wt_qkv) + lax.ppermute(one_other, "ctx", core_route).astype(jnp.float32)
         result, gain_one, shift_one = ln_back(stream, one_grad, gain[0])
         input_grad = (hidden_grad + result).astype(jnp.bfloat16)
         ends = jnp.where(first, input_grad, final_out)
+        far_out = far_term(attended, attn_grad)
         small = vector_sums((jnp.stack([gain_one, gain_two]), jnp.stack([shift_one, shift_two]), bias_grad))
-        done = (settled(sum_down), jnp.stack([settled(sum_gate).T, settled(sum_up).T]))
-
-        arriving_b, ends, qkv_b, small, done = together((arriving_b, ends, qkv_b, small, done))
+
+        arriving_b, far_out, ends, qkv_b, small = together((arriving_b, far_out, ends, qkv_b, small))
+        arriving_out = across(far_out)
         ends = lax.all_to_all(
             ends.reshape(ctx_count * tp_count, piece, width), ("ctx", "tp"), 0, 0, tiled=True
         )
         sum_qkv_b = over_tp(near_total(qkv_b, normed, arriving_b))
+        done = (settled(sum_down), jnp.stack([settled(sum_gate).T, settled(sum_up).T]))
+
+        arriving_out, attn_grad, done, ends = together((arriving_out, attn_grad, done, ends))
+        sum_out = over_tp(near_total(attended, attn_grad, arriving_out))
         sum_qkv = jnp.concatenate([sum_qkv_a, sum_qkv_b], axis=0)
         grads = (*done, settled(sum_out), settled(sum_qkv.reshape(3, columns, half_width)))
         return ends, small, grads

time: 1810 us -> 1770 us (0.978)
  waiting for transfers between devices: 747 us -> 714 us
    reduce_scatter x6, waiting for transfers between devices: 139 us -> 37.2 us  [over_tp(): return lax.psum_scatter(term, 'tp', scatter_dimension=0, tiled=True)]
    ppermute x8 -> x9, waiting for transfers between devices: 189 us -> 223 us  [across(): lax.ppermute(after(term, *others) if others else term, 'ctx', across_route)]
    all_to_all x1, waiting for transfers between devices: 0.01 us -> 26.5 us  [last_backward(): lax.all_to_all(ends.reshape(ctx_count * tp_count, piece, width), ('ctx',...]
  transfers between devices with their start and end apart: 59 -> 60, of which waited for: 31 -> 27; matrix products, arithmetic and copies ran while one was open for 35% -> 36% of each run, Pallas kernels for 9% -> 9%
where the time goes in v6:
time: 1770 us; the launch traced here: 1760 us
  waiting for transfers between devices  714 us (40%)
  matrix products  488 us (28%)
  Pallas kernels  191 us (11%)
  other arithmetic  177 us (10%)
  local copies, waits for them, and re-layouts  113 us (6%)
  starting transfers between devices  47.1 us (3%)
  between operations  31.5 us (2%)
    all_gather x6, waiting for transfers between devices, gathered(): own = lax.all_gather(block, 'tp', axis=0, tiled=True)  254 us
    ppermute x9, waiting for transfers between devices, across(): lax.ppermute(after(term, *others) if others else term, 'ctx', across_route)  223 us
    dot_general x18, matrix products, dot_n(): lax.dot_general(a, b, (((1,), (0,)), ((), ())), preferred_element_type=jn...  206 us
    dot_general x8, matrix products, dot_t(): lax.dot_general(a, b, (((1,), (1,)), ((), ())), preferred_element_type=jn...  184 us
    pallas_call x2, Pallas kernels, attn_bwd(): pl.pallas_call(functools.partial(attn_bwd_kernel, heads, chunk), grid=(gr...  110 us
    dot_general x12, matrix products, dot_0(): lax.dot_general(a, b, (((0,), (0,)), ((), ())), preferred_element_type=jn...  98.3 us
    pallas_call x2, Pallas kernels, attn_fwd(): pl.pallas_call(functools.partial(attn_fwd_kernel, heads, chunk), grid=(gr...  80.6 us
    ppermute x3, waiting for transfers between devices, over_x(): lax.ppermute(part, 'section', route)  68.4 us
  transfers between devices with their start and end apart: 60, of which 27 were waited for; matrix products, arithmetic and copies ran while one was open for 36% of the time, Pallas kernels for 9%

profile of v6, /device:TPU:0, one launch (start us, length us, event | category | flops | bytes accessed | tf_op | source)
XLA Modules:
  0.0 1762.5 jit_solution(17574290143604550416)
XLA Ops:
  40.4 7.4 all-to-all-start
  47.9 28.8 %all-gather.18.cloned.1.call-done = bf16[1,1024,1024]{2,1,0:T(8,128)(2,1)} async-done(((bf16[1,256,1024]{2,1,0:T(8,128)(2,1)}), bf16[1,1024,1024]{2,1,0:T(8,128)(2,1)}) %all-gather.18.cloned.1.call-update) | async-done | bytes 2097168 | tf_op jit(solution)/shard_map/all_gather | solution.py:325
  81.2 9.6 constant_dynamic-slice_fusion.25
  93.4 42.5 %all-to-all-done = bf16[16,32,2048]{2,1,0:T(8,128)(2,1)S(1)} async-done(((bf16[16,32,2048]{2,1,0:T(8,128)(2,1)}), bf16[16,32,2048]{2,1,0:T(8,128)(2,1)S(1)}, u32[]{:S(2)}, u32[]{:S(2)}) %all-to-all-start) | async-done | bytes 2097184 | tf_op jit(solution)/shard_map/all_to_all | solution.py:291
  138.6 66.5 %all-gather.8.cloned.1.call-done = bf16[3072,1024]{1,0:T(8,128)(2,1)} async-done(((bf16[768,1024]{1,0:T(8,128)(2,1)}), bf16[3072,1024]{1,0:T(8,128)(2,1)}) %all-gather.8.cloned.1.call-update) | async-done | bytes 6291472 | tf_op jit(solution)/shard_map/all_gather | solution.py:325
  243.5 68.6 %all-gather.10.cloned.1.call-done = bf16[2816,1024]{1,0:T(8,128)(2,1)} async-done(((bf16[704,1024]{1,0:T(8,128)(2,1)}), bf16[2816,1024]{1,0:T(8,128)(2,1)}) %all-gather.10.cloned.1.call-update) | async-done | bytes 5767184 | tf_op jit(solution)/shard_map/all_gather | solution.py:325
  319.2 11.4 fusion.3
  330.6 21.7 %fusion.49.mixed = f32[1024,3072]{1,0:T(8,128)} fusion(bf16[512,2048]{1,0:T(8,128)(2,1)} %collective-permute-done, bf16[512,2048]{1,0:T(8,128)(2,1)} %fusion.48, bf16[3072,1024]{1,0:T(8,128)(2,1)} %fusion.3, bf16[3072,1024]{1,0:T(8,128)(2,1)} %all-gather.8.cloned.1.call-done, pred[]{:T(512)S(6)} %eq.31), kind=kOutput, calls=%fused_computation.117 | convolution fusion | flops 12949913600 | bytes 29360128 | tf_op jit(solution)/shard_map/dot_general | solution.py:59
  352.4 40.6 %shard_map.170 = (bf16[1024,3072]{1,0:T(8,128)(2,1)}, bf16[1024,1024]{1,0:T(8,128)(2,1)}, f32[4,1024,4]{2,1,0:T(8,128)}) custom-call(f32[1024,3072]{1,0:T(8,128)} %fusion.49.mixed, f32[4,1,768]{2,1,0:T(1,128)} %reshape.344.bias, f32[1024,128]{1,0:T(8,128)} %concatenate.261.cos_t, f32[1024,128]{1,0:T(8,128)} %concatenate.262.low_t, ...), custom_call_target="tpu_custom_call" | custom-call | flops 12884901888 | bytes 22020096 | tf_op jit(solution)/shard_map/pallas_call | solution.py:188
  393.0 6.3 convolution_convert_fusion.7
  403.8 9.8 fusion.187
  428.3 12.1 fusion.12
  440.4 7.0 maximum_select_fusion.1
  447.5 30.7 %all-gather.14.cloned.1.call-done = bf16[1408,1024]{1,0:T(8,128)(2,1)} async-done(((bf16[352,1024]{1,0:T(8,128)(2,1)}), bf16[1408,1024]{1,0:T(8,128)(2,1)}) %all-gather.14.cloned.1.call-update) | async-done | bytes 2883600 | tf_op jit(solution)/shard_map/all_gather | solution.py:325
  482.8 54.6 %all-gather.16.cloned.1.call-done = bf16[1408,1024]{1,0:T(8,128)(2,1)} async-done(((bf16[352,1024]{1,0:T(8,128)(2,1)}), bf16[1408,1024]{1,0:T(8,128)(2,1)}) %all-gather.16.cloned.1.call-update) | async-done | bytes 2883600 | tf_op jit(solution)/shard_map/all_gather | solution.py:325
  542.2 11.9 fusion.9
  554.1 7.1 maximum_select_fusion.2
  561.2 34.2 %fusion.53 = f32[1024,5632]{1,0:T(8,128)} fusion(bf16[512,2048]{1,0:T(8,128)(2,1)} %collective-permute-done.7, bf16[512,2048]{1,0:T(8,128)(2,1)} %add_convert_fusion.7, bf16[2816,2048]{1,0:T(8,128)(2,1)} %maximum_select_fusion.2, bf16[2816,2048]{1,0:T(8,128)(2,1)} %maximum_select_fusion.1), kind=kOutput, calls=%fused_computation.126 | convolution fusion | flops 23676846080 | bytes 50331648 | tf_op jit(solution)/shard_map/dot_general | solution.py:59
  595.4 9.4 fusion
  604.8 7.6 collective-permute-done.11
  612.4 8.2 fusion.100
  625.9 9.0 pad_maximum_fusion.1
  653.1 18.8 %collective-permute-done.13 = bf16[256,2048]{1,0:T(8,128)(2,1)S(1)} collective-permute-done((bf16[256,2048]{1,0:T(8,128)(2,1)S(1)}, bf16[256,2048]{1,0:T(8,128)(2,1)S(1)}, u32[]{:S(2)}, u32[]{:S(2)}) %collective-permute-start.13) | collective-permute-done | bytes 1048608 | tf_op jit(solution)/shard_map/ppermute | solution.py:389
  672.0 21.5 %collective-permute-done.15 = bf16[256,2048]{1,0:T(8,128)(2,1)S(1)} collective-permute-done((bf16[256,2048]{1,0:T(8,128)(2,1)S(1)}, bf16[256,2048]{1,0:T(8,128)(2,1)S(1)}, u32[]{:S(2)}, u32[]{:S(2)}) %collective-permute-start.15) | collective-permute-done | bytes 1048608 | tf_op jit(solution)/shard_map/ppermute | solution.py:389
  704.9 22.1 %fusion.44.mixed = f32[1024,3072]{1,0:T(8,128)} fusion(bf16[512,2048]{1,0:T(8,128)(2,1)} %collective-permute-done.16, bf16[512,2048]{1,0:T(8,128)(2,1)} %copy-done.32, bf16[3072,1024]{1,0:T(8,128)(2,1)} %fusion.3, bf16[3072,1024]{1,0:T(8,128)(2,1)} %all-gather.8.cloned.1.call-done, pred[]{:T(512)S(6)} %eq.31), kind=kOutput, calls=%fused_computation.112 | convolution fusion | flops 12949913600 | bytes 29360128 | tf_op jit(solution)/shard_map/dot_general | solution.py:59
  727.0 40.0 %shard_map.171 = (bf16[1024,3072]{1,0:T(8,128)(2,1)}, bf16[1024,1024]{1,0:T(8,128)(2,1)}, f32[4,1024,4]{2,1,0:T(8,128)}) custom-call(f32[1024,3072]{1,0:T(8,128)} %fusion.44.mixed, f32[4,1,768]{2,1,0:T(1,128)} %reshape.344.bias, f32[1024,128]{1,0:T(8,128)} %concatenate.261.cos_t, f32[1024,128]{1,0:T(8,128)} %concatenate.262.low_t, ...), custom_call_target="tpu_custom_call" | custom-call | flops 12884901888 | bytes 22020096 | tf_op jit(solution)/shard_map/pallas_call | solution.py:188
  786.3 33.8 %fusion.43 = f32[1024,5632]{1,0:T(8,128)} fusion(bf16[512,2048]{1,0:T(8,128)(2,1)} %collective-permute-done.19, bf16[512,2048]{1,0:T(8,128)(2,1)} %copy-done.17, bf16[2816,2048]{1,0:T(8,128)(2,1)} %maximum_select_fusion.2, bf16[2816,2048]{1,0:T(8,128)(2,1)} %maximum_select_fusion.1), kind=kOutput, calls=%fused_computation.111 | convolution fusion | flops 23676846080 | bytes 50331648 | tf_op jit(solution)/shard_map/dot_general | solution.py:59
  820.0 26.8 %multiply_convert_fusion.4 = (bf16[1024,2816]{1,0:T(8,128)(2,1)}, bf16[1024,2816]{1,0:T(8,128)(2,1)}, bf16[1024,2816]{1,0:T(8,128)(2,1)}) fusion(f32[1024,5632]{1,0:T(8,128)} %fusion.43, bf16[2816,2048]{1,0:T(8,128)(2,1)} %bitcast.186, bf16[512,2048]{1,0:T(8,128)(2,1)} %collective-permute-done.18, bf16[512,2048]{1,0:T(8,128)(2,1)S(1)} %bitcast.174), kind=kOutput, calls=%fused_computation.28 | convolution fusion | flops 11865686016 | bytes 56098816 | tf_op jit(solution)/shard_map/dot_general | solution.py:59
  846.9 17.1 fusion.94
  868.3 21.9 %fusion.177 = (f32[512]{0:T(512)S(1)}, f32[512]{0:T(512)S(1)}, f32[512,2048]{1,0:T(8,128)}) fusion(f32[512]{0:T(512)S(1)} %add_rsqrt_fusion.2, f32[512,2048]{1,0:T(8,128)} %copy-done.2, f32[512]{0:T(512)S(1)} %broadcast_multiply_fusion.10, f32[2048]{0:T(1024)S(1)} %bitcast.229, bf16[512,2048]{1,0:T(8,128)(2,1)} %collective-permute-done.20, ...), kind=kOutput, calls=%fused_computation.357 | convolution fusion | flops 11877220352 | bytes 45105152 | tf_op jit(solution)/shard_map/dot_general | solution.py:67
  900.8 10.5 fusion.128.ctx
  911.3 55.1 %shard_map.172 = (bf16[1024,3072]{1,0:T(8,128)(2,1)}, f32[4,1,768]{2,1,0:T(1,128)}) custom-call(bf16[1024,3072]{1,0:T(8,128)(2,1)} %get-tuple-element.73.qkv, f32[4,4,1024]{2,1,0:T(4,128)} %bitcast.225, bf16[1024,1024]{1,0:T(8,128)(2,1)} %fusion.128.ctx, f32[1024,128]{1,0:T(8,128)} %concatenate.261.cos_t, f32[1024,128]{1,0:T(8,128)} %concatenate.262.low_t, ...), custom_call_target="tpu_custom_call" | custom-call | flops 3145728 | bytes 3145728 | tf_op jit(solution)/shard_map/pallas_call | solution.py:225
  966.4 16.6 fusion.88
  983.1 9.2 convolution_convert_fusion.8
  993.0 30.3 %collective-permute-done.22 = bf16[1024,2816]{1,0:T(8,128)(2,1)} collective-permute-done((bf16[1024,2816]{1,0:T(8,128)(2,1)}, bf16[1024,2816]{1,0:T(8,128)(2,1)}, u32[]{:S(2)}, u32[]{:S(2)}) %collective-permute-start.22) | collective-permute-done | bytes 5767200 | tf_op jit(solution)/shard_map/ppermute | solution.py:421
  1023.3 17.0 fusion.176
  1043.3 11.6 add_convert_fusion.5
  1054.9 11.1 pad_maximum_fusion.2
  1066.0 28.1 %collective-permute-done.24 = bf16[512,2048]{1,0:T(8,128)(2,1)S(1)} collective-permute-done((bf16[512,2048]{1,0:T(8,128)(2,1)S(1)}, bf16[512,2048]{1,0:T(8,128)(2,1)S(1)}, u32[]{:S(2)}, u32[]{:S(2)}) %collective-permute-start.24) | collective-permute-done | bytes 2097184 | tf_op jit(solution)/shard_map/ppermute | solution.py:389
  1099.7 24.5 %multiply_convert_fusion = (bf16[1024,2816]{1,0:T(8,128)(2,1)}, bf16[1024,2816]{1,0:T(8,128)(2,1)}) fusion(f32[1024,5632]{1,0:T(8,128)} %fusion.43, bf16[2816,2048]{1,0:T(8,128)(2,1)} %bitcast.188, bf16[512,2048]{1,0:T(8,128)(2,1)} %collective-permute-done.27, bf16[512,2048]{1,0:T(8,128)(2,1)} %copy-done.6), kind=kOutput, calls=%fused_computation.24 | convolution fusion | flops 11857035264 | bytes 50331648 | tf_op jit(solution)/shard_map/dot_general | solution.py:59
  1124.2 9.1 convolution_convert_fusion.1
  1144.3 19.4 %fusion.95 = bf16[512,2048]{1,0:T(8,128)(2,1)} fusion(bf16[1024,5632]{1,0:T(8,128)(2,1)} %constant_dynamic-update-slice_fusion.3, bf16[2816,2048]{1,0:T(8,128)(2,1)} %maximum_select_fusion.2, bf16[2816,2048]{1,0:T(8,128)(2,1)} %maximum_select_fusion.1), kind=kOutput, calls=%fused_computation.183 | convolution fusion | flops 11858345984 | bytes 30932992 | tf_op jit(solution)/shard_map/dot_general | solution.py:67
  1163.7 17.5 convolution_convert_fusion
  1181.2 20.9 %collective-permute-done.28 = bf16[1408,1024]{1,0:T(8,128)(2,1)} collective-permute-done((bf16[1408,1024]{1,0:T(8,128)(2,1)}, bf16[1408,1024]{1,0:T(8,128)(2,1)}, u32[]{:S(2)}, u32[]{:S(2)}) %collective-permute-start.28) | collective-permute-done | bytes 2883616 | tf_op jit(solution)/shard_map/ppermute | solution.py:421
  1206.6 19.7 %multiply_reduce_fusion = (f32[2048]{0:T(1024)}, f32[512]{0:T(512)S(1)}, f32[512]{0:T(512)S(1)}, f32[2048]{0:T(1024)}, f32[512,2048]{1,0:T(8,128)S(1)}) fusion(f32[512]{0:T(512)S(1)} %copy-done.60, f32[512,2048]{1,0:T(8,128)} %copy-done.2, f32[512]{0:T(512)S(1)} %copy-done.50, f32[2048]{0:T(1024)S(1)} %bitcast.230, ...), kind=kOutput, calls=%fused_computation.151 | convolution fusion | flops 11868827648 | bytes 39354368 | tf_op jit(solution)/shard_map/dot_general | solution.py:67
  1229.7 6.5 convolution_convert_fusion.5
  1240.7 26.8 %collective-permute-done.31 = bf16[1408,1024]{1,0:T(8,128)(2,1)} collective-permute-done((bf16[1408,1024]{1,0:T(8,128)(2,1)}, bf16[1408,1024]{1,0:T(8,128)(2,1)}, u32[]{:S(2)}, u32[]{:S(2)}) %collective-permute-start.31) | collective-permute-done | bytes 2883616 | tf_op jit(solution)/shard_map/ppermute | solution.py:421
  1278.0 9.4 add_convert_fusion.1
  1288.3 10.8 convolution_convert_fusion.11.ctx
  1299.1 52.9 %collective-permute-done.34 = bf16[1408,1024]{1,0:T(8,128)(2,1)} collective-permute-done((bf16[1408,1024]{1,0:T(8,128)(2,1)}, bf16[1408,1024]{1,0:T(8,128)(2,1)}, u32[]{:S(2)}, u32[]{:S(2)}) %collective-permute-start.34) | collective-permute-done | bytes 2883616 | tf_op jit(solution)/shard_map/ppermute | solution.py:421
  1352.6 55.0 %shard_map.173 = (bf16[1024,3072]{1,0:T(8,128)(2,1)}, f32[4,1,768]{2,1,0:T(1,128)}) custom-call(bf16[1024,3072]{1,0:T(8,128)(2,1)} %get-tuple-element.73.qkv, f32[4,4,1024]{2,1,0:T(4,128)} %bitcast.226, bf16[1024,1024]{1,0:T(8,128)(2,1)} %convolution_convert_fusion.11.ctx, f32[1024,128]{1,0:T(8,128)} %concatenate.261.cos_t, f32[1024,128]{1,0:T(8,128)} %concatenate.262.low_t, ...), custom_call_target="tpu_custom_call" | custom-call | flops 3145728 | bytes 3145728 | tf_op jit(solution)/shard_map/pallas_call | solution.py:225
  1415.8 6.6 convolution_convert_fusion.3
  1425.8 9.5 add_convert_fusion
  1436.8 7.8 convolution_convert_fusion.2
  1444.7 16.8 fusion.91
  1461.5 42.6 %collective-permute-done.36 = bf16[1536,1024]{1,0:T(8,128)(2,1)S(1)} collective-permute-done((bf16[1536,1024]{1,0:T(8,128)(2,1)}, bf16[1536,1024]{1,0:T(8,128)(2,1)S(1)}, u32[]{:S(2)}, u32[]{:S(2)}) %collective-permute-start.36) | collective-permute-done | bytes 3145760 | tf_op jit(solution)/shard_map/ppermute | solution.py:421
  1518.0 18.8 %fusion.40 = (f32[2048]{0:T(1024)S(1)}, f32[512]{0:T(512)S(1)}, f32[512]{0:T(512)S(1)}, f32[2048]{0:T(1024)S(1)}, f32[512,2048]{1,0:T(8,128)}) fusion(bf16[512,2048]{1,0:T(8,128)(2,1)S(1)} %copy-done.10, f32[512]{0:T(512)S(1)} %copy-done.58, f32[512]{0:T(512)S(1)} %copy-done.55, f32[2048]{0:T(1024)S(1)} %bitcast.235, ...), kind=kOutput, calls=%fused_computation.108 | convolution fusion | flops 6511651840 | bytes 24150016 | tf_op jit(solution)/shard_map/dot_general | solution.py:67
  1541.1 6.3 fusion.114
  1547.4 34.6 %all-to-all-done.1 = f32[16,7,128]{2,1,0:T(8,128)S(1)} async-done(((f32[16,7,128]{2,1,0:T(8,128)}), f32[16,7,128]{2,1,0:T(8,128)S(1)}, u32[]{:S(2)}, u32[]{:S(2)}) %all-to-all-start.1) | async-done | bytes 57376 | tf_op jit(solution)/shard_map/all_to_all | solution.py:483
  1582.0 8.7 add_convert_fusion.2
  1614.0 49.7 %collective-permute-done.39 = bf16[1024,1024]{1,0:T(8,128)(2,1)} collective-permute-done((bf16[1024,1024]{1,0:T(8,128)(2,1)}, bf16[1024,1024]{1,0:T(8,128)(2,1)}, u32[]{:S(2)}, u32[]{:S(2)}) %collective-permute-start.39) | collective-permute-done | bytes 2097184 | tf_op jit(solution)/shard_map/ppermute | solution.py:421
  1663.7 26.5 %all-to-all-done.2 = bf16[16,32,2048]{2,1,0:T(8,128)(2,1)S(1)} async-done(((bf16[16,32,2048]{2,1,0:T(8,128)(2,1)}), bf16[16,32,2048]{2,1,0:T(8,128)(2,1)S(1)}, u32[]{:S(2)}, u32[]{:S(2)}) %all-to-all-start.2) | async-done | bytes 2097184 | tf_op jit(solution)/shard_map/all_to_all | solution.py:548
  1690.2 6.6 add_convert_fusion.4
  1701.9 37.2 %reduce-scatter.17.cloned.1.call-done = bf16[256,1024]{1,0:T(8,128)(2,1)} async-done(((bf16[1024,1024]{1,0:T(8,128)(2,1)}), bf16[256,1024]{1,0:T(8,128)(2,1)}) %reduce-scatter.17.cloned.1.call-update) | async-done | bytes 524304 | tf_op jit(solution)/shard_map/reduce_scatter | solution.py:424
  (460 shorter events, 290.5 us)
Async XLA Ops:
  7.2 198.0 %copy-start = (f32[1,3,512]{2,0,1:T(1,128)S(1)}, f32[1,3,512]{2,0,1:T(1,128)}, u32[]{:S(2)}) copy-start(f32[1,3,512]{2,0,1:T(1,128)} %param.18) | copy-start | bytes 18436
  7.2 69.5 %all-gather.18.cloned.1.call-start = ((), (), s32[]{:S(2)}) async-start(), calls=%async_computation.20 | async-start | bytes 2621440 | tf_op jit(solution)/shard_map/all_gather | solution.py:325
  9.5 195.6 %all-gather.8.cloned.1.call-start = ((), (), s32[]{:S(2)}) async-start(), calls=%async_computation.9 | async-start | bytes 7864320 | tf_op jit(solution)/shard_map/all_gather | solution.py:325
  40.4 95.4 %all-to-all-start = ((bf16[16,32,2048]{2,1,0:T(8,128)(2,1)}), bf16[16,32,2048]{2,1,0:T(8,128)(2,1)S(1)}, u32[]{:S(2)}, u32[]{:S(2)}) async-start(bf16[16,32,2048]{2,1,0:T(8,128)(2,1)} %bitcast.197), calls=%async_computation | async-start | bytes 4194304 | tf_op jit(solution)/shard_map/all_to_all | solution.py:291
  47.8 264.3 %all-gather.10.cloned.1.call-start = ((), (), s32[]{:S(2)}) async-start(), calls=%async_computation.10 | async-start | bytes 7208960 | tf_op jit(solution)/shard_map/all_gather | solution.py:325
  79.4 56.4 %collective-permute-start.5 = (bf16[768,1024]{1,0:T(8,128)(2,1)}, bf16[768,1024]{1,0:T(8,128)(2,1)}, u32[]{:S(2)}, u32[]{:S(2)}) collective-permute-start(bf16[768,1024]{1,0:T(8,128)(2,1)} %pad_maximum_fusion.21), channel_id=1, source_target_pairs={{0,8},{4,12},{8,0},{12,4},{1,9},{5,13},{9,1},{13,5},{2,10},{6,14},... | collective-permute-start | bytes 4718600 | tf_op jit(solution)/shard_map/ppermute | solution.py:330
  90.8 117.2 %copy-start.66 = (s32[1,1024]{1,0:T(1,128)S(1)}, s32[1,1024]{1,0:T(1,128)}, u32[]{:S(2)}) copy-start(s32[1,1024]{1,0:T(1,128)} %param.14) | copy-start | bytes 12292
  135.9 282.7 %all-gather.12.cloned.1.call-start = ((), (), s32[]{:S(2)}) async-start(), calls=%async_computation.11 | async-start | bytes 7208960 | tf_op jit(solution)/shard_map/all_gather | solution.py:325
  205.1 273.0 %all-gather.14.cloned.1.call-start = ((), (), s32[]{:S(2)}) async-start(), calls=%async_computation.12 | async-start | bytes 3604480 | tf_op jit(solution)/shard_map/all_gather | solution.py:325
  205.2 32.3 %collective-permute-start.2 = (f32[1,768]{1,0:T(1,128)S(1)}, f32[1,768]{1,0:T(1,128)S(1)}, u32[]{:S(2)}, u32[]{:S(2)}) collective-permute-start(f32[1,768]{1,0:T(1,128)S(1)} %bitcast.252), channel_id=1, source_target_pairs={{1,0},{2,1},{3,2},{0,3},{5,4},{6,5},{7,6},{4,7},{9,8},{10,9},{11,1... | collective-permute-start | bytes 9224 | tf_op jit(solution)/shard_map/ppermute | solution.py:369
  206.4 31.1 %collective-permute-start.3 = (f32[1,768]{1,0:T(1,128)S(1)}, f32[1,768]{1,0:T(1,128)S(1)}, u32[]{:S(2)}, u32[]{:S(2)}) collective-permute-start(f32[1,768]{1,0:T(1,128)S(1)} %bitcast.253), channel_id=1, source_target_pairs={{2,0},{3,1},{0,2},{1,3},{6,4},{7,5},{4,6},{5,7},{10,8},{11,9},{8,1... | collective-permute-start | bytes 9224 | tf_op jit(solution)/shard_map/ppermute | solution.py:369
  206.4 31.1 %collective-permute-start.4 = (f32[1,768]{1,0:T(1,128)S(1)}, f32[1,768]{1,0:T(1,128)S(1)}, u32[]{:S(2)}, u32[]{:S(2)}) collective-permute-start(f32[1,768]{1,0:T(1,128)S(1)} %bitcast.254), channel_id=1, source_target_pairs={{3,0},{0,1},{1,2},{2,3},{7,4},{4,5},{5,6},{6,7},{11,8},{8,9},{9,10... | collective-permute-start | bytes 9224 | tf_op jit(solution)/shard_map/ppermute | solution.py:369
  215.4 103.5 %collective-permute-start.1 = (bf16[2304,1024]{1,0:T(8,128)(2,1)}, bf16[2304,1024]{1,0:T(8,128)(2,1)}, u32[]{:S(2)}, u32[]{:S(2)}) collective-permute-start(bf16[2304,1024]{1,0:T(8,128)(2,1)} %pad_maximum_fusion.9), channel_id=1, source_target_pairs={{0,8},{4,12},{8,0},{12,4},{1,9},{5,13},{9,1},{13,5},{2,10},{6,14},... | collective-permute-start | bytes 14155784 | tf_op jit(solution)/shard_map/ppermute | solution.py:330
  221.7 204.4 %copy-start.45 = (f32[1,1,2048]{2,1,0:T(1,128)}, f32[1,1,2048]{2,1,0:T(1,128)S(1)}, u32[]{:S(2)}) copy-start(f32[1,1,2048]{2,1,0:T(1,128)S(1)} %get-tuple-element.246) | copy-start | bytes 24580
  221.8 204.4 %copy-start.38 = (f32[1,1,2048]{2,1,0:T(1,128)}, f32[1,1,2048]{2,1,0:T(1,128)S(1)}, u32[]{:S(2)}) copy-start(f32[1,1,2048]{2,1,0:T(1,128)S(1)} %get-tuple-element.244) | copy-start | bytes 24580
  225.2 105.4 %collective-permute-start = (bf16[512,2048]{1,0:T(8,128)(2,1)}, bf16[512,2048]{1,0:T(8,128)(2,1)}, u32[]{:S(2)}, u32[]{:S(2)}) collective-permute-start(bf16[512,2048]{1,0:T(8,128)(2,1)} %fusion.48), channel_id=1, source_target_pairs={{0,4},{4,0},{8,12},{12,8},{1,5},{5,1},{9,13},{13,9},{2,6},{6,2},{1... | collective-permute-start | bytes 6291464 | tf_op jit(solution)/shard_map/ppermute | solution.py:374
  317.1 96.4 %collective-permute-start.8 = (bf16[2112,1024]{1,0:T(8,128)(2,1)}, bf16[2112,1024]{1,0:T(8,128)(2,1)}, u32[]{:S(2)}, u32[]{:S(2)}) collective-permute-start(bf16[2112,1024]{1,0:T(8,128)(2,1)} %pad_maximum_fusion.10), channel_id=1, source_target_pairs={{0,8},{4,12},{8,0},{12,4},{1,9},{5,13},{9,1},{13,5},{2,10},{6,14},... | collective-permute-start | bytes 12976136 | tf_op jit(solution)/shard_map/ppermute | solution.py:330
  318.9 218.6 %all-gather.16.cloned.1.call-start = ((), (), s32[]{:S(2)}) async-start(), calls=%async_computation.13 | async-start | bytes 3604480 | tf_op jit(solution)/shard_map/all_gather | solution.py:325
  399.3 4.5 collective-permute-start.6
  418.6 1177.8 %reduce-scatter.7.cloned.1.call-start = ((), (), s32[]{:S(2)}) async-start(), calls=%async_computation.14 | async-start | bytes 7208960 | tf_op jit(solution)/shard_map/reduce_scatter | solution.py:424
  424.1 118.1 %collective-permute-start.9 = (bf16[2112,1024]{1,0:T(8,128)(2,1)}, bf16[2112,1024]{1,0:T(8,128)(2,1)}, u32[]{:S(2)}, u32[]{:S(2)}) collective-permute-start(bf16[2112,1024]{1,0:T(8,128)(2,1)} %pad_maximum_fusion.11), channel_id=1, source_target_pairs={{0,8},{4,12},{8,0},{12,4},{1,9},{5,13},{9,1},{13,5},{2,10},{6,14},... | collective-permute-start | bytes 12976136 | tf_op jit(solution)/shard_map/ppermute | solution.py:330
  428.3 133.0 %collective-permute-start.7 = (bf16[512,2048]{1,0:T(8,128)(2,1)}, bf16[512,2048]{1,0:T(8,128)(2,1)}, u32[]{:S(2)}, u32[]{:S(2)}) collective-permute-start(bf16[512,2048]{1,0:T(8,128)(2,1)} %add_convert_fusion.7), channel_id=1, source_target_pairs={{0,4},{4,0},{8,12},{12,8},{1,5},{5,1},{9,13},{13,9},{2,6},{6,2},{1... | collective-permute-start | bytes 6291464 | tf_op jit(solution)/shard_map/ppermute | solution.py:374
  481.4 123.5 %collective-permute-start.10 = (bf16[1056,1024]{1,0:T(8,128)(2,1)}, bf16[1056,1024]{1,0:T(8,128)(2,1)}, u32[]{:S(2)}, u32[]{:S(2)}) collective-permute-start(bf16[1056,1024]{1,0:T(8,128)(2,1)} %pad_maximum_fusion.19), channel_id=1, source_target_pairs={{0,8},{4,12},{8,0},{12,4},{1,9},{5,13},{9,1},{13,5},{2,10},{6,14},... | collective-permute-start | bytes 6488072 | tf_op jit(solution)/shard_map/ppermute | solution.py:330
  540.7 71.7 %collective-permute-start.11 = (bf16[1056,1024]{1,0:T(8,128)(2,1)}, bf16[1056,1024]{1,0:T(8,128)(2,1)}, u32[]{:S(2)}, u32[]{:S(2)}) collective-permute-start(bf16[1056,1024]{1,0:T(8,128)(2,1)} %pad_maximum_fusion.20), channel_id=1, source_target_pairs={{0,8},{4,12},{8,0},{12,4},{1,9},{5,13},{9,1},{13,5},{2,10},{6,14},... | collective-permute-start | bytes 6488072 | tf_op jit(solution)/shard_map/ppermute | solution.py:330
  638.0 3.8 collective-permute-start.12
  641.3 7.3 collective-permute-start.14
  645.1 26.9 %collective-permute-start.13 = (bf16[256,2048]{1,0:T(8,128)(2,1)S(1)}, bf16[256,2048]{1,0:T(8,128)(2,1)S(1)}, u32[]{:S(2)}, u32[]{:S(2)}) collective-permute-start(bf16[256,2048]{1,0:T(8,128)(2,1)S(1)} %fusion.120), channel_id=1, source_target_pairs={{0,16},{1,17},{2,18},{3,19},{4,20},{5,21},{6,22},{7,23},{8,24},{9,... | collective-permute-start | bytes 3145736 | tf_op jit(solution)/shard_map/ppermute | solution.py:389
  651.8 41.7 %collective-permute-start.15 = (bf16[256,2048]{1,0:T(8,128)(2,1)S(1)}, bf16[256,2048]{1,0:T(8,128)(2,1)S(1)}, u32[]{:S(2)}, u32[]{:S(2)}) collective-permute-start(bf16[256,2048]{1,0:T(8,128)(2,1)S(1)} %fusion.119), channel_id=1, source_target_pairs={{0,16},{1,17},{2,18},{3,19},{4,20},{5,21},{6,22},{7,23},{8,24},{9,... | collective-permute-start | bytes 3145736 | tf_op jit(solution)/shard_map/ppermute | solution.py:389
  700.6 4.3 collective-permute-start.16
  772.7 4.2 collective-permute-start.17
  782.0 4.3 collective-permute-start.19
  783.3 36.7 %collective-permute-start.18 = (bf16[512,2048]{1,0:T(8,128)(2,1)S(1)}, bf16[512,2048]{1,0:T(8,128)(2,1)}, u32[]{:S(2)}, u32[]{:S(2)}) collective-permute-start(bf16[512,2048]{1,0:T(8,128)(2,1)S(1)} %bitcast.173), channel_id=1, source_target_pairs={{0,4},{4,0},{8,12},{12,8},{1,5},{5,1},{9,13},{13,9},{2,6},{6,2},{1... | collective-permute-start | bytes 6291464 | tf_op jit(solution)/shard_map/ppermute | solution.py:374
  863.9 4.4 collective-permute-start.20
  896.3 4.5 collective-permute-start.21
  896.4 126.9 %collective-permute-start.22 = (bf16[1024,2816]{1,0:T(8,128)(2,1)}, bf16[1024,2816]{1,0:T(8,128)(2,1)}, u32[]{:S(2)}, u32[]{:S(2)}) collective-permute-start(bf16[1024,2816]{1,0:T(8,128)(2,1)} %get-tuple-element.188), channel_id=1, source_target_pairs={{0,8},{4,12},{8,0},{12,4},{1,9},{5,13},{9,1},{13,5},{2,10},{6,14},... | collective-permute-start | bytes 17301512 | tf_op jit(solution)/shard_map/ppermute | solution.py:421
  983.0 40.3 %collective-permute-start.23 = (bf16[512,2048]{1,0:T(8,128)(2,1)}, bf16[512,2048]{1,0:T(8,128)(2,1)}, u32[]{:S(2)}, u32[]{:S(2)}) collective-permute-start(bf16[512,2048]{1,0:T(8,128)(2,1)} %fusion.88), channel_id=1, source_target_pairs={{0,4},{4,0},{8,12},{12,8},{1,5},{5,1},{9,13},{13,9},{2,6},{6,2},{1... | collective-permute-start | bytes 6291464 | tf_op jit(solution)/shard_map/ppermute | solution.py:450
  992.3 50.9 %collective-permute-start.25 = (bf16[512,2048]{1,0:T(8,128)(2,1)}, bf16[512,2048]{1,0:T(8,128)(2,1)}, u32[]{:S(2)}, u32[]{:S(2)}) collective-permute-start(bf16[512,2048]{1,0:T(8,128)(2,1)} %convolution_convert_fusion.8), channel_id=1, source_target_pairs={{0,4},{4,0},{8,12},{12,8},{1,5},{5,1},{9,13},{13,9},{2,6},{6,2},{1... | collective-permute-start | bytes 6291464 | tf_op jit(solution)/shard_map/ppermute | solution.py:380
  1041.9 52.1 %collective-permute-start.24 = (bf16[512,2048]{1,0:T(8,128)(2,1)S(1)}, bf16[512,2048]{1,0:T(8,128)(2,1)S(1)}, u32[]{:S(2)}, u32[]{:S(2)}) collective-permute-start(bf16[512,2048]{1,0:T(8,128)(2,1)S(1)} %fusion.34), channel_id=1, source_target_pairs={{16,0},{17,1},{18,2},{19,3},{20,4},{21,5},{22,6},{23,7},{24,8},{25... | collective-permute-start | bytes 6291464 | tf_op jit(solution)/shard_map/ppermute | solution.py:389
  1094.6 5.1 collective-permute-start.27
  1098.2 35.0 %collective-permute-start.26 = (bf16[512,1024]{1,0:T(8,128)(2,1)}, bf16[512,1024]{1,0:T(8,128)(2,1)}, u32[]{:S(2)}, u32[]{:S(2)}) collective-permute-start(bf16[512,1024]{1,0:T(8,128)(2,1)} %get-tuple-element.225), channel_id=1, source_target_pairs={{0,8},{4,12},{8,0},{12,4},{1,9},{5,13},{9,1},{13,5},{2,10},{6,14},... | collective-permute-start | bytes 3145736 | tf_op jit(solution)/shard_map/ppermute | solution.py:421
  1099.7 64.0 %collective-permute-start.29 = (bf16[512,1024]{1,0:T(8,128)(2,1)S(1)}, bf16[512,1024]{1,0:T(8,128)(2,1)}, u32[]{:S(2)}, u32[]{:S(2)}) collective-permute-start(bf16[512,1024]{1,0:T(8,128)(2,1)S(1)} %get-tuple-element.224), channel_id=1, source_target_pairs={{0,4},{4,0},{8,12},{12,8},{1,5},{5,1},{9,13},{13,9},{2,6},{6,2},{1... | collective-permute-start | bytes 3145736 | tf_op jit(solution)/shard_map/ppermute | solution.py:374
  1136.9 65.2 %collective-permute-start.28 = (bf16[1408,1024]{1,0:T(8,128)(2,1)}, bf16[1408,1024]{1,0:T(8,128)(2,1)}, u32[]{:S(2)}, u32[]{:S(2)}) collective-permute-start(bf16[1408,1024]{1,0:T(8,128)(2,1)} %get-tuple-element.207), channel_id=1, source_target_pairs={{0,8},{4,12},{8,0},{12,4},{1,9},{5,13},{9,1},{13,5},{2,10},{6,14},... | collective-permute-start | bytes 8650760 | tf_op jit(solution)/shard_map/ppermute | solution.py:421
  1140.8 22.9 %collective-permute-start.30 = (bf16[512,1024]{1,0:T(8,128)(2,1)}, bf16[512,1024]{1,0:T(8,128)(2,1)S(1)}, u32[]{:S(2)}, u32[]{:S(2)}) collective-permute-start(bf16[512,1024]{1,0:T(8,128)(2,1)} %collective-permute-done.26), channel_id=1, source_target_pairs={{0,4},{4,0},{8,12},{12,8},{1,5},{5,1},{9,13},{13,9},{2,6},{6,2},{1... | collective-permute-start | bytes 3145736 | tf_op jit(solution)/shard_map/ppermute | solution.py:374
  1202.1 396.7 %reduce-scatter.9.cloned.1.call-start = ((), (), s32[]{:S(2)}) async-start(), calls=%async_computation.15 | async-start | bytes 7208960 | tf_op jit(solution)/shard_map/reduce_scatter | solution.py:424
  1202.2 4.4 collective-permute-start.32
  1202.2 65.2 %collective-permute-start.31 = (bf16[1408,1024]{1,0:T(8,128)(2,1)}, bf16[1408,1024]{1,0:T(8,128)(2,1)}, u32[]{:S(2)}, u32[]{:S(2)}) collective-permute-start(bf16[1408,1024]{1,0:T(8,128)(2,1)} %get-tuple-element.84), channel_id=1, source_target_pairs={{0,8},{4,12},{8,0},{12,4},{1,9},{5,13},{9,1},{13,5},{2,10},{6,14},... | collective-permute-start | bytes 8650760 | tf_op jit(solution)/shard_map/ppermute | solution.py:421
  1229.5 43.7 %collective-permute-start.33 = (bf16[512,2048]{1,0:T(8,128)(2,1)S(1)}, bf16[512,2048]{1,0:T(8,128)(2,1)S(1)}, u32[]{:S(2)}, u32[]{:S(2)}) collective-permute-start(bf16[512,2048]{1,0:T(8,128)(2,1)S(1)} %get-tuple-element.178), channel_id=1, source_target_pairs={{0,4},{4,0},{8,12},{12,8},{1,5},{5,1},{9,13},{13,9},{2,6},{6,2},{1... | collective-permute-start | bytes 6291464 | tf_op jit(solution)/shard_map/ppermute | solution.py:374
  1287.5 314.1 %reduce-scatter.11.cloned.1.call-start = ((), (), s32[]{:S(2)}) async-start(), calls=%async_computation.16 | async-start | bytes 7208960 | tf_op jit(solution)/shard_map/reduce_scatter | solution.py:424
  1287.5 64.5 %collective-permute-start.34 = (bf16[1408,1024]{1,0:T(8,128)(2,1)}, bf16[1408,1024]{1,0:T(8,128)(2,1)}, u32[]{:S(2)}, u32[]{:S(2)}) collective-permute-start(bf16[1408,1024]{1,0:T(8,128)(2,1)} %convolution_convert_fusion.5), channel_id=1, source_target_pairs={{0,8},{4,12},{8,0},{12,4},{1,9},{5,13},{9,1},{13,5},{2,10},{6,14},... | collective-permute-start | bytes 8650760 | tf_op jit(solution)/shard_map/ppermute | solution.py:421
  1352.0 70.4 %collective-permute-start.35 = (bf16[1408,1024]{1,0:T(8,128)(2,1)S(1)}, bf16[1408,1024]{1,0:T(8,128)(2,1)}, u32[]{:S(2)}, u32[]{:S(2)}) collective-permute-start(bf16[1408,1024]{1,0:T(8,128)(2,1)S(1)} %copy-done.68), channel_id=1, source_target_pairs={{0,8},{4,12},{8,0},{12,4},{1,9},{5,13},{9,1},{13,5},{2,10},{6,14},... | collective-permute-start | bytes 8650760 | tf_op jit(solution)/shard_map/ppermute | solution.py:421
  1435.3 261.5 %reduce-scatter.13.cloned.1.call-start = ((), (), s32[]{:S(2)}) async-start(), calls=%async_computation.17 | async-start | bytes 3932160 | tf_op jit(solution)/shard_map/reduce_scatter | solution.py:424
  1435.3 68.8 %collective-permute-start.36 = (bf16[1536,1024]{1,0:T(8,128)(2,1)}, bf16[1536,1024]{1,0:T(8,128)(2,1)S(1)}, u32[]{:S(2)}, u32[]{:S(2)}) collective-permute-start(bf16[1536,1024]{1,0:T(8,128)(2,1)} %convolution_convert_fusion.3), channel_id=1, source_target_pairs={{0,8},{4,12},{8,0},{12,4},{1,9},{5,13},{9,1},{13,5},{2,10},{6,14},... | collective-permute-start | bytes 9437192 | tf_op jit(solution)/shard_map/ppermute | solution.py:421
  1504.1 13.9 collective-permute-start.38
  1510.5 71.5 %collective-permute-start.37 = (bf16[1536,1024]{1,0:T(8,128)(2,1)}, bf16[1536,1024]{1,0:T(8,128)(2,1)}, u32[]{:S(2)}, u32[]{:S(2)}) collective-permute-start(bf16[1536,1024]{1,0:T(8,128)(2,1)} %convolution_convert_fusion.2), channel_id=1, source_target_pairs={{0,8},{4,12},{8,0},{12,4},{1,9},{5,13},{9,1},{13,5},{2,10},{6,14},... | collective-permute-start | bytes 9437192 | tf_op jit(solution)/shard_map/ppermute | solution.py:421
  1537.5 44.5 %all-to-all-start.1 = ((f32[16,7,128]{2,1,0:T(8,128)}), f32[16,7,128]{2,1,0:T(8,128)S(1)}, u32[]{:S(2)}, u32[]{:S(2)}) async-start(f32[16,7,128]{2,1,0:T(8,128)} %copy.98), calls=%async_computation.1 | async-start | bytes 131072 | tf_op jit(solution)/shard_map/all_to_all | solution.py:483
  1541.0 155.8 %reduce-scatter.15.cloned.1.call-start = ((), (), s32[]{:S(2)}) async-start(), calls=%async_computation.18 | async-start | bytes 3932160 | tf_op jit(solution)/shard_map/reduce_scatter | solution.py:424
  1590.8 99.4 %all-to-all-start.2 = ((bf16[16,32,2048]{2,1,0:T(8,128)(2,1)}), bf16[16,32,2048]{2,1,0:T(8,128)(2,1)S(1)}, u32[]{:S(2)}, u32[]{:S(2)}) async-start(bf16[16,32,2048]{2,1,0:T(8,128)(2,1)} %bitcast.69), calls=%async_computation.5 | async-start | bytes 4194304 | tf_op jit(solution)/shard_map/all_to_all | solution.py:548
  1594.5 144.6 %reduce-scatter.17.cloned.1.call-start = ((), (), s32[]{:S(2)}) async-start(), calls=%async_computation.19 | async-start | bytes 2621440 | tf_op jit(solution)/shard_map/reduce_scatter | solution.py:424
  1594.6 69.1 %collective-permute-start.39 = (bf16[1024,1024]{1,0:T(8,128)(2,1)}, bf16[1024,1024]{1,0:T(8,128)(2,1)}, u32[]{:S(2)}, u32[]{:S(2)}) collective-permute-start(bf16[1024,1024]{1,0:T(8,128)(2,1)} %fusion.125), channel_id=1, source_target_pairs={{0,8},{4,12},{8,0},{12,4},{1,9},{5,13},{9,1},{13,5},{2,10},{6,14},... | collective-permute-start | bytes 6291464 | tf_op jit(solution)/shard_map/ppermute | solution.py:421
  1598.8 5.3 collective-permute-start.40
  1601.1 6.4 collective-permute-start.41
  1604.1 5.2 collective-permute-start.42
  1701.6 47.7 %collective-permute-start.43 = (bf16[3,256,512]{1,2,0:T(8,128)(2,1)}, bf16[3,256,512]{1,2,0:T(8,128)(2,1)}, u32[]{:S(2)}, u32[]{:S(2)}) collective-permute-start(bf16[3,256,512]{1,2,0:T(8,128)(2,1)} %copy.106), channel_id=1, source_target_pairs={{0,4},{4,0},{8,12},{12,8},{1,5},{5,1},{9,13},{13,9},{2,6},{6,2},{1... | collective-permute-start | bytes 2359304 | tf_op jit(solution)/shard_map/ppermute | solution.py:468
  1740.2 12.9 collective-permute-start.44
  (83 other events, 1479.7 us)
Sparse Core Ops, SparseCore 0:
  10.2 66.4 all-gather.17
  78.8 126.2 all-gather.7
  206.7 105.4 all-gather.9
  313.6 104.9 all-gather.11
  420.6 57.4 all-gather.13
  479.5 57.8 all-gather.15
  1202.2 98.6 reduce-scatter.6
  1303.2 102.7 reduce-scatter.8
  1435.4 99.4 reduce-scatter.10
  1537.0 60.8 reduce-scatter.12
  1600.2 85.0 reduce-scatter.14
  1696.9 42.1 reduce-scatter.16

commit v7 on v6

--- a/solution.py
+++ b/solution.py
@@ -4,6 +4,7 @@
 import jax.numpy as jnp
 from jax import lax
 from jax.experimental import pallas as pl
+from jax.experimental.layout import Layout, with_layout_constraint
 from jax.experimental.pallas import tpu as pltpu
 from jax.sharding import PartitionSpec as P
 
@@ -449,7 +450,7 @@
     def from_core(term):
         return lax.ppermute(term.astype(jnp.bfloat16), "ctx", core_route).astype(jnp.float32)
 
-    def backward(grad_out, stored, wait):
+    def backward(grad_out, stored, waits):
         stream, normed, (qkv, lse), attended, hidden_state, normed_two, gate_up, activation = stored
         gate_grad, up_grad = mlp_back(dot_t(both(grad_out), wt_down), gate_up)
         gu_grad = jnp.concatenate([gate_grad, up_grad], axis=1)
@@ -457,8 +458,9 @@
         hidden_grad = grad_out.astype(jnp.float32) + ln_back(hidden_state, two_grad, gain[1])[0]
         ctx_grad = dot_t(both(hidden_grad.astype(jnp.bfloat16)), wt_out).astype(jnp.bfloat16)
         qkv_grad, _ = attn_bwd(qkv, lse, ctx_grad, context, tp_count, chunk)
+        qkv_grad = after(qkv_grad, waits[0])
         one_other = from_core(dot_n(qkv_grad[own_rows:], wt_qkv))
-        one_grad = dot_n(after(qkv_grad[:own_rows], wait), wt_qkv) + one_other
+        one_grad = dot_n(after(qkv_grad[:own_rows], waits[1]), wt_qkv) + one_other
         return (hidden_grad + ln_back(stream, one_grad, gain[0])[0]).astype(jnp.bfloat16)
 
     def settled(term):
@@ -521,12 +523,11 @@
         arriving_up = jnp.concatenate([arriving, across(far_up_b)], axis=0)
         qkv_grad, bias_grad = attn_bwd(qkv, lse, ctx_grad, context, tp_count, chunk)
         qkv_a, qkv_b = (part_of(qkv_grad, i, 2, 1) for i in range(2))
-        far_a = far_term(qkv_a, normed)
-
-        arriving_up, far_a, qkv_a, qkv_b, qkv_grad, up_grad, attn_grad = together(
-            (arriving_up, far_a, qkv_a, qkv_b, qkv_grad, up_grad, attn_grad)
+
+        arriving_up, qkv_a, qkv_b, qkv_grad, up_grad, attn_grad = together(
+            (arriving_up, qkv_a, qkv_b, qkv_grad, up_grad, attn_grad)
         )
-        arriving = across(far_a)
+        arriving = across(far_term(qkv_a, normed))
         sum_up = over_tp(near_total(up_grad, normed_two, arriving_up))
         far_b = far_term(qkv_b, normed)
         one_other = dot_n(qkv_grad[own_rows:], wt_qkv).astype(jnp.bfloat16)
@@ -549,7 +550,8 @@
             ends.reshape(ctx_count * tp_count, piece, width), ("ctx", "tp"), 0, 0, tiled=True
         )
         sum_qkv_b = over_tp(near_total(qkv_b, normed, arriving_b))
-        done = (settled(sum_down), jnp.stack([settled(sum_gate).T, settled(sum_up).T]))
+        grad_gu = jnp.stack([settled(sum_gate).T, settled(sum_up).T])[None]
+        done = (settled(sum_down)[None], with_layout_constraint(grad_gu, Layout((0, 1, 2, 3))))
 
         arriving_out, attn_grad, done, ends = together((arriving_out, attn_grad, done, ends))
         sum_out = over_tp(near_total(attended, attn_grad, arriving_out))
@@ -560,10 +562,10 @@
     sent, _ = forward(inbound.astype(jnp.float32), 2)
     arriving = over_x(sent, [(0, 1)])
     final_out, stored = forward(jnp.where(first, inbound, arriving).astype(jnp.float32), 1)
-    act_across = across(stored[7])
+    act_across = [across(part) for part in split(stored[7], 2)]
     arriving_back = over_x([backward(inbound, stored, act_across)], [(1, 0)])
     arriving_back, final_out, act_both = together(
-        (arriving_back, final_out[0], jnp.concatenate([stored[7], act_across], axis=0))
+        (arriving_back, final_out[0], jnp.concatenate([stored[7], *act_across], axis=0))
     )
     grad_out = jnp.where(first, arriving_back, inbound)
     ends, vectors, grads = last_backward(grad_out, stored, final_out, act_both)
@@ -578,8 +580,8 @@
         vectors[None, 4:],
         grad_qkv.transpose(0, 2, 1)[None],
         grad_out_w[None],
-        grad_gu[None],
-        grad_down[None],
+        grad_gu,
+        grad_down,
     )
 
 

time: 1770 us -> 1770 us (level)
  waiting for transfers between devices: 714 us -> 696 us
    ppermute x9 -> x10, waiting for transfers between devices: 223 us -> 214 us  [across(): lax.ppermute(after(term, *others) if others else term, 'ctx', across_route)]
    reduce_scatter x6 -> x4, waiting for transfers between devices: 37.2 us -> 38 us  [over_tp(): return lax.psum_scatter(term, 'tp', scatter_dimension=0, tiled=True)]
  transfers between devices with their start and end apart: 60 -> 61, of which waited for: 27 -> 28; matrix products, arithmetic and copies ran while one was open for 36% -> 37% of each run, Pallas kernels for 9% -> 9%
where the time goes in v7:
time: 1770 us
  waiting for transfers between devices  696 us (39%)
  matrix products  491 us (28%)
  other arithmetic  191 us (11%)
  Pallas kernels  190 us (11%)
  local copies, waits for them, and re-layouts  122 us (7%)
  starting transfers between devices  46.1 us (3%)
  between operations  31.2 us (2%)
    all_gather x6, waiting for transfers between devices, gathered(): own = lax.all_gather(block, 'tp', axis=0, tiled=True)  255 us
    ppermute x10, waiting for transfers between devices, across(): lax.ppermute(after(term, *others) if others else term, 'ctx', across_route)  214 us
    dot_general x18, matrix products, dot_n(): lax.dot_general(a, b, (((1,), (0,)), ((), ())), preferred_element_type=jn...  207 us
    dot_general x8, matrix products, dot_t(): lax.dot_general(a, b, (((1,), (1,)), ((), ())), preferred_element_type=jn...  185 us
    pallas_call x2, Pallas kernels, attn_bwd(): pl.pallas_call(functools.partial(attn_bwd_kernel, heads, chunk), grid=(gr...  110 us
    dot_general x12, matrix products, dot_0(): lax.dot_general(a, b, (((0,), (0,)), ((), ())), preferred_element_type=jn...  99.5 us
    pallas_call x2, Pallas kernels, attn_fwd(): pl.pallas_call(functools.partial(attn_fwd_kernel, heads, chunk), grid=(gr...  80.6 us
    ppermute x3, waiting for transfers between devices, over_x(): lax.ppermute(part, 'section', route)  57.2 us
  transfers between devices with their start and end apart: 61, of which 28 were waited for; matrix products, arithmetic and copies ran while one was open for 37% of the time, Pallas kernels for 9%

profile of v7, /device:TPU:0, one launch (start us, length us, event | category | flops | bytes accessed | tf_op | source)
XLA Modules:
  0.0 1767.1 jit_solution(13799719677481325209)
XLA Ops:
  40.3 7.4 all-to-all-start
  47.8 29.0 %all-gather.18.cloned.1.call-done = bf16[1,1024,1024]{2,1,0:T(8,128)(2,1)} async-done(((bf16[1,256,1024]{2,1,0:T(8,128)(2,1)}), bf16[1,1024,1024]{2,1,0:T(8,128)(2,1)}) %all-gather.18.cloned.1.call-update) | async-done | bytes 2097168 | tf_op jit(solution)/shard_map/all_gather | solution.py:326
  81.0 9.6 constant_dynamic-slice_fusion.24
  93.2 42.5 %all-to-all-done = bf16[16,32,2048]{2,1,0:T(8,128)(2,1)S(1)} async-done(((bf16[16,32,2048]{2,1,0:T(8,128)(2,1)}), bf16[16,32,2048]{2,1,0:T(8,128)(2,1)S(1)}, u32[]{:S(2)}, u32[]{:S(2)}) %all-to-all-start) | async-done | bytes 2097184 | tf_op jit(solution)/shard_map/all_to_all | solution.py:292
  138.4 66.7 %all-gather.8.cloned.1.call-done = bf16[3072,1024]{1,0:T(8,128)(2,1)} async-done(((bf16[768,1024]{1,0:T(8,128)(2,1)}), bf16[3072,1024]{1,0:T(8,128)(2,1)}) %all-gather.8.cloned.1.call-update) | async-done | bytes 6291472 | tf_op jit(solution)/shard_map/all_gather | solution.py:326
  243.4 68.8 %all-gather.10.cloned.1.call-done = bf16[2816,1024]{1,0:T(8,128)(2,1)} async-done(((bf16[704,1024]{1,0:T(8,128)(2,1)}), bf16[2816,1024]{1,0:T(8,128)(2,1)}) %all-gather.10.cloned.1.call-update) | async-done | bytes 5767184 | tf_op jit(solution)/shard_map/all_gather | solution.py:326
  319.1 11.4 fusion.3
  330.5 22.2 %fusion.49.mixed = f32[1024,3072]{1,0:T(8,128)} fusion(bf16[512,2048]{1,0:T(8,128)(2,1)} %collective-permute-done, bf16[512,2048]{1,0:T(8,128)(2,1)} %fusion.48, bf16[3072,1024]{1,0:T(8,128)(2,1)} %fusion.3, bf16[3072,1024]{1,0:T(8,128)(2,1)} %all-gather.8.cloned.1.call-done, pred[]{:T(512)S(6)} %eq.31), kind=kOutput, calls=%fused_computation.117 | convolution fusion | flops 12949913600 | bytes 29360128 | tf_op jit(solution)/shard_map/dot_general | solution.py:60
  352.6 40.5 %shard_map.170 = (bf16[1024,3072]{1,0:T(8,128)(2,1)}, bf16[1024,1024]{1,0:T(8,128)(2,1)}, f32[4,1024,4]{2,1,0:T(8,128)}) custom-call(f32[1024,3072]{1,0:T(8,128)} %fusion.49.mixed, f32[4,1,768]{2,1,0:T(1,128)} %reshape.402.bias, f32[1024,128]{1,0:T(8,128)} %concatenate.279.cos_t, f32[1024,128]{1,0:T(8,128)} %concatenate.280.low_t, ...), custom_call_target="tpu_custom_call" | custom-call | flops 12884901888 | bytes 22020096 | tf_op jit(solution)/shard_map/pallas_call | solution.py:189
  404.0 9.8 fusion.189
  428.3 12.1 fusion.12
  440.4 7.0 maximum_select_fusion.1
  447.5 30.7 %all-gather.14.cloned.1.call-done = bf16[1408,1024]{1,0:T(8,128)(2,1)} async-done(((bf16[352,1024]{1,0:T(8,128)(2,1)}), bf16[1408,1024]{1,0:T(8,128)(2,1)}) %all-gather.14.cloned.1.call-update) | async-done | bytes 2883600 | tf_op jit(solution)/shard_map/all_gather | solution.py:326
  482.9 54.6 %all-gather.16.cloned.1.call-done = bf16[1408,1024]{1,0:T(8,128)(2,1)} async-done(((bf16[352,1024]{1,0:T(8,128)(2,1)}), bf16[1408,1024]{1,0:T(8,128)(2,1)}) %all-gather.16.cloned.1.call-update) | async-done | bytes 2883600 | tf_op jit(solution)/shard_map/all_gather | solution.py:326
  542.2 11.9 fusion.9
  554.2 7.1 maximum_select_fusion.2
  561.2 34.1 %fusion.53 = f32[1024,5632]{1,0:T(8,128)} fusion(bf16[512,2048]{1,0:T(8,128)(2,1)} %collective-permute-done.7, bf16[512,2048]{1,0:T(8,128)(2,1)} %add_convert_fusion.7, bf16[2816,2048]{1,0:T(8,128)(2,1)} %maximum_select_fusion.2, bf16[2816,2048]{1,0:T(8,128)(2,1)} %maximum_select_fusion.1), kind=kOutput, calls=%fused_computation.126 | convolution fusion | flops 23676846080 | bytes 50331648 | tf_op jit(solution)/shard_map/dot_general | solution.py:60
  595.3 9.4 fusion
  604.7 7.7 collective-permute-done.11
  612.4 8.2 fusion.100
  625.9 9.0 pad_maximum_fusion.1
  653.1 18.8 %collective-permute-done.13 = bf16[256,2048]{1,0:T(8,128)(2,1)S(1)} collective-permute-done((bf16[256,2048]{1,0:T(8,128)(2,1)S(1)}, bf16[256,2048]{1,0:T(8,128)(2,1)S(1)}, u32[]{:S(2)}, u32[]{:S(2)}) %collective-permute-start.13) | collective-permute-done | bytes 1048608 | tf_op jit(solution)/shard_map/ppermute | solution.py:390
  672.1 21.5 %collective-permute-done.15 = bf16[256,2048]{1,0:T(8,128)(2,1)S(1)} collective-permute-done((bf16[256,2048]{1,0:T(8,128)(2,1)S(1)}, bf16[256,2048]{1,0:T(8,128)(2,1)S(1)}, u32[]{:S(2)}, u32[]{:S(2)}) %collective-permute-start.15) | collective-permute-done | bytes 1048608 | tf_op jit(solution)/shard_map/ppermute | solution.py:390
  704.9 22.5 %fusion.44.mixed = f32[1024,3072]{1,0:T(8,128)} fusion(bf16[512,2048]{1,0:T(8,128)(2,1)} %collective-permute-done.16, bf16[512,2048]{1,0:T(8,128)(2,1)} %copy-done.33, bf16[3072,1024]{1,0:T(8,128)(2,1)} %fusion.3, bf16[3072,1024]{1,0:T(8,128)(2,1)} %all-gather.8.cloned.1.call-done, pred[]{:T(512)S(6)} %eq.31), kind=kOutput, calls=%fused_computation.112 | convolution fusion | flops 12949913600 | bytes 29360128 | tf_op jit(solution)/shard_map/dot_general | solution.py:60
  727.4 40.0 %shard_map.171 = (bf16[1024,3072]{1,0:T(8,128)(2,1)}, bf16[1024,1024]{1,0:T(8,128)(2,1)}, f32[4,1024,4]{2,1,0:T(8,128)}) custom-call(f32[1024,3072]{1,0:T(8,128)} %fusion.44.mixed, f32[4,1,768]{2,1,0:T(1,128)} %reshape.402.bias, f32[1024,128]{1,0:T(8,128)} %concatenate.279.cos_t, f32[1024,128]{1,0:T(8,128)} %concatenate.280.low_t, ...), custom_call_target="tpu_custom_call" | custom-call | flops 12884901888 | bytes 22020096 | tf_op jit(solution)/shard_map/pallas_call | solution.py:189
  786.7 33.7 %fusion.43 = f32[1024,5632]{1,0:T(8,128)} fusion(bf16[512,2048]{1,0:T(8,128)(2,1)} %collective-permute-done.19, bf16[512,2048]{1,0:T(8,128)(2,1)} %copy-done.18, bf16[2816,2048]{1,0:T(8,128)(2,1)} %maximum_select_fusion.2, bf16[2816,2048]{1,0:T(8,128)(2,1)} %maximum_select_fusion.1), kind=kOutput, calls=%fused_computation.111 | convolution fusion | flops 23676846080 | bytes 50331648 | tf_op jit(solution)/shard_map/dot_general | solution.py:60
  820.4 26.8 %multiply_convert_fusion.4 = (bf16[1024,2816]{1,0:T(8,128)(2,1)}, bf16[1024,2816]{1,0:T(8,128)(2,1)}, bf16[1024,2816]{1,0:T(8,128)(2,1)}) fusion(f32[1024,5632]{1,0:T(8,128)} %fusion.43, bf16[2816,2048]{1,0:T(8,128)(2,1)} %bitcast.196, bf16[512,2048]{1,0:T(8,128)(2,1)} %collective-permute-done.18, bf16[512,2048]{1,0:T(8,128)(2,1)S(1)} %bitcast.183), kind=kOutput, calls=%fused_computation.28 | convolution fusion | flops 11865686016 | bytes 56098816 | tf_op jit(solution)/shard_map/dot_general | solution.py:60
  847.3 17.1 fusion.94
  868.7 21.8 %fusion.178 = (f32[512]{0:T(512)S(1)}, f32[512]{0:T(512)S(1)}, f32[512,2048]{1,0:T(8,128)}) fusion(f32[512]{0:T(512)S(1)} %add_rsqrt_fusion.2, f32[512,2048]{1,0:T(8,128)} %copy-done.2, f32[512]{0:T(512)S(1)} %broadcast_multiply_fusion.10, f32[2048]{0:T(1024)S(1)} %bitcast.240, bf16[512,2048]{1,0:T(8,128)(2,1)} %collective-permute-done.20, ...), kind=kOutput, calls=%fused_computation.358 | convolution fusion | flops 11877220352 | bytes 45105152 | tf_op jit(solution)/shard_map/dot_general | solution.py:68
  890.5 6.4 fusion.180
  905.6 10.5 fusion.124.ctx
  916.1 54.9 %shard_map.172 = (bf16[1024,3072]{1,0:T(8,128)(2,1)}, f32[4,1,768]{2,1,0:T(1,128)}) custom-call(bf16[1024,3072]{1,0:T(8,128)(2,1)} %get-tuple-element.73.qkv, f32[4,4,1024]{2,1,0:T(4,128)} %bitcast.236, bf16[1024,1024]{1,0:T(8,128)(2,1)} %fusion.124.ctx, f32[1024,128]{1,0:T(8,128)} %concatenate.279.cos_t, f32[1024,128]{1,0:T(8,128)} %concatenate.280.low_t, ...), custom_call_target="tpu_custom_call" | custom-call | flops 3145728 | bytes 3145728 | tf_op jit(solution)/shard_map/pallas_call | solution.py:226
  971.0 16.8 fusion.88
  987.8 10.3 convolution_convert_fusion.8
  1000.7 26.6 %collective-permute-done.23 = bf16[512,2816]{1,0:T(8,128)(2,1)} collective-permute-done((bf16[512,2816]{1,0:T(8,128)(2,1)}, bf16[512,2816]{1,0:T(8,128)(2,1)}, u32[]{:S(2)}, u32[]{:S(2)}) %collective-permute-start.23) | collective-permute-done | bytes 2883616 | tf_op jit(solution)/shard_map/ppermute | solution.py:422
  1027.4 18.4 %fusion.177 = (f32[512]{0:T(512)S(1)}, f32[512]{0:T(512)S(1)}, f32[512,2048]{1,0:T(8,128)}) fusion(f32[512]{0:T(512)S(1)} %copy-done.57, f32[512]{0:T(512)S(1)} %copy-done.54, bf16[512,2048]{1,0:T(8,128)(2,1)S(1)} %copy-done.10, f32[2048]{0:T(1024)S(1)} %bitcast.245, bf16[512,2048]{1,0:T(8,128)(2,1)} %collective-permute-done.24, ...), kind=kOutput, calls=%fused_computation.357 | convolution fusion | flops 6508510208 | bytes 24133632 | tf_op jit(solution)/shard_map/dot_general | solution.py:68
  1050.5 12.9 add_convert_fusion.5
  1063.4 20.7 %pad_maximum_fusion.2 = bf16[2048,2816]{1,0:T(8,128)(2,1)} fusion(bf16[512,2816]{1,0:T(8,128)(2,1)} %collective-permute-done.23, bf16[512,2816]{1,0:T(8,128)(2,1)} %collective-permute-done.22, bf16[1024,2816]{1,0:T(8,128)(2,1)S(1)} %bitcast.187), kind=kLoop, calls=%fused_computation.21 | loop fusion | flops 34603008 | bytes 23068672 | tf_op jit(solution)/shard_map/concatenate | solution.py:568
  1084.2 16.9 collective-permute-done.25
  1106.7 24.5 %multiply_convert_fusion = (bf16[1024,2816]{1,0:T(8,128)(2,1)}, bf16[1024,2816]{1,0:T(8,128)(2,1)}) fusion(f32[1024,5632]{1,0:T(8,128)} %fusion.43, bf16[2816,2048]{1,0:T(8,128)(2,1)} %bitcast.199, bf16[512,2048]{1,0:T(8,128)(2,1)} %collective-permute-done.28, bf16[512,2048]{1,0:T(8,128)(2,1)} %copy-done.7), kind=kOutput, calls=%fused_computation.24 | convolution fusion | flops 11857035264 | bytes 50331648 | tf_op jit(solution)/shard_map/dot_general | solution.py:60
  1131.2 9.2 convolution_convert_fusion.1
  1151.5 19.2 %fusion.95 = bf16[512,2048]{1,0:T(8,128)(2,1)} fusion(bf16[1024,5632]{1,0:T(8,128)(2,1)} %constant_dynamic-update-slice_fusion.3, bf16[2816,2048]{1,0:T(8,128)(2,1)} %maximum_select_fusion.2, bf16[2816,2048]{1,0:T(8,128)(2,1)} %maximum_select_fusion.1), kind=kOutput, calls=%fused_computation.183 | convolution fusion | flops 11858345984 | bytes 30932992 | tf_op jit(solution)/shard_map/dot_general | solution.py:68
  1170.7 17.3 convolution_convert_fusion
  1188.1 21.2 %collective-permute-done.29 = bf16[1408,1024]{1,0:T(8,128)(2,1)} collective-permute-done((bf16[1408,1024]{1,0:T(8,128)(2,1)}, bf16[1408,1024]{1,0:T(8,128)(2,1)}, u32[]{:S(2)}, u32[]{:S(2)}) %collective-permute-start.29) | collective-permute-done | bytes 2883616 | tf_op jit(solution)/shard_map/ppermute | solution.py:422
  1213.8 19.8 %multiply_reduce_fusion = (f32[2048]{0:T(1024)}, f32[512]{0:T(512)S(1)}, f32[512]{0:T(512)S(1)}, f32[2048]{0:T(1024)}, f32[512,2048]{1,0:T(8,128)S(1)}) fusion(f32[512]{0:T(512)S(1)} %copy-done.60, f32[512,2048]{1,0:T(8,128)} %copy-done.2, f32[512]{0:T(512)S(1)} %copy-done.50, f32[2048]{0:T(1024)S(1)} %bitcast.241, ...), kind=kOutput, calls=%fused_computation.151 | convolution fusion | flops 11868827648 | bytes 39354368 | tf_op jit(solution)/shard_map/dot_general | solution.py:68
  1237.0 6.5 convolution_convert_fusion.5
  1248.1 26.6 %collective-permute-done.32 = bf16[1408,1024]{1,0:T(8,128)(2,1)} collective-permute-done((bf16[1408,1024]{1,0:T(8,128)(2,1)}, bf16[1408,1024]{1,0:T(8,128)(2,1)}, u32[]{:S(2)}, u32[]{:S(2)}) %collective-permute-start.32) | collective-permute-done | bytes 2883616 | tf_op jit(solution)/shard_map/ppermute | solution.py:422
  1285.3 9.4 add_convert_fusion.1
  1295.5 10.7 convolution_convert_fusion.11.ctx
  1306.2 53.0 %collective-permute-done.35 = bf16[1408,1024]{1,0:T(8,128)(2,1)} collective-permute-done((bf16[1408,1024]{1,0:T(8,128)(2,1)}, bf16[1408,1024]{1,0:T(8,128)(2,1)}, u32[]{:S(2)}, u32[]{:S(2)}) %collective-permute-start.35) | collective-permute-done | bytes 2883616 | tf_op jit(solution)/shard_map/ppermute | solution.py:422
  1359.8 54.8 %shard_map.173 = (bf16[1024,3072]{1,0:T(8,128)(2,1)}, f32[4,1,768]{2,1,0:T(1,128)}) custom-call(bf16[1024,3072]{1,0:T(8,128)(2,1)} %get-tuple-element.73.qkv, f32[4,4,1024]{2,1,0:T(4,128)} %bitcast.237, bf16[1024,1024]{1,0:T(8,128)(2,1)} %convolution_convert_fusion.11.ctx, f32[1024,128]{1,0:T(8,128)} %concatenate.279.cos_t, f32[1024,128]{1,0:T(8,128)} %concatenate.280.low_t, ...), custom_call_target="tpu_custom_call" | custom-call | flops 3145728 | bytes 3145728 | tf_op jit(solution)/shard_map/pallas_call | solution.py:226
  1426.3 9.5 add_convert_fusion
  1437.4 8.4 convolution_convert_fusion.3
  1446.0 6.8 convolution_convert_fusion.2
  1452.8 13.8 fusion.91
  1466.5 46.7 %collective-permute-done.37 = bf16[1536,1024]{1,0:T(8,128)(2,1)} collective-permute-done((bf16[1536,1024]{1,0:T(8,128)(2,1)}, bf16[1536,1024]{1,0:T(8,128)(2,1)}, u32[]{:S(2)}, u32[]{:S(2)}) %collective-permute-start.37) | collective-permute-done | bytes 3145760 | tf_op jit(solution)/shard_map/ppermute | solution.py:422
  1513.3 6.6 add_convert_fusion.3
  1528.1 19.1 %fusion.40 = (f32[2048]{0:T(1024)S(1)}, f32[512]{0:T(512)S(1)}, f32[512]{0:T(512)S(1)}, f32[2048]{0:T(1024)S(1)}, f32[512,2048]{1,0:T(8,128)}) fusion(bf16[512,2048]{1,0:T(8,128)(2,1)S(1)} %copy-done.11, f32[512]{0:T(512)S(1)} %copy-done.58, f32[512]{0:T(512)S(1)} %copy-done.55, f32[2048]{0:T(1024)S(1)} %bitcast.246, ...), kind=kOutput, calls=%fused_computation.108 | convolution fusion | flops 6511651840 | bytes 24150016 | tf_op jit(solution)/shard_map/dot_general | solution.py:68
  1556.9 35.4 %all-to-all-done.1 = f32[16,7,128]{2,1,0:T(8,128)S(1)} async-done(((f32[16,7,128]{2,1,0:T(8,128)}), f32[16,7,128]{2,1,0:T(8,128)S(1)}, u32[]{:S(2)}, u32[]{:S(2)}) %all-to-all-start.1) | async-done | bytes 57376 | tf_op jit(solution)/shard_map/all_to_all | solution.py:485
  1592.3 8.7 add_convert_fusion.2
  1634.8 39.2 %collective-permute-done.40 = bf16[1024,1024]{1,0:T(8,128)(2,1)} collective-permute-done((bf16[1024,1024]{1,0:T(8,128)(2,1)}, bf16[1024,1024]{1,0:T(8,128)(2,1)}, u32[]{:S(2)}, u32[]{:S(2)}) %collective-permute-start.40) | collective-permute-done | bytes 2097184 | tf_op jit(solution)/shard_map/ppermute | solution.py:422
  1674.0 26.4 %all-to-all-done.2 = bf16[16,32,2048]{2,1,0:T(8,128)(2,1)S(1)} async-done(((bf16[16,32,2048]{2,1,0:T(8,128)(2,1)}), bf16[16,32,2048]{2,1,0:T(8,128)(2,1)S(1)}, u32[]{:S(2)}, u32[]{:S(2)}) %all-to-all-start.2) | async-done | bytes 2097184 | tf_op jit(solution)/shard_map/all_to_all | solution.py:549
  1700.4 6.6 add_convert_fusion.4
  1712.2 38.0 %reduce-scatter.17.cloned.1.call-done = bf16[256,1024]{1,0:T(8,128)(2,1)} async-done(((bf16[1024,1024]{1,0:T(8,128)(2,1)}), bf16[256,1024]{1,0:T(8,128)(2,1)}) %reduce-scatter.17.cloned.1.call-update) | async-done | bytes 524304 | tf_op jit(solution)/shard_map/reduce_scatter | solution.py:425
  (472 shorter events, 302.3 us)
Async XLA Ops:
  7.2 198.0 %copy-start = (f32[1,3,512]{2,0,1:T(1,128)S(1)}, f32[1,3,512]{2,0,1:T(1,128)}, u32[]{:S(2)}) copy-start(f32[1,3,512]{2,0,1:T(1,128)} %param.18) | copy-start | bytes 18436
  7.2 69.6 %all-gather.18.cloned.1.call-start = ((), (), s32[]{:S(2)}) async-start(), calls=%async_computation.18 | async-start | bytes 2621440 | tf_op jit(solution)/shard_map/all_gather | solution.py:326
  9.5 195.5 %all-gather.8.cloned.1.call-start = ((), (), s32[]{:S(2)}) async-start(), calls=%async_computation.9 | async-start | bytes 7864320 | tf_op jit(solution)/shard_map/all_gather | solution.py:326
  40.3 95.4 %all-to-all-start = ((bf16[16,32,2048]{2,1,0:T(8,128)(2,1)}), bf16[16,32,2048]{2,1,0:T(8,128)(2,1)S(1)}, u32[]{:S(2)}, u32[]{:S(2)}) async-start(bf16[16,32,2048]{2,1,0:T(8,128)(2,1)} %bitcast.205), calls=%async_computation | async-start | bytes 4194304 | tf_op jit(solution)/shard_map/all_to_all | solution.py:292
  47.7 264.5 %all-gather.10.cloned.1.call-start = ((), (), s32[]{:S(2)}) async-start(), calls=%async_computation.10 | async-start | bytes 7208960 | tf_op jit(solution)/shard_map/all_gather | solution.py:326
  79.5 56.2 %collective-permute-start.5 = (bf16[768,1024]{1,0:T(8,128)(2,1)}, bf16[768,1024]{1,0:T(8,128)(2,1)}, u32[]{:S(2)}, u32[]{:S(2)}) collective-permute-start(bf16[768,1024]{1,0:T(8,128)(2,1)} %pad_maximum_fusion.21), channel_id=1, source_target_pairs={{0,8},{4,12},{8,0},{12,4},{1,9},{5,13},{9,1},{13,5},{2,10},{6,14},... | collective-permute-start | bytes 4718600 | tf_op jit(solution)/shard_map/ppermute | solution.py:331
  135.7 282.9 %all-gather.12.cloned.1.call-start = ((), (), s32[]{:S(2)}) async-start(), calls=%async_computation.11 | async-start | bytes 7208960 | tf_op jit(solution)/shard_map/all_gather | solution.py:326
  205.1 273.0 %all-gather.14.cloned.1.call-start = ((), (), s32[]{:S(2)}) async-start(), calls=%async_computation.12 | async-start | bytes 3604480 | tf_op jit(solution)/shard_map/all_gather | solution.py:326
  205.2 32.2 %collective-permute-start.2 = (f32[1,768]{1,0:T(1,128)S(1)}, f32[1,768]{1,0:T(1,128)S(1)}, u32[]{:S(2)}, u32[]{:S(2)}) collective-permute-start(f32[1,768]{1,0:T(1,128)S(1)} %bitcast.263), channel_id=1, source_target_pairs={{1,0},{2,1},{3,2},{0,3},{5,4},{6,5},{7,6},{4,7},{9,8},{10,9},{11,1... | collective-permute-start | bytes 9224 | tf_op jit(solution)/shard_map/ppermute | solution.py:370
  206.4 31.0 %collective-permute-start.3 = (f32[1,768]{1,0:T(1,128)S(1)}, f32[1,768]{1,0:T(1,128)S(1)}, u32[]{:S(2)}, u32[]{:S(2)}) collective-permute-start(f32[1,768]{1,0:T(1,128)S(1)} %bitcast.264), channel_id=1, source_target_pairs={{2,0},{3,1},{0,2},{1,3},{6,4},{7,5},{4,6},{5,7},{10,8},{11,9},{8,1... | collective-permute-start | bytes 9224 | tf_op jit(solution)/shard_map/ppermute | solution.py:370
  206.4 31.0 %collective-permute-start.4 = (f32[1,768]{1,0:T(1,128)S(1)}, f32[1,768]{1,0:T(1,128)S(1)}, u32[]{:S(2)}, u32[]{:S(2)}) collective-permute-start(f32[1,768]{1,0:T(1,128)S(1)} %bitcast.265), channel_id=1, source_target_pairs={{3,0},{0,1},{1,2},{2,3},{7,4},{4,5},{5,6},{6,7},{11,8},{8,9},{9,10... | collective-permute-start | bytes 9224 | tf_op jit(solution)/shard_map/ppermute | solution.py:370
  215.3 103.5 %collective-permute-start.1 = (bf16[2304,1024]{1,0:T(8,128)(2,1)}, bf16[2304,1024]{1,0:T(8,128)(2,1)}, u32[]{:S(2)}, u32[]{:S(2)}) collective-permute-start(bf16[2304,1024]{1,0:T(8,128)(2,1)} %pad_maximum_fusion.9), channel_id=1, source_target_pairs={{0,8},{4,12},{8,0},{12,4},{1,9},{5,13},{9,1},{13,5},{2,10},{6,14},... | collective-permute-start | bytes 14155784 | tf_op jit(solution)/shard_map/ppermute | solution.py:331
  221.6 204.6 %copy-start.45 = (f32[1,1,2048]{2,1,0:T(1,128)}, f32[1,1,2048]{2,1,0:T(1,128)S(1)}, u32[]{:S(2)}) copy-start(f32[1,1,2048]{2,1,0:T(1,128)S(1)} %get-tuple-element.208) | copy-start | bytes 24580
  221.6 204.6 %copy-start.38 = (f32[1,1,2048]{2,1,0:T(1,128)}, f32[1,1,2048]{2,1,0:T(1,128)S(1)}, u32[]{:S(2)}) copy-start(f32[1,1,2048]{2,1,0:T(1,128)S(1)} %get-tuple-element.206) | copy-start | bytes 24580
  225.0 105.5 %collective-permute-start = (bf16[512,2048]{1,0:T(8,128)(2,1)}, bf16[512,2048]{1,0:T(8,128)(2,1)}, u32[]{:S(2)}, u32[]{:S(2)}) collective-permute-start(bf16[512,2048]{1,0:T(8,128)(2,1)} %fusion.48), channel_id=1, source_target_pairs={{0,4},{4,0},{8,12},{12,8},{1,5},{5,1},{9,13},{13,9},{2,6},{6,2},{1... | collective-permute-start | bytes 6291464 | tf_op jit(solution)/shard_map/ppermute | solution.py:375
  317.2 96.6 %collective-permute-start.8 = (bf16[2112,1024]{1,0:T(8,128)(2,1)}, bf16[2112,1024]{1,0:T(8,128)(2,1)}, u32[]{:S(2)}, u32[]{:S(2)}) collective-permute-start(bf16[2112,1024]{1,0:T(8,128)(2,1)} %pad_maximum_fusion.10), channel_id=1, source_target_pairs={{0,8},{4,12},{8,0},{12,4},{1,9},{5,13},{9,1},{13,5},{2,10},{6,14},... | collective-permute-start | bytes 12976136 | tf_op jit(solution)/shard_map/ppermute | solution.py:331
  318.8 218.6 %all-gather.16.cloned.1.call-start = ((), (), s32[]{:S(2)}) async-start(), calls=%async_computation.13 | async-start | bytes 3604480 | tf_op jit(solution)/shard_map/all_gather | solution.py:326
  399.5 4.5 collective-permute-start.6
  418.7 1188.3 %reduce-scatter.11.cloned.1.call-start = ((), (), s32[]{:S(2)}) async-start(), calls=%async_computation.14 | async-start | bytes 7208960 | tf_op jit(solution)/shard_map/reduce_scatter | solution.py:425
  424.1 118.1 %collective-permute-start.9 = (bf16[2112,1024]{1,0:T(8,128)(2,1)}, bf16[2112,1024]{1,0:T(8,128)(2,1)}, u32[]{:S(2)}, u32[]{:S(2)}) collective-permute-start(bf16[2112,1024]{1,0:T(8,128)(2,1)} %pad_maximum_fusion.11), channel_id=1, source_target_pairs={{0,8},{4,12},{8,0},{12,4},{1,9},{5,13},{9,1},{13,5},{2,10},{6,14},... | collective-permute-start | bytes 12976136 | tf_op jit(solution)/shard_map/ppermute | solution.py:331
  428.3 132.9 %collective-permute-start.7 = (bf16[512,2048]{1,0:T(8,128)(2,1)}, bf16[512,2048]{1,0:T(8,128)(2,1)}, u32[]{:S(2)}, u32[]{:S(2)}) collective-permute-start(bf16[512,2048]{1,0:T(8,128)(2,1)} %add_convert_fusion.7), channel_id=1, source_target_pairs={{0,4},{4,0},{8,12},{12,8},{1,5},{5,1},{9,13},{13,9},{2,6},{6,2},{1... | collective-permute-start | bytes 6291464 | tf_op jit(solution)/shard_map/ppermute | solution.py:375
  481.4 123.4 %collective-permute-start.10 = (bf16[1056,1024]{1,0:T(8,128)(2,1)}, bf16[1056,1024]{1,0:T(8,128)(2,1)}, u32[]{:S(2)}, u32[]{:S(2)}) collective-permute-start(bf16[1056,1024]{1,0:T(8,128)(2,1)} %pad_maximum_fusion.19), channel_id=1, source_target_pairs={{0,8},{4,12},{8,0},{12,4},{1,9},{5,13},{9,1},{13,5},{2,10},{6,14},... | collective-permute-start | bytes 6488072 | tf_op jit(solution)/shard_map/ppermute | solution.py:331
  540.7 71.7 %collective-permute-start.11 = (bf16[1056,1024]{1,0:T(8,128)(2,1)}, bf16[1056,1024]{1,0:T(8,128)(2,1)}, u32[]{:S(2)}, u32[]{:S(2)}) collective-permute-start(bf16[1056,1024]{1,0:T(8,128)(2,1)} %pad_maximum_fusion.20), channel_id=1, source_target_pairs={{0,8},{4,12},{8,0},{12,4},{1,9},{5,13},{9,1},{13,5},{2,10},{6,14},... | collective-permute-start | bytes 6488072 | tf_op jit(solution)/shard_map/ppermute | solution.py:331
  638.0 3.8 collective-permute-start.12
  641.3 7.3 collective-permute-start.14
  645.1 26.9 %collective-permute-start.13 = (bf16[256,2048]{1,0:T(8,128)(2,1)S(1)}, bf16[256,2048]{1,0:T(8,128)(2,1)S(1)}, u32[]{:S(2)}, u32[]{:S(2)}) collective-permute-start(bf16[256,2048]{1,0:T(8,128)(2,1)S(1)} %fusion.116), channel_id=1, source_target_pairs={{0,16},{1,17},{2,18},{3,19},{4,20},{5,21},{6,22},{7,23},{8,24},{9,... | collective-permute-start | bytes 3145736 | tf_op jit(solution)/shard_map/ppermute | solution.py:390
  651.8 41.7 %collective-permute-start.15 = (bf16[256,2048]{1,0:T(8,128)(2,1)S(1)}, bf16[256,2048]{1,0:T(8,128)(2,1)S(1)}, u32[]{:S(2)}, u32[]{:S(2)}) collective-permute-start(bf16[256,2048]{1,0:T(8,128)(2,1)S(1)} %fusion.115), channel_id=1, source_target_pairs={{0,16},{1,17},{2,18},{3,19},{4,20},{5,21},{6,22},{7,23},{8,24},{9,... | collective-permute-start | bytes 3145736 | tf_op jit(solution)/shard_map/ppermute | solution.py:390
  700.6 4.3 collective-permute-start.16
  773.2 4.2 collective-permute-start.17
  782.4 4.3 collective-permute-start.19
  783.8 36.7 %collective-permute-start.18 = (bf16[512,2048]{1,0:T(8,128)(2,1)S(1)}, bf16[512,2048]{1,0:T(8,128)(2,1)}, u32[]{:S(2)}, u32[]{:S(2)}) collective-permute-start(bf16[512,2048]{1,0:T(8,128)(2,1)S(1)} %bitcast.182), channel_id=1, source_target_pairs={{0,4},{4,0},{8,12},{12,8},{1,5},{5,1},{9,13},{13,9},{2,6},{6,2},{1... | collective-permute-start | bytes 6291464 | tf_op jit(solution)/shard_map/ppermute | solution.py:375
  864.3 4.4 collective-permute-start.20
  896.9 8.7 collective-permute-start.21
  900.7 70.3 %collective-permute-start.22 = (bf16[512,2816]{1,0:T(8,128)(2,1)}, bf16[512,2816]{1,0:T(8,128)(2,1)}, u32[]{:S(2)}, u32[]{:S(2)}) collective-permute-start(bf16[512,2816]{1,0:T(8,128)(2,1)} %get-tuple-element.169), channel_id=1, source_target_pairs={{0,8},{4,12},{8,0},{12,4},{1,9},{5,13},{9,1},{13,5},{2,10},{6,14},... | collective-permute-start | bytes 8650760 | tf_op jit(solution)/shard_map/ppermute | solution.py:422
  905.0 122.3 %collective-permute-start.23 = (bf16[512,2816]{1,0:T(8,128)(2,1)}, bf16[512,2816]{1,0:T(8,128)(2,1)}, u32[]{:S(2)}, u32[]{:S(2)}) collective-permute-start(bf16[512,2816]{1,0:T(8,128)(2,1)} %get-tuple-element.168), channel_id=1, source_target_pairs={{0,8},{4,12},{8,0},{12,4},{1,9},{5,13},{9,1},{13,5},{2,10},{6,14},... | collective-permute-start | bytes 8650760 | tf_op jit(solution)/shard_map/ppermute | solution.py:422
  987.8 39.6 %collective-permute-start.24 = (bf16[512,2048]{1,0:T(8,128)(2,1)}, bf16[512,2048]{1,0:T(8,128)(2,1)}, u32[]{:S(2)}, u32[]{:S(2)}) collective-permute-start(bf16[512,2048]{1,0:T(8,128)(2,1)} %fusion.88), channel_id=1, source_target_pairs={{0,4},{4,0},{8,12},{12,8},{1,5},{5,1},{9,13},{13,9},{2,6},{6,2},{1... | collective-permute-start | bytes 6291464 | tf_op jit(solution)/shard_map/ppermute | solution.py:451
  998.1 52.4 %collective-permute-start.26 = (bf16[512,2048]{1,0:T(8,128)(2,1)}, bf16[512,2048]{1,0:T(8,128)(2,1)}, u32[]{:S(2)}, u32[]{:S(2)}) collective-permute-start(bf16[512,2048]{1,0:T(8,128)(2,1)} %convolution_convert_fusion.8), channel_id=1, source_target_pairs={{0,4},{4,0},{8,12},{12,8},{1,5},{5,1},{9,13},{13,9},{2,6},{6,2},{1... | collective-permute-start | bytes 6291464 | tf_op jit(solution)/shard_map/ppermute | solution.py:381
  1049.2 51.9 %collective-permute-start.25 = (bf16[512,2048]{1,0:T(8,128)(2,1)S(1)}, bf16[512,2048]{1,0:T(8,128)(2,1)S(1)}, u32[]{:S(2)}, u32[]{:S(2)}) collective-permute-start(bf16[512,2048]{1,0:T(8,128)(2,1)S(1)} %fusion.34), channel_id=1, source_target_pairs={{16,0},{17,1},{18,2},{19,3},{20,4},{21,5},{22,6},{23,7},{24,8},{25... | collective-permute-start | bytes 6291464 | tf_op jit(solution)/shard_map/ppermute | solution.py:390
  1101.6 5.1 collective-permute-start.28
  1105.2 35.2 %collective-permute-start.27 = (bf16[512,1024]{1,0:T(8,128)(2,1)}, bf16[512,1024]{1,0:T(8,128)(2,1)}, u32[]{:S(2)}, u32[]{:S(2)}) collective-permute-start(bf16[512,1024]{1,0:T(8,128)(2,1)} %get-tuple-element.187), channel_id=1, source_target_pairs={{0,8},{4,12},{8,0},{12,4},{1,9},{5,13},{9,1},{13,5},{2,10},{6,14},... | collective-permute-start | bytes 3145736 | tf_op jit(solution)/shard_map/ppermute | solution.py:422
  1106.7 64.0 %collective-permute-start.30 = (bf16[512,1024]{1,0:T(8,128)(2,1)S(1)}, bf16[512,1024]{1,0:T(8,128)(2,1)}, u32[]{:S(2)}, u32[]{:S(2)}) collective-permute-start(bf16[512,1024]{1,0:T(8,128)(2,1)S(1)} %get-tuple-element.186), channel_id=1, source_target_pairs={{0,4},{4,0},{8,12},{12,8},{1,5},{5,1},{9,13},{13,9},{2,6},{6,2},{1... | collective-permute-start | bytes 3145736 | tf_op jit(solution)/shard_map/ppermute | solution.py:375
  1144.1 65.2 %collective-permute-start.29 = (bf16[1408,1024]{1,0:T(8,128)(2,1)}, bf16[1408,1024]{1,0:T(8,128)(2,1)}, u32[]{:S(2)}, u32[]{:S(2)}) collective-permute-start(bf16[1408,1024]{1,0:T(8,128)(2,1)} %get-tuple-element.167), channel_id=1, source_target_pairs={{0,8},{4,12},{8,0},{12,4},{1,9},{5,13},{9,1},{13,5},{2,10},{6,14},... | collective-permute-start | bytes 8650760 | tf_op jit(solution)/shard_map/ppermute | solution.py:422
  1148.1 22.7 %collective-permute-start.31 = (bf16[512,1024]{1,0:T(8,128)(2,1)}, bf16[512,1024]{1,0:T(8,128)(2,1)S(1)}, u32[]{:S(2)}, u32[]{:S(2)}) collective-permute-start(bf16[512,1024]{1,0:T(8,128)(2,1)} %collective-permute-done.27), channel_id=1, source_target_pairs={{0,4},{4,0},{8,12},{12,8},{1,5},{5,1},{9,13},{13,9},{2,6},{6,2},{1... | collective-permute-start | bytes 3145736 | tf_op jit(solution)/shard_map/ppermute | solution.py:375
  1209.3 400.2 %reduce-scatter.19.cloned.1.call-start = ((), (), s32[]{:S(2)}) async-start(), calls=%async_computation.19 | async-start | bytes 7208960
  1209.4 4.4 collective-permute-start.33
  1209.4 65.2 %collective-permute-start.32 = (bf16[1408,1024]{1,0:T(8,128)(2,1)}, bf16[1408,1024]{1,0:T(8,128)(2,1)}, u32[]{:S(2)}, u32[]{:S(2)}) collective-permute-start(bf16[1408,1024]{1,0:T(8,128)(2,1)} %get-tuple-element.85), channel_id=1, source_target_pairs={{0,8},{4,12},{8,0},{12,4},{1,9},{5,13},{9,1},{13,5},{2,10},{6,14},... | collective-permute-start | bytes 8650760 | tf_op jit(solution)/shard_map/ppermute | solution.py:422
  1236.9 43.5 %collective-permute-start.34 = (bf16[512,2048]{1,0:T(8,128)(2,1)S(1)}, bf16[512,2048]{1,0:T(8,128)(2,1)S(1)}, u32[]{:S(2)}, u32[]{:S(2)}) collective-permute-start(bf16[512,2048]{1,0:T(8,128)(2,1)S(1)} %get-tuple-element.138), channel_id=1, source_target_pairs={{0,4},{4,0},{8,12},{12,8},{1,5},{5,1},{9,13},{13,9},{2,6},{6,2},{1... | collective-permute-start | bytes 6291464 | tf_op jit(solution)/shard_map/ppermute | solution.py:375
  1294.7 317.6 %reduce-scatter.21.cloned.1.call-start = ((), (), s32[]{:S(2)}) async-start(), calls=%async_computation.20 | async-start | bytes 7208960
  1294.7 64.5 %collective-permute-start.35 = (bf16[1408,1024]{1,0:T(8,128)(2,1)}, bf16[1408,1024]{1,0:T(8,128)(2,1)}, u32[]{:S(2)}, u32[]{:S(2)}) collective-permute-start(bf16[1408,1024]{1,0:T(8,128)(2,1)} %convolution_convert_fusion.5), channel_id=1, source_target_pairs={{0,8},{4,12},{8,0},{12,4},{1,9},{5,13},{9,1},{13,5},{2,10},{6,14},... | collective-permute-start | bytes 8650760 | tf_op jit(solution)/shard_map/ppermute | solution.py:422
  1359.2 63.3 %collective-permute-start.36 = (bf16[1408,1024]{1,0:T(8,128)(2,1)S(1)}, bf16[1408,1024]{1,0:T(8,128)(2,1)}, u32[]{:S(2)}, u32[]{:S(2)}) collective-permute-start(bf16[1408,1024]{1,0:T(8,128)(2,1)S(1)} %copy-done.67), channel_id=1, source_target_pairs={{0,8},{4,12},{8,0},{12,4},{1,9},{5,13},{9,1},{13,5},{2,10},{6,14},... | collective-permute-start | bytes 8650760 | tf_op jit(solution)/shard_map/ppermute | solution.py:422
  1435.8 271.2 %reduce-scatter.13.cloned.1.call-start = ((), (), s32[]{:S(2)}) async-start(), calls=%async_computation.15 | async-start | bytes 3932160 | tf_op jit(solution)/shard_map/reduce_scatter | solution.py:425
  1445.8 67.5 %collective-permute-start.37 = (bf16[1536,1024]{1,0:T(8,128)(2,1)}, bf16[1536,1024]{1,0:T(8,128)(2,1)}, u32[]{:S(2)}, u32[]{:S(2)}) collective-permute-start(bf16[1536,1024]{1,0:T(8,128)(2,1)} %convolution_convert_fusion.3), channel_id=1, source_target_pairs={{0,8},{4,12},{8,0},{12,4},{1,9},{5,13},{9,1},{13,5},{2,10},{6,14},... | collective-permute-start | bytes 9437192 | tf_op jit(solution)/shard_map/ppermute | solution.py:422
  1513.3 14.8 collective-permute-start.39
  1520.8 71.5 %collective-permute-start.38 = (bf16[1536,1024]{1,0:T(8,128)(2,1)}, bf16[1536,1024]{1,0:T(8,128)(2,1)}, u32[]{:S(2)}, u32[]{:S(2)}) collective-permute-start(bf16[1536,1024]{1,0:T(8,128)(2,1)} %convolution_convert_fusion.2), channel_id=1, source_target_pairs={{0,8},{4,12},{8,0},{12,4},{1,9},{5,13},{9,1},{13,5},{2,10},{6,14},... | collective-permute-start | bytes 9437192 | tf_op jit(solution)/shard_map/ppermute | solution.py:422
  1547.9 44.4 %all-to-all-start.1 = ((f32[16,7,128]{2,1,0:T(8,128)}), f32[16,7,128]{2,1,0:T(8,128)S(1)}, u32[]{:S(2)}, u32[]{:S(2)}) async-start(f32[16,7,128]{2,1,0:T(8,128)} %copy.120), calls=%async_computation.1 | async-start | bytes 131072 | tf_op jit(solution)/shard_map/all_to_all | solution.py:485
  1551.4 155.6 %reduce-scatter.15.cloned.1.call-start = ((), (), s32[]{:S(2)}) async-start(), calls=%async_computation.16 | async-start | bytes 3932160 | tf_op jit(solution)/shard_map/reduce_scatter | solution.py:425
  1601.1 99.4 %all-to-all-start.2 = ((bf16[16,32,2048]{2,1,0:T(8,128)(2,1)}), bf16[16,32,2048]{2,1,0:T(8,128)(2,1)S(1)}, u32[]{:S(2)}, u32[]{:S(2)}) async-start(bf16[16,32,2048]{2,1,0:T(8,128)(2,1)} %bitcast.72), calls=%async_computation.3 | async-start | bytes 4194304 | tf_op jit(solution)/shard_map/all_to_all | solution.py:549
  1604.8 145.3 %reduce-scatter.17.cloned.1.call-start = ((), (), s32[]{:S(2)}) async-start(), calls=%async_computation.17 | async-start | bytes 2621440 | tf_op jit(solution)/shard_map/reduce_scatter | solution.py:425
  1605.1 68.9 %collective-permute-start.40 = (bf16[1024,1024]{1,0:T(8,128)(2,1)}, bf16[1024,1024]{1,0:T(8,128)(2,1)}, u32[]{:S(2)}, u32[]{:S(2)}) collective-permute-start(bf16[1024,1024]{1,0:T(8,128)(2,1)} %fusion.121), channel_id=1, source_target_pairs={{0,8},{4,12},{8,0},{12,4},{1,9},{5,13},{9,1},{13,5},{2,10},{6,14},... | collective-permute-start | bytes 6291464 | tf_op jit(solution)/shard_map/ppermute | solution.py:422
  1609.5 5.4 collective-permute-start.41
  1611.8 7.6 collective-permute-start.42
  1614.9 11.9 collective-permute-start.43
  1711.9 42.4 %collective-permute-start.44 = (bf16[3,256,512]{1,2,0:T(8,128)(2,1)}, bf16[3,256,512]{1,2,0:T(8,128)(2,1)}, u32[]{:S(2)}, u32[]{:S(2)}) collective-permute-start(bf16[3,256,512]{1,2,0:T(8,128)(2,1)} %copy.143), channel_id=1, source_target_pairs={{0,4},{4,0},{8,12},{12,8},{1,5},{5,1},{9,13},{13,9},{2,6},{6,2},{1... | collective-permute-start | bytes 2359304 | tf_op jit(solution)/shard_map/ppermute | solution.py:470
  1751.2 6.7 collective-permute-start.45
  (86 other events, 1551.2 us)
Sparse Core Ops, SparseCore 0:
  10.2 66.5 all-gather.17
  78.9 126.1 all-gather.7
  206.7 105.4 all-gather.9
  313.6 104.9 all-gather.11
  420.6 57.4 all-gather.13
  479.6 57.8 all-gather.15
  1209.4 98.6 reduce-scatter.10
  1310.4 102.7 reduce-scatter.18
  1435.9 99.0 reduce-scatter.20
  1537.1 61.7 reduce-scatter.12
  1601.2 94.2 reduce-scatter.14
  1707.1 42.9 reduce-scatter.16

commit v8 on v7

--- a/solution.py
+++ b/solution.py
@@ -450,7 +450,7 @@
     def from_core(term):
         return lax.ppermute(term.astype(jnp.bfloat16), "ctx", core_route).astype(jnp.float32)
 
-    def backward(grad_out, stored, waits):
+    def backward(grad_out, stored, wait):
         stream, normed, (qkv, lse), attended, hidden_state, normed_two, gate_up, activation = stored
         gate_grad, up_grad = mlp_back(dot_t(both(grad_out), wt_down), gate_up)
         gu_grad = jnp.concatenate([gate_grad, up_grad], axis=1)
@@ -458,10 +458,10 @@
         hidden_grad = grad_out.astype(jnp.float32) + ln_back(hidden_state, two_grad, gain[1])[0]
         ctx_grad = dot_t(both(hidden_grad.astype(jnp.bfloat16)), wt_out).astype(jnp.bfloat16)
         qkv_grad, _ = attn_bwd(qkv, lse, ctx_grad, context, tp_count, chunk)
-        qkv_grad = after(qkv_grad, waits[0])
-        one_other = from_core(dot_n(qkv_grad[own_rows:], wt_qkv))
-        one_grad = dot_n(after(qkv_grad[:own_rows], waits[1]), wt_qkv) + one_other
-        return (hidden_grad + ln_back(stream, one_grad, gain[0])[0]).astype(jnp.bfloat16)
+        final_other = dot_n(activation[own_rows:], wt_down).astype(jnp.bfloat16)
+        qkv_grad, final_other = together((qkv_grad, final_other))
+        one_grad = summed(after(qkv_grad, wait), wt_qkv)[0]
+        return (hidden_grad + ln_back(stream, one_grad, gain[0])[0]).astype(jnp.bfloat16), final_other
 
     def settled(term):
         share = half_width // 2
@@ -561,11 +561,13 @@
 
     sent, _ = forward(inbound.astype(jnp.float32), 2)
     arriving = over_x(sent, [(0, 1)])
-    final_out, stored = forward(jnp.where(first, inbound, arriving).astype(jnp.float32), 1)
-    act_across = [across(part) for part in split(stored[7], 2)]
-    arriving_back = over_x([backward(inbound, stored, act_across)], [(1, 0)])
+    _, stored = forward(jnp.where(first, inbound, arriving).astype(jnp.float32), 1)
+    act_across = across(stored[7])
+    sent_back, final_other = backward(inbound, stored, act_across)
+    final_out = stored[4] + dot_n(stored[7][:own_rows], wt_down) + from_core(final_other)
+    arriving_back = over_x([sent_back], [(1, 0)])
     arriving_back, final_out, act_both = together(
-        (arriving_back, final_out[0], jnp.concatenate([stored[7], *act_across], axis=0))
+        (arriving_back, final_out.astype(jnp.bfloat16), jnp.concatenate([stored[7], act_across], axis=0))
     )
     grad_out = jnp.where(first, arriving_back, inbound)
     ends, vectors, grads = last_backward(grad_out, stored, final_out, act_both)

time: 1770 us -> 1760 us (level)
    ppermute x10 -> x9, waiting for transfers between devices: 214 us -> 205 us  [across(): lax.ppermute(after(term, *others) if others else term, 'ctx', across_route)]
  transfers between devices with their start and end apart: 61 -> 60, of which waited for: 28 -> 29; matrix products, arithmetic and copies ran while one was open for 37% -> 37% of each run, Pallas kernels for 9% -> 9%
where the time goes in v8:
time: 1760 us; the launch traced here: 1750 us
  waiting for transfers between devices  704 us (40%)
  matrix products  483 us (27%)
  Pallas kernels  190 us (11%)
  other arithmetic  181 us (10%)
  local copies, waits for them, and re-layouts  117 us (7%)
  starting transfers between devices  46 us (3%)
  between operations  31.5 us (2%)
    all_gather x6, waiting for transfers between devices, gathered(): own = lax.all_gather(block, 'tp', axis=0, tiled=True)  254 us
    ppermute x9, waiting for transfers between devices, across(): lax.ppermute(after(term, *others) if others else term, 'ctx', across_route)  205 us
    dot_general x18, matrix products, dot_n(): lax.dot_general(a, b, (((1,), (0,)), ((), ())), preferred_element_type=jn...  201 us
    dot_general x8, matrix products, dot_t(): lax.dot_general(a, b, (((1,), (1,)), ((), ())), preferred_element_type=jn...  183 us
    pallas_call x2, Pallas kernels, attn_bwd(): pl.pallas_call(functools.partial(attn_bwd_kernel, heads, chunk), grid=(gr...  110 us
    dot_general x12, matrix products, dot_0(): lax.dot_general(a, b, (((0,), (0,)), ((), ())), preferred_element_type=jn...  99.1 us
    pallas_call x2, Pallas kernels, attn_fwd(): pl.pallas_call(functools.partial(attn_fwd_kernel, heads, chunk), grid=(gr...  80.6 us
    ppermute x3, waiting for transfers between devices, over_x(): lax.ppermute(part, 'section', route)  70 us
  transfers between devices with their start and end apart: 60, of which 29 were waited for; matrix products, arithmetic and copies ran while one was open for 37% of the time, Pallas kernels for 9%

profile of v8, /device:TPU:0, one launch (start us, length us, event | category | flops | bytes accessed | tf_op | source)
XLA Modules:
  0.0 1752.1 jit_solution(13454209526700031565)
XLA Ops:
  40.3 7.4 all-to-all-start
  47.8 29.0 %all-gather.18.cloned.1.call-done = bf16[1,1024,1024]{2,1,0:T(8,128)(2,1)} async-done(((bf16[1,256,1024]{2,1,0:T(8,128)(2,1)}), bf16[1,1024,1024]{2,1,0:T(8,128)(2,1)}) %all-gather.18.cloned.1.call-update) | async-done | bytes 2097168 | tf_op jit(solution)/shard_map/all_gather | solution.py:326
  81.0 9.6 constant_dynamic-slice_fusion.24
  93.2 42.5 %all-to-all-done = bf16[16,32,2048]{2,1,0:T(8,128)(2,1)S(1)} async-done(((bf16[16,32,2048]{2,1,0:T(8,128)(2,1)}), bf16[16,32,2048]{2,1,0:T(8,128)(2,1)S(1)}, u32[]{:S(2)}, u32[]{:S(2)}) %all-to-all-start) | async-done | bytes 2097184 | tf_op jit(solution)/shard_map/all_to_all | solution.py:292
  138.4 66.7 %all-gather.8.cloned.1.call-done = bf16[3072,1024]{1,0:T(8,128)(2,1)} async-done(((bf16[768,1024]{1,0:T(8,128)(2,1)}), bf16[3072,1024]{1,0:T(8,128)(2,1)}) %all-gather.8.cloned.1.call-update) | async-done | bytes 6291472 | tf_op jit(solution)/shard_map/all_gather | solution.py:326
  243.5 68.7 %all-gather.10.cloned.1.call-done = bf16[2816,1024]{1,0:T(8,128)(2,1)} async-done(((bf16[704,1024]{1,0:T(8,128)(2,1)}), bf16[2816,1024]{1,0:T(8,128)(2,1)}) %all-gather.10.cloned.1.call-update) | async-done | bytes 5767184 | tf_op jit(solution)/shard_map/all_gather | solution.py:326
  319.2 11.4 fusion.3
  330.6 22.2 %fusion.49.mixed = f32[1024,3072]{1,0:T(8,128)} fusion(bf16[512,2048]{1,0:T(8,128)(2,1)} %collective-permute-done, bf16[512,2048]{1,0:T(8,128)(2,1)} %fusion.48, bf16[3072,1024]{1,0:T(8,128)(2,1)} %fusion.3, bf16[3072,1024]{1,0:T(8,128)(2,1)} %all-gather.8.cloned.1.call-done, pred[]{:T(512)S(6)} %eq.31), kind=kOutput, calls=%fused_computation.117 | convolution fusion | flops 12949913600 | bytes 29360128 | tf_op jit(solution)/shard_map/dot_general | solution.py:60
  352.7 40.6 %shard_map.170 = (bf16[1024,3072]{1,0:T(8,128)(2,1)}, bf16[1024,1024]{1,0:T(8,128)(2,1)}, f32[4,1024,4]{2,1,0:T(8,128)}) custom-call(f32[1024,3072]{1,0:T(8,128)} %fusion.49.mixed, f32[4,1,768]{2,1,0:T(1,128)} %reshape.402.bias, f32[1024,128]{1,0:T(8,128)} %concatenate.279.cos_t, f32[1024,128]{1,0:T(8,128)} %concatenate.280.low_t, ...), custom_call_target="tpu_custom_call" | custom-call | flops 12884901888 | bytes 22020096 | tf_op jit(solution)/shard_map/pallas_call | solution.py:189
  393.3 6.3 convolution_convert_fusion.7
  404.1 9.8 fusion.189
  428.3 12.1 fusion.12
  440.4 7.0 maximum_select_fusion.1
  447.5 30.7 %all-gather.14.cloned.1.call-done = bf16[1408,1024]{1,0:T(8,128)(2,1)} async-done(((bf16[352,1024]{1,0:T(8,128)(2,1)}), bf16[1408,1024]{1,0:T(8,128)(2,1)}) %all-gather.14.cloned.1.call-update) | async-done | bytes 2883600 | tf_op jit(solution)/shard_map/all_gather | solution.py:326
  482.9 54.6 %all-gather.16.cloned.1.call-done = bf16[1408,1024]{1,0:T(8,128)(2,1)} async-done(((bf16[352,1024]{1,0:T(8,128)(2,1)}), bf16[1408,1024]{1,0:T(8,128)(2,1)}) %all-gather.16.cloned.1.call-update) | async-done | bytes 2883600 | tf_op jit(solution)/shard_map/all_gather | solution.py:326
  542.2 11.9 fusion.9
  554.2 7.1 maximum_select_fusion.2
  561.2 34.1 %fusion.53 = f32[1024,5632]{1,0:T(8,128)} fusion(bf16[512,2048]{1,0:T(8,128)(2,1)} %collective-permute-done.7, bf16[512,2048]{1,0:T(8,128)(2,1)} %add_convert_fusion.7, bf16[2816,2048]{1,0:T(8,128)(2,1)} %maximum_select_fusion.2, bf16[2816,2048]{1,0:T(8,128)(2,1)} %maximum_select_fusion.1), kind=kOutput, calls=%fused_computation.126 | convolution fusion | flops 23676846080 | bytes 50331648 | tf_op jit(solution)/shard_map/dot_general | solution.py:60
  595.3 9.4 fusion
  604.7 7.7 collective-permute-done.11
  612.4 8.2 fusion.104
  625.9 9.0 pad_maximum_fusion.1
  653.1 18.8 %collective-permute-done.13 = bf16[256,2048]{1,0:T(8,128)(2,1)S(1)} collective-permute-done((bf16[256,2048]{1,0:T(8,128)(2,1)S(1)}, bf16[256,2048]{1,0:T(8,128)(2,1)S(1)}, u32[]{:S(2)}, u32[]{:S(2)}) %collective-permute-start.13) | collective-permute-done | bytes 1048608 | tf_op jit(solution)/shard_map/ppermute | solution.py:390
  672.1 21.5 %collective-permute-done.15 = bf16[256,2048]{1,0:T(8,128)(2,1)S(1)} collective-permute-done((bf16[256,2048]{1,0:T(8,128)(2,1)S(1)}, bf16[256,2048]{1,0:T(8,128)(2,1)S(1)}, u32[]{:S(2)}, u32[]{:S(2)}) %collective-permute-start.15) | collective-permute-done | bytes 1048608 | tf_op jit(solution)/shard_map/ppermute | solution.py:390
  704.9 22.5 %fusion.44.mixed = f32[1024,3072]{1,0:T(8,128)} fusion(bf16[512,2048]{1,0:T(8,128)(2,1)} %collective-permute-done.16, bf16[512,2048]{1,0:T(8,128)(2,1)} %copy-done.33, bf16[3072,1024]{1,0:T(8,128)(2,1)} %fusion.3, bf16[3072,1024]{1,0:T(8,128)(2,1)} %all-gather.8.cloned.1.call-done, pred[]{:T(512)S(6)} %eq.31), kind=kOutput, calls=%fused_computation.112 | convolution fusion | flops 12949913600 | bytes 29360128 | tf_op jit(solution)/shard_map/dot_general | solution.py:60
  727.4 40.0 %shard_map.171 = (bf16[1024,3072]{1,0:T(8,128)(2,1)}, bf16[1024,1024]{1,0:T(8,128)(2,1)}, f32[4,1024,4]{2,1,0:T(8,128)}) custom-call(f32[1024,3072]{1,0:T(8,128)} %fusion.44.mixed, f32[4,1,768]{2,1,0:T(1,128)} %reshape.402.bias, f32[1024,128]{1,0:T(8,128)} %concatenate.279.cos_t, f32[1024,128]{1,0:T(8,128)} %concatenate.280.low_t, ...), custom_call_target="tpu_custom_call" | custom-call | flops 12884901888 | bytes 22020096 | tf_op jit(solution)/shard_map/pallas_call | solution.py:189
  786.7 33.7 %fusion.43 = f32[1024,5632]{1,0:T(8,128)} fusion(bf16[512,2048]{1,0:T(8,128)(2,1)} %collective-permute-done.19, bf16[512,2048]{1,0:T(8,128)(2,1)} %copy-done.17, bf16[2816,2048]{1,0:T(8,128)(2,1)} %maximum_select_fusion.2, bf16[2816,2048]{1,0:T(8,128)(2,1)} %maximum_select_fusion.1), kind=kOutput, calls=%fused_computation.111 | convolution fusion | flops 23676846080 | bytes 50331648 | tf_op jit(solution)/shard_map/dot_general | solution.py:60
  820.4 26.8 %multiply_convert_fusion.4 = (bf16[1024,2816]{1,0:T(8,128)(2,1)}, bf16[1024,2816]{1,0:T(8,128)(2,1)}, bf16[1024,2816]{1,0:T(8,128)(2,1)}) fusion(f32[1024,5632]{1,0:T(8,128)} %fusion.43, bf16[2816,2048]{1,0:T(8,128)(2,1)} %bitcast.193, bf16[512,2048]{1,0:T(8,128)(2,1)} %collective-permute-done.18, bf16[512,2048]{1,0:T(8,128)(2,1)S(1)} %bitcast.182), kind=kOutput, calls=%fused_computation.28 | convolution fusion | flops 11865686016 | bytes 56098816 | tf_op jit(solution)/shard_map/dot_general | solution.py:60
  847.2 17.1 fusion.98
  868.6 21.8 %fusion.179 = (f32[512]{0:T(512)S(1)}, f32[512]{0:T(512)S(1)}, f32[512,2048]{1,0:T(8,128)}) fusion(f32[512]{0:T(512)S(1)} %add_rsqrt_fusion.2, f32[512,2048]{1,0:T(8,128)} %copy-done.2, f32[512]{0:T(512)S(1)} %broadcast_multiply_fusion.10, f32[2048]{0:T(1024)S(1)} %bitcast.239, bf16[512,2048]{1,0:T(8,128)(2,1)} %collective-permute-done.20, ...), kind=kOutput, calls=%fused_computation.359 | convolution fusion | flops 11877220352 | bytes 45105152 | tf_op jit(solution)/shard_map/dot_general | solution.py:68
  899.4 10.9 convolution_convert_fusion.8
  910.4 8.1 fusion.130.ctx
  918.5 54.7 %shard_map.172 = (bf16[1024,3072]{1,0:T(8,128)(2,1)}, f32[4,1,768]{2,1,0:T(1,128)}) custom-call(bf16[1024,3072]{1,0:T(8,128)(2,1)} %get-tuple-element.74.qkv, f32[4,4,1024]{2,1,0:T(4,128)} %bitcast.235, bf16[1024,1024]{1,0:T(8,128)(2,1)} %fusion.130.ctx, f32[1024,128]{1,0:T(8,128)} %concatenate.279.cos_t, f32[1024,128]{1,0:T(8,128)} %concatenate.280.low_t, ...), custom_call_target="tpu_custom_call" | custom-call | flops 3145728 | bytes 3145728 | tf_op jit(solution)/shard_map/pallas_call | solution.py:226
  973.3 18.1 %collective-permute-done.22 = bf16[1024,2816]{1,0:T(8,128)(2,1)} collective-permute-done((bf16[1024,2816]{1,0:T(8,128)(2,1)}, bf16[1024,2816]{1,0:T(8,128)(2,1)}, u32[]{:S(2)}, u32[]{:S(2)}) %collective-permute-start.22) | collective-permute-done | bytes 5767200 | tf_op jit(solution)/shard_map/ppermute | solution.py:422
  991.3 15.5 fusion.92
  1013.4 16.7 fusion.178
  1034.2 12.2 pad_maximum_fusion.2
  1046.5 9.7 add_convert_fusion.5
  1056.2 29.7 %collective-permute-done.24 = bf16[512,2048]{1,0:T(8,128)(2,1)S(1)} collective-permute-done((bf16[512,2048]{1,0:T(8,128)(2,1)}, bf16[512,2048]{1,0:T(8,128)(2,1)S(1)}, u32[]{:S(2)}, u32[]{:S(2)}) %collective-permute-start.24) | collective-permute-done | bytes 2097184 | tf_op jit(solution)/shard_map/ppermute | solution.py:390
  1091.5 24.5 %multiply_convert_fusion = (bf16[1024,2816]{1,0:T(8,128)(2,1)}, bf16[1024,2816]{1,0:T(8,128)(2,1)}) fusion(f32[1024,5632]{1,0:T(8,128)} %fusion.43, bf16[2816,2048]{1,0:T(8,128)(2,1)} %bitcast.195, bf16[512,2048]{1,0:T(8,128)(2,1)} %collective-permute-done.27, bf16[512,2048]{1,0:T(8,128)(2,1)} %copy-done.6), kind=kOutput, calls=%fused_computation.24 | convolution fusion | flops 11857035264 | bytes 50331648 | tf_op jit(solution)/shard_map/dot_general | solution.py:60
  1116.0 9.1 convolution_convert_fusion.1
  1136.1 19.4 %fusion.99 = bf16[512,2048]{1,0:T(8,128)(2,1)} fusion(bf16[1024,5632]{1,0:T(8,128)(2,1)} %constant_dynamic-update-slice_fusion.3, bf16[2816,2048]{1,0:T(8,128)(2,1)} %maximum_select_fusion.2, bf16[2816,2048]{1,0:T(8,128)(2,1)} %maximum_select_fusion.1), kind=kOutput, calls=%fused_computation.185 | convolution fusion | flops 11858345984 | bytes 30932992 | tf_op jit(solution)/shard_map/dot_general | solution.py:68
  1155.5 17.4 convolution_convert_fusion
  1172.9 21.0 %collective-permute-done.28 = bf16[1408,1024]{1,0:T(8,128)(2,1)} collective-permute-done((bf16[1408,1024]{1,0:T(8,128)(2,1)}, bf16[1408,1024]{1,0:T(8,128)(2,1)}, u32[]{:S(2)}, u32[]{:S(2)}) %collective-permute-start.28) | collective-permute-done | bytes 2883616 | tf_op jit(solution)/shard_map/ppermute | solution.py:422
  1198.4 19.7 %multiply_reduce_fusion = (f32[2048]{0:T(1024)}, f32[512]{0:T(512)S(1)}, f32[512]{0:T(512)S(1)}, f32[2048]{0:T(1024)}, f32[512,2048]{1,0:T(8,128)S(1)}) fusion(f32[512]{0:T(512)S(1)} %copy-done.60, f32[512,2048]{1,0:T(8,128)} %copy-done.2, f32[512]{0:T(512)S(1)} %copy-done.50, f32[2048]{0:T(1024)S(1)} %bitcast.240, ...), kind=kOutput, calls=%fused_computation.151 | convolution fusion | flops 11868827648 | bytes 39354368 | tf_op jit(solution)/shard_map/dot_general | solution.py:68
  1221.5 6.5 convolution_convert_fusion.5
  1232.5 26.8 %collective-permute-done.31 = bf16[1408,1024]{1,0:T(8,128)(2,1)} collective-permute-done((bf16[1408,1024]{1,0:T(8,128)(2,1)}, bf16[1408,1024]{1,0:T(8,128)(2,1)}, u32[]{:S(2)}, u32[]{:S(2)}) %collective-permute-start.31) | collective-permute-done | bytes 2883616 | tf_op jit(solution)/shard_map/ppermute | solution.py:422
  1269.9 9.4 add_convert_fusion.1
  1280.1 10.7 convolution_convert_fusion.11.ctx
  1290.8 53.0 %collective-permute-done.34 = bf16[1408,1024]{1,0:T(8,128)(2,1)} collective-permute-done((bf16[1408,1024]{1,0:T(8,128)(2,1)}, bf16[1408,1024]{1,0:T(8,128)(2,1)}, u32[]{:S(2)}, u32[]{:S(2)}) %collective-permute-start.34) | collective-permute-done | bytes 2883616 | tf_op jit(solution)/shard_map/ppermute | solution.py:422
  1344.5 55.0 %shard_map.173 = (bf16[1024,3072]{1,0:T(8,128)(2,1)}, f32[4,1,768]{2,1,0:T(1,128)}) custom-call(bf16[1024,3072]{1,0:T(8,128)(2,1)} %get-tuple-element.74.qkv, f32[4,4,1024]{2,1,0:T(4,128)} %bitcast.236, bf16[1024,1024]{1,0:T(8,128)(2,1)} %convolution_convert_fusion.11.ctx, f32[1024,128]{1,0:T(8,128)} %concatenate.279.cos_t, f32[1024,128]{1,0:T(8,128)} %concatenate.280.low_t, ...), custom_call_target="tpu_custom_call" | custom-call | flops 3145728 | bytes 3145728 | tf_op jit(solution)/shard_map/pallas_call | solution.py:226
  1411.1 9.5 add_convert_fusion
  1422.2 8.4 convolution_convert_fusion.3
  1430.8 6.5 convolution_convert_fusion.2
  1437.4 13.7 fusion.95
  1451.1 46.9 %collective-permute-done.36 = bf16[1536,1024]{1,0:T(8,128)(2,1)} collective-permute-done((bf16[1536,1024]{1,0:T(8,128)(2,1)}, bf16[1536,1024]{1,0:T(8,128)(2,1)}, u32[]{:S(2)}, u32[]{:S(2)}) %collective-permute-start.36) | collective-permute-done | bytes 3145760 | tf_op jit(solution)/shard_map/ppermute | solution.py:422
  1498.0 6.6 add_convert_fusion.3
  1513.0 19.1 %fusion.40 = (f32[2048]{0:T(1024)S(1)}, f32[512]{0:T(512)S(1)}, f32[512]{0:T(512)S(1)}, f32[2048]{0:T(1024)S(1)}, f32[512,2048]{1,0:T(8,128)}) fusion(bf16[512,2048]{1,0:T(8,128)(2,1)S(1)} %copy-done.10, f32[512]{0:T(512)S(1)} %copy-done.58, f32[512]{0:T(512)S(1)} %copy-done.55, f32[2048]{0:T(1024)S(1)} %bitcast.245, ...), kind=kOutput, calls=%fused_computation.108 | convolution fusion | flops 6511651840 | bytes 24150016 | tf_op jit(solution)/shard_map/dot_general | solution.py:68
  1541.8 35.1 %all-to-all-done.1 = f32[16,7,128]{2,1,0:T(8,128)S(1)} async-done(((f32[16,7,128]{2,1,0:T(8,128)}), f32[16,7,128]{2,1,0:T(8,128)S(1)}, u32[]{:S(2)}, u32[]{:S(2)}) %all-to-all-start.1) | async-done | bytes 57376 | tf_op jit(solution)/shard_map/all_to_all | solution.py:485
  1577.0 8.7 add_convert_fusion.2
  1619.6 39.1 %collective-permute-done.39 = bf16[1024,1024]{1,0:T(8,128)(2,1)} collective-permute-done((bf16[1024,1024]{1,0:T(8,128)(2,1)}, bf16[1024,1024]{1,0:T(8,128)(2,1)}, u32[]{:S(2)}, u32[]{:S(2)}) %collective-permute-start.39) | collective-permute-done | bytes 2097184 | tf_op jit(solution)/shard_map/ppermute | solution.py:422
  1658.7 26.4 %all-to-all-done.2 = bf16[16,32,2048]{2,1,0:T(8,128)(2,1)S(1)} async-done(((bf16[16,32,2048]{2,1,0:T(8,128)(2,1)}), bf16[16,32,2048]{2,1,0:T(8,128)(2,1)S(1)}, u32[]{:S(2)}, u32[]{:S(2)}) %all-to-all-start.2) | async-done | bytes 2097184 | tf_op jit(solution)/shard_map/all_to_all | solution.py:549
  1685.1 6.6 add_convert_fusion.4
  1696.9 38.0 %reduce-scatter.17.cloned.1.call-done = bf16[256,1024]{1,0:T(8,128)(2,1)} async-done(((bf16[1024,1024]{1,0:T(8,128)(2,1)}), bf16[256,1024]{1,0:T(8,128)(2,1)}) %reduce-scatter.17.cloned.1.call-update) | async-done | bytes 524304 | tf_op jit(solution)/shard_map/reduce_scatter | solution.py:425
  (470 shorter events, 299.9 us)
Async XLA Ops:
  7.2 198.0 %copy-start = (f32[1,3,512]{2,0,1:T(1,128)S(1)}, f32[1,3,512]{2,0,1:T(1,128)}, u32[]{:S(2)}) copy-start(f32[1,3,512]{2,0,1:T(1,128)} %param.18) | copy-start | bytes 18436
  7.2 69.6 %all-gather.18.cloned.1.call-start = ((), (), s32[]{:S(2)}) async-start(), calls=%async_computation.18 | async-start | bytes 2621440 | tf_op jit(solution)/shard_map/all_gather | solution.py:326
  9.5 195.5 %all-gather.8.cloned.1.call-start = ((), (), s32[]{:S(2)}) async-start(), calls=%async_computation.9 | async-start | bytes 7864320 | tf_op jit(solution)/shard_map/all_gather | solution.py:326
  40.3 95.4 %all-to-all-start = ((bf16[16,32,2048]{2,1,0:T(8,128)(2,1)}), bf16[16,32,2048]{2,1,0:T(8,128)(2,1)S(1)}, u32[]{:S(2)}, u32[]{:S(2)}) async-start(bf16[16,32,2048]{2,1,0:T(8,128)(2,1)} %bitcast.204), calls=%async_computation | async-start | bytes 4194304 | tf_op jit(solution)/shard_map/all_to_all | solution.py:292
  47.7 264.5 %all-gather.10.cloned.1.call-start = ((), (), s32[]{:S(2)}) async-start(), calls=%async_computation.10 | async-start | bytes 7208960 | tf_op jit(solution)/shard_map/all_gather | solution.py:326
  79.5 56.2 %collective-permute-start.5 = (bf16[768,1024]{1,0:T(8,128)(2,1)}, bf16[768,1024]{1,0:T(8,128)(2,1)}, u32[]{:S(2)}, u32[]{:S(2)}) collective-permute-start(bf16[768,1024]{1,0:T(8,128)(2,1)} %pad_maximum_fusion.21), channel_id=1, source_target_pairs={{0,8},{4,12},{8,0},{12,4},{1,9},{5,13},{9,1},{13,5},{2,10},{6,14},... | collective-permute-start | bytes 4718600 | tf_op jit(solution)/shard_map/ppermute | solution.py:331
  90.6 117.3 %copy-start.65 = (s32[1,1024]{1,0:T(1,128)S(1)}, s32[1,1024]{1,0:T(1,128)}, u32[]{:S(2)}) copy-start(s32[1,1024]{1,0:T(1,128)} %param.14) | copy-start | bytes 12292
  135.7 282.9 %all-gather.12.cloned.1.call-start = ((), (), s32[]{:S(2)}) async-start(), calls=%async_computation.11 | async-start | bytes 7208960 | tf_op jit(solution)/shard_map/all_gather | solution.py:326
  205.1 273.0 %all-gather.14.cloned.1.call-start = ((), (), s32[]{:S(2)}) async-start(), calls=%async_computation.12 | async-start | bytes 3604480 | tf_op jit(solution)/shard_map/all_gather | solution.py:326
  205.2 32.2 %collective-permute-start.2 = (f32[1,768]{1,0:T(1,128)S(1)}, f32[1,768]{1,0:T(1,128)S(1)}, u32[]{:S(2)}, u32[]{:S(2)}) collective-permute-start(f32[1,768]{1,0:T(1,128)S(1)} %bitcast.262), channel_id=1, source_target_pairs={{1,0},{2,1},{3,2},{0,3},{5,4},{6,5},{7,6},{4,7},{9,8},{10,9},{11,1... | collective-permute-start | bytes 9224 | tf_op jit(solution)/shard_map/ppermute | solution.py:370
  206.4 31.1 %collective-permute-start.3 = (f32[1,768]{1,0:T(1,128)S(1)}, f32[1,768]{1,0:T(1,128)S(1)}, u32[]{:S(2)}, u32[]{:S(2)}) collective-permute-start(f32[1,768]{1,0:T(1,128)S(1)} %bitcast.263), channel_id=1, source_target_pairs={{2,0},{3,1},{0,2},{1,3},{6,4},{7,5},{4,6},{5,7},{10,8},{11,9},{8,1... | collective-permute-start | bytes 9224 | tf_op jit(solution)/shard_map/ppermute | solution.py:370
  206.4 31.1 %collective-permute-start.4 = (f32[1,768]{1,0:T(1,128)S(1)}, f32[1,768]{1,0:T(1,128)S(1)}, u32[]{:S(2)}, u32[]{:S(2)}) collective-permute-start(f32[1,768]{1,0:T(1,128)S(1)} %bitcast.264), channel_id=1, source_target_pairs={{3,0},{0,1},{1,2},{2,3},{7,4},{4,5},{5,6},{6,7},{11,8},{8,9},{9,10... | collective-permute-start | bytes 9224 | tf_op jit(solution)/shard_map/ppermute | solution.py:370
  215.4 103.5 %collective-permute-start.1 = (bf16[2304,1024]{1,0:T(8,128)(2,1)}, bf16[2304,1024]{1,0:T(8,128)(2,1)}, u32[]{:S(2)}, u32[]{:S(2)}) collective-permute-start(bf16[2304,1024]{1,0:T(8,128)(2,1)} %pad_maximum_fusion.9), channel_id=1, source_target_pairs={{0,8},{4,12},{8,0},{12,4},{1,9},{5,13},{9,1},{13,5},{2,10},{6,14},... | collective-permute-start | bytes 14155784 | tf_op jit(solution)/shard_map/ppermute | solution.py:331
  221.6 204.5 %copy-start.45 = (f32[1,1,2048]{2,1,0:T(1,128)}, f32[1,1,2048]{2,1,0:T(1,128)S(1)}, u32[]{:S(2)}) copy-start(f32[1,1,2048]{2,1,0:T(1,128)S(1)} %get-tuple-element.208) | copy-start | bytes 24580
  221.7 204.5 %copy-start.38 = (f32[1,1,2048]{2,1,0:T(1,128)}, f32[1,1,2048]{2,1,0:T(1,128)S(1)}, u32[]{:S(2)}) copy-start(f32[1,1,2048]{2,1,0:T(1,128)S(1)} %get-tuple-element.206) | copy-start | bytes 24580
  225.1 105.5 %collective-permute-start = (bf16[512,2048]{1,0:T(8,128)(2,1)}, bf16[512,2048]{1,0:T(8,128)(2,1)}, u32[]{:S(2)}, u32[]{:S(2)}) collective-permute-start(bf16[512,2048]{1,0:T(8,128)(2,1)} %fusion.48), channel_id=1, source_target_pairs={{0,4},{4,0},{8,12},{12,8},{1,5},{5,1},{9,13},{13,9},{2,6},{6,2},{1... | collective-permute-start | bytes 6291464 | tf_op jit(solution)/shard_map/ppermute | solution.py:375
  317.2 96.8 %collective-permute-start.8 = (bf16[2112,1024]{1,0:T(8,128)(2,1)}, bf16[2112,1024]{1,0:T(8,128)(2,1)}, u32[]{:S(2)}, u32[]{:S(2)}) collective-permute-start(bf16[2112,1024]{1,0:T(8,128)(2,1)} %pad_maximum_fusion.10), channel_id=1, source_target_pairs={{0,8},{4,12},{8,0},{12,4},{1,9},{5,13},{9,1},{13,5},{2,10},{6,14},... | collective-permute-start | bytes 12976136 | tf_op jit(solution)/shard_map/ppermute | solution.py:331
  318.9 218.6 %all-gather.16.cloned.1.call-start = ((), (), s32[]{:S(2)}) async-start(), calls=%async_computation.13 | async-start | bytes 3604480 | tf_op jit(solution)/shard_map/all_gather | solution.py:326
  399.6 4.5 collective-permute-start.6
  418.7 1173.1 %reduce-scatter.11.cloned.1.call-start = ((), (), s32[]{:S(2)}) async-start(), calls=%async_computation.14 | async-start | bytes 7208960 | tf_op jit(solution)/shard_map/reduce_scatter | solution.py:425
  424.1 118.1 %collective-permute-start.9 = (bf16[2112,1024]{1,0:T(8,128)(2,1)}, bf16[2112,1024]{1,0:T(8,128)(2,1)}, u32[]{:S(2)}, u32[]{:S(2)}) collective-permute-start(bf16[2112,1024]{1,0:T(8,128)(2,1)} %pad_maximum_fusion.11), channel_id=1, source_target_pairs={{0,8},{4,12},{8,0},{12,4},{1,9},{5,13},{9,1},{13,5},{2,10},{6,14},... | collective-permute-start | bytes 12976136 | tf_op jit(solution)/shard_map/ppermute | solution.py:331
  428.3 132.9 %collective-permute-start.7 = (bf16[512,2048]{1,0:T(8,128)(2,1)}, bf16[512,2048]{1,0:T(8,128)(2,1)}, u32[]{:S(2)}, u32[]{:S(2)}) collective-permute-start(bf16[512,2048]{1,0:T(8,128)(2,1)} %add_convert_fusion.7), channel_id=1, source_target_pairs={{0,4},{4,0},{8,12},{12,8},{1,5},{5,1},{9,13},{13,9},{2,6},{6,2},{1... | collective-permute-start | bytes 6291464 | tf_op jit(solution)/shard_map/ppermute | solution.py:375
  481.4 123.4 %collective-permute-start.10 = (bf16[1056,1024]{1,0:T(8,128)(2,1)}, bf16[1056,1024]{1,0:T(8,128)(2,1)}, u32[]{:S(2)}, u32[]{:S(2)}) collective-permute-start(bf16[1056,1024]{1,0:T(8,128)(2,1)} %pad_maximum_fusion.19), channel_id=1, source_target_pairs={{0,8},{4,12},{8,0},{12,4},{1,9},{5,13},{9,1},{13,5},{2,10},{6,14},... | collective-permute-start | bytes 6488072 | tf_op jit(solution)/shard_map/ppermute | solution.py:331
  540.7 71.7 %collective-permute-start.11 = (bf16[1056,1024]{1,0:T(8,128)(2,1)}, bf16[1056,1024]{1,0:T(8,128)(2,1)}, u32[]{:S(2)}, u32[]{:S(2)}) collective-permute-start(bf16[1056,1024]{1,0:T(8,128)(2,1)} %pad_maximum_fusion.20), channel_id=1, source_target_pairs={{0,8},{4,12},{8,0},{12,4},{1,9},{5,13},{9,1},{13,5},{2,10},{6,14},... | collective-permute-start | bytes 6488072 | tf_op jit(solution)/shard_map/ppermute | solution.py:331
  638.0 3.8 collective-permute-start.12
  641.3 7.3 collective-permute-start.14
  645.1 26.9 %collective-permute-start.13 = (bf16[256,2048]{1,0:T(8,128)(2,1)S(1)}, bf16[256,2048]{1,0:T(8,128)(2,1)S(1)}, u32[]{:S(2)}, u32[]{:S(2)}) collective-permute-start(bf16[256,2048]{1,0:T(8,128)(2,1)S(1)} %fusion.122), channel_id=1, source_target_pairs={{0,16},{1,17},{2,18},{3,19},{4,20},{5,21},{6,22},{7,23},{8,24},{9,... | collective-permute-start | bytes 3145736 | tf_op jit(solution)/shard_map/ppermute | solution.py:390
  651.8 41.7 %collective-permute-start.15 = (bf16[256,2048]{1,0:T(8,128)(2,1)S(1)}, bf16[256,2048]{1,0:T(8,128)(2,1)S(1)}, u32[]{:S(2)}, u32[]{:S(2)}) collective-permute-start(bf16[256,2048]{1,0:T(8,128)(2,1)S(1)} %fusion.121), channel_id=1, source_target_pairs={{0,16},{1,17},{2,18},{3,19},{4,20},{5,21},{6,22},{7,23},{8,24},{9,... | collective-permute-start | bytes 3145736 | tf_op jit(solution)/shard_map/ppermute | solution.py:390
  700.6 4.3 collective-permute-start.16
  773.1 4.2 collective-permute-start.17
  782.4 4.3 collective-permute-start.19
  783.7 36.7 %collective-permute-start.18 = (bf16[512,2048]{1,0:T(8,128)(2,1)S(1)}, bf16[512,2048]{1,0:T(8,128)(2,1)}, u32[]{:S(2)}, u32[]{:S(2)}) collective-permute-start(bf16[512,2048]{1,0:T(8,128)(2,1)S(1)} %bitcast.181), channel_id=1, source_target_pairs={{0,4},{4,0},{8,12},{12,8},{1,5},{5,1},{9,13},{13,9},{2,6},{6,2},{1... | collective-permute-start | bytes 6291464 | tf_op jit(solution)/shard_map/ppermute | solution.py:375
  864.3 4.4 collective-permute-start.20
  864.5 126.9 %collective-permute-start.22 = (bf16[1024,2816]{1,0:T(8,128)(2,1)}, bf16[1024,2816]{1,0:T(8,128)(2,1)}, u32[]{:S(2)}, u32[]{:S(2)}) collective-permute-start(bf16[1024,2816]{1,0:T(8,128)(2,1)} %get-tuple-element.150), channel_id=1, source_target_pairs={{0,8},{4,12},{8,0},{12,4},{1,9},{5,13},{9,1},{13,5},{2,10},{6,14},... | collective-permute-start | bytes 17301512 | tf_op jit(solution)/shard_map/ppermute | solution.py:422
  896.4 13.9 collective-permute-start.21
  1006.9 6.6 collective-permute-start.23
  1006.9 39.5 %collective-permute-start.25 = (bf16[512,2048]{1,0:T(8,128)(2,1)}, bf16[512,2048]{1,0:T(8,128)(2,1)}, u32[]{:S(2)}, u32[]{:S(2)}) collective-permute-start(bf16[512,2048]{1,0:T(8,128)(2,1)} %convolution_convert_fusion.8), channel_id=1, source_target_pairs={{0,4},{4,0},{8,12},{12,8},{1,5},{5,1},{9,13},{13,9},{2,6},{6,2},{1... | collective-permute-start | bytes 6291464 | tf_op jit(solution)/shard_map/ppermute | solution.py:451
  1032.7 53.2 %collective-permute-start.24 = (bf16[512,2048]{1,0:T(8,128)(2,1)}, bf16[512,2048]{1,0:T(8,128)(2,1)S(1)}, u32[]{:S(2)}, u32[]{:S(2)}) collective-permute-start(bf16[512,2048]{1,0:T(8,128)(2,1)} %fusion.34), channel_id=1, source_target_pairs={{16,0},{17,1},{18,2},{19,3},{20,4},{21,5},{22,6},{23,7},{24,8},{25... | collective-permute-start | bytes 6291464 | tf_op jit(solution)/shard_map/ppermute | solution.py:390
  1086.4 5.1 collective-permute-start.27
  1090.0 35.0 %collective-permute-start.26 = (bf16[512,1024]{1,0:T(8,128)(2,1)}, bf16[512,1024]{1,0:T(8,128)(2,1)}, u32[]{:S(2)}, u32[]{:S(2)}) collective-permute-start(bf16[512,1024]{1,0:T(8,128)(2,1)} %get-tuple-element.187), channel_id=1, source_target_pairs={{0,8},{4,12},{8,0},{12,4},{1,9},{5,13},{9,1},{13,5},{2,10},{6,14},... | collective-permute-start | bytes 3145736 | tf_op jit(solution)/shard_map/ppermute | solution.py:422
  1091.5 64.0 %collective-permute-start.29 = (bf16[512,1024]{1,0:T(8,128)(2,1)S(1)}, bf16[512,1024]{1,0:T(8,128)(2,1)}, u32[]{:S(2)}, u32[]{:S(2)}) collective-permute-start(bf16[512,1024]{1,0:T(8,128)(2,1)S(1)} %get-tuple-element.186), channel_id=1, source_target_pairs={{0,4},{4,0},{8,12},{12,8},{1,5},{5,1},{9,13},{13,9},{2,6},{6,2},{1... | collective-permute-start | bytes 3145736 | tf_op jit(solution)/shard_map/ppermute | solution.py:375
  1128.7 65.2 %collective-permute-start.28 = (bf16[1408,1024]{1,0:T(8,128)(2,1)}, bf16[1408,1024]{1,0:T(8,128)(2,1)}, u32[]{:S(2)}, u32[]{:S(2)}) collective-permute-start(bf16[1408,1024]{1,0:T(8,128)(2,1)} %get-tuple-element.169), channel_id=1, source_target_pairs={{0,8},{4,12},{8,0},{12,4},{1,9},{5,13},{9,1},{13,5},{2,10},{6,14},... | collective-permute-start | bytes 8650760 | tf_op jit(solution)/shard_map/ppermute | solution.py:422
  1132.7 22.8 %collective-permute-start.30 = (bf16[512,1024]{1,0:T(8,128)(2,1)}, bf16[512,1024]{1,0:T(8,128)(2,1)S(1)}, u32[]{:S(2)}, u32[]{:S(2)}) collective-permute-start(bf16[512,1024]{1,0:T(8,128)(2,1)} %collective-permute-done.26), channel_id=1, source_target_pairs={{0,4},{4,0},{8,12},{12,8},{1,5},{5,1},{9,13},{13,9},{2,6},{6,2},{1... | collective-permute-start | bytes 3145736 | tf_op jit(solution)/shard_map/ppermute | solution.py:375
  1193.9 400.4 %reduce-scatter.19.cloned.1.call-start = ((), (), s32[]{:S(2)}) async-start(), calls=%async_computation.19 | async-start | bytes 7208960
  1194.0 4.4 collective-permute-start.32
  1194.1 65.2 %collective-permute-start.31 = (bf16[1408,1024]{1,0:T(8,128)(2,1)}, bf16[1408,1024]{1,0:T(8,128)(2,1)}, u32[]{:S(2)}, u32[]{:S(2)}) collective-permute-start(bf16[1408,1024]{1,0:T(8,128)(2,1)} %get-tuple-element.87), channel_id=1, source_target_pairs={{0,8},{4,12},{8,0},{12,4},{1,9},{5,13},{9,1},{13,5},{2,10},{6,14},... | collective-permute-start | bytes 8650760 | tf_op jit(solution)/shard_map/ppermute | solution.py:422
  1221.4 43.7 %collective-permute-start.33 = (bf16[512,2048]{1,0:T(8,128)(2,1)S(1)}, bf16[512,2048]{1,0:T(8,128)(2,1)S(1)}, u32[]{:S(2)}, u32[]{:S(2)}) collective-permute-start(bf16[512,2048]{1,0:T(8,128)(2,1)S(1)} %get-tuple-element.140), channel_id=1, source_target_pairs={{0,4},{4,0},{8,12},{12,8},{1,5},{5,1},{9,13},{13,9},{2,6},{6,2},{1... | collective-permute-start | bytes 6291464 | tf_op jit(solution)/shard_map/ppermute | solution.py:375
  1279.3 317.8 %reduce-scatter.21.cloned.1.call-start = ((), (), s32[]{:S(2)}) async-start(), calls=%async_computation.20 | async-start | bytes 7208960
  1279.4 64.5 %collective-permute-start.34 = (bf16[1408,1024]{1,0:T(8,128)(2,1)}, bf16[1408,1024]{1,0:T(8,128)(2,1)}, u32[]{:S(2)}, u32[]{:S(2)}) collective-permute-start(bf16[1408,1024]{1,0:T(8,128)(2,1)} %convolution_convert_fusion.5), channel_id=1, source_target_pairs={{0,8},{4,12},{8,0},{12,4},{1,9},{5,13},{9,1},{13,5},{2,10},{6,14},... | collective-permute-start | bytes 8650760 | tf_op jit(solution)/shard_map/ppermute | solution.py:422
  1343.9 63.3 %collective-permute-start.35 = (bf16[1408,1024]{1,0:T(8,128)(2,1)S(1)}, bf16[1408,1024]{1,0:T(8,128)(2,1)}, u32[]{:S(2)}, u32[]{:S(2)}) collective-permute-start(bf16[1408,1024]{1,0:T(8,128)(2,1)S(1)} %copy-done.67), channel_id=1, source_target_pairs={{0,8},{4,12},{8,0},{12,4},{1,9},{5,13},{9,1},{13,5},{2,10},{6,14},... | collective-permute-start | bytes 8650760 | tf_op jit(solution)/shard_map/ppermute | solution.py:422
  1420.6 271.1 %reduce-scatter.13.cloned.1.call-start = ((), (), s32[]{:S(2)}) async-start(), calls=%async_computation.15 | async-start | bytes 3932160 | tf_op jit(solution)/shard_map/reduce_scatter | solution.py:425
  1430.7 67.3 %collective-permute-start.36 = (bf16[1536,1024]{1,0:T(8,128)(2,1)}, bf16[1536,1024]{1,0:T(8,128)(2,1)}, u32[]{:S(2)}, u32[]{:S(2)}) collective-permute-start(bf16[1536,1024]{1,0:T(8,128)(2,1)} %convolution_convert_fusion.3), channel_id=1, source_target_pairs={{0,8},{4,12},{8,0},{12,4},{1,9},{5,13},{9,1},{13,5},{2,10},{6,14},... | collective-permute-start | bytes 9437192 | tf_op jit(solution)/shard_map/ppermute | solution.py:422
  1498.0 14.9 collective-permute-start.38
  1505.5 71.5 %collective-permute-start.37 = (bf16[1536,1024]{1,0:T(8,128)(2,1)}, bf16[1536,1024]{1,0:T(8,128)(2,1)}, u32[]{:S(2)}, u32[]{:S(2)}) collective-permute-start(bf16[1536,1024]{1,0:T(8,128)(2,1)} %convolution_convert_fusion.2), channel_id=1, source_target_pairs={{0,8},{4,12},{8,0},{12,4},{1,9},{5,13},{9,1},{13,5},{2,10},{6,14},... | collective-permute-start | bytes 9437192 | tf_op jit(solution)/shard_map/ppermute | solution.py:422
  1532.8 44.2 %all-to-all-start.1 = ((f32[16,7,128]{2,1,0:T(8,128)}), f32[16,7,128]{2,1,0:T(8,128)S(1)}, u32[]{:S(2)}, u32[]{:S(2)}) async-start(f32[16,7,128]{2,1,0:T(8,128)} %copy.120), calls=%async_computation.1 | async-start | bytes 131072 | tf_op jit(solution)/shard_map/all_to_all | solution.py:485
  1536.3 155.4 %reduce-scatter.15.cloned.1.call-start = ((), (), s32[]{:S(2)}) async-start(), calls=%async_computation.16 | async-start | bytes 3932160 | tf_op jit(solution)/shard_map/reduce_scatter | solution.py:425
  1585.8 99.4 %all-to-all-start.2 = ((bf16[16,32,2048]{2,1,0:T(8,128)(2,1)}), bf16[16,32,2048]{2,1,0:T(8,128)(2,1)S(1)}, u32[]{:S(2)}, u32[]{:S(2)}) async-start(bf16[16,32,2048]{2,1,0:T(8,128)(2,1)} %bitcast.72), calls=%async_computation.3 | async-start | bytes 4194304 | tf_op jit(solution)/shard_map/all_to_all | solution.py:549
  1589.5 145.3 %reduce-scatter.17.cloned.1.call-start = ((), (), s32[]{:S(2)}) async-start(), calls=%async_computation.17 | async-start | bytes 2621440 | tf_op jit(solution)/shard_map/reduce_scatter | solution.py:425
  1589.9 68.8 %collective-permute-start.39 = (bf16[1024,1024]{1,0:T(8,128)(2,1)}, bf16[1024,1024]{1,0:T(8,128)(2,1)}, u32[]{:S(2)}, u32[]{:S(2)}) collective-permute-start(bf16[1024,1024]{1,0:T(8,128)(2,1)} %fusion.127), channel_id=1, source_target_pairs={{0,8},{4,12},{8,0},{12,4},{1,9},{5,13},{9,1},{13,5},{2,10},{6,14},... | collective-permute-start | bytes 6291464 | tf_op jit(solution)/shard_map/ppermute | solution.py:422
  1594.3 5.4 collective-permute-start.40
  1596.6 7.6 collective-permute-start.41
  1599.7 11.9 collective-permute-start.42
  1696.6 42.4 %collective-permute-start.43 = (bf16[3,256,512]{1,2,0:T(8,128)(2,1)}, bf16[3,256,512]{1,2,0:T(8,128)(2,1)}, u32[]{:S(2)}, u32[]{:S(2)}) collective-permute-start(bf16[3,256,512]{1,2,0:T(8,128)(2,1)} %copy.143), channel_id=1, source_target_pairs={{0,4},{4,0},{8,12},{12,8},{1,5},{5,1},{9,13},{13,9},{2,6},{6,2},{1... | collective-permute-start | bytes 2359304 | tf_op jit(solution)/shard_map/ppermute | solution.py:470
  1735.9 6.7 collective-permute-start.44
  (86 other events, 1438.1 us)
Sparse Core Ops, SparseCore 0:
  10.2 66.5 all-gather.17
  78.9 126.1 all-gather.7
  206.7 105.4 all-gather.9
  313.6 105.0 all-gather.11
  420.6 57.4 all-gather.13
  479.6 57.8 all-gather.15
  1194.0 98.6 reduce-scatter.10
  1295.0 102.7 reduce-scatter.18
  1420.7 98.9 reduce-scatter.20
  1521.9 61.7 reduce-scatter.12
  1586.1 94.1 reduce-scatter.14
  1691.8 42.9 reduce-scatter.16
